TPU v7x, 32 devices: a whole 2x2x4 slice. The times are simulated.
32 devices in a mesh: row: 8 (over y, x, core), col: 4 (over z).
Axes of the slice: x: 2, y: 2, z: 4, core: 2. Of those that a mesh axis runs over, the one named last changes fastest.
Arguments:
- amplitudes: bfloat16 [16384, 2048], P('row', 'col'), may hold values from -6 to 6
- couplings: bfloat16 [2048, 16384], P('row', 'col'), may hold values from -0.125 to 0.125
- ladder: bfloat16 [1024, 1024], replicated, may hold values from -0.1875 to 0.1875
Outputs:
- update: bfloat16 [512, 512, 1024], P('row', 'col')
All inputs are finite; a program needn't handle non-finite values.
Results may differ from a plain program's by a relative error of at most 0.0049.
Values may be sent and summed in bfloat16 or wider, within the bound.
No kernel may reach another device: no remote copies, remote signals or barrier semaphores. Data moves between devices by JAX's collectives and lax.ppermute only.
A program may use at most 128 MiB of HBM per device.

v0:
```python
import jax
import jax.numpy as jnp
from jax import lax
from jax.sharding import PartitionSpec as P

V = 512


def local(amplitudes, couplings, ladder):
    row_count = amplitudes.shape[0]
    col_count = couplings.shape[1]
    panel_t = lax.all_gather(amplitudes, "col", axis=1, tiled=True)
    cycle = jnp.dot(
        panel_t,
        lax.all_gather(couplings, "row", axis=0, tiled=True),
        preferred_element_type=jnp.float32,
    )
    cycle = cycle.astype(jnp.bfloat16)
    i_local = row_count // V
    j_local = col_count // V
    blocks = cycle.reshape(i_local, V, j_local, V)
    moved = lax.all_to_all(
        lax.all_to_all(blocks, "col", split_axis=3, concat_axis=2, tiled=True),
        "row",
        split_axis=1,
        concat_axis=0,
        tiled=True,
    )
    occupied = moved.shape[0]
    a_local = moved.shape[1]
    b_local = moved.shape[3]
    pairs = jnp.transpose(moved, (1, 3, 0, 2)).reshape(a_local * b_local, occupied * occupied)
    mixed = lax.dot_general(
        pairs, ladder, (((1,), (1,)), ((), ())), preferred_element_type=jnp.float32
    )
    total = mixed + pairs.astype(jnp.float32)
    return total.astype(jnp.bfloat16).reshape(a_local, b_local, occupied * occupied)


def solution(mesh):
    in_specs = (P("row", "col"), P("row", "col"), P())
    out_specs = P("row", "col", None)
    return jax.shard_map(local, mesh=mesh, in_specs=in_specs, out_specs=out_specs, check_vma=False)
```

profile of v0, /device:TPU:0, one launch (start us, length us, event | category | flops | bytes accessed | tf_op | source)
XLA Modules:
  0.0 1197.0 jit_solution(7208904001370338674)
XLA Ops:
  6.5 0.0 copy-start
  6.5 0.0 all-gather.3.cloned.1.call-start
  6.5 0.7 all-gather.3.cloned.1.call-update
  7.3 0.0 all-gather.5.cloned.1.call-start
  7.3 0.7 all-gather.5.cloned.1.call-update
  8.0 153.3 %all-gather.3.cloned.1.call-done = bf16[2048,2048]{1,0:T(8,128)(2,1)} async-done(((bf16[2048,512]{1,0:T(8,128)(2,1)}), bf16[2048,2048]{1,0:T(8,128)(2,1)}) %all-gather.3.cloned.1.call-update) | async-done | bytes 8388624 | tf_op jit(solution)/shard_map/all_gather | solution.py:12
  161.3 90.0 %all-gather.5.cloned.1.call-done = bf16[2048,4096]{1,0:T(8,128)(2,1)} async-done(((bf16[256,4096]{1,0:T(8,128)(2,1)}), bf16[2048,4096]{1,0:T(8,128)(2,1)}) %all-gather.5.cloned.1.call-update) | async-done | bytes 16777232 | tf_op jit(solution)/shard_map/all_gather | solution.py:15
  251.3 40.3 %convolution_convert_fusion = bf16[2048,4096]{1,0:T(8,128)(2,1)S(1)} fusion(bf16[2048,2048]{1,0:T(8,128)(2,1)} %all-gather.3.cloned.1.call-done, bf16[2048,4096]{1,0:T(8,128)(2,1)} %all-gather.5.cloned.1.call-done), kind=kOutput, calls=%fused_computation.2 | convolution fusion | flops 34368126976 | bytes 41943040 | tf_op jit(solution)/shard_map/dot_general | solution.py:13
  291.6 10.4 copy.21
  302.0 30.7 %copy.14 = bf16[4,512,8,512]{1,2,0,3:T(8,128)(2,1)} copy(bf16[4,512,8,512]{3,2,1,0:T(8,128)(2,1)} %bitcast.27) | data formatting | bytes 33554432 | tf_op jit(solution)/shard_map/reshape | solution.py:21
  332.8 374.6 %all_to_all.36 = bf16[4,512,8,512]{1,2,0,3:T(8,128)(2,1)} all-to-all(bf16[4,512,8,512]{1,2,0,3:T(8,128)(2,1)} %copy.14), channel_id=1, replica_groups=mesh['row'=8,'col'=4] {'col'}, dimensions={3} | all-to-all | bytes 33554432 | tf_op jit(solution)/shard_map/all_to_all | solution.py:23
  707.4 30.1 %copy.15 = bf16[4,512,4,8,128]{4,3,2,0,1:T(8,128)(2,1)} copy(bf16[4,512,4,8,128]{1,3,0,4,2:T(8,128)(2,1)} %bitcast.28) | data formatting | bytes 33554432 | tf_op jit(solution)/shard_map/all_to_all | solution.py:23
  737.4 188.0 %all_to_all.37 = bf16[4,512,32,128]{3,2,0,1:T(8,128)(2,1)S(1)} all-to-all(bf16[4,512,32,128]{3,2,0,1:T(8,128)(2,1)} %bitcast.29), channel_id=1, replica_groups=mesh['row'=8,'col'=4] {'row'}, dimensions={1} | all-to-all | bytes 33554432 | tf_op jit(solution)/shard_map/all_to_all | solution.py:22
  925.5 2.4 copy.17
  927.9 19.2 %copy.18 = bf16[64,128,32,32]{1,0,3,2:T(8,128)(2,1)S(1)} copy(bf16[64,128,32,32]{1,3,0,2:T(8,128)(2,1)S(1)} %bitcast.31) | data formatting | bytes 33554432 | tf_op jit(solution)/shard_map/transpose | solution.py:32
  947.1 0.0 copy-start.1
  947.2 18.4 %copy.25 = bf16[128,8,64,128]{3,1,2,0:T(8,128)(2,1)} copy(bf16[128,8,64,128]{3,2,1,0:T(8,128)(2,1)S(1)} %bitcast.25) | data formatting | bytes 33554432
  965.6 0.0 copy-done.1
  965.6 22.4 %copy.19 = bf16[8192,1024]{1,0:T(8,128)(2,1)} copy(bf16[8192,1024]{0,1:T(8,128)(2,1)} %bitcast.32) | data formatting | bytes 33554432 | tf_op jit(solution)/shard_map/reshape | solution.py:32
  988.0 0.0 copy-done
  988.0 201.9 %add_convert_fusion = bf16[8192,1024]{1,0:T(8,128)(2,1)} fusion(bf16[8192,1024]{1,0:T(8,128)(2,1)} %copy.19, bf16[1024,1024]{1,0:T(8,128)(2,1)S(1)} %copy-done, bf16[128,8,64,128]{3,2,1,0:T(8,128)(2,1)} %bitcast.26), kind=kOutput, calls=%fused_computation | convolution fusion | flops 17205035008 | bytes 52428800 | tf_op jit(solution)/shard_map/dot_general | solution.py:33
Async XLA Ops:
  6.5 981.4 %copy-start = (bf16[1024,1024]{1,0:T(8,128)(2,1)S(1)}, bf16[1024,1024]{1,0:T(8,128)(2,1)}, u32[]{:S(2)}) copy-start(bf16[1024,1024]{1,0:T(8,128)(2,1)} %param.5) | copy-start | bytes 6291460
  6.5 154.8 %all-gather.3.cloned.1.call-start = ((), (), s32[]{:S(2)}) async-start(), calls=%async_computation.2 | async-start | bytes 10485760 | tf_op jit(solution)/shard_map/all_gather | solution.py:12
  7.3 244.0 %all-gather.5.cloned.1.call-start = ((), (), s32[]{:S(2)}) async-start(), calls=%async_computation.3 | async-start | bytes 18874368 | tf_op jit(solution)/shard_map/all_gather | solution.py:15
  947.1 18.5 %copy-start.1 = (bf16[64,128,32,32]{1,0,3,2:T(8,128)(2,1)}, bf16[64,128,32,32]{1,0,3,2:T(8,128)(2,1)S(1)}, u32[]{:S(2)}) copy-start(bf16[64,128,32,32]{1,0,3,2:T(8,128)(2,1)S(1)} %copy.18) | copy-start | bytes 50331652
Sparse Core Ops, SparseCore 0:
  8.9 152.3 all-gather.2
  163.2 88.0 all-gather.4
where the time goes:
time: 1210 us; the launch traced here: 1200 us
  blocking collectives  563 us (47%)
  waiting for transfers between devices  245 us (20%)
  matrix products  242 us (20%)
  local copies, waits for them, and re-layouts  134 us (11%)
  between operations  13.7 us (1%)
    all_to_all x1, blocking collectives, local(): lax.all_to_all(blocks, 'col', split_axis=3, concat_axis=2, tiled=True)  375 us
    dot_general x1, matrix products, local(): lax.dot_general(pairs, ladder, (((1,), (1,)), ((), ())), preferred_elemen...  202 us
    all_to_all x1, blocking collectives, local(): lax.all_to_all(lax.all_to_all(blocks, 'col', split_axis=3, concat_axis=2,...  188 us
    all_gather x1, waiting for transfers between devices, local(): panel_t = lax.all_gather(amplitudes, 'col', axis=1, tiled=True)  153 us
    all_gather x1, waiting for transfers between devices, local(): lax.all_gather(couplings, 'row', axis=0, tiled=True)  90 us
    dot_general x1, matrix products, local(): jnp.dot(panel_t, lax.all_gather(couplings, 'row', axis=0, tiled=True), pr...  40.3 us
    reshape x1, local copies, waits for them, and re-layouts, local(): blocks = cycle.reshape(i_local, V, j_local, V)  30.7 us
    all_to_all x1, local copies, waits for them, and re-layouts, local(): lax.all_to_all(blocks, 'col', split_axis=3, concat_axis=2, tiled=True)  30.1 us
  transfers between devices with their start and end apart: 2, of which 2 were waited for; matrix products, arithmetic and copies ran while one was open for 0% of the time, Pallas kernels for 0%

commit v1 on v0

v1 whole, which is shorter than its diff:
```python
import functools

import jax
import jax.numpy as jnp
from jax import lax
from jax.experimental import pallas as pl
from jax.experimental.pallas import tpu as pltpu
from jax.sharding import PartitionSpec as P

V = 512
GROUP = 16
STEP_J = 8
STEP_A = 4


def chunk_kernel(own, *refs, parts, occupied, b_local, steps_w):
    t_refs = refs[:parts]
    w_ref, ladder_ref, out_ref, t_all, pairs, lhs = (
        refs[parts], refs[parts + 1], *refs[-4:])
    step = pl.program_id(0)
    depth = t_refs[0].shape[1]
    count = occupied * occupied

    @pl.when(step == 0)
    def _():
        for s in range(parts):
            block = lax.rem(own[0] - s + parts, parts)
            t_all[:, pl.ds(pl.multiple_of(block * depth, depth), depth)] = t_refs[s][...]

    @pl.when(step < steps_w)
    def _():
        per_part = occupied // parts
        first = step * STEP_J
        shift = first // per_part
        j0 = lax.rem(own[0] - shift + parts, parts) * per_part + lax.rem(first, per_part)
        wide = 256 // b_local

        @pl.loop(0, STEP_J // wide)
        def _(tile):
            cols = pl.ds(pl.multiple_of(tile * 256, 256), 256)
            acc = jnp.dot(t_all[...], w_ref[:, cols], preferred_element_type=jnp.float32)
            for k in range(wide):
                j = j0 + tile * wide + k
                for i in range(occupied):
                    for h in range(GROUP // 8):
                        row = i * GROUP + h * 8
                        pairs[pl.ds(h * 8 * count + i * occupied + j, 8, stride=count), :] = (
                            acc[row:row + 8, k * b_local:(k + 1) * b_local])

    @pl.when(step >= steps_w)
    def _():
        a0 = (step - steps_w) * STEP_A
        for k in range(STEP_A):
            rows = pl.ds(pl.multiple_of((a0 + k) * count, count), count)
            lhs[k * b_local:(k + 1) * b_local, :] = pairs[rows, :].astype(jnp.bfloat16).T
        for m in range(count // 256):
            cols = slice(m * 256, (m + 1) * 256)
            mixed = jnp.dot(lhs[...], ladder_ref[:, cols], preferred_element_type=jnp.float32)
            total = (mixed + lhs[:, cols].astype(jnp.float32)).astype(jnp.bfloat16)
            out_ref[:, :, cols] = total.reshape(STEP_A, b_local, 256)


def chunk_update(own, pieces, panel_w, ladder_t, out, q, a_local, b_local, occupied):
    parts = len(pieces)
    rows, depth = pieces[0].shape
    count = occupied * occupied
    steps_w = occupied // STEP_J
    steps_a = GROUP // STEP_A
    k_all = panel_w.shape[0]
    whole = lambda s, own: (0, 0)
    in_specs = [pl.BlockSpec((rows, depth), whole, pipeline_mode=pl.Buffered(1))] * parts
    in_specs.append(pl.BlockSpec((k_all, STEP_J * b_local), lambda s, own: (0, jnp.minimum(s, steps_w - 1))))
    in_specs.append(pl.BlockSpec((count, count), whole, pipeline_mode=pl.Buffered(1)))
    args = [own, *pieces, panel_w, ladder_t]
    aliases = {}
    if out is not None:
        in_specs.append(pl.BlockSpec(memory_space=pl.ANY))
        aliases = {len(args): 0}
        args.append(out)
    flops = 2 * rows * k_all * occupied * b_local + 2 * GROUP * b_local * count * count
    return pl.pallas_call(
        functools.partial(chunk_kernel, parts=parts, occupied=occupied, b_local=b_local, steps_w=steps_w),
        out_shape=jax.ShapeDtypeStruct((a_local, b_local, count), jnp.bfloat16),
        grid_spec=pltpu.PrefetchScalarGridSpec(
            num_scalar_prefetch=1,
            grid=(steps_w + steps_a,),
            in_specs=in_specs,
            out_specs=pl.BlockSpec(
                (STEP_A, b_local, count),
                lambda s, own: (q * steps_a + jnp.maximum(s - steps_w, 0), 0, 0)),
            scratch_shapes=[
                pltpu.VMEM((rows, k_all), jnp.bfloat16),
                pltpu.VMEM((GROUP * count, b_local), jnp.float32),
                pltpu.VMEM((STEP_A * b_local, count), jnp.bfloat16),
            ],
        ),
        input_output_aliases=aliases,
        compiler_params=pltpu.CompilerParams(vmem_limit_bytes=48 * 1024 * 1024),
        cost_estimate=pl.CostEstimate(
            flops=flops, bytes_accessed=2 * (panel_w.size + count * count + rows * k_all + GROUP * b_local * count),
            transcendentals=0),
    )(*args)


def plain_update(own, pieces, panel_w, ladder, b_local, occupied):
    parts = len(pieces)
    order = lax.rem(own - jnp.arange(parts) + parts, parts)
    panel_t = jnp.stack(pieces, 1)[:, jnp.argsort(order)].reshape(pieces[0].shape[0], -1)
    cycle = jnp.dot(panel_t, panel_w, preferred_element_type=jnp.float32).astype(jnp.bfloat16)
    cycle = cycle.reshape(occupied, -1, parts, occupied // parts, b_local)[:, :, jnp.argsort(order)]
    cycle = cycle.reshape(occupied, -1, occupied, b_local)
    a_count = cycle.shape[1]
    pairs = jnp.transpose(cycle, (1, 3, 0, 2)).reshape(a_count * b_local, occupied * occupied)
    mixed = lax.dot_general(pairs, ladder, (((1,), (1,)), ((), ())), preferred_element_type=jnp.float32)
    total = (mixed + pairs.astype(jnp.float32)).astype(jnp.bfloat16)
    return total.reshape(a_count, b_local, occupied * occupied)


def local(rows, cols, amplitudes, couplings, ladder):
    depth = amplitudes.shape[1]
    i_local = amplitudes.shape[0] // V
    j_local = couplings.shape[1] // V
    occupied = i_local * rows
    a_local, b_local = V // rows, V // cols
    own = lax.axis_index("col")

    split = couplings.reshape(couplings.shape[0], j_local, cols, b_local)
    arrived = []
    for s in range(cols):
        to = lax.rem(own + s, cols)
        part = lax.dynamic_slice_in_dim(split, to, 1, axis=2)
        part = part.reshape(couplings.shape[0], j_local * b_local)
        if s:
            part = lax.ppermute(part, "col", [(c, (c + s) % cols) for c in range(cols)])
        arrived.append(part)
    panel_w = lax.all_gather(jnp.concatenate(arrived, axis=1), "row", axis=0, tiled=True)

    chunks = a_local // GROUP
    blocks = amplitudes.reshape(i_local, rows, chunks, GROUP, depth).transpose(1, 2, 0, 3, 4)
    blocks = lax.all_to_all(blocks, "row", split_axis=0, concat_axis=0, tiled=True)
    ring = [(c, (c + 1) % cols) for c in range(cols)]
    pieces = []
    for q in range(chunks):
        held = blocks[:, q].reshape(occupied * GROUP, depth)
        got = [held]
        for _ in range(cols - 1):
            held = lax.ppermute(held, "col", ring)
            got.append(held)
        pieces.append(got)

    if b_local % 128 or 256 % b_local or depth % 128 or (occupied // cols) % STEP_J:
        return jnp.concatenate(
            [plain_update(own, got, panel_w, ladder, b_local, occupied) for got in pieces], axis=0)
    ladder_t = ladder.T
    out = None
    for q in range(chunks):
        out = chunk_update(own.reshape(1), pieces[q], panel_w, ladder_t, out, q, a_local, b_local, occupied)
    return out


def solution(mesh):
    in_specs = (P("row", "col"), P("row", "col"), P())
    out_specs = P("row", "col", None)
    body = functools.partial(local, mesh.shape["row"], mesh.shape["col"])
    return jax.shard_map(body, mesh=mesh, in_specs=in_specs, out_specs=out_specs, check_vma=False)
```

time: 1210 us -> 341 us (0.28); the launches traced: 1200 us -> 341 us
  blocking collectives: 563 us -> 39.2 us
  matrix products: 242 us -> 0 us
  waiting for transfers between devices: 245 us -> 114 us
  local copies, waits for them, and re-layouts: 134 us -> 25.8 us
  Pallas kernels: 0 us -> 102 us
  starting transfers between devices: 0.04 us -> 45 us
    all_to_all x2 -> x1, blocking collectives: 563 us -> 39.2 us  [local(): lax.all_to_all(blocks, 'row', split_axis=0, concat_axis=0, tiled=True)]
    all_gather x2 -> x1, waiting for transfers between devices: 243 us -> 0.01 us  [local(): lax.all_gather(jnp.concatenate(arrived, axis=1), 'row', axis=0, tiled=True)]
    dot_general x2 -> x0, matrix products: 242 us -> none  [the longest x1 202 us: local(): lax.dot_general(pairs, ladder, (((1,), (1,)), ((), ())), preferred_elemen...]
    ppermute x0 -> x15, waiting for transfers between devices: none -> 114 us  [the longest x12 81.8 us: local(): held = lax.ppermute(held, 'col', ring)]
    pallas_call x0 -> x4, Pallas kernels: none -> 102 us  [chunk_update(): pl.pallas_call(functools.partial(chunk_kernel, parts=parts, occupied=occu...]
    reshape x2 -> x1, local copies, waits for them, and re-layouts: 53.1 us -> 3.23 us  [local(): split = couplings.reshape(couplings.shape[0], j_local, cols, b_local)]
    ppermute x0 -> x15, starting transfers between devices: none -> 45 us  [the longest x12 37.9 us: local(): held = lax.ppermute(held, 'col', ring)]
    all_to_all x2 -> x0, local copies, waits for them, and re-layouts: 32.5 us -> none  [the longest x1 30.1 us: local(): lax.all_to_all(blocks, 'col', split_axis=3, concat_axis=2, tiled=True)]
  transfers between devices with their start and end apart: 2 -> 16, of which waited for: 2 -> 11; matrix products, arithmetic and copies ran while one was open for 0% -> 1% of each run, Pallas kernels for 0% -> 22%
where the time goes in v1:
time: 341 us
  waiting for transfers between devices  114 us (33%)
  Pallas kernels  102 us (30%)
  starting transfers between devices  45 us (13%)
  blocking collectives  39.2 us (11%)
  local copies, waits for them, and re-layouts  25.8 us (8%)
  between operations  13.5 us (4%)
    pallas_call x4, Pallas kernels, chunk_update(): pl.pallas_call(functools.partial(chunk_kernel, parts=parts, occupied=occu...  102 us
    ppermute x12, waiting for transfers between devices, local(): held = lax.ppermute(held, 'col', ring)  81.8 us
    all_to_all x1, blocking collectives, local(): lax.all_to_all(blocks, 'row', split_axis=0, concat_axis=0, tiled=True)  39.2 us
    ppermute x12, starting transfers between devices, local(): held = lax.ppermute(held, 'col', ring)  37.9 us
    ppermute x3, waiting for transfers between devices, local(): part = lax.ppermute(part, 'col', [(c, (c + s) % cols) for c in range(cols)])  32.2 us
    dynamic_slice x1, local copies, waits for them, and re-layouts, local(): part = lax.dynamic_slice_in_dim(split, to, 1, axis=2)  12.9 us
    unnamed x19, local copies, waits for them, and re-layouts  9.29 us
    ppermute x3, starting transfers between devices, local(): part = lax.ppermute(part, 'col', [(c, (c + s) % cols) for c in range(cols)])  7.13 us
  transfers between devices with their start and end apart: 16, of which 11 were waited for; matrix products, arithmetic and copies ran while one was open for 1% of the time, Pallas kernels for 22%

profile of v1, /device:TPU:0, one launch (start us, length us, event | category | flops | bytes accessed | tf_op | source)
XLA Modules:
  0.0 340.6 jit_solution(11044482519265446248)
XLA Ops:
  6.5 0.0 all-gather.2.cloned.1.call-start
  6.5 3.2 reshape.26
  9.8 12.9 %dynamic-slice_reduce_fusion.3 = (bf16[256,8,128]{2,1,0:T(8,128)(2,1)S(1)}, bf16[256,8,128]{2,1,0:T(8,128)(2,1)S(1)}, bf16[256,8,128]{2,1,0:T(8,128)(2,1)S(1)}, bf16[256,8,128]{2,1,0:T(8,128)(2,1)S(1)}) fusion(bf16[256,8,4,128]{3,2,1,0:T(4,128)(2,1)S(1)} %reshape.26, s32[]{:T(128)S(6)} %select_n.12, s32[]{:T(128)S(6)} %select_n.14, s32[]{:T(128)S(6)} %select_n.13, ...), kind=kLoop, calls=%fused_computation.4 | loop fusion | bytes 4194320 | tf_op jit(solution)/shard_map/dynamic_slice | solution.py:131
  22.7 0.1 copy.38
  22.8 3.1 collective-permute-start.3
  25.9 0.1 copy.37
  26.0 2.7 collective-permute-start.4
  28.6 0.1 copy.36
  28.7 1.4 collective-permute-start.5
  30.1 0.1 copy.39
  30.2 10.6 %collective-permute-done.3 = bf16[256,1024]{1,0:T(8,128)(2,1)S(1)} collective-permute-done((bf16[256,1024]{1,0:T(8,128)(2,1)S(1)}, bf16[256,1024]{1,0:T(8,128)(2,1)S(1)}, u32[]{:S(2)}, u32[]{:S(2)}) %collective-permute-start.3) | collective-permute-done | bytes 524320 | tf_op jit(solution)/shard_map/ppermute | solution.py:134
  40.8 21.6 %collective-permute-done.4 = bf16[256,1024]{1,0:T(8,128)(2,1)S(1)} collective-permute-done((bf16[256,1024]{1,0:T(8,128)(2,1)S(1)}, bf16[256,1024]{1,0:T(8,128)(2,1)S(1)}, u32[]{:S(2)}, u32[]{:S(2)}) %collective-permute-start.4) | collective-permute-done | bytes 524320 | tf_op jit(solution)/shard_map/ppermute | solution.py:134
  62.4 0.0 collective-permute-done.5
  62.4 1.5 pad_maximum_fusion
  63.9 0.0 copy-start.6
  63.9 0.0 all-gather.2.cloned.1.call-update
  64.0 1.6 copy-done.6
  65.5 0.2 copy.18
  65.7 39.2 %all_to_all.5 = bf16[8,4,4,16,512]{4,3,2,1,0:T(8,128)(2,1)S(1)} all-to-all(bf16[8,4,4,16,512]{4,3,2,1,0:T(8,128)(2,1)S(1)} %copy.18), channel_id=1, replica_groups=mesh['row'=8,'col'=4] {'row'}, dimensions={0} | all-to-all | bytes 4194304 | tf_op jit(solution)/shard_map/all_to_all | solution.py:140
  104.9 0.2 fusion
  105.2 22.0 %collective-permute-start.12 = (bf16[512,512]{1,0:T(8,128)(2,1)S(1)}, bf16[512,512]{1,0:T(8,128)(2,1)S(1)}, u32[]{:S(2)}, u32[]{:S(2)}) collective-permute-start(bf16[512,512]{1,0:T(8,128)(2,1)S(1)} %bitcast.35), channel_id=1, source_target_pairs={{0,1},{1,2},{2,3},{3,0},{4,5},{5,6},{6,7},{7,4},{8,9},{9,10},{10,1... | collective-permute-start | bytes 1572872 | tf_op jit(solution)/shard_map/ppermute | solution.py:147
  127.1 0.0 copy-start.2
  127.1 0.8 copy-done.2
  127.9 0.0 collective-permute-start.9
  127.9 0.0 copy-start
  127.9 0.8 copy-done
  128.8 1.3 collective-permute-start.6
  130.1 0.0 collective-permute-start
  130.1 10.1 %collective-permute-done.12.refs_1_ = bf16[512,512]{1,0:T(8,128)(2,1)S(1)} collective-permute-done((bf16[512,512]{1,0:T(8,128)(2,1)S(1)}, bf16[512,512]{1,0:T(8,128)(2,1)S(1)}, u32[]{:S(2)}, u32[]{:S(2)}) %collective-permute-start.12) | collective-permute-done | bytes 524320 | tf_op jit(solution)/shard_map/ppermute | solution.py:147
  140.2 1.8 collective-permute-start.13
  142.0 0.0 copy-start.4
  142.0 0.8 copy-done.4
  142.8 8.7 %collective-permute-done.9.refs_1_ = bf16[512,512]{1,0:T(8,128)(2,1)} collective-permute-done((bf16[512,512]{1,0:T(8,128)(2,1)S(1)}, bf16[512,512]{1,0:T(8,128)(2,1)}, u32[]{:S(2)}, u32[]{:S(2)}) %collective-permute-start.9) | collective-permute-done | bytes 524320 | tf_op jit(solution)/shard_map/ppermute | solution.py:147
  151.5 1.8 collective-permute-start.10
  153.3 9.4 %collective-permute-done.6.refs_1_ = bf16[512,512]{1,0:T(8,128)(2,1)} collective-permute-done((bf16[512,512]{1,0:T(8,128)(2,1)S(1)}, bf16[512,512]{1,0:T(8,128)(2,1)}, u32[]{:S(2)}, u32[]{:S(2)}) %collective-permute-start.6) | collective-permute-done | bytes 524320 | tf_op jit(solution)/shard_map/ppermute | solution.py:147
  162.7 1.8 collective-permute-start.7
  164.6 9.4 %collective-permute-done.refs_1_ = bf16[512,512]{1,0:T(8,128)(2,1)} collective-permute-done((bf16[512,512]{1,0:T(8,128)(2,1)S(1)}, bf16[512,512]{1,0:T(8,128)(2,1)}, u32[]{:S(2)}, u32[]{:S(2)}) %collective-permute-start) | collective-permute-done | bytes 524320 | tf_op jit(solution)/shard_map/ppermute | solution.py:147
  174.0 1.8 collective-permute-start.1
  175.8 9.4 %collective-permute-done.13.refs_2_ = bf16[512,512]{1,0:T(8,128)(2,1)} collective-permute-done((bf16[512,512]{1,0:T(8,128)(2,1)S(1)}, bf16[512,512]{1,0:T(8,128)(2,1)}, u32[]{:S(2)}, u32[]{:S(2)}) %collective-permute-start.13) | collective-permute-done | bytes 524320 | tf_op jit(solution)/shard_map/ppermute | solution.py:147
  185.2 1.8 collective-permute-start.14
  187.0 2.9 copy.23
  189.9 6.6 %collective-permute-done.10.refs_2_ = bf16[512,512]{1,0:T(8,128)(2,1)} collective-permute-done((bf16[512,512]{1,0:T(8,128)(2,1)}, bf16[512,512]{1,0:T(8,128)(2,1)}, u32[]{:S(2)}, u32[]{:S(2)}) %collective-permute-start.10) | collective-permute-done | bytes 524320 | tf_op jit(solution)/shard_map/ppermute | solution.py:147
  196.5 1.8 collective-permute-start.11
  198.3 9.4 %collective-permute-done.7.refs_2_ = bf16[512,512]{1,0:T(8,128)(2,1)} collective-permute-done((bf16[512,512]{1,0:T(8,128)(2,1)}, bf16[512,512]{1,0:T(8,128)(2,1)}, u32[]{:S(2)}, u32[]{:S(2)}) %collective-permute-start.7) | collective-permute-done | bytes 524320 | tf_op jit(solution)/shard_map/ppermute | solution.py:147
  207.7 1.8 collective-permute-start.8
  209.5 9.4 %collective-permute-done.1.refs_2_ = bf16[512,512]{1,0:T(8,128)(2,1)} collective-permute-done((bf16[512,512]{1,0:T(8,128)(2,1)}, bf16[512,512]{1,0:T(8,128)(2,1)}, u32[]{:S(2)}, u32[]{:S(2)}) %collective-permute-start.1) | collective-permute-done | bytes 524320 | tf_op jit(solution)/shard_map/ppermute | solution.py:147
  218.9 1.8 collective-permute-start.2
  220.7 9.4 %collective-permute-done.14.refs_3_ = bf16[512,512]{1,0:T(8,128)(2,1)} collective-permute-done((bf16[512,512]{1,0:T(8,128)(2,1)}, bf16[512,512]{1,0:T(8,128)(2,1)}, u32[]{:S(2)}, u32[]{:S(2)}) %collective-permute-start.14) | collective-permute-done | bytes 524320 | tf_op jit(solution)/shard_map/ppermute | solution.py:147
  230.2 0.0 all-gather.2.cloned.1.call-done.refs_4_
  230.2 0.0 copy-start.3
  230.2 1.0 copy-done.3
  231.2 0.0 copy-start.5
  231.2 1.0 copy-done.5
  232.2 0.0 copy-start.1
  232.2 25.3 %shard_map.37.refs_6_ = bf16[64,128,1024]{2,1,0:T(8,128)(2,1)} custom-call(s32[1]{0:T(128)} %bitcast.own, bf16[512,512]{1,0:T(8,128)(2,1)S(1)} %bitcast.36, bf16[512,512]{1,0:T(8,128)(2,1)S(1)} %copy-done.5, bf16[512,512]{1,0:T(8,128)(2,1)} %collective-permute-done.13.refs_2_, bf16[512,512]{1,0:T(8,128)(2,1)} %collective-permute-done.14.refs_3_, ...), custom_call_target="tpu_custom_call" | custom-call | flops 12884901888 | bytes 25165824 | tf_op jit(solution)/shard_map/pallas_call | solution.py:81
  257.5 0.0 collective-permute-done.11.refs_3_
  257.5 0.0 copy-done.1
  257.5 25.4 %shard_map.38.refs_6_ = bf16[64,128,1024]{2,1,0:T(8,128)(2,1)} custom-call(s32[1]{0:T(128)} %bitcast.own, bf16[512,512]{1,0:T(8,128)(2,1)S(1)} %bitcast.34, bf16[512,512]{1,0:T(8,128)(2,1)} %collective-permute-done.9.refs_1_, bf16[512,512]{1,0:T(8,128)(2,1)} %collective-permute-done.10.refs_2_, ...), custom_call_target="tpu_custom_call", output_to_operand_aliasing={{}: (7, {})} | custom-call | flops 12884901888 | bytes 25165824 | tf_op jit(solution)/shard_map/pallas_call | solution.py:81
  283.0 0.0 collective-permute-done.8.refs_3_
  283.0 25.4 %shard_map.39.refs_6_ = bf16[64,128,1024]{2,1,0:T(8,128)(2,1)} custom-call(s32[1]{0:T(128)} %bitcast.own, bf16[512,512]{1,0:T(8,128)(2,1)S(1)} %bitcast.32, bf16[512,512]{1,0:T(8,128)(2,1)} %collective-permute-done.6.refs_1_, bf16[512,512]{1,0:T(8,128)(2,1)} %collective-permute-done.7.refs_2_, ...), custom_call_target="tpu_custom_call", output_to_operand_aliasing={{}: (7, {})} | custom-call | flops 12884901888 | bytes 25165824 | tf_op jit(solution)/shard_map/pallas_call | solution.py:81
  308.4 0.0 collective-permute-done.2.refs_3_
  308.4 25.4 %shard_map.40 = bf16[64,128,1024]{2,1,0:T(8,128)(2,1)} custom-call(s32[1]{0:T(128)} %bitcast.own, bf16[512,512]{1,0:T(8,128)(2,1)S(1)} %bitcast.30, bf16[512,512]{1,0:T(8,128)(2,1)} %collective-permute-done.refs_1_, bf16[512,512]{1,0:T(8,128)(2,1)} %collective-permute-done.1.refs_2_, ...), custom_call_target="tpu_custom_call", output_to_operand_aliasing={{}: (7, {})} | custom-call | flops 12884901888 | bytes 25165824 | tf_op jit(solution)/shard_map/pallas_call | solution.py:81
Async XLA Ops:
  6.5 223.6 %all-gather.2.cloned.1.call-start = ((), (), s32[]{:S(2)}) async-start(), calls=%async_computation.1 | async-start | bytes 18874368 | tf_op jit(solution)/shard_map/all_gather | solution.py:136
  22.8 18.0 %collective-permute-start.3 = (bf16[256,1024]{1,0:T(8,128)(2,1)S(1)}, bf16[256,1024]{1,0:T(8,128)(2,1)S(1)}, u32[]{:S(2)}, u32[]{:S(2)}) collective-permute-start(bf16[256,1024]{1,0:T(8,128)(2,1)S(1)} %bitcast.43), channel_id=1, source_target_pairs={{0,1},{1,2},{2,3},{3,0},{4,5},{5,6},{6,7},{7,4},{8,9},{9,10},{10,1... | collective-permute-start | bytes 1572872 | tf_op jit(solution)/shard_map/ppermute | solution.py:134
  26.0 36.5 %collective-permute-start.4 = (bf16[256,1024]{1,0:T(8,128)(2,1)S(1)}, bf16[256,1024]{1,0:T(8,128)(2,1)S(1)}, u32[]{:S(2)}, u32[]{:S(2)}) collective-permute-start(bf16[256,1024]{1,0:T(8,128)(2,1)S(1)} %bitcast.44), channel_id=1, source_target_pairs={{0,2},{1,3},{2,0},{3,1},{4,6},{5,7},{6,4},{7,5},{8,10},{9,11},{10,... | collective-permute-start | bytes 1572872 | tf_op jit(solution)/shard_map/ppermute | solution.py:134
  28.7 33.7 %collective-permute-start.5 = (bf16[256,1024]{1,0:T(8,128)(2,1)S(1)}, bf16[256,1024]{1,0:T(8,128)(2,1)S(1)}, u32[]{:S(2)}, u32[]{:S(2)}) collective-permute-start(bf16[256,1024]{1,0:T(8,128)(2,1)S(1)} %bitcast.45), channel_id=1, source_target_pairs={{0,3},{1,0},{2,1},{3,2},{4,7},{5,4},{6,5},{7,6},{8,11},{9,8},{10,9... | collective-permute-start | bytes 1572872 | tf_op jit(solution)/shard_map/ppermute | solution.py:134
  63.9 1.6 copy-start.6
  105.2 35.0 %collective-permute-start.12 = (bf16[512,512]{1,0:T(8,128)(2,1)S(1)}, bf16[512,512]{1,0:T(8,128)(2,1)S(1)}, u32[]{:S(2)}, u32[]{:S(2)}) collective-permute-start(bf16[512,512]{1,0:T(8,128)(2,1)S(1)} %bitcast.35), channel_id=1, source_target_pairs={{0,1},{1,2},{2,3},{3,0},{4,5},{5,6},{6,7},{7,4},{8,9},{9,10},{10,1... | collective-permute-start | bytes 1572872 | tf_op jit(solution)/shard_map/ppermute | solution.py:147
  127.1 0.8 copy-start.2
  127.9 23.6 %collective-permute-start.9 = (bf16[512,512]{1,0:T(8,128)(2,1)S(1)}, bf16[512,512]{1,0:T(8,128)(2,1)}, u32[]{:S(2)}, u32[]{:S(2)}) collective-permute-start(bf16[512,512]{1,0:T(8,128)(2,1)S(1)} %bitcast.33), channel_id=1, source_target_pairs={{0,1},{1,2},{2,3},{3,0},{4,5},{5,6},{6,7},{7,4},{8,9},{9,10},{10,1... | collective-permute-start | bytes 1572872 | tf_op jit(solution)/shard_map/ppermute | solution.py:147
  127.9 0.8 copy-start
  128.8 34.0 %collective-permute-start.6 = (bf16[512,512]{1,0:T(8,128)(2,1)S(1)}, bf16[512,512]{1,0:T(8,128)(2,1)}, u32[]{:S(2)}, u32[]{:S(2)}) collective-permute-start(bf16[512,512]{1,0:T(8,128)(2,1)S(1)} %bitcast.31), channel_id=1, source_target_pairs={{0,1},{1,2},{2,3},{3,0},{4,5},{5,6},{6,7},{7,4},{8,9},{9,10},{10,1... | collective-permute-start | bytes 1572872 | tf_op jit(solution)/shard_map/ppermute | solution.py:147
  130.1 43.9 %collective-permute-start = (bf16[512,512]{1,0:T(8,128)(2,1)S(1)}, bf16[512,512]{1,0:T(8,128)(2,1)}, u32[]{:S(2)}, u32[]{:S(2)}) collective-permute-start(bf16[512,512]{1,0:T(8,128)(2,1)S(1)} %bitcast.29), channel_id=1, source_target_pairs={{0,1},{1,2},{2,3},{3,0},{4,5},{5,6},{6,7},{7,4},{8,9},{9,10},{10,1... | collective-permute-start | bytes 1572872 | tf_op jit(solution)/shard_map/ppermute | solution.py:147
  140.2 45.0 %collective-permute-start.13 = (bf16[512,512]{1,0:T(8,128)(2,1)S(1)}, bf16[512,512]{1,0:T(8,128)(2,1)}, u32[]{:S(2)}, u32[]{:S(2)}) collective-permute-start(bf16[512,512]{1,0:T(8,128)(2,1)S(1)} %collective-permute-done.12.refs_1_), channel_id=1, source_target_pairs={{0,1},{1,2},{2,3},{3,0},{4,5},{5,6},{6,7},{7,4},{8,9},{9,10},{10,1... | collective-permute-start | bytes 1572872 | tf_op jit(solution)/shard_map/ppermute | solution.py:147
  142.0 0.8 copy-start.4
  151.5 44.9 %collective-permute-start.10 = (bf16[512,512]{1,0:T(8,128)(2,1)}, bf16[512,512]{1,0:T(8,128)(2,1)}, u32[]{:S(2)}, u32[]{:S(2)}) collective-permute-start(bf16[512,512]{1,0:T(8,128)(2,1)} %collective-permute-done.9.refs_1_), channel_id=1, source_target_pairs={{0,1},{1,2},{2,3},{3,0},{4,5},{5,6},{6,7},{7,4},{8,9},{9,10},{10,1... | collective-permute-start | bytes 1572872 | tf_op jit(solution)/shard_map/ppermute | solution.py:147
  162.7 44.9 %collective-permute-start.7 = (bf16[512,512]{1,0:T(8,128)(2,1)}, bf16[512,512]{1,0:T(8,128)(2,1)}, u32[]{:S(2)}, u32[]{:S(2)}) collective-permute-start(bf16[512,512]{1,0:T(8,128)(2,1)} %collective-permute-done.6.refs_1_), channel_id=1, source_target_pairs={{0,1},{1,2},{2,3},{3,0},{4,5},{5,6},{6,7},{7,4},{8,9},{9,10},{10,1... | collective-permute-start | bytes 1572872 | tf_op jit(solution)/shard_map/ppermute | solution.py:147
  174.0 44.9 %collective-permute-start.1 = (bf16[512,512]{1,0:T(8,128)(2,1)}, bf16[512,512]{1,0:T(8,128)(2,1)}, u32[]{:S(2)}, u32[]{:S(2)}) collective-permute-start(bf16[512,512]{1,0:T(8,128)(2,1)} %collective-permute-done.refs_1_), channel_id=1, source_target_pairs={{0,1},{1,2},{2,3},{3,0},{4,5},{5,6},{6,7},{7,4},{8,9},{9,10},{10,1... | collective-permute-start | bytes 1572872 | tf_op jit(solution)/shard_map/ppermute | solution.py:147
  185.2 44.9 %collective-permute-start.14 = (bf16[512,512]{1,0:T(8,128)(2,1)}, bf16[512,512]{1,0:T(8,128)(2,1)}, u32[]{:S(2)}, u32[]{:S(2)}) collective-permute-start(bf16[512,512]{1,0:T(8,128)(2,1)} %collective-permute-done.13.refs_2_), channel_id=1, source_target_pairs={{0,1},{1,2},{2,3},{3,0},{4,5},{5,6},{6,7},{7,4},{8,9},{9,10},{10,1... | collective-permute-start | bytes 1572872 | tf_op jit(solution)/shard_map/ppermute | solution.py:147
  196.5 61.1 %collective-permute-start.11 = (bf16[512,512]{1,0:T(8,128)(2,1)}, bf16[512,512]{1,0:T(8,128)(2,1)}, u32[]{:S(2)}, u32[]{:S(2)}) collective-permute-start(bf16[512,512]{1,0:T(8,128)(2,1)} %collective-permute-done.10.refs_2_), channel_id=1, source_target_pairs={{0,1},{1,2},{2,3},{3,0},{4,5},{5,6},{6,7},{7,4},{8,9},{9,10},{10,1... | collective-permute-start | bytes 1572872 | tf_op jit(solution)/shard_map/ppermute | solution.py:147
  207.7 75.3 %collective-permute-start.8 = (bf16[512,512]{1,0:T(8,128)(2,1)}, bf16[512,512]{1,0:T(8,128)(2,1)}, u32[]{:S(2)}, u32[]{:S(2)}) collective-permute-start(bf16[512,512]{1,0:T(8,128)(2,1)} %collective-permute-done.7.refs_2_), channel_id=1, source_target_pairs={{0,1},{1,2},{2,3},{3,0},{4,5},{5,6},{6,7},{7,4},{8,9},{9,10},{10,1... | collective-permute-start | bytes 1572872 | tf_op jit(solution)/shard_map/ppermute | solution.py:147
  218.9 89.5 %collective-permute-start.2 = (bf16[512,512]{1,0:T(8,128)(2,1)}, bf16[512,512]{1,0:T(8,128)(2,1)}, u32[]{:S(2)}, u32[]{:S(2)}) collective-permute-start(bf16[512,512]{1,0:T(8,128)(2,1)} %collective-permute-done.1.refs_2_), channel_id=1, source_target_pairs={{0,1},{1,2},{2,3},{3,0},{4,5},{5,6},{6,7},{7,4},{8,9},{9,10},{10,1... | collective-permute-start | bytes 1572872 | tf_op jit(solution)/shard_map/ppermute | solution.py:147
  230.2 1.0 copy-start.3
  231.2 1.0 copy-start.5
  232.2 25.3 %copy-start.1 = (bf16[8,1,4,16,512]{4,3,2,1,0:T(8,128)(2,1)S(1)}, bf16[8,1,4,16,512]{4,3,2,1,0:T(8,128)(2,1)}, u32[]{:S(2)}) copy-start(bf16[8,1,4,16,512]{4,3,2,1,0:T(8,128)(2,1)} %copy-done) | copy-start | bytes 1572868
Sparse Core Ops, SparseCore 0:
  64.1 117.8 all-gather.1

commit v2 on v1

v2 whole, which is shorter than its diff:
```python
import functools

import jax
import jax.numpy as jnp
from jax import lax
from jax.experimental import pallas as pl
from jax.experimental.pallas import tpu as pltpu
from jax.sharding import PartitionSpec as P

V = 512
GROUP = 16
STEP_J = 8
STEP_A = 4
PAD = 8


def partner(own, k, count):
    if count & (count - 1) == 0:
        return own ^ k, own ^ k
    return (own + k) % count, (own - k + count) % count


def split_kernel(own, w_ref, *out_refs, j_local, b_local):
    cols = len(out_refs)
    for s in range(cols):
        to = lax.rem(own[0] + s, cols)
        for j in range(j_local):
            start = pl.multiple_of((j * cols + to) * b_local, b_local)
            out_refs[s][:, j * b_local:(j + 1) * b_local] = w_ref[:, pl.ds(start, b_local)]


def split_columns(own, couplings, cols, j_local, b_local):
    depth = couplings.shape[0]
    if b_local % 128:
        split = couplings.reshape(depth, j_local, cols, b_local)
        return [
            lax.dynamic_index_in_dim(split, lax.rem(own + s, cols), 2, keepdims=False).reshape(depth, -1)
            for s in range(cols)
        ]
    return pl.pallas_call(
        functools.partial(split_kernel, j_local=j_local, b_local=b_local),
        out_shape=[jax.ShapeDtypeStruct((depth, j_local * b_local), couplings.dtype)] * cols,
        in_specs=[pl.BlockSpec(memory_space=pltpu.SMEM), pl.BlockSpec(memory_space=pltpu.VMEM)],
        out_specs=[pl.BlockSpec(memory_space=pltpu.VMEM)] * cols,
        compiler_params=pltpu.CompilerParams(vmem_limit_bytes=24 * 1024 * 1024),
        cost_estimate=pl.CostEstimate(flops=0, bytes_accessed=4 * couplings.size, transcendentals=0),
    )(own.reshape(1), couplings)


def chunk_kernel(own, *refs, parts, occupied, b_local, steps_w):
    t_refs = refs[:parts]
    w_ref, ladder_ref, out_ref, t_all, pairs = refs[parts], refs[parts + 1], *refs[-3:]
    step = pl.program_id(0)
    depth = t_refs[0].shape[1]
    count = occupied * occupied
    pitch = count + PAD
    sources = own.shape[0] - 1
    i_local = occupied // sources

    @pl.when(step == 0)
    def _():
        for s in range(parts):
            block = lax.rem(own[0] - s + parts, parts)
            t_all[:, pl.ds(pl.multiple_of(block * depth, depth), depth)] = t_refs[s][...]

    @pl.when(step < steps_w)
    def _():
        per_part = occupied // parts
        first = step * STEP_J
        shift = first // per_part
        j0 = lax.rem(own[0] - shift + parts, parts) * per_part + lax.rem(first, per_part)
        wide = 256 // b_local
        for tile in range(STEP_J // wide):
            acc = jnp.dot(
                t_all[...], w_ref[:, tile * 256:(tile + 1) * 256], preferred_element_type=jnp.float32)
            for source in range(sources):
                start = own[1 + source] * (i_local * occupied) + j0
                for i in range(i_local):
                    for k in range(wide):
                        n = start + (i * occupied + tile * wide + k)
                        for h in range(GROUP // 8):
                            row = (source * i_local + i) * GROUP + h * 8
                            pairs[pl.ds(h * 8 * pitch + n, 8, stride=pitch), :] = (
                                acc[row:row + 8, k * b_local:(k + 1) * b_local])

    @pl.when(step >= steps_w)
    def _():
        a0 = (step - steps_w) * STEP_A
        wide = 256 // b_local
        for g in range(STEP_A // wide):
            blocks = []
            for k in range(wide):
                row = pl.multiple_of((a0 + g * wide + k) * pitch, 8)
                blocks.append(pairs[pl.ds(row, count), :].astype(jnp.bfloat16))
            both = jnp.concatenate(blocks, axis=1)
            for m in range(count // 256):
                rows = slice(m * 256, (m + 1) * 256)
                mixed = jnp.dot(ladder_ref[rows, :], both, preferred_element_type=jnp.float32)
                total = (mixed + both[rows, :].astype(jnp.float32)).astype(jnp.bfloat16)
                out_ref[g * wide:(g + 1) * wide, :, rows] = total.T.reshape(wide, b_local, 256)


def chunk_update(own, pieces, panel_w, ladder, out, q, a_local, b_local, occupied):
    parts = len(pieces)
    rows, depth = pieces[0].shape
    count = occupied * occupied
    steps_w = occupied // STEP_J
    steps_a = GROUP // STEP_A
    k_all = panel_w.shape[0]
    whole = lambda s, own: (0, 0)
    in_specs = [pl.BlockSpec((rows, depth), whole, pipeline_mode=pl.Buffered(1))] * parts
    in_specs.append(pl.BlockSpec((k_all, STEP_J * b_local), lambda s, own: (0, jnp.minimum(s, steps_w - 1))))
    in_specs.append(pl.BlockSpec((count, count), whole, pipeline_mode=pl.Buffered(1)))
    args = [own, *pieces, panel_w, ladder]
    aliases = {}
    if out is not None:
        in_specs.append(pl.BlockSpec(memory_space=pl.ANY))
        aliases = {len(args): 0}
        args.append(out)
    flops = 2 * rows * k_all * occupied * b_local + 2 * GROUP * b_local * count * count
    return pl.pallas_call(
        functools.partial(chunk_kernel, parts=parts, occupied=occupied, b_local=b_local, steps_w=steps_w),
        out_shape=jax.ShapeDtypeStruct((a_local, b_local, count), jnp.bfloat16),
        grid_spec=pltpu.PrefetchScalarGridSpec(
            num_scalar_prefetch=1,
            grid=(steps_w + steps_a,),
            in_specs=in_specs,
            out_specs=pl.BlockSpec(
                (STEP_A, b_local, count),
                lambda s, own: (q * steps_a + jnp.maximum(s - steps_w, 0), 0, 0)),
            scratch_shapes=[
                pltpu.VMEM((rows, k_all), jnp.bfloat16),
                pltpu.VMEM((GROUP * (count + PAD), b_local), jnp.float32),
            ],
        ),
        input_output_aliases=aliases,
        compiler_params=pltpu.CompilerParams(vmem_limit_bytes=48 * 1024 * 1024),
        cost_estimate=pl.CostEstimate(
            flops=flops, bytes_accessed=2 * (panel_w.size + count * count + rows * k_all + GROUP * b_local * count),
            transcendentals=0),
    )(*args)


def plain_update(own, sources, pieces, panel_w, ladder, b_local, occupied):
    parts = len(pieces)
    back = jnp.argsort(lax.rem(own - jnp.arange(parts) + parts, parts))
    rows, depth = pieces[0].shape
    panel_t = jnp.stack(pieces, 0)[back].reshape(parts, sources.shape[0], -1, depth)
    panel_t = panel_t[:, jnp.argsort(sources)].reshape(parts, rows, depth)
    panel_t = jnp.transpose(panel_t, (1, 0, 2)).reshape(rows, -1)
    cycle = jnp.dot(panel_t, panel_w, preferred_element_type=jnp.float32).astype(jnp.bfloat16)
    cycle = cycle.reshape(occupied, -1, parts, occupied // parts, b_local)[:, :, back]
    cycle = cycle.reshape(occupied, -1, occupied, b_local)
    a_count = cycle.shape[1]
    pairs = jnp.transpose(cycle, (1, 3, 0, 2)).reshape(a_count * b_local, occupied * occupied)
    mixed = lax.dot_general(pairs, ladder, (((1,), (1,)), ((), ())), preferred_element_type=jnp.float32)
    total = (mixed + pairs.astype(jnp.float32)).astype(jnp.bfloat16)
    return total.reshape(a_count, b_local, occupied * occupied)


def local(rows, cols, amplitudes, couplings, ladder):
    depth = amplitudes.shape[1]
    i_local = amplitudes.shape[0] // V
    j_local = couplings.shape[1] // V
    occupied = i_local * rows
    a_local, b_local = V // rows, V // cols
    own, own_row = lax.axis_index("col"), lax.axis_index("row")

    arrived = list(split_columns(own, couplings, cols, j_local, b_local))
    for s in range(1, cols):
        arrived[s] = lax.ppermute(arrived[s], "col", [(c, (c + s) % cols) for c in range(cols)])

    by_row = amplitudes.reshape(i_local, V, depth)
    blocks, sources = [], []
    for k in range(rows):
        to, source = partner(own_row, k, rows)
        blocks.append(lax.dynamic_slice_in_dim(by_row, to * a_local, a_local, axis=1))
        sources.append(source)
    sources = jnp.stack(sources)
    half = rows // 2
    order = [k for pair in zip(range(half, rows), [*range(2, half), 1]) for k in pair]
    order += [k for k in range(1, rows) if k not in order]
    for n, k in enumerate(order):
        if n >= 2:
            blocks[k], blocks[order[n - 2]] = lax.optimization_barrier((blocks[k], blocks[order[n - 2]]))
        blocks[k] = lax.ppermute(blocks[k], "row", [(r, partner(r, k, rows)[0]) for r in range(rows)])

    arrived, blocks = lax.optimization_barrier((arrived, blocks))
    panel_w = lax.all_gather(jnp.concatenate(arrived, axis=1), "row", axis=0, tiled=True)

    ring = [(c, (c + 1) % cols) for c in range(cols)]
    pieces = []
    for q in range(a_local // GROUP):
        held = jnp.concatenate([block[:, q * GROUP:(q + 1) * GROUP] for block in blocks], axis=0)
        held = held.reshape(occupied * GROUP, depth)
        got = [held]
        for _ in range(cols - 1):
            held = lax.ppermute(held, "col", ring)
            got.append(held)
        pieces.append(got)

    if b_local % 128 or 256 % b_local or depth % 128 or (occupied // cols) % STEP_J:
        return jnp.concatenate(
            [plain_update(own, sources, got, panel_w, ladder, b_local, occupied) for got in pieces], axis=0)
    place = jnp.concatenate([own.reshape(1), sources])
    out = None
    for q in range(a_local // GROUP):
        out = chunk_update(place, pieces[q], panel_w, ladder, out, q, a_local, b_local, occupied)
    return out


def solution(mesh):
    in_specs = (P("row", "col"), P("row", "col"), P())
    out_specs = P("row", "col", None)
    body = functools.partial(local, mesh.shape["row"], mesh.shape["col"])
    return jax.shard_map(body, mesh=mesh, in_specs=in_specs, out_specs=out_specs, check_vma=False)
```

time: 341 us -> 273 us (0.80)
  blocking collectives: 39.2 us -> 0 us
  Pallas kernels: 102 us -> 80.8 us
  local copies, waits for them, and re-layouts: 25.8 us -> 14.9 us
  waiting for transfers between devices: 114 us -> 121 us
  starting transfers between devices: 45 us -> 40.2 us
    all_to_all x1 -> x0, blocking collectives: 39.2 us -> none  [local(): lax.all_to_all(blocks, 'row', split_axis=0, concat_axis=0, tiled=True)]
    pallas_call x4, Pallas kernels: 102 us -> 80.2 us  [chunk_update(): pl.pallas_call(functools.partial(chunk_kernel, parts=parts, occupied=occu...]
    ppermute x12, starting transfers between devices: 37.9 us -> 25.2 us  [local(): held = lax.ppermute(held, 'col', ring)]
    dynamic_slice x1, local copies, waits for them, and re-layouts: 12.9 us -> 2.63 us  [local(): lax.dynamic_slice_in_dim(by_row, to * a_local, a_local, axis=1)]
    ppermute x3 -> x10, starting transfers between devices: 7.13 us -> 14.9 us  [the longest x7 9.35 us: local(): lax.ppermute(blocks[k], 'row', [(r, partner(r, k, rows)[0]) for r in rang...]
    ppermute x12, waiting for transfers between devices: 81.8 us -> 87.3 us  [local(): held = lax.ppermute(held, 'col', ring)]
    unnamed x19 -> x33, local copies, waits for them, and re-layouts: 9.29 us -> 11.2 us
    ppermute x3 -> x10, waiting for transfers between devices: 32.2 us -> 34 us  [the longest x3 22.2 us: local(): lax.ppermute(arrived[s], 'col', [(c, (c + s) % cols) for c in range(cols)])]
  transfers between devices with their start and end apart: 16 -> 23, of which waited for: 11 -> 13; matrix products, arithmetic and copies ran while one was open for 1% -> 3% of each run, Pallas kernels for 22% -> 22%
where the time goes in v2:
time: 273 us; the launch traced here: 272 us
  waiting for transfers between devices  121 us (44%)
  Pallas kernels  80.8 us (30%)
  starting transfers between devices  40.2 us (15%)
  local copies, waits for them, and re-layouts  14.9 us (5%)
  between operations  13.5 us (5%)
    ppermute x12, waiting for transfers between devices, local(): held = lax.ppermute(held, 'col', ring)  87.3 us
    pallas_call x4, Pallas kernels, chunk_update(): pl.pallas_call(functools.partial(chunk_kernel, parts=parts, occupied=occu...  80.2 us
    ppermute x12, starting transfers between devices, local(): held = lax.ppermute(held, 'col', ring)  25.2 us
    ppermute x3, waiting for transfers between devices, local(): lax.ppermute(arrived[s], 'col', [(c, (c + s) % cols) for c in range(cols)])  22.2 us
    ppermute x7, waiting for transfers between devices, local(): lax.ppermute(blocks[k], 'row', [(r, partner(r, k, rows)[0]) for r in rang...  11.8 us
    unnamed x33, local copies, waits for them, and re-layouts  11.2 us
    ppermute x7, starting transfers between devices, local(): lax.ppermute(blocks[k], 'row', [(r, partner(r, k, rows)[0]) for r in rang...  9.35 us
    ppermute x3, starting transfers between devices, local(): lax.ppermute(arrived[s], 'col', [(c, (c + s) % cols) for c in range(cols)])  5.57 us
  transfers between devices with their start and end apart: 23, of which 13 were waited for; matrix products, arithmetic and copies ran while one was open for 3% of the time, Pallas kernels for 22%

profile of v2, /device:TPU:0, one launch (start us, length us, event | category | flops | bytes accessed | tf_op | source)
XLA Modules:
  0.0 272.2 jit_solution(7046986598166081502)
XLA Ops:
  6.5 2.6 constant_dynamic-slice_fusion
  9.2 3.0 %collective-permute-start.6 = (bf16[4,64,512]{2,1,0:T(8,128)(2,1)S(1)}, bf16[4,64,512]{2,1,0:T(8,128)(2,1)S(1)}, u32[]{:S(2)}, u32[]{:S(2)}) collective-permute-start(bf16[4,64,512]{2,1,0:T(8,128)(2,1)S(1)} %get-tuple-element.59), channel_id=1, source_target_pairs={{0,16},{4,20},{8,24},{12,28},{16,0},{20,4},{24,8},{28,12},{1,17},{... | collective-permute-start | bytes 786440 | tf_op jit(solution)/shard_map/ppermute | solution.py:186
  12.1 1.5 collective-permute-start.3
  13.6 4.8 %collective-permute-done.6 = bf16[4,64,512]{2,1,0:T(8,128)(2,1)S(1)} collective-permute-done((bf16[4,64,512]{2,1,0:T(8,128)(2,1)S(1)}, bf16[4,64,512]{2,1,0:T(8,128)(2,1)S(1)}, u32[]{:S(2)}, u32[]{:S(2)}) %collective-permute-start.6) | collective-permute-done | bytes 262176 | tf_op jit(solution)/shard_map/ppermute | solution.py:186
  18.4 0.7 copy-done.8
  19.1 0.4 collective-permute-start.7
  19.6 0.6 shard_map.37
  20.1 1.6 collective-permute-start
  21.8 0.0 collective-permute-done.3
  21.8 2.3 collective-permute-start.4
  24.0 3.7 %collective-permute-done.7 = bf16[4,64,512]{2,1,0:T(8,128)(2,1)} collective-permute-done((bf16[4,64,512]{2,1,0:T(8,128)(2,1)}, bf16[4,64,512]{2,1,0:T(8,128)(2,1)}, u32[]{:S(2)}, u32[]{:S(2)}) %collective-permute-start.7) | collective-permute-done | bytes 262176 | tf_op jit(solution)/shard_map/ppermute | solution.py:186
  27.8 2.2 collective-permute-start.8
  30.0 2.6 collective-permute-start.1
  32.6 1.3 collective-permute-start.2
  33.9 0.0 collective-permute-done.4
  33.9 0.0 collective-permute-start.5
  33.9 3.3 %collective-permute-done.8 = bf16[4,64,512]{2,1,0:T(8,128)(2,1)S(1)} collective-permute-done((bf16[4,64,512]{2,1,0:T(8,128)(2,1)S(1)}, bf16[4,64,512]{2,1,0:T(8,128)(2,1)S(1)}, u32[]{:S(2)}, u32[]{:S(2)}) %collective-permute-start.8) | collective-permute-done | bytes 262176 | tf_op jit(solution)/shard_map/ppermute | solution.py:186
  37.2 0.0 collective-permute-start.9
  37.2 0.0 collective-permute-done
  37.2 22.2 %collective-permute-done.1 = bf16[256,1024]{1,0:T(8,128)(2,1)S(1)} collective-permute-done((bf16[256,1024]{1,0:T(8,128)(2,1)S(1)}, bf16[256,1024]{1,0:T(8,128)(2,1)S(1)}, u32[]{:S(2)}, u32[]{:S(2)}) %collective-permute-start.1) | collective-permute-done | bytes 524320 | tf_op jit(solution)/shard_map/ppermute | solution.py:171
  59.4 0.0 collective-permute-done.2
  59.4 0.0 collective-permute-done.5
  59.4 0.0 collective-permute-done.9
  59.4 1.5 pad_maximum_fusion
  60.9 0.0 all-gather.2.cloned.1.call-update
  61.0 1.1 constant_dynamic-update-slice_fusion.30
  62.1 1.0 constant_dynamic-update-slice_fusion.29
  63.1 1.0 constant_dynamic-update-slice_fusion.28
  64.0 1.0 constant_dynamic-update-slice_fusion.27
  65.0 1.0 constant_dynamic-update-slice_fusion.26
  66.0 1.0 constant_dynamic-update-slice_fusion.25
  66.9 1.0 constant_dynamic-update-slice_fusion.24
  67.9 11.8 %collective-permute-start.19 = (bf16[512,512]{1,0:T(8,128)(2,1)S(1)}, bf16[512,512]{1,0:T(8,128)(2,1)S(1)}, u32[]{:S(2)}, u32[]{:S(2)}) collective-permute-start(bf16[512,512]{1,0:T(8,128)(2,1)S(1)} %bitcast.20), channel_id=1, source_target_pairs={{0,1},{1,2},{2,3},{3,0},{4,5},{5,6},{6,7},{7,4},{8,9},{9,10},{10,1... | collective-permute-start | bytes 1572872 | tf_op jit(solution)/shard_map/ppermute | solution.py:198
  79.7 0.8 copy-done.4
  80.5 0.0 collective-permute-start.16
  80.5 1.7 collective-permute-start.13
  82.3 0.0 collective-permute-start.10
  82.3 0.8 copy-done.2
  83.2 9.9 %collective-permute-done.19.refs_1_ = bf16[512,512]{1,0:T(8,128)(2,1)S(1)} collective-permute-done((bf16[512,512]{1,0:T(8,128)(2,1)S(1)}, bf16[512,512]{1,0:T(8,128)(2,1)S(1)}, u32[]{:S(2)}, u32[]{:S(2)}) %collective-permute-start.19) | collective-permute-done | bytes 524320 | tf_op jit(solution)/shard_map/ppermute | solution.py:198
  93.0 1.5 collective-permute-start.20
  94.5 0.8 copy-done.6
  95.3 9.1 %collective-permute-done.16.refs_1_ = bf16[512,512]{1,0:T(8,128)(2,1)} collective-permute-done((bf16[512,512]{1,0:T(8,128)(2,1)S(1)}, bf16[512,512]{1,0:T(8,128)(2,1)}, u32[]{:S(2)}, u32[]{:S(2)}) %collective-permute-start.16) | collective-permute-done | bytes 524320 | tf_op jit(solution)/shard_map/ppermute | solution.py:198
  104.4 1.5 collective-permute-start.17
  105.8 9.8 %collective-permute-done.13.refs_1_ = bf16[512,512]{1,0:T(8,128)(2,1)} collective-permute-done((bf16[512,512]{1,0:T(8,128)(2,1)S(1)}, bf16[512,512]{1,0:T(8,128)(2,1)}, u32[]{:S(2)}, u32[]{:S(2)}) %collective-permute-start.13) | collective-permute-done | bytes 524320 | tf_op jit(solution)/shard_map/ppermute | solution.py:198
  115.6 1.5 collective-permute-start.14
  117.1 9.8 %collective-permute-done.10.refs_1_ = bf16[512,512]{1,0:T(8,128)(2,1)} collective-permute-done((bf16[512,512]{1,0:T(8,128)(2,1)S(1)}, bf16[512,512]{1,0:T(8,128)(2,1)}, u32[]{:S(2)}, u32[]{:S(2)}) %collective-permute-start.10) | collective-permute-done | bytes 524320 | tf_op jit(solution)/shard_map/ppermute | solution.py:198
  126.9 1.5 collective-permute-start.11
  128.3 9.8 %collective-permute-done.20.refs_2_ = bf16[512,512]{1,0:T(8,128)(2,1)} collective-permute-done((bf16[512,512]{1,0:T(8,128)(2,1)S(1)}, bf16[512,512]{1,0:T(8,128)(2,1)}, u32[]{:S(2)}, u32[]{:S(2)}) %collective-permute-start.20) | collective-permute-done | bytes 524320 | tf_op jit(solution)/shard_map/ppermute | solution.py:198
  138.1 1.5 collective-permute-start.21
  139.5 0.1 concatenate.18.own
  139.6 9.7 %collective-permute-done.17.refs_2_ = bf16[512,512]{1,0:T(8,128)(2,1)} collective-permute-done((bf16[512,512]{1,0:T(8,128)(2,1)}, bf16[512,512]{1,0:T(8,128)(2,1)}, u32[]{:S(2)}, u32[]{:S(2)}) %collective-permute-start.17) | collective-permute-done | bytes 524320 | tf_op jit(solution)/shard_map/ppermute | solution.py:198
  149.3 1.5 collective-permute-start.18
  150.8 9.8 %collective-permute-done.14.refs_2_ = bf16[512,512]{1,0:T(8,128)(2,1)} collective-permute-done((bf16[512,512]{1,0:T(8,128)(2,1)}, bf16[512,512]{1,0:T(8,128)(2,1)}, u32[]{:S(2)}, u32[]{:S(2)}) %collective-permute-start.14) | collective-permute-done | bytes 524320 | tf_op jit(solution)/shard_map/ppermute | solution.py:198
  160.6 1.5 collective-permute-start.15
  162.0 9.8 %collective-permute-done.11.refs_2_ = bf16[512,512]{1,0:T(8,128)(2,1)} collective-permute-done((bf16[512,512]{1,0:T(8,128)(2,1)}, bf16[512,512]{1,0:T(8,128)(2,1)}, u32[]{:S(2)}, u32[]{:S(2)}) %collective-permute-start.11) | collective-permute-done | bytes 524320 | tf_op jit(solution)/shard_map/ppermute | solution.py:198
  171.8 1.5 collective-permute-start.12
  173.3 9.8 %collective-permute-done.21.refs_3_ = bf16[512,512]{1,0:T(8,128)(2,1)} collective-permute-done((bf16[512,512]{1,0:T(8,128)(2,1)}, bf16[512,512]{1,0:T(8,128)(2,1)}, u32[]{:S(2)}, u32[]{:S(2)}) %collective-permute-start.21) | collective-permute-done | bytes 524320 | tf_op jit(solution)/shard_map/ppermute | solution.py:198
  183.0 1.0 copy-done.5
  184.1 1.0 copy-done.7
  185.1 19.9 %shard_map.38.refs_6_ = bf16[64,128,1024]{2,1,0:T(8,128)(2,1)} custom-call(s32[9]{0:T(128)S(1)} %concatenate.18.own, bf16[512,512]{1,0:T(8,128)(2,1)S(1)} %bitcast.21, bf16[512,512]{1,0:T(8,128)(2,1)S(1)} %copy-done.7, bf16[512,512]{1,0:T(8,128)(2,1)} %collective-permute-done.20.refs_2_, bf16[512,512]{1,0:T(8,128)(2,1)} %collective-permute-done.21.refs_3_, ...), custom_call_target="tpu_custom_call" | custom-call | flops 12884901888 | bytes 25165824 | tf_op jit(solution)/shard_map/pallas_call | solution.py:121
  205.0 20.1 %shard_map.39.refs_6_ = bf16[64,128,1024]{2,1,0:T(8,128)(2,1)} custom-call(s32[9]{0:T(128)S(1)} %concatenate.18.own, bf16[512,512]{1,0:T(8,128)(2,1)S(1)} %bitcast.15, bf16[512,512]{1,0:T(8,128)(2,1)} %collective-permute-done.16.refs_1_, bf16[512,512]{1,0:T(8,128)(2,1)} %collective-permute-done.17.refs_2_, ...), custom_call_target="tpu_custom_call", output_to_operand_aliasing={{}: (7, {})} | custom-call | flops 12884901888 | bytes 25165824 | tf_op jit(solution)/shard_map/pallas_call | solution.py:121
  225.2 20.1 %shard_map.40.refs_6_ = bf16[64,128,1024]{2,1,0:T(8,128)(2,1)} custom-call(s32[9]{0:T(128)S(1)} %concatenate.18.own, bf16[512,512]{1,0:T(8,128)(2,1)S(1)} %bitcast.17, bf16[512,512]{1,0:T(8,128)(2,1)} %collective-permute-done.13.refs_1_, bf16[512,512]{1,0:T(8,128)(2,1)} %collective-permute-done.14.refs_2_, ...), custom_call_target="tpu_custom_call", output_to_operand_aliasing={{}: (7, {})} | custom-call | flops 12884901888 | bytes 25165824 | tf_op jit(solution)/shard_map/pallas_call | solution.py:121
  245.3 0.0 collective-permute-done.12.refs_3_
  245.3 20.1 %shard_map.41 = bf16[64,128,1024]{2,1,0:T(8,128)(2,1)} custom-call(s32[9]{0:T(128)S(1)} %concatenate.18.own, bf16[512,512]{1,0:T(8,128)(2,1)S(1)} %bitcast.19, bf16[512,512]{1,0:T(8,128)(2,1)} %collective-permute-done.10.refs_1_, bf16[512,512]{1,0:T(8,128)(2,1)} %collective-permute-done.11.refs_2_, ...), custom_call_target="tpu_custom_call", output_to_operand_aliasing={{}: (7, {})} | custom-call | flops 12884901888 | bytes 25165824 | tf_op jit(solution)/shard_map/pallas_call | solution.py:121
  (25 shorter events, 0.1 us)
Async XLA Ops:
  6.5 13.0 %copy-start.1 = (bf16[256,4096]{1,0:T(8,128)(2,1)S(1)}, bf16[256,4096]{1,0:T(8,128)(2,1)}, u32[]{:S(2)}) copy-start(bf16[256,4096]{1,0:T(8,128)(2,1)} %w_ref.1) | copy-start | bytes 6291460
  6.5 176.5 %all-gather.2.cloned.1.call-start = ((), (), s32[]{:S(2)}) async-start(), calls=%async_computation | async-start | bytes 18874368 | tf_op jit(solution)/shard_map/all_gather | solution.py:189
  9.2 9.3 %collective-permute-start.6 = (bf16[4,64,512]{2,1,0:T(8,128)(2,1)S(1)}, bf16[4,64,512]{2,1,0:T(8,128)(2,1)S(1)}, u32[]{:S(2)}, u32[]{:S(2)}) collective-permute-start(bf16[4,64,512]{2,1,0:T(8,128)(2,1)S(1)} %get-tuple-element.59), channel_id=1, source_target_pairs={{0,16},{4,20},{8,24},{12,28},{16,0},{20,4},{24,8},{28,12},{1,17},{... | collective-permute-start | bytes 786440 | tf_op jit(solution)/shard_map/ppermute | solution.py:186
  12.1 9.6 %collective-permute-start.3 = (bf16[4,64,512]{2,1,0:T(8,128)(2,1)}, bf16[4,64,512]{2,1,0:T(8,128)(2,1)}, u32[]{:S(2)}, u32[]{:S(2)}) collective-permute-start(bf16[4,64,512]{2,1,0:T(8,128)(2,1)} %get-tuple-element.61), channel_id=1, source_target_pairs={{0,8},{4,12},{8,0},{12,4},{16,24},{20,28},{24,16},{28,20},{1,9},{5... | collective-permute-start | bytes 786440 | tf_op jit(solution)/shard_map/ppermute | solution.py:186
  18.4 0.7 copy-start.8
  19.1 8.6 %collective-permute-start.7 = (bf16[4,64,512]{2,1,0:T(8,128)(2,1)}, bf16[4,64,512]{2,1,0:T(8,128)(2,1)}, u32[]{:S(2)}, u32[]{:S(2)}) collective-permute-start(bf16[4,64,512]{2,1,0:T(8,128)(2,1)} %get-tuple-element.40), channel_id=1, source_target_pairs={{0,20},{4,16},{8,28},{12,24},{16,4},{20,0},{24,12},{28,8},{1,21},{... | collective-permute-start | bytes 786440 | tf_op jit(solution)/shard_map/ppermute | solution.py:186
  20.1 17.1 %collective-permute-start = (bf16[256,1024]{1,0:T(8,128)(2,1)S(1)}, bf16[256,1024]{1,0:T(8,128)(2,1)S(1)}, u32[]{:S(2)}, u32[]{:S(2)}) collective-permute-start(bf16[256,1024]{1,0:T(8,128)(2,1)S(1)} %get-tuple-element.32), channel_id=1, source_target_pairs={{0,1},{1,2},{2,3},{3,0},{4,5},{5,6},{6,7},{7,4},{8,9},{9,10},{10,1... | collective-permute-start | bytes 1572872 | tf_op jit(solution)/shard_map/ppermute | solution.py:171
  21.8 12.2 %collective-permute-start.4 = (bf16[4,64,512]{2,1,0:T(8,128)(2,1)S(1)}, bf16[4,64,512]{2,1,0:T(8,128)(2,1)S(1)}, u32[]{:S(2)}, u32[]{:S(2)}) collective-permute-start(bf16[4,64,512]{2,1,0:T(8,128)(2,1)S(1)} %get-tuple-element.35), channel_id=1, source_target_pairs={{0,12},{4,8},{8,4},{12,0},{16,28},{20,24},{24,20},{28,16},{1,13},{... | collective-permute-start | bytes 786440 | tf_op jit(solution)/shard_map/ppermute | solution.py:186
  27.8 9.4 %collective-permute-start.8 = (bf16[4,64,512]{2,1,0:T(8,128)(2,1)S(1)}, bf16[4,64,512]{2,1,0:T(8,128)(2,1)S(1)}, u32[]{:S(2)}, u32[]{:S(2)}) collective-permute-start(bf16[4,64,512]{2,1,0:T(8,128)(2,1)S(1)} %get-tuple-element.42), channel_id=1, source_target_pairs={{0,24},{4,28},{8,16},{12,20},{16,8},{20,12},{24,0},{28,4},{1,25},{... | collective-permute-start | bytes 786440 | tf_op jit(solution)/shard_map/ppermute | solution.py:186
  30.0 29.4 %collective-permute-start.1 = (bf16[256,1024]{1,0:T(8,128)(2,1)S(1)}, bf16[256,1024]{1,0:T(8,128)(2,1)S(1)}, u32[]{:S(2)}, u32[]{:S(2)}) collective-permute-start(bf16[256,1024]{1,0:T(8,128)(2,1)S(1)} %get-tuple-element.33), channel_id=1, source_target_pairs={{0,2},{1,3},{2,0},{3,1},{4,6},{5,7},{6,4},{7,5},{8,10},{9,11},{10,... | collective-permute-start | bytes 1572872 | tf_op jit(solution)/shard_map/ppermute | solution.py:171
  32.6 26.8 %collective-permute-start.2 = (bf16[256,1024]{1,0:T(8,128)(2,1)S(1)}, bf16[256,1024]{1,0:T(8,128)(2,1)S(1)}, u32[]{:S(2)}, u32[]{:S(2)}) collective-permute-start(bf16[256,1024]{1,0:T(8,128)(2,1)S(1)} %get-tuple-element.34), channel_id=1, source_target_pairs={{0,3},{1,0},{2,1},{3,2},{4,7},{5,4},{6,5},{7,6},{8,11},{9,8},{10,9... | collective-permute-start | bytes 1572872 | tf_op jit(solution)/shard_map/ppermute | solution.py:171
  33.9 25.5 %copy-start.11 = (bf16[4,64,512]{2,1,0:T(8,128)(2,1)}, bf16[4,64,512]{2,1,0:T(8,128)(2,1)S(1)}, u32[]{:S(2)}) copy-start(bf16[4,64,512]{2,1,0:T(8,128)(2,1)S(1)} %collective-permute-done.4) | copy-start | bytes 786436
  33.9 25.5 %collective-permute-start.5 = (bf16[4,64,512]{2,1,0:T(8,128)(2,1)S(1)}, bf16[4,64,512]{2,1,0:T(8,128)(2,1)S(1)}, u32[]{:S(2)}, u32[]{:S(2)}) collective-permute-start(bf16[4,64,512]{2,1,0:T(8,128)(2,1)S(1)} %get-tuple-element.36), channel_id=1, source_target_pairs={{0,4},{4,0},{8,12},{12,8},{16,20},{20,16},{24,28},{28,24},{1,5},{5... | collective-permute-start | bytes 786440 | tf_op jit(solution)/shard_map/ppermute | solution.py:186
  37.2 22.2 %copy-start.9 = (bf16[4,64,512]{2,1,0:T(8,128)(2,1)}, bf16[4,64,512]{2,1,0:T(8,128)(2,1)S(1)}, u32[]{:S(2)}) copy-start(bf16[4,64,512]{2,1,0:T(8,128)(2,1)S(1)} %collective-permute-done.8) | copy-start | bytes 786436
  37.2 22.2 %collective-permute-start.9 = (bf16[4,64,512]{2,1,0:T(8,128)(2,1)S(1)}, bf16[4,64,512]{2,1,0:T(8,128)(2,1)S(1)}, u32[]{:S(2)}, u32[]{:S(2)}) collective-permute-start(bf16[4,64,512]{2,1,0:T(8,128)(2,1)S(1)} %get-tuple-element.44), channel_id=1, source_target_pairs={{0,28},{4,24},{8,20},{12,16},{16,12},{20,8},{24,4},{28,0},{1,29},{... | collective-permute-start | bytes 786440 | tf_op jit(solution)/shard_map/ppermute | solution.py:186
  59.4 1.5 copy-start.12
  59.4 1.5 copy-start.10
  60.9 122.1 %copy-start = (bf16[1024,1024]{1,0:T(8,128)(2,1)S(1)}, bf16[1024,1024]{1,0:T(8,128)(2,1)}, u32[]{:S(2)}) copy-start(bf16[1024,1024]{1,0:T(8,128)(2,1)} %refs_5_.7) | copy-start | bytes 6291460
  67.9 25.1 %collective-permute-start.19 = (bf16[512,512]{1,0:T(8,128)(2,1)S(1)}, bf16[512,512]{1,0:T(8,128)(2,1)S(1)}, u32[]{:S(2)}, u32[]{:S(2)}) collective-permute-start(bf16[512,512]{1,0:T(8,128)(2,1)S(1)} %bitcast.20), channel_id=1, source_target_pairs={{0,1},{1,2},{2,3},{3,0},{4,5},{5,6},{6,7},{7,4},{8,9},{9,10},{10,1... | collective-permute-start | bytes 1572872 | tf_op jit(solution)/shard_map/ppermute | solution.py:198
  79.7 0.8 copy-start.4
  80.5 23.9 %collective-permute-start.16 = (bf16[512,512]{1,0:T(8,128)(2,1)S(1)}, bf16[512,512]{1,0:T(8,128)(2,1)}, u32[]{:S(2)}, u32[]{:S(2)}) collective-permute-start(bf16[512,512]{1,0:T(8,128)(2,1)S(1)} %bitcast.14), channel_id=1, source_target_pairs={{0,1},{1,2},{2,3},{3,0},{4,5},{5,6},{6,7},{7,4},{8,9},{9,10},{10,1... | collective-permute-start | bytes 1572872 | tf_op jit(solution)/shard_map/ppermute | solution.py:198
  80.5 35.1 %collective-permute-start.13 = (bf16[512,512]{1,0:T(8,128)(2,1)S(1)}, bf16[512,512]{1,0:T(8,128)(2,1)}, u32[]{:S(2)}, u32[]{:S(2)}) collective-permute-start(bf16[512,512]{1,0:T(8,128)(2,1)S(1)} %bitcast.16), channel_id=1, source_target_pairs={{0,1},{1,2},{2,3},{3,0},{4,5},{5,6},{6,7},{7,4},{8,9},{9,10},{10,1... | collective-permute-start | bytes 1572872 | tf_op jit(solution)/shard_map/ppermute | solution.py:198
  82.3 44.6 %collective-permute-start.10 = (bf16[512,512]{1,0:T(8,128)(2,1)S(1)}, bf16[512,512]{1,0:T(8,128)(2,1)}, u32[]{:S(2)}, u32[]{:S(2)}) collective-permute-start(bf16[512,512]{1,0:T(8,128)(2,1)S(1)} %bitcast.18), channel_id=1, source_target_pairs={{0,1},{1,2},{2,3},{3,0},{4,5},{5,6},{6,7},{7,4},{8,9},{9,10},{10,1... | collective-permute-start | bytes 1572872 | tf_op jit(solution)/shard_map/ppermute | solution.py:198
  82.3 0.8 copy-start.2
  93.0 45.0 %collective-permute-start.20 = (bf16[512,512]{1,0:T(8,128)(2,1)S(1)}, bf16[512,512]{1,0:T(8,128)(2,1)}, u32[]{:S(2)}, u32[]{:S(2)}) collective-permute-start(bf16[512,512]{1,0:T(8,128)(2,1)S(1)} %collective-permute-done.19.refs_1_), channel_id=1, source_target_pairs={{0,1},{1,2},{2,3},{3,0},{4,5},{5,6},{6,7},{7,4},{8,9},{9,10},{10,1... | collective-permute-start | bytes 1572872 | tf_op jit(solution)/shard_map/ppermute | solution.py:198
  94.5 0.8 copy-start.6
  104.4 44.9 %collective-permute-start.17 = (bf16[512,512]{1,0:T(8,128)(2,1)}, bf16[512,512]{1,0:T(8,128)(2,1)}, u32[]{:S(2)}, u32[]{:S(2)}) collective-permute-start(bf16[512,512]{1,0:T(8,128)(2,1)} %collective-permute-done.16.refs_1_), channel_id=1, source_target_pairs={{0,1},{1,2},{2,3},{3,0},{4,5},{5,6},{6,7},{7,4},{8,9},{9,10},{10,1... | collective-permute-start | bytes 1572872 | tf_op jit(solution)/shard_map/ppermute | solution.py:198
  115.6 44.9 %collective-permute-start.14 = (bf16[512,512]{1,0:T(8,128)(2,1)}, bf16[512,512]{1,0:T(8,128)(2,1)}, u32[]{:S(2)}, u32[]{:S(2)}) collective-permute-start(bf16[512,512]{1,0:T(8,128)(2,1)} %collective-permute-done.13.refs_1_), channel_id=1, source_target_pairs={{0,1},{1,2},{2,3},{3,0},{4,5},{5,6},{6,7},{7,4},{8,9},{9,10},{10,1... | collective-permute-start | bytes 1572872 | tf_op jit(solution)/shard_map/ppermute | solution.py:198
  126.9 44.9 %collective-permute-start.11 = (bf16[512,512]{1,0:T(8,128)(2,1)}, bf16[512,512]{1,0:T(8,128)(2,1)}, u32[]{:S(2)}, u32[]{:S(2)}) collective-permute-start(bf16[512,512]{1,0:T(8,128)(2,1)} %collective-permute-done.10.refs_1_), channel_id=1, source_target_pairs={{0,1},{1,2},{2,3},{3,0},{4,5},{5,6},{6,7},{7,4},{8,9},{9,10},{10,1... | collective-permute-start | bytes 1572872 | tf_op jit(solution)/shard_map/ppermute | solution.py:198
  138.1 44.9 %collective-permute-start.21 = (bf16[512,512]{1,0:T(8,128)(2,1)}, bf16[512,512]{1,0:T(8,128)(2,1)}, u32[]{:S(2)}, u32[]{:S(2)}) collective-permute-start(bf16[512,512]{1,0:T(8,128)(2,1)} %collective-permute-done.20.refs_2_), channel_id=1, source_target_pairs={{0,1},{1,2},{2,3},{3,0},{4,5},{5,6},{6,7},{7,4},{8,9},{9,10},{10,1... | collective-permute-start | bytes 1572872 | tf_op jit(solution)/shard_map/ppermute | solution.py:198
  149.3 55.7 %collective-permute-start.18 = (bf16[512,512]{1,0:T(8,128)(2,1)}, bf16[512,512]{1,0:T(8,128)(2,1)}, u32[]{:S(2)}, u32[]{:S(2)}) collective-permute-start(bf16[512,512]{1,0:T(8,128)(2,1)} %collective-permute-done.17.refs_2_), channel_id=1, source_target_pairs={{0,1},{1,2},{2,3},{3,0},{4,5},{5,6},{6,7},{7,4},{8,9},{9,10},{10,1... | collective-permute-start | bytes 1572872 | tf_op jit(solution)/shard_map/ppermute | solution.py:198
  160.6 64.6 %collective-permute-start.15 = (bf16[512,512]{1,0:T(8,128)(2,1)}, bf16[512,512]{1,0:T(8,128)(2,1)}, u32[]{:S(2)}, u32[]{:S(2)}) collective-permute-start(bf16[512,512]{1,0:T(8,128)(2,1)} %collective-permute-done.14.refs_2_), channel_id=1, source_target_pairs={{0,1},{1,2},{2,3},{3,0},{4,5},{5,6},{6,7},{7,4},{8,9},{9,10},{10,1... | collective-permute-start | bytes 1572872 | tf_op jit(solution)/shard_map/ppermute | solution.py:198
  171.8 73.5 %collective-permute-start.12 = (bf16[512,512]{1,0:T(8,128)(2,1)}, bf16[512,512]{1,0:T(8,128)(2,1)}, u32[]{:S(2)}, u32[]{:S(2)}) collective-permute-start(bf16[512,512]{1,0:T(8,128)(2,1)} %collective-permute-done.11.refs_2_), channel_id=1, source_target_pairs={{0,1},{1,2},{2,3},{3,0},{4,5},{5,6},{6,7},{7,4},{8,9},{9,10},{10,1... | collective-permute-start | bytes 1572872 | tf_op jit(solution)/shard_map/ppermute | solution.py:198
  183.0 1.0 copy-start.5
  184.1 1.0 copy-start.7
  225.1 20.1 %copy-start.3 = (bf16[32,16,512]{2,1,0:T(8,128)(2,1)S(1)}, bf16[32,16,512]{2,1,0:T(8,128)(2,1)}, u32[]{:S(2)}) copy-start(bf16[32,16,512]{2,1,0:T(8,128)(2,1)} %copy-done.2) | copy-start | bytes 1572868
Sparse Core Ops, SparseCore 0:
  61.1 99.7 all-gather.1

commit v3 on v0

v3 whole, which is shorter than its diff:
```python
import functools

import jax
import jax.numpy as jnp
from jax import lax
from jax.experimental import pallas as pl
from jax.experimental.pallas import tpu as pltpu
from jax.sharding import PartitionSpec as P

V = 512
GROUP = 16
STEP_A = 4
PAD = 8
WIDE = 512
ANY = pl.BlockSpec(memory_space=pl.ANY)


def split_kernel(own, w_ref, *out_refs, j_local, b_local):
    cols = len(out_refs)
    for s in range(cols):
        to = lax.rem(own[0] + s, cols)
        for j in range(j_local):
            start = pl.multiple_of((j * cols + to) * b_local, b_local)
            out_refs[s][:, j * b_local:(j + 1) * b_local] = w_ref[:, pl.ds(start, b_local)]


def split_columns(own, couplings, cols, j_local, b_local):
    depth = couplings.shape[0]
    if b_local % 128:
        split = couplings.reshape(depth, j_local, cols, b_local)
        return [
            lax.dynamic_index_in_dim(split, lax.rem(own + s, cols), 2, keepdims=False).reshape(depth, -1)
            for s in range(cols)
        ]
    return pl.pallas_call(
        functools.partial(split_kernel, j_local=j_local, b_local=b_local),
        out_shape=[jax.ShapeDtypeStruct((depth, j_local * b_local), couplings.dtype)] * cols,
        in_specs=[pl.BlockSpec(memory_space=pltpu.SMEM), pl.BlockSpec(memory_space=pltpu.VMEM)],
        out_specs=[pl.BlockSpec(memory_space=pltpu.VMEM)] * cols,
        compiler_params=pltpu.CompilerParams(vmem_limit_bytes=24 * 1024 * 1024),
        cost_estimate=pl.CostEstimate(flops=0, bytes_accessed=4 * couplings.size, transcendentals=0),
    )(own.reshape(1), couplings)


def chunk_kernel(own, *refs, parts, occupied, b_local, q):
    t_own, t_right, t_left = refs[0], refs[1:parts], refs[parts:2 * parts - 1]
    w_refs = refs[2 * parts - 1:3 * parts - 1]
    ladder_hbm = refs[3 * parts - 1]
    out_ref, t_all, w_buf, ladder, pairs, out_buf, t_sem, w_sem, l_sem, out_sem = refs[-10:]
    depth = t_own.shape[1]
    count = occupied * occupied
    pitch = count + PAD
    per_part = occupied // parts
    wide = WIDE // b_local

    def t_copy(src, block, s):
        cols = pl.ds(pl.multiple_of(block * depth, depth), depth)
        return pltpu.make_async_copy(src, t_all.at[:, cols], t_sem.at[s])

    def w_copy(s, slot):
        return pltpu.make_async_copy(w_refs[s], w_buf.at[slot], w_sem.at[slot])

    blocks = [lax.rem(own[0] - s + parts, parts) for s in range(parts)]
    t_copy(t_own, blocks[0], 0).start()
    for s in range(1, parts):
        @pl.when(own[0] >= s)
        def _():
            t_copy(t_right[s - 1], blocks[s], s).start()

        @pl.when(own[0] < s)
        def _():
            t_copy(t_left[parts - s - 1], blocks[s], s).start()
    w_copy(0, 0).start()
    w_copy(1 % parts, 1).start()
    ladder_copy = pltpu.make_async_copy(ladder_hbm, ladder, l_sem)
    ladder_copy.start()
    for s in range(parts):
        t_copy(t_own, blocks[s], s).wait()

    @pl.loop(0, parts)
    def _(step):
        slot = lax.rem(step, 2)
        w_copy(0, slot).wait()
        j0 = lax.rem(own[0] - step + parts, parts) * per_part
        for tile in range(per_part // wide):
            acc = jnp.dot(
                t_all[...], w_buf[slot, :, tile * WIDE:(tile + 1) * WIDE], preferred_element_type=jnp.float32)
            for i in range(occupied):
                for k in range(wide):
                    n = j0 + (i * occupied + tile * wide + k)
                    for h in range(GROUP // 8):
                        row = i * GROUP + h * 8
                        pairs[pl.ds(h * 8 * pitch + n, 8, stride=pitch), :] = (
                            acc[row:row + 8, k * b_local:(k + 1) * b_local])
        for s in range(2, parts):
            @pl.when(step + 2 == s)
            def _():
                w_copy(s, slot).start()

    ladder_copy.wait()
    steps = GROUP // STEP_A

    def out_copy(step, slot):
        rows = pl.ds(q * GROUP + step * STEP_A, STEP_A)
        return pltpu.make_async_copy(out_buf.at[slot], out_ref.at[rows], out_sem.at[slot])

    @pl.loop(0, steps)
    def _(step):
        slot = lax.rem(step, 2)

        @pl.when(step >= 2)
        def _():
            out_copy(step - 2, slot).wait()

        for g in range(STEP_A // wide):
            blocks = []
            for k in range(wide):
                row = pl.multiple_of((step * STEP_A + g * wide + k) * pitch, 8)
                blocks.append(pairs[pl.ds(row, count), :].astype(jnp.bfloat16))
            both = jnp.concatenate(blocks, axis=1)
            for m in range(count // 256):
                rows = slice(m * 256, (m + 1) * 256)
                mixed = jnp.dot(ladder[rows, :], both, preferred_element_type=jnp.float32)
                total = (mixed + both[rows, :].astype(jnp.float32)).astype(jnp.bfloat16)
                out_buf[slot, g * wide:(g + 1) * wide, :, rows] = total.T.reshape(wide, b_local, 256)
        out_copy(step, slot).start()

    for step in range(max(steps - 2, 0), steps):
        out_copy(step, step % 2).wait()


def chunk_update(own, pieces, panel_w, ladder, out, after, q, a_local, b_local, occupied):
    parts = len(panel_w)
    rows, depth = pieces[0].shape
    count = occupied * occupied
    k_all, width = panel_w[0].shape
    args = [*pieces, *panel_w, ladder, *after]
    aliases = {}
    if out is not None:
        aliases = {len(args) + 1: 0}
        args.append(out)
    flops = 2 * rows * k_all * occupied * b_local + 2 * GROUP * b_local * count * count
    size = parts * k_all * width + count * count + rows * k_all + GROUP * b_local * count
    return pl.pallas_call(
        functools.partial(chunk_kernel, parts=parts, occupied=occupied, b_local=b_local, q=q),
        out_shape=jax.ShapeDtypeStruct((a_local, b_local, count), jnp.bfloat16),
        in_specs=[pl.BlockSpec(memory_space=pltpu.SMEM)] + [ANY] * len(args),
        out_specs=ANY,
        scratch_shapes=[
            pltpu.VMEM((rows, k_all), jnp.bfloat16),
            pltpu.VMEM((2, k_all, width), jnp.bfloat16),
            pltpu.VMEM((count, count), jnp.bfloat16),
            pltpu.VMEM((GROUP * (count + PAD), b_local), jnp.float32),
            pltpu.VMEM((2, STEP_A, b_local, count), jnp.bfloat16),
            pltpu.SemaphoreType.DMA((parts,)),
            pltpu.SemaphoreType.DMA((2,)),
            pltpu.SemaphoreType.DMA,
            pltpu.SemaphoreType.DMA((2,)),
        ],
        input_output_aliases=aliases,
        compiler_params=pltpu.CompilerParams(vmem_limit_bytes=60 * 1024 * 1024),
        cost_estimate=pl.CostEstimate(flops=flops, bytes_accessed=2 * size, transcendentals=0),
    )(own.reshape(1), *args)


def plain_update(own, pieces, panel_w, ladder, b_local, occupied):
    parts = len(panel_w)
    back = jnp.argsort(lax.rem(own - jnp.arange(parts) + parts, parts))
    rows, depth = pieces[0].shape
    right, left = pieces[1:parts], pieces[parts:]
    by_shift = [pieces[0]] + [jnp.where(own >= s, right[s - 1], left[parts - s - 1]) for s in range(1, parts)]
    panel_t = jnp.transpose(jnp.stack(by_shift, 0)[back], (1, 0, 2)).reshape(rows, -1)
    cycle = jnp.dot(panel_t, jnp.concatenate(panel_w, axis=1), preferred_element_type=jnp.float32)
    cycle = cycle.astype(jnp.bfloat16).reshape(occupied, -1, parts, occupied // parts, b_local)[:, :, back]
    cycle = cycle.reshape(occupied, -1, occupied, b_local)
    a_count = cycle.shape[1]
    pairs = jnp.transpose(cycle, (1, 3, 0, 2)).reshape(a_count * b_local, occupied * occupied)
    mixed = lax.dot_general(pairs, ladder, (((1,), (1,)), ((), ())), preferred_element_type=jnp.float32)
    total = (mixed + pairs.astype(jnp.float32)).astype(jnp.bfloat16)
    return total.reshape(a_count, b_local, occupied * occupied)


def local(rows, cols, amplitudes, couplings, ladder):
    depth = amplitudes.shape[1]
    i_local = amplitudes.shape[0] // V
    j_local = couplings.shape[1] // V
    occupied = i_local * rows
    a_local, b_local = V // rows, V // cols
    own = lax.axis_index("col")

    arrived = list(split_columns(own, couplings, cols, j_local, b_local))
    arrived[0], amplitudes = lax.optimization_barrier((arrived[0], amplitudes))
    for s in range(1, cols):
        arrived[s] = lax.ppermute(arrived[s], "col", [(c, (c + s) % cols) for c in range(cols)])

    chunks = a_local // GROUP
    blocks = amplitudes.reshape(i_local, rows, chunks, GROUP, depth).transpose(1, 2, 0, 3, 4)
    blocks = lax.all_to_all(blocks, "row", split_axis=0, concat_axis=0, tiled=True)

    arrived[1:], blocks = lax.optimization_barrier((arrived[1:], blocks))
    panel_w = [lax.all_gather(part, "row", axis=0, tiled=True) for part in arrived]

    pieces = []
    for q in range(0, chunks, 2):
        both = [blocks[:, p].reshape(occupied * GROUP, depth) for p in range(q, min(q + 2, chunks))]
        if q:
            middle = (cols - 1) // 2
            for n, (right, left) in enumerate(pieces[-2:][:len(both)]):
                both[n], right[middle + 1], left[middle + 1] = lax.optimization_barrier(
                    (both[n], right[middle + 1], left[middle + 1]))
        pair = [([held], [held]) for held in both]
        for s in range(1, cols):
            for right, left in pair:
                right.append(lax.ppermute(right[-1], "col", [(c, c + 1) for c in range(s - 1, cols - 1)]))
                left.append(lax.ppermute(left[-1], "col", [(c + 1, c) for c in range(cols - s)]))
            if s == 1:
                started = [got[-1] for sides in pair for got in sides]
        pieces += pair
    pieces = [[right[0], *right[1:], *left[1:]] for right, left in pieces]

    per_part = occupied // cols
    if b_local % 128 or WIDE % b_local or depth % 128 or cols < 2 or per_part * b_local % WIDE:
        return jnp.concatenate(
            [plain_update(own, got, panel_w, ladder, b_local, occupied) for got in pieces], axis=0)
    out = None
    for q in range(chunks):
        after = () if q else started
        out = chunk_update(own, pieces[q], panel_w, ladder, out, after, q, a_local, b_local, occupied)
    return out


def solution(mesh):
    in_specs = (P("row", "col"), P("row", "col"), P())
    out_specs = P("row", "col", None)
    body = functools.partial(local, mesh.shape["row"], mesh.shape["col"])
    return jax.shard_map(body, mesh=mesh, in_specs=in_specs, out_specs=out_specs, check_vma=False)
```

time: 1210 us -> 273 us (0.23)
  blocking collectives: 563 us -> 0 us
  matrix products: 242 us -> 0 us
  waiting for transfers between devices: 245 us -> 110 us
  local copies, waits for them, and re-layouts: 134 us -> 11.4 us
  Pallas kernels: 0 us -> 76 us
  starting transfers between devices: 0.04 us -> 60.6 us
    all_to_all x2 -> x0, blocking collectives: 563 us -> none  [the longest x1 375 us: local(): lax.all_to_all(blocks, 'col', split_axis=3, concat_axis=2, tiled=True)]
    dot_general x2 -> x0, matrix products: 242 us -> none  [the longest x1 202 us: local(): lax.dot_general(pairs, ladder, (((1,), (1,)), ((), ())), preferred_elemen...]
    all_gather x2 -> x4, waiting for transfers between devices: 243 us -> 20.1 us  [local(): lax.all_gather(part, 'row', axis=0, tiled=True)]
    ppermute x0 -> x27, waiting for transfers between devices: none -> 88.4 us  [the longest x12 45.7 us: local(): lax.ppermute(left[-1], 'col', [(c + 1, c) for c in range(cols - s)])]
    pallas_call x0 -> x5, Pallas kernels: none -> 76 us  [the longest x4 74.6 us: chunk_update(): pl.pallas_call(functools.partial(chunk_kernel, parts=parts, occupied=occu...]
    ppermute x0 -> x27, starting transfers between devices: none -> 55.3 us  [the longest x12 33.6 us: local(): lax.ppermute(right[-1], 'col', [(c, c + 1) for c in range(s - 1, cols - 1)])]
    reshape x2 -> x0, local copies, waits for them, and re-layouts: 53.1 us -> none  [the longest x1 30.7 us: local(): blocks = cycle.reshape(i_local, V, j_local, V)]
    all_to_all x2 -> x0, local copies, waits for them, and re-layouts: 32.5 us -> none  [the longest x1 30.1 us: local(): lax.all_to_all(blocks, 'col', split_axis=3, concat_axis=2, tiled=True)]
  transfers between devices with their start and end apart: 2 -> 32, of which waited for: 2 -> 12; matrix products, arithmetic and copies ran while one was open for 0% -> 2% of each run, Pallas kernels for 0% -> 21%
where the time goes in v3:
time: 273 us; the launch traced here: 271 us
  waiting for transfers between devices  110 us (40%)
  Pallas kernels  76 us (28%)
  starting transfers between devices  60.6 us (22%)
  between operations  13.7 us (5%)
  local copies, waits for them, and re-layouts  11.4 us (4%)
    pallas_call x4, Pallas kernels, chunk_update(): pl.pallas_call(functools.partial(chunk_kernel, parts=parts, occupied=occu...  74.6 us
    ppermute x12, waiting for transfers between devices, local(): lax.ppermute(left[-1], 'col', [(c + 1, c) for c in range(cols - s)])  45.7 us
    ppermute x12, starting transfers between devices, local(): lax.ppermute(right[-1], 'col', [(c, c + 1) for c in range(s - 1, cols - 1)])  33.6 us
    ppermute x3, waiting for transfers between devices, local(): lax.ppermute(arrived[s], 'col', [(c, (c + s) % cols) for c in range(cols)])  33.1 us
    all_gather x4, waiting for transfers between devices, local(): lax.all_gather(part, 'row', axis=0, tiled=True)  20.1 us
    ppermute x12, starting transfers between devices, local(): lax.ppermute(left[-1], 'col', [(c + 1, c) for c in range(cols - s)])  15.4 us
    ppermute x12, waiting for transfers between devices, local(): lax.ppermute(right[-1], 'col', [(c, c + 1) for c in range(s - 1, cols - 1)])  9.64 us
    unnamed x46, local copies, waits for them, and re-layouts  6.45 us
  transfers between devices with their start and end apart: 32, of which 12 were waited for; matrix products, arithmetic and copies ran while one was open for 2% of the time, Pallas kernels for 21%

profile of v3, /device:TPU:0, one launch (start us, length us, event | category | flops | bytes accessed | tf_op | source)
XLA Modules:
  0.0 271.3 jit_solution(5666878360600103235)
XLA Ops:
  6.5 1.6 copy-done
  8.1 1.4 shard_map.37
  9.5 0.0 all-gather.5.cloned.1.call-update
  9.5 3.2 %copy.8 = bf16[8,4,4,16,512]{4,3,2,1,0:T(8,128)(2,1)} copy(bf16[8,4,4,16,512]{4,3,1,0,2:T(8,128)(2,1)} %bitcast.17) | data formatting | bytes 4194304 | tf_op jit(solution)/shard_map/transpose | solution.py:197
  12.7 5.2 %all-to-all-start = ((bf16[8,4,4,16,512]{4,3,2,1,0:T(8,128)(2,1)}), bf16[8,4,4,16,512]{4,3,2,1,0:T(8,128)(2,1)}, u32[]{:S(2)}, u32[]{:S(2)}) async-start(bf16[8,4,4,16,512]{4,3,2,1,0:T(8,128)(2,1)} %copy.8), calls=%async_computation | async-start | bytes 4194304 | tf_op jit(solution)/shard_map/all_to_all | solution.py:198
  17.8 0.0 all-gather.11.cloned.1.call-start
  17.9 2.3 collective-permute-start
  20.2 2.6 collective-permute-start.1
  22.8 1.3 collective-permute-start.2
  24.1 10.9 %collective-permute-done = bf16[256,1024]{1,0:T(8,128)(2,1)S(1)} collective-permute-done((bf16[256,1024]{1,0:T(8,128)(2,1)S(1)}, bf16[256,1024]{1,0:T(8,128)(2,1)S(1)}, u32[]{:S(2)}, u32[]{:S(2)}) %collective-permute-start) | collective-permute-done | bytes 524320 | tf_op jit(solution)/shard_map/ppermute | solution.py:194
  35.0 22.1 %collective-permute-done.1 = bf16[256,1024]{1,0:T(8,128)(2,1)S(1)} collective-permute-done((bf16[256,1024]{1,0:T(8,128)(2,1)S(1)}, bf16[256,1024]{1,0:T(8,128)(2,1)S(1)}, u32[]{:S(2)}, u32[]{:S(2)}) %collective-permute-start.1) | collective-permute-done | bytes 524320 | tf_op jit(solution)/shard_map/ppermute | solution.py:194
  57.2 0.8 copy-done.15
  58.0 0.0 all-gather.11.cloned.1.call-update
  58.0 0.0 all-gather.7.cloned.1.call-start
  58.1 0.7 all-gather.7.cloned.1.call-update
  58.7 0.0 all-gather.9.cloned.1.call-start
  58.8 0.5 all-gather.9.cloned.1.call-update
  59.3 1.7 fusion
  61.1 13.6 %collective-permute-start.13 = (bf16[512,512]{1,0:T(8,128)(2,1)S(1)}, bf16[512,512]{1,0:T(8,128)(2,1)S(1)}, u32[]{:S(2)}, u32[]{:S(2)}) collective-permute-start(bf16[512,512]{1,0:T(8,128)(2,1)S(1)} %bitcast.18), channel_id=1, source_target_pairs={{0,1},{1,2},{2,3},{4,5},{5,6},{6,7},{8,9},{9,10},{10,11},{12,13},{... | collective-permute-start | bytes 1572872 | tf_op jit(solution)/shard_map/ppermute | solution.py:214
  74.7 1.3 collective-permute-start.15
  76.0 4.6 %collective-permute-start.3 = (bf16[512,512]{1,0:T(8,128)(2,1)S(1)}, bf16[512,512]{1,0:T(8,128)(2,1)S(1)}, u32[]{:S(2)}, u32[]{:S(2)}) collective-permute-start(bf16[512,512]{1,0:T(8,128)(2,1)S(1)} %bitcast.14), channel_id=1, source_target_pairs={{0,1},{1,2},{2,3},{4,5},{5,6},{6,7},{8,9},{9,10},{10,11},{12,13},{... | collective-permute-start | bytes 1572872 | tf_op jit(solution)/shard_map/ppermute | solution.py:214
  80.6 1.3 collective-permute-start.5
  81.9 5.1 %collective-permute-done.13.refs_1_ = bf16[512,512]{1,0:T(8,128)(2,1)S(1)} collective-permute-done((bf16[512,512]{1,0:T(8,128)(2,1)S(1)}, bf16[512,512]{1,0:T(8,128)(2,1)S(1)}, u32[]{:S(2)}, u32[]{:S(2)}) %collective-permute-start.13) | collective-permute-done | bytes 524320 | tf_op jit(solution)/shard_map/ppermute | solution.py:214
  87.0 0.7 collective-permute-start.14
  87.7 3.8 %collective-permute-done.15.refs_4_ = bf16[512,512]{1,0:T(8,128)(2,1)S(1)} collective-permute-done((bf16[512,512]{1,0:T(8,128)(2,1)S(1)}, bf16[512,512]{1,0:T(8,128)(2,1)S(1)}, u32[]{:S(2)}, u32[]{:S(2)}) %collective-permute-start.15) | collective-permute-done | bytes 524320 | tf_op jit(solution)/shard_map/ppermute | solution.py:215
  91.4 1.3 collective-permute-start.16
  92.7 4.5 %collective-permute-done.3.refs_1_ = bf16[512,512]{1,0:T(8,128)(2,1)S(1)} collective-permute-done((bf16[512,512]{1,0:T(8,128)(2,1)S(1)}, bf16[512,512]{1,0:T(8,128)(2,1)S(1)}, u32[]{:S(2)}, u32[]{:S(2)}) %collective-permute-start.3) | collective-permute-done | bytes 524320 | tf_op jit(solution)/shard_map/ppermute | solution.py:214
  97.3 0.7 collective-permute-start.4
  98.0 4.7 %collective-permute-done.5.refs_4_ = bf16[512,512]{1,0:T(8,128)(2,1)S(1)} collective-permute-done((bf16[512,512]{1,0:T(8,128)(2,1)S(1)}, bf16[512,512]{1,0:T(8,128)(2,1)S(1)}, u32[]{:S(2)}, u32[]{:S(2)}) %collective-permute-start.5) | collective-permute-done | bytes 524320 | tf_op jit(solution)/shard_map/ppermute | solution.py:215
  102.7 1.3 collective-permute-start.6
  104.0 0.0 collective-permute-done.14.refs_2_
  104.0 9.9 %collective-permute-done.16.refs_5_ = bf16[512,512]{1,0:T(8,128)(2,1)S(1)} collective-permute-done((bf16[512,512]{1,0:T(8,128)(2,1)S(1)}, bf16[512,512]{1,0:T(8,128)(2,1)S(1)}, u32[]{:S(2)}, u32[]{:S(2)}) %collective-permute-start.16) | collective-permute-done | bytes 524320 | tf_op jit(solution)/shard_map/ppermute | solution.py:215
  113.9 2.8 %collective-permute-start.17 = (bf16[512,512]{1,0:T(8,128)(2,1)S(1)}, bf16[512,512]{1,0:T(8,128)(2,1)}, u32[]{:S(2)}, u32[]{:S(2)}) collective-permute-start(bf16[512,512]{1,0:T(8,128)(2,1)S(1)} %bitcast.11), channel_id=1, source_target_pairs={{0,1},{1,2},{2,3},{4,5},{5,6},{6,7},{8,9},{9,10},{10,11},{12,13},{... | collective-permute-start | bytes 1572872 | tf_op jit(solution)/shard_map/ppermute | solution.py:214
  116.8 1.3 collective-permute-start.20
  118.0 0.0 collective-permute-done.4.refs_2_
  118.1 7.2 %collective-permute-done.6.refs_5_ = bf16[512,512]{1,0:T(8,128)(2,1)} collective-permute-done((bf16[512,512]{1,0:T(8,128)(2,1)S(1)}, bf16[512,512]{1,0:T(8,128)(2,1)}, u32[]{:S(2)}, u32[]{:S(2)}) %collective-permute-start.6) | collective-permute-done | bytes 524320 | tf_op jit(solution)/shard_map/ppermute | solution.py:215
  125.2 1.3 collective-permute-start.10
  126.5 5.4 %collective-permute-start.7 = (bf16[512,512]{1,0:T(8,128)(2,1)S(1)}, bf16[512,512]{1,0:T(8,128)(2,1)}, u32[]{:S(2)}, u32[]{:S(2)}) collective-permute-start(bf16[512,512]{1,0:T(8,128)(2,1)S(1)} %bitcast.9), channel_id=1, source_target_pairs={{0,1},{1,2},{2,3},{4,5},{5,6},{6,7},{8,9},{9,10},{10,11},{12,13},{... | collective-permute-start | bytes 1572872 | tf_op jit(solution)/shard_map/ppermute | solution.py:214
  131.9 0.7 collective-permute-start.25
  132.6 0.0 collective-permute-done.17.refs_12_.refs_1_
  132.6 1.3 collective-permute-start.26
  133.9 2.6 collective-permute-done.20.refs_13_.refs_4_
  136.5 0.7 collective-permute-start.23
  137.2 10.4 %collective-permute-done.10.refs_15_.refs_4_ = bf16[512,512]{1,0:T(8,128)(2,1)S(1)} collective-permute-done((bf16[512,512]{1,0:T(8,128)(2,1)S(1)}, bf16[512,512]{1,0:T(8,128)(2,1)S(1)}, u32[]{:S(2)}, u32[]{:S(2)}) %collective-permute-start.10) | collective-permute-done | bytes 524320 | tf_op jit(solution)/shard_map/ppermute | solution.py:215
  147.6 1.3 collective-permute-start.24
  148.9 1.5 collective-permute-start.18
  150.4 1.3 collective-permute-start.21
  151.7 7.1 %collective-permute-done.26.refs_6_ = bf16[512,512]{1,0:T(8,128)(2,1)S(1)} collective-permute-done((bf16[512,512]{1,0:T(8,128)(2,1)S(1)}, bf16[512,512]{1,0:T(8,128)(2,1)S(1)}, u32[]{:S(2)}, u32[]{:S(2)}) %collective-permute-start.26) | collective-permute-done | bytes 524320 | tf_op jit(solution)/shard_map/ppermute | solution.py:215
  158.8 1.3 collective-permute-start.11
  160.2 0.8 copy-done.8
  161.0 1.5 collective-permute-start.8
  162.5 20.1 %all-gather.9.cloned.1.call-done.refs_9_ = bf16[2048,1024]{1,0:T(8,128)(2,1)} async-done(((bf16[256,1024]{1,0:T(8,128)(2,1)}), bf16[2048,1024]{1,0:T(8,128)(2,1)}) %all-gather.9.cloned.1.call-update) | async-done | bytes 4194320 | tf_op jit(solution)/shard_map/all_gather | solution.py:201
  182.6 18.7 %shard_map.38.refs_12_ = bf16[64,128,1024]{2,1,0:T(8,128)(2,1)} custom-call(s32[1]{0:T(128)} %bitcast.own, bf16[512,512]{1,0:T(8,128)(2,1)} %bitcast.20, bf16[512,512]{1,0:T(8,128)(2,1)} %copy-done.17, bf16[512,512]{1,0:T(8,128)(2,1)} %copy-done.19, bf16[512,512]{1,0:T(8,128)(2,1)} %copy-done.21, bf16[512,512]{1,0:T(8,128)(2,1)} %copy-done.18, ...), custom_call_target="tpu_custom_call" | custom-call | flops 12884901888 | bytes 25165824 | tf_op jit(solution)/shard_map/pallas_call | solution.py:144
  201.3 0.7 collective-permute-start.19
  202.0 1.3 collective-permute-start.22
  203.3 1.3 collective-permute-start.12
  204.6 0.9 collective-permute-start.9
  205.5 18.7 %shard_map.39.refs_12_ = bf16[64,128,1024]{2,1,0:T(8,128)(2,1)} custom-call(s32[1]{0:T(128)} %bitcast.own, bf16[512,512]{1,0:T(8,128)(2,1)} %bitcast.16, bf16[512,512]{1,0:T(8,128)(2,1)} %copy-done.4, bf16[512,512]{1,0:T(8,128)(2,1)} %copy-done.7, bf16[512,512]{1,0:T(8,128)(2,1)} %copy-done.8, ...), custom_call_target="tpu_custom_call", output_to_operand_aliasing={{}: (13, {})} | custom-call | flops 12884901888 | bytes 25165824 | tf_op jit(solution)/shard_map/pallas_call | solution.py:144
  224.2 0.8 copy-done.10
  225.0 0.9 copy-done.12
  225.8 18.7 %shard_map.40.refs_12_ = bf16[64,128,1024]{2,1,0:T(8,128)(2,1)} custom-call(s32[1]{0:T(128)} %bitcast.own, bf16[512,512]{1,0:T(8,128)(2,1)} %bitcast.13, bf16[512,512]{1,0:T(8,128)(2,1)} %collective-permute-done.17.refs_12_.refs_1_, bf16[512,512]{1,0:T(8,128)(2,1)} %collective-permute-done.18.refs_2_, ...), custom_call_target="tpu_custom_call", output_to_operand_aliasing={{}: (13, {})} | custom-call | flops 12884901888 | bytes 25165824 | tf_op jit(solution)/shard_map/pallas_call | solution.py:144
  244.5 0.8 copy-done.9
  245.3 0.8 copy-done.11
  246.1 18.6 %shard_map.41 = bf16[64,128,1024]{2,1,0:T(8,128)(2,1)} custom-call(s32[1]{0:T(128)} %bitcast.own, bf16[512,512]{1,0:T(8,128)(2,1)} %bitcast.10, bf16[512,512]{1,0:T(8,128)(2,1)} %collective-permute-done.7.refs_14_.refs_1_, bf16[512,512]{1,0:T(8,128)(2,1)} %collective-permute-done.8.refs_2_, ...), custom_call_target="tpu_custom_call", output_to_operand_aliasing={{}: (13, {})} | custom-call | flops 12884901888 | bytes 25165824 | tf_op jit(solution)/shard_map/pallas_call | solution.py:144
  (57 shorter events, 0.1 us)
Async XLA Ops:
  6.5 155.9 %all-gather.5.cloned.1.call-start = ((), (), s32[]{:S(2)}) async-start(), calls=%async_computation.1 | async-start | bytes 4718592 | tf_op jit(solution)/shard_map/all_gather | solution.py:201
  6.5 1.6 copy-start
  12.7 44.5 %all-to-all-start = ((bf16[8,4,4,16,512]{4,3,2,1,0:T(8,128)(2,1)}), bf16[8,4,4,16,512]{4,3,2,1,0:T(8,128)(2,1)}, u32[]{:S(2)}, u32[]{:S(2)}) async-start(bf16[8,4,4,16,512]{4,3,2,1,0:T(8,128)(2,1)} %copy.8), calls=%async_computation | async-start | bytes 4194304 | tf_op jit(solution)/shard_map/all_to_all | solution.py:198
  17.8 144.6 %all-gather.11.cloned.1.call-start = ((), (), s32[]{:S(2)}) async-start(), calls=%async_computation.4 | async-start | bytes 4718592 | tf_op jit(solution)/shard_map/all_gather | solution.py:201
  17.9 17.1 %collective-permute-start = (bf16[256,1024]{1,0:T(8,128)(2,1)S(1)}, bf16[256,1024]{1,0:T(8,128)(2,1)S(1)}, u32[]{:S(2)}, u32[]{:S(2)}) collective-permute-start(bf16[256,1024]{1,0:T(8,128)(2,1)S(1)} %get-tuple-element.21), channel_id=1, source_target_pairs={{0,1},{1,2},{2,3},{3,0},{4,5},{5,6},{6,7},{7,4},{8,9},{9,10},{10,1... | collective-permute-start | bytes 1572872 | tf_op jit(solution)/shard_map/ppermute | solution.py:194
  20.2 37.0 %collective-permute-start.1 = (bf16[256,1024]{1,0:T(8,128)(2,1)S(1)}, bf16[256,1024]{1,0:T(8,128)(2,1)S(1)}, u32[]{:S(2)}, u32[]{:S(2)}) collective-permute-start(bf16[256,1024]{1,0:T(8,128)(2,1)S(1)} %get-tuple-element.22), channel_id=1, source_target_pairs={{0,2},{1,3},{2,0},{3,1},{4,6},{5,7},{6,4},{7,5},{8,10},{9,11},{10,... | collective-permute-start | bytes 1572872 | tf_op jit(solution)/shard_map/ppermute | solution.py:194
  22.8 34.4 %collective-permute-start.2 = (bf16[256,1024]{1,0:T(8,128)(2,1)S(1)}, bf16[256,1024]{1,0:T(8,128)(2,1)S(1)}, u32[]{:S(2)}, u32[]{:S(2)}) collective-permute-start(bf16[256,1024]{1,0:T(8,128)(2,1)S(1)} %get-tuple-element.23), channel_id=1, source_target_pairs={{0,3},{1,0},{2,1},{3,2},{4,7},{5,4},{6,5},{7,6},{8,11},{9,8},{10,9... | collective-permute-start | bytes 1572872 | tf_op jit(solution)/shard_map/ppermute | solution.py:194
  35.0 23.0 %copy-start.13 = (bf16[256,1024]{1,0:T(8,128)(2,1)}, bf16[256,1024]{1,0:T(8,128)(2,1)S(1)}, u32[]{:S(2)}) copy-start(bf16[256,1024]{1,0:T(8,128)(2,1)S(1)} %collective-permute-done) | copy-start | bytes 1572868
  57.2 1.6 copy-start.14
  57.2 0.8 copy-start.15
  58.0 104.4 %all-gather.7.cloned.1.call-start = ((), (), s32[]{:S(2)}) async-start(), calls=%async_computation.2 | async-start | bytes 4718592 | tf_op jit(solution)/shard_map/all_gather | solution.py:201
  58.7 123.8 %all-gather.9.cloned.1.call-start = ((), (), s32[]{:S(2)}) async-start(), calls=%async_computation.3 | async-start | bytes 4718592 | tf_op jit(solution)/shard_map/all_gather | solution.py:201
  61.1 99.1 %copy-start.16 = (bf16[8,1,4,16,512]{4,3,2,1,0:T(8,128)(2,1)}, bf16[8,1,4,16,512]{4,3,2,1,0:T(8,128)(2,1)S(1)}, u32[]{:S(2)}) copy-start(bf16[8,1,4,16,512]{4,3,2,1,0:T(8,128)(2,1)S(1)} %get-tuple-element.37) | copy-start | bytes 1572868
  61.1 140.1 %copy-start.1 = (bf16[8,1,4,16,512]{4,3,2,1,0:T(8,128)(2,1)}, bf16[8,1,4,16,512]{4,3,2,1,0:T(8,128)(2,1)S(1)}, u32[]{:S(2)}) copy-start(bf16[8,1,4,16,512]{4,3,2,1,0:T(8,128)(2,1)S(1)} %get-tuple-element.40) | copy-start | bytes 1572868
  61.1 140.1 %copy-start.2 = (bf16[8,1,4,16,512]{4,3,2,1,0:T(8,128)(2,1)}, bf16[8,1,4,16,512]{4,3,2,1,0:T(8,128)(2,1)S(1)}, u32[]{:S(2)}) copy-start(bf16[8,1,4,16,512]{4,3,2,1,0:T(8,128)(2,1)S(1)} %get-tuple-element.38) | copy-start | bytes 1572868
  61.1 140.1 %copy-start.3 = (bf16[8,1,4,16,512]{4,3,2,1,0:T(8,128)(2,1)}, bf16[8,1,4,16,512]{4,3,2,1,0:T(8,128)(2,1)S(1)}, u32[]{:S(2)}) copy-start(bf16[8,1,4,16,512]{4,3,2,1,0:T(8,128)(2,1)S(1)} %get-tuple-element.39) | copy-start | bytes 1572868
  61.1 25.9 %collective-permute-start.13 = (bf16[512,512]{1,0:T(8,128)(2,1)S(1)}, bf16[512,512]{1,0:T(8,128)(2,1)S(1)}, u32[]{:S(2)}, u32[]{:S(2)}) collective-permute-start(bf16[512,512]{1,0:T(8,128)(2,1)S(1)} %bitcast.18), channel_id=1, source_target_pairs={{0,1},{1,2},{2,3},{4,5},{5,6},{6,7},{8,9},{9,10},{10,11},{12,13},{... | collective-permute-start | bytes 1572872 | tf_op jit(solution)/shard_map/ppermute | solution.py:214
  74.7 16.7 %collective-permute-start.15 = (bf16[512,512]{1,0:T(8,128)(2,1)S(1)}, bf16[512,512]{1,0:T(8,128)(2,1)S(1)}, u32[]{:S(2)}, u32[]{:S(2)}) collective-permute-start(bf16[512,512]{1,0:T(8,128)(2,1)S(1)} %bitcast.19), channel_id=1, source_target_pairs={{1,0},{2,1},{3,2},{5,4},{6,5},{7,6},{9,8},{10,9},{11,10},{13,12},{... | collective-permute-start | bytes 1572872 | tf_op jit(solution)/shard_map/ppermute | solution.py:215
  76.0 21.3 %collective-permute-start.3 = (bf16[512,512]{1,0:T(8,128)(2,1)S(1)}, bf16[512,512]{1,0:T(8,128)(2,1)S(1)}, u32[]{:S(2)}, u32[]{:S(2)}) collective-permute-start(bf16[512,512]{1,0:T(8,128)(2,1)S(1)} %bitcast.14), channel_id=1, source_target_pairs={{0,1},{1,2},{2,3},{4,5},{5,6},{6,7},{8,9},{9,10},{10,11},{12,13},{... | collective-permute-start | bytes 1572872 | tf_op jit(solution)/shard_map/ppermute | solution.py:214
  80.6 22.1 %collective-permute-start.5 = (bf16[512,512]{1,0:T(8,128)(2,1)S(1)}, bf16[512,512]{1,0:T(8,128)(2,1)S(1)}, u32[]{:S(2)}, u32[]{:S(2)}) collective-permute-start(bf16[512,512]{1,0:T(8,128)(2,1)S(1)} %bitcast.15), channel_id=1, source_target_pairs={{1,0},{2,1},{3,2},{5,4},{6,5},{7,6},{9,8},{10,9},{11,10},{13,12},{... | collective-permute-start | bytes 1572872 | tf_op jit(solution)/shard_map/ppermute | solution.py:215
  87.0 46.9 %copy-start.17 = (bf16[512,512]{1,0:T(8,128)(2,1)}, bf16[512,512]{1,0:T(8,128)(2,1)S(1)}, u32[]{:S(2)}) copy-start(bf16[512,512]{1,0:T(8,128)(2,1)S(1)} %collective-permute-done.13.refs_1_) | copy-start | bytes 1572868
  87.0 17.0 %collective-permute-start.14 = (bf16[512,512]{1,0:T(8,128)(2,1)S(1)}, bf16[512,512]{1,0:T(8,128)(2,1)S(1)}, u32[]{:S(2)}, u32[]{:S(2)}) collective-permute-start(bf16[512,512]{1,0:T(8,128)(2,1)S(1)} %collective-permute-done.13.refs_1_), channel_id=1, source_target_pairs={{1,2},{2,3},{5,6},{6,7},{9,10},{10,11},{13,14},{14,15},{17,18},{18... | collective-permute-start | bytes 1572872 | tf_op jit(solution)/shard_map/ppermute | solution.py:214
  91.4 68.7 %copy-start.18 = (bf16[512,512]{1,0:T(8,128)(2,1)}, bf16[512,512]{1,0:T(8,128)(2,1)S(1)}, u32[]{:S(2)}) copy-start(bf16[512,512]{1,0:T(8,128)(2,1)S(1)} %collective-permute-done.15.refs_4_) | copy-start | bytes 1572868
  91.4 22.5 %collective-permute-start.16 = (bf16[512,512]{1,0:T(8,128)(2,1)S(1)}, bf16[512,512]{1,0:T(8,128)(2,1)S(1)}, u32[]{:S(2)}, u32[]{:S(2)}) collective-permute-start(bf16[512,512]{1,0:T(8,128)(2,1)S(1)} %collective-permute-done.15.refs_4_), channel_id=1, source_target_pairs={{1,0},{2,1},{5,4},{6,5},{9,8},{10,9},{13,12},{14,13},{17,16},{18,1... | collective-permute-start | bytes 1572872 | tf_op jit(solution)/shard_map/ppermute | solution.py:215
  97.3 104.0 %copy-start.4 = (bf16[512,512]{1,0:T(8,128)(2,1)}, bf16[512,512]{1,0:T(8,128)(2,1)S(1)}, u32[]{:S(2)}) copy-start(bf16[512,512]{1,0:T(8,128)(2,1)S(1)} %collective-permute-done.3.refs_1_) | copy-start | bytes 1572868
  97.3 20.8 %collective-permute-start.4 = (bf16[512,512]{1,0:T(8,128)(2,1)S(1)}, bf16[512,512]{1,0:T(8,128)(2,1)S(1)}, u32[]{:S(2)}, u32[]{:S(2)}) collective-permute-start(bf16[512,512]{1,0:T(8,128)(2,1)S(1)} %collective-permute-done.3.refs_1_), channel_id=1, source_target_pairs={{1,2},{2,3},{5,6},{6,7},{9,10},{10,11},{13,14},{14,15},{17,18},{18... | collective-permute-start | bytes 1572872 | tf_op jit(solution)/shard_map/ppermute | solution.py:214
  102.7 98.6 %copy-start.5 = (bf16[512,512]{1,0:T(8,128)(2,1)}, bf16[512,512]{1,0:T(8,128)(2,1)S(1)}, u32[]{:S(2)}) copy-start(bf16[512,512]{1,0:T(8,128)(2,1)S(1)} %collective-permute-done.5.refs_4_) | copy-start | bytes 1572868
  102.7 22.6 %collective-permute-start.6 = (bf16[512,512]{1,0:T(8,128)(2,1)S(1)}, bf16[512,512]{1,0:T(8,128)(2,1)}, u32[]{:S(2)}, u32[]{:S(2)}) collective-permute-start(bf16[512,512]{1,0:T(8,128)(2,1)S(1)} %collective-permute-done.5.refs_4_), channel_id=1, source_target_pairs={{1,0},{2,1},{5,4},{6,5},{9,8},{10,9},{13,12},{14,13},{17,16},{18,1... | collective-permute-start | bytes 1572872 | tf_op jit(solution)/shard_map/ppermute | solution.py:215
  104.0 56.2 %copy-start.19 = (bf16[512,512]{1,0:T(8,128)(2,1)}, bf16[512,512]{1,0:T(8,128)(2,1)S(1)}, u32[]{:S(2)}) copy-start(bf16[512,512]{1,0:T(8,128)(2,1)S(1)} %collective-permute-done.14.refs_2_) | copy-start | bytes 1572868
  113.9 46.3 %copy-start.20 = (bf16[512,512]{1,0:T(8,128)(2,1)}, bf16[512,512]{1,0:T(8,128)(2,1)S(1)}, u32[]{:S(2)}) copy-start(bf16[512,512]{1,0:T(8,128)(2,1)S(1)} %collective-permute-done.16.refs_5_) | copy-start | bytes 1572868
  113.9 18.7 %collective-permute-start.17 = (bf16[512,512]{1,0:T(8,128)(2,1)S(1)}, bf16[512,512]{1,0:T(8,128)(2,1)}, u32[]{:S(2)}, u32[]{:S(2)}) collective-permute-start(bf16[512,512]{1,0:T(8,128)(2,1)S(1)} %bitcast.11), channel_id=1, source_target_pairs={{0,1},{1,2},{2,3},{4,5},{5,6},{6,7},{8,9},{9,10},{10,11},{12,13},{... | collective-permute-start | bytes 1572872 | tf_op jit(solution)/shard_map/ppermute | solution.py:214
  116.8 19.7 %collective-permute-start.20 = (bf16[512,512]{1,0:T(8,128)(2,1)S(1)}, bf16[512,512]{1,0:T(8,128)(2,1)}, u32[]{:S(2)}, u32[]{:S(2)}) collective-permute-start(bf16[512,512]{1,0:T(8,128)(2,1)S(1)} %bitcast.12), channel_id=1, source_target_pairs={{1,0},{2,1},{3,2},{5,4},{6,5},{7,6},{9,8},{10,9},{11,10},{13,12},{... | collective-permute-start | bytes 1572872 | tf_op jit(solution)/shard_map/ppermute | solution.py:215
  118.0 33.6 %copy-start.7 = (bf16[512,512]{1,0:T(8,128)(2,1)}, bf16[512,512]{1,0:T(8,128)(2,1)S(1)}, u32[]{:S(2)}) copy-start(bf16[512,512]{1,0:T(8,128)(2,1)S(1)} %collective-permute-done.4.refs_2_) | copy-start | bytes 1572868
  125.2 22.4 %collective-permute-start.10 = (bf16[512,512]{1,0:T(8,128)(2,1)S(1)}, bf16[512,512]{1,0:T(8,128)(2,1)S(1)}, u32[]{:S(2)}, u32[]{:S(2)}) collective-permute-start(bf16[512,512]{1,0:T(8,128)(2,1)S(1)} %bitcast.8), channel_id=1, source_target_pairs={{1,0},{2,1},{3,2},{5,4},{6,5},{7,6},{9,8},{10,9},{11,10},{13,12},{... | collective-permute-start | bytes 1572872 | tf_op jit(solution)/shard_map/ppermute | solution.py:215
  126.5 22.4 %collective-permute-start.7 = (bf16[512,512]{1,0:T(8,128)(2,1)S(1)}, bf16[512,512]{1,0:T(8,128)(2,1)}, u32[]{:S(2)}, u32[]{:S(2)}) collective-permute-start(bf16[512,512]{1,0:T(8,128)(2,1)S(1)} %bitcast.9), channel_id=1, source_target_pairs={{0,1},{1,2},{2,3},{4,5},{5,6},{6,7},{8,9},{9,10},{10,11},{12,13},{... | collective-permute-start | bytes 1572872 | tf_op jit(solution)/shard_map/ppermute | solution.py:214
  131.9 18.5 %collective-permute-start.25 = (bf16[512,512]{1,0:T(8,128)(2,1)S(1)}, bf16[512,512]{1,0:T(8,128)(2,1)S(1)}, u32[]{:S(2)}, u32[]{:S(2)}) collective-permute-start(bf16[512,512]{1,0:T(8,128)(2,1)S(1)} %collective-permute-done.14.refs_2_), channel_id=1, source_target_pairs={{2,3},{6,7},{10,11},{14,15},{18,19},{22,23},{26,27},{30,31}} | collective-permute-start | bytes 1572872 | tf_op jit(solution)/shard_map/ppermute | solution.py:214
  132.6 26.2 %collective-permute-start.26 = (bf16[512,512]{1,0:T(8,128)(2,1)S(1)}, bf16[512,512]{1,0:T(8,128)(2,1)S(1)}, u32[]{:S(2)}, u32[]{:S(2)}) collective-permute-start(bf16[512,512]{1,0:T(8,128)(2,1)S(1)} %collective-permute-done.16.refs_5_), channel_id=1, source_target_pairs={{1,0},{5,4},{9,8},{13,12},{17,16},{21,20},{25,24},{29,28}} | collective-permute-start | bytes 1572872 | tf_op jit(solution)/shard_map/ppermute | solution.py:215
  136.5 23.7 %collective-permute-start.23 = (bf16[512,512]{1,0:T(8,128)(2,1)S(1)}, bf16[512,512]{1,0:T(8,128)(2,1)S(1)}, u32[]{:S(2)}, u32[]{:S(2)}) collective-permute-start(bf16[512,512]{1,0:T(8,128)(2,1)S(1)} %collective-permute-done.4.refs_2_), channel_id=1, source_target_pairs={{2,3},{6,7},{10,11},{14,15},{18,19},{22,23},{26,27},{30,31}} | collective-permute-start | bytes 1572872 | tf_op jit(solution)/shard_map/ppermute | solution.py:214
  147.6 34.9 %copy-start.6 = (bf16[512,512]{1,0:T(8,128)(2,1)}, bf16[512,512]{1,0:T(8,128)(2,1)S(1)}, u32[]{:S(2)}) copy-start(bf16[512,512]{1,0:T(8,128)(2,1)S(1)} %collective-permute-done.10.refs_15_.refs_4_) | copy-start | bytes 1572868
  147.6 57.9 %collective-permute-start.24 = (bf16[512,512]{1,0:T(8,128)(2,1)}, bf16[512,512]{1,0:T(8,128)(2,1)}, u32[]{:S(2)}, u32[]{:S(2)}) collective-permute-start(bf16[512,512]{1,0:T(8,128)(2,1)} %collective-permute-done.6.refs_5_), channel_id=1, source_target_pairs={{1,0},{5,4},{9,8},{13,12},{17,16},{21,20},{25,24},{29,28}} | collective-permute-start | bytes 1572872 | tf_op jit(solution)/shard_map/ppermute | solution.py:215
  148.9 52.4 %collective-permute-start.18 = (bf16[512,512]{1,0:T(8,128)(2,1)}, bf16[512,512]{1,0:T(8,128)(2,1)}, u32[]{:S(2)}, u32[]{:S(2)}) collective-permute-start(bf16[512,512]{1,0:T(8,128)(2,1)} %collective-permute-done.17.refs_12_.refs_1_), channel_id=1, source_target_pairs={{1,2},{2,3},{5,6},{6,7},{9,10},{10,11},{13,14},{14,15},{17,18},{18... | collective-permute-start | bytes 1572872 | tf_op jit(solution)/shard_map/ppermute | solution.py:214
  150.4 9.8 %copy-start.21 = (bf16[512,512]{1,0:T(8,128)(2,1)}, bf16[512,512]{1,0:T(8,128)(2,1)S(1)}, u32[]{:S(2)}) copy-start(bf16[512,512]{1,0:T(8,128)(2,1)S(1)} %collective-permute-done.25.refs_3_) | copy-start | bytes 1572868
  150.4 51.6 %collective-permute-start.21 = (bf16[512,512]{1,0:T(8,128)(2,1)}, bf16[512,512]{1,0:T(8,128)(2,1)}, u32[]{:S(2)}, u32[]{:S(2)}) collective-permute-start(bf16[512,512]{1,0:T(8,128)(2,1)} %collective-permute-done.20.refs_13_.refs_4_), channel_id=1, source_target_pairs={{1,0},{2,1},{5,4},{6,5},{9,8},{10,9},{13,12},{14,13},{17,16},{18,1... | collective-permute-start | bytes 1572872 | tf_op jit(solution)/shard_map/ppermute | solution.py:215
  158.8 1.4 copy-start.22
  158.8 44.5 %collective-permute-start.11 = (bf16[512,512]{1,0:T(8,128)(2,1)S(1)}, bf16[512,512]{1,0:T(8,128)(2,1)}, u32[]{:S(2)}, u32[]{:S(2)}) collective-permute-start(bf16[512,512]{1,0:T(8,128)(2,1)S(1)} %collective-permute-done.10.refs_15_.refs_4_), channel_id=1, source_target_pairs={{1,0},{2,1},{5,4},{6,5},{9,8},{10,9},{13,12},{14,13},{17,16},{18,1... | collective-permute-start | bytes 1572872 | tf_op jit(solution)/shard_map/ppermute | solution.py:215
  160.2 0.8 copy-start.8
  161.0 43.6 %collective-permute-start.8 = (bf16[512,512]{1,0:T(8,128)(2,1)}, bf16[512,512]{1,0:T(8,128)(2,1)}, u32[]{:S(2)}, u32[]{:S(2)}) collective-permute-start(bf16[512,512]{1,0:T(8,128)(2,1)} %collective-permute-done.7.refs_14_.refs_1_), channel_id=1, source_target_pairs={{1,2},{2,3},{5,6},{6,7},{9,10},{10,11},{13,14},{14,15},{17,18},{18... | collective-permute-start | bytes 1572872 | tf_op jit(solution)/shard_map/ppermute | solution.py:214
  201.3 22.9 %collective-permute-start.19 = (bf16[512,512]{1,0:T(8,128)(2,1)}, bf16[512,512]{1,0:T(8,128)(2,1)S(1)}, u32[]{:S(2)}, u32[]{:S(2)}) collective-permute-start(bf16[512,512]{1,0:T(8,128)(2,1)} %collective-permute-done.18.refs_2_), channel_id=1, source_target_pairs={{2,3},{6,7},{10,11},{14,15},{18,19},{22,23},{26,27},{30,31}} | collective-permute-start | bytes 1572872 | tf_op jit(solution)/shard_map/ppermute | solution.py:214
  202.0 22.2 %collective-permute-start.22 = (bf16[512,512]{1,0:T(8,128)(2,1)}, bf16[512,512]{1,0:T(8,128)(2,1)S(1)}, u32[]{:S(2)}, u32[]{:S(2)}) collective-permute-start(bf16[512,512]{1,0:T(8,128)(2,1)} %collective-permute-done.21.refs_5_), channel_id=1, source_target_pairs={{1,0},{5,4},{9,8},{13,12},{17,16},{21,20},{25,24},{29,28}} | collective-permute-start | bytes 1572872 | tf_op jit(solution)/shard_map/ppermute | solution.py:215
  203.3 41.2 %collective-permute-start.12 = (bf16[512,512]{1,0:T(8,128)(2,1)}, bf16[512,512]{1,0:T(8,128)(2,1)S(1)}, u32[]{:S(2)}, u32[]{:S(2)}) collective-permute-start(bf16[512,512]{1,0:T(8,128)(2,1)} %collective-permute-done.11.refs_5_), channel_id=1, source_target_pairs={{1,0},{5,4},{9,8},{13,12},{17,16},{21,20},{25,24},{29,28}} | collective-permute-start | bytes 1572872 | tf_op jit(solution)/shard_map/ppermute | solution.py:215
  204.6 39.9 %collective-permute-start.9 = (bf16[512,512]{1,0:T(8,128)(2,1)}, bf16[512,512]{1,0:T(8,128)(2,1)S(1)}, u32[]{:S(2)}, u32[]{:S(2)}) collective-permute-start(bf16[512,512]{1,0:T(8,128)(2,1)} %collective-permute-done.8.refs_2_), channel_id=1, source_target_pairs={{2,3},{6,7},{10,11},{14,15},{18,19},{22,23},{26,27},{30,31}} | collective-permute-start | bytes 1572872 | tf_op jit(solution)/shard_map/ppermute | solution.py:214
  224.2 0.8 copy-start.10
  225.0 0.9 copy-start.12
  244.5 0.8 copy-start.9
  245.3 0.8 copy-start.11
Sparse Core Ops, SparseCore 0:
  9.6 55.0 all-gather.4
  66.6 38.7 all-gather.10
  107.3 36.7 all-gather.6
  145.8 36.7 all-gather.8

commit v4 on v3

--- a/solution.py
+++ b/solution.py
@@ -10,8 +10,6 @@
 V = 512
 GROUP = 16
 STEP_A = 4
-PAD = 8
-WIDE = 512
 ANY = pl.BlockSpec(memory_space=pl.ANY)
 
 
@@ -42,23 +40,37 @@
     )(own.reshape(1), couplings)
 
 
+def swap_tiles(tiles):
+    row = lax.broadcasted_iota(jnp.int32, tiles[0].shape, 0)
+    for k in (4, 2, 1):
+        keep = (row & k) == 0
+        moved = list(tiles)
+        for c in range(8):
+            if c & k == 0:
+                low, high = tiles[c], tiles[c | k]
+                moved[c] = jnp.where(keep, low, pltpu.roll(high, k, 0))
+                moved[c | k] = jnp.where(keep, pltpu.roll(low, 8 - k, 0), high)
+        tiles = moved
+    return tiles
+
+
 def chunk_kernel(own, *refs, parts, occupied, b_local, q):
     t_own, t_right, t_left = refs[0], refs[1:parts], refs[parts:2 * parts - 1]
-    w_refs = refs[2 * parts - 1:3 * parts - 1]
-    ladder_hbm = refs[3 * parts - 1]
-    out_ref, t_all, w_buf, ladder, pairs, out_buf, t_sem, w_sem, l_sem, out_sem = refs[-10:]
+    w_own, w_rest, ladder_hbm = refs[2 * parts - 1:2 * parts + 2]
+    (out_ref, t_all, w_all, ladder, cycle_a, cycle_b, pairs, mixed_a, mixed_b, out_buf,
+     t_sem, w_sem, l_sem, out_sem) = refs[-14:]
     depth = t_own.shape[1]
+    width = w_own.shape[1]
     count = occupied * occupied
-    pitch = count + PAD
     per_part = occupied // parts
-    wide = WIDE // b_local
 
     def t_copy(src, block, s):
         cols = pl.ds(pl.multiple_of(block * depth, depth), depth)
         return pltpu.make_async_copy(src, t_all.at[:, cols], t_sem.at[s])
 
-    def w_copy(s, slot):
-        return pltpu.make_async_copy(w_refs[s], w_buf.at[slot], w_sem.at[slot])
+    def w_copy(s):
+        src = w_rest.at[:, (s - 1) * width:s * width] if s else w_own
+        return pltpu.make_async_copy(src, w_all.at[s], w_sem.at[s])
 
     blocks = [lax.rem(own[0] - s + parts, parts) for s in range(parts)]
     t_copy(t_own, blocks[0], 0).start()
@@ -70,70 +82,68 @@
         @pl.when(own[0] < s)
         def _():
             t_copy(t_left[parts - s - 1], blocks[s], s).start()
-    w_copy(0, 0).start()
-    w_copy(1 % parts, 1).start()
+    for s in range(parts):
+        w_copy(s).start()
     ladder_copy = pltpu.make_async_copy(ladder_hbm, ladder, l_sem)
     ladder_copy.start()
     for s in range(parts):
         t_copy(t_own, blocks[s], s).wait()
 
-    @pl.loop(0, parts)
-    def _(step):
-        slot = lax.rem(step, 2)
-        w_copy(0, slot).wait()
-        j0 = lax.rem(own[0] - step + parts, parts) * per_part
-        for tile in range(per_part // wide):
-            acc = jnp.dot(
-                t_all[...], w_buf[slot, :, tile * WIDE:(tile + 1) * WIDE], preferred_element_type=jnp.float32)
+    cycles = (cycle_a, cycle_b)
+
+    def regroup(s):
+        src = cycles[s % 2]
+        j0 = blocks[s] * per_part
+        for j in range(0, per_part, 8):
             for i in range(occupied):
-                for k in range(wide):
-                    n = j0 + (i * occupied + tile * wide + k)
-                    for h in range(GROUP // 8):
-                        row = i * GROUP + h * 8
-                        pairs[pl.ds(h * 8 * pitch + n, 8, stride=pitch), :] = (
-                            acc[row:row + 8, k * b_local:(k + 1) * b_local])
-        for s in range(2, parts):
-            @pl.when(step + 2 == s)
-            def _():
-                w_copy(s, slot).start()
+                for h in range(0, GROUP, 8):
+                    rows = slice(i * GROUP + h, i * GROUP + h + 8)
+                    tiles = [src[rows, (j + k) * b_local:(j + k + 1) * b_local] for k in range(8)]
+                    for a, tile in enumerate(swap_tiles(tiles)):
+                        row = pl.multiple_of((h + a) * count + i * occupied + j + j0, 8)
+                        pairs[pl.ds(row, 8), :] = tile
+
+    for s in range(parts):
+        w_copy(s).wait()
+        cycles[s % 2][...] = jnp.dot(t_all[...], w_all[s], preferred_element_type=jnp.float32)
+        if s:
+            regroup(s - 1)
+    regroup(parts - 1)
 
     ladder_copy.wait()
     steps = GROUP // STEP_A
-
-    def out_copy(step, slot):
+    mixes = (mixed_a, mixed_b)
+
+    def block(step, k):
+        a = step * STEP_A + k
+        return pairs[a * count:(a + 1) * count, :].astype(jnp.bfloat16)
+
+    def out_copy(step):
         rows = pl.ds(q * GROUP + step * STEP_A, STEP_A)
-        return pltpu.make_async_copy(out_buf.at[slot], out_ref.at[rows], out_sem.at[slot])
-
-    @pl.loop(0, steps)
-    def _(step):
-        slot = lax.rem(step, 2)
-
-        @pl.when(step >= 2)
-        def _():
-            out_copy(step - 2, slot).wait()
-
-        for g in range(STEP_A // wide):
-            blocks = []
-            for k in range(wide):
-                row = pl.multiple_of((step * STEP_A + g * wide + k) * pitch, 8)
-                blocks.append(pairs[pl.ds(row, count), :].astype(jnp.bfloat16))
-            both = jnp.concatenate(blocks, axis=1)
-            for m in range(count // 256):
-                rows = slice(m * 256, (m + 1) * 256)
-                mixed = jnp.dot(ladder[rows, :], both, preferred_element_type=jnp.float32)
-                total = (mixed + both[rows, :].astype(jnp.float32)).astype(jnp.bfloat16)
-                out_buf[slot, g * wide:(g + 1) * wide, :, rows] = total.T.reshape(wide, b_local, 256)
-        out_copy(step, slot).start()
-
-    for step in range(max(steps - 2, 0), steps):
-        out_copy(step, step % 2).wait()
+        return pltpu.make_async_copy(out_buf.at[step], out_ref.at[rows], out_sem.at[step])
+
+    def finish(step):
+        src = mixes[step % 2]
+        for k in range(STEP_A):
+            total = src[:, k * b_local:(k + 1) * b_local] + block(step, k).astype(jnp.float32)
+            out_buf[step, k] = total.astype(jnp.bfloat16).T
+        out_copy(step).start()
+
+    for step in range(steps):
+        both = jnp.concatenate([block(step, k) for k in range(STEP_A)], axis=1)
+        mixes[step % 2][...] = jnp.dot(ladder[...], both, preferred_element_type=jnp.float32)
+        if step:
+            finish(step - 1)
+    finish(steps - 1)
+    for step in range(steps):
+        out_copy(step).wait()
 
 
 def chunk_update(own, pieces, panel_w, ladder, out, after, q, a_local, b_local, occupied):
-    parts = len(panel_w)
     rows, depth = pieces[0].shape
     count = occupied * occupied
     k_all, width = panel_w[0].shape
+    parts = 1 + panel_w[1].shape[1] // width
     args = [*pieces, *panel_w, ladder, *after]
     aliases = {}
     if out is not None:
@@ -148,14 +158,18 @@
         out_specs=ANY,
         scratch_shapes=[
             pltpu.VMEM((rows, k_all), jnp.bfloat16),
-            pltpu.VMEM((2, k_all, width), jnp.bfloat16),
+            pltpu.VMEM((parts, k_all, width), jnp.bfloat16),
             pltpu.VMEM((count, count), jnp.bfloat16),
-            pltpu.VMEM((GROUP * (count + PAD), b_local), jnp.float32),
-            pltpu.VMEM((2, STEP_A, b_local, count), jnp.bfloat16),
+            pltpu.VMEM((rows, width), jnp.float32),
+            pltpu.VMEM((rows, width), jnp.float32),
+            pltpu.VMEM((GROUP * count, b_local), jnp.float32),
+            pltpu.VMEM((count, STEP_A * b_local), jnp.float32),
+            pltpu.VMEM((count, STEP_A * b_local), jnp.float32),
+            pltpu.VMEM((GROUP // STEP_A, STEP_A, b_local, count), jnp.bfloat16),
             pltpu.SemaphoreType.DMA((parts,)),
-            pltpu.SemaphoreType.DMA((2,)),
+            pltpu.SemaphoreType.DMA((parts,)),
             pltpu.SemaphoreType.DMA,
-            pltpu.SemaphoreType.DMA((2,)),
+            pltpu.SemaphoreType.DMA((GROUP // STEP_A,)),
         ],
         input_output_aliases=aliases,
         compiler_params=pltpu.CompilerParams(vmem_limit_bytes=60 * 1024 * 1024),
@@ -164,7 +178,7 @@
 
 
 def plain_update(own, pieces, panel_w, ladder, b_local, occupied):
-    parts = len(panel_w)
+    parts = (len(pieces) + 1) // 2
     back = jnp.argsort(lax.rem(own - jnp.arange(parts) + parts, parts))
     rows, depth = pieces[0].shape
     right, left = pieces[1:parts], pieces[parts:]
@@ -197,8 +211,10 @@
     blocks = amplitudes.reshape(i_local, rows, chunks, GROUP, depth).transpose(1, 2, 0, 3, 4)
     blocks = lax.all_to_all(blocks, "row", split_axis=0, concat_axis=0, tiled=True)
 
-    arrived[1:], blocks = lax.optimization_barrier((arrived[1:], blocks))
-    panel_w = [lax.all_gather(part, "row", axis=0, tiled=True) for part in arrived]
+    rest, _ = lax.optimization_barrier((arrived[1:], blocks))
+    panel_w = [
+        lax.all_gather(part, "row", axis=0, tiled=True) for part in (arrived[0], jnp.concatenate(rest, axis=1))
+    ]
 
     pieces = []
     for q in range(0, chunks, 2):
@@ -219,7 +235,7 @@
     pieces = [[right[0], *right[1:], *left[1:]] for right, left in pieces]
 
     per_part = occupied // cols
-    if b_local % 128 or WIDE % b_local or depth % 128 or cols < 2 or per_part * b_local % WIDE:
+    if b_local % 128 or depth % 128 or cols < 2 or per_part % 8:
         return jnp.concatenate(
             [plain_update(own, got, panel_w, ladder, b_local, occupied) for got in pieces], axis=0)
     out = None

time: 273 us -> 274 us (level)
  waiting for transfers between devices: 110 us -> 96.4 us
  Pallas kernels: 76 us -> 89.3 us
    all_gather x4 -> x2, waiting for transfers between devices: 20.1 us -> 0.04 us  [local(): lax.all_gather(part, 'row', axis=0, tiled=True)]
    pallas_call x4, Pallas kernels: 74.6 us -> 88 us  [chunk_update(): pl.pallas_call(functools.partial(chunk_kernel, parts=parts, occupied=occu...]
    ppermute x12, waiting for transfers between devices: 45.7 us -> 53.6 us  [local(): lax.ppermute(left[-1], 'col', [(c + 1, c) for c in range(cols - s)])]
    unnamed x46 -> x38, local copies, waits for them, and re-layouts: 6.45 us -> 5.57 us
  transfers between devices with their start and end apart: 32 -> 30, of which waited for: 12 -> 12; matrix products, arithmetic and copies ran while one was open for 2% -> 2% of each run, Pallas kernels for 21% -> 24%
where the time goes in v4:
time: 274 us; the launch traced here: 270 us
  waiting for transfers between devices  96.4 us (35%)
  Pallas kernels  89.3 us (33%)
  starting transfers between devices  58.3 us (21%)
  between operations  14.1 us (5%)
  local copies, waits for them, and re-layouts  10.5 us (4%)
    pallas_call x4, Pallas kernels, chunk_update(): pl.pallas_call(functools.partial(chunk_kernel, parts=parts, occupied=occu...  88 us
    ppermute x12, waiting for transfers between devices, local(): lax.ppermute(left[-1], 'col', [(c + 1, c) for c in range(cols - s)])  53.6 us
    ppermute x3, waiting for transfers between devices, local(): lax.ppermute(arrived[s], 'col', [(c, (c + s) % cols) for c in range(cols)])  33.1 us
    ppermute x12, starting transfers between devices, local(): lax.ppermute(right[-1], 'col', [(c, c + 1) for c in range(s - 1, cols - 1)])  30.9 us
    ppermute x12, starting transfers between devices, local(): lax.ppermute(left[-1], 'col', [(c + 1, c) for c in range(cols - s)])  16 us
    ppermute x12, waiting for transfers between devices, local(): lax.ppermute(right[-1], 'col', [(c, c + 1) for c in range(s - 1, cols - 1)])  9.64 us
    ppermute x3, starting transfers between devices, local(): lax.ppermute(arrived[s], 'col', [(c, (c + s) % cols) for c in range(cols)])  6.19 us
    unnamed x38, local copies, waits for them, and re-layouts  5.57 us
  transfers between devices with their start and end apart: 30, of which 12 were waited for; matrix products, arithmetic and copies ran while one was open for 2% of the time, Pallas kernels for 24%

profile of v4, /device:TPU:0, one launch (start us, length us, event | category | flops | bytes accessed | tf_op | source)
XLA Modules:
  0.0 269.8 jit_solution(2631046307472010259)
XLA Ops:
  6.5 1.6 copy-done
  8.1 1.3 shard_map.37
  9.5 0.0 all-gather.3.cloned.1.call-update
  9.5 3.2 %copy.8 = bf16[8,4,4,16,512]{4,3,2,1,0:T(8,128)(2,1)} copy(bf16[8,4,4,16,512]{4,3,1,0,2:T(8,128)(2,1)} %bitcast.17) | data formatting | bytes 4194304 | tf_op jit(solution)/shard_map/transpose | solution.py:211
  12.7 5.2 %all-to-all-start = ((bf16[8,4,4,16,512]{4,3,2,1,0:T(8,128)(2,1)}), bf16[8,4,4,16,512]{4,3,2,1,0:T(8,128)(2,1)}, u32[]{:S(2)}, u32[]{:S(2)}) async-start(bf16[8,4,4,16,512]{4,3,2,1,0:T(8,128)(2,1)} %copy.8), calls=%async_computation | async-start | bytes 4194304 | tf_op jit(solution)/shard_map/all_to_all | solution.py:212
  17.8 0.0 all-gather.5.cloned.1.call-start
  17.9 2.3 collective-permute-start.10
  20.1 2.6 collective-permute-start.11
  22.7 1.3 collective-permute-start.12
  24.1 10.9 %collective-permute-done.10 = bf16[256,1024]{1,0:T(8,128)(2,1)S(1)} collective-permute-done((bf16[256,1024]{1,0:T(8,128)(2,1)S(1)}, bf16[256,1024]{1,0:T(8,128)(2,1)S(1)}, u32[]{:S(2)}, u32[]{:S(2)}) %collective-permute-start.10) | collective-permute-done | bytes 524320 | tf_op jit(solution)/shard_map/ppermute | solution.py:208
  35.0 22.1 %collective-permute-done.11 = bf16[256,1024]{1,0:T(8,128)(2,1)S(1)} collective-permute-done((bf16[256,1024]{1,0:T(8,128)(2,1)S(1)}, bf16[256,1024]{1,0:T(8,128)(2,1)S(1)}, u32[]{:S(2)}, u32[]{:S(2)}) %collective-permute-start.11) | collective-permute-done | bytes 524320 | tf_op jit(solution)/shard_map/ppermute | solution.py:208
  57.1 0.0 collective-permute-done.12
  57.1 0.0 all-to-all-done
  57.1 1.2 pad_maximum_fusion
  58.4 0.0 all-gather.5.cloned.1.call-update
  58.4 1.7 fusion
  60.2 13.6 %collective-permute-start.13 = (bf16[512,512]{1,0:T(8,128)(2,1)S(1)}, bf16[512,512]{1,0:T(8,128)(2,1)S(1)}, u32[]{:S(2)}, u32[]{:S(2)}) collective-permute-start(bf16[512,512]{1,0:T(8,128)(2,1)S(1)} %bitcast.18), channel_id=1, source_target_pairs={{0,1},{1,2},{2,3},{4,5},{5,6},{6,7},{8,9},{9,10},{10,11},{12,13},{... | collective-permute-start | bytes 1572872 | tf_op jit(solution)/shard_map/ppermute | solution.py:230
  73.8 1.3 collective-permute-start.15
  75.1 4.6 %collective-permute-start = (bf16[512,512]{1,0:T(8,128)(2,1)S(1)}, bf16[512,512]{1,0:T(8,128)(2,1)S(1)}, u32[]{:S(2)}, u32[]{:S(2)}) collective-permute-start(bf16[512,512]{1,0:T(8,128)(2,1)S(1)} %bitcast.14), channel_id=1, source_target_pairs={{0,1},{1,2},{2,3},{4,5},{5,6},{6,7},{8,9},{9,10},{10,11},{12,13},{... | collective-permute-start | bytes 1572872 | tf_op jit(solution)/shard_map/ppermute | solution.py:230
  79.7 1.3 collective-permute-start.2
  81.0 5.1 %collective-permute-done.13.refs_1_ = bf16[512,512]{1,0:T(8,128)(2,1)S(1)} collective-permute-done((bf16[512,512]{1,0:T(8,128)(2,1)S(1)}, bf16[512,512]{1,0:T(8,128)(2,1)S(1)}, u32[]{:S(2)}, u32[]{:S(2)}) %collective-permute-start.13) | collective-permute-done | bytes 524320 | tf_op jit(solution)/shard_map/ppermute | solution.py:230
  86.1 0.7 collective-permute-start.14
  86.8 3.8 %collective-permute-done.15.refs_4_ = bf16[512,512]{1,0:T(8,128)(2,1)S(1)} collective-permute-done((bf16[512,512]{1,0:T(8,128)(2,1)S(1)}, bf16[512,512]{1,0:T(8,128)(2,1)S(1)}, u32[]{:S(2)}, u32[]{:S(2)}) %collective-permute-start.15) | collective-permute-done | bytes 524320 | tf_op jit(solution)/shard_map/ppermute | solution.py:231
  90.5 1.3 collective-permute-start.16
  91.8 4.5 %collective-permute-done.refs_1_ = bf16[512,512]{1,0:T(8,128)(2,1)S(1)} collective-permute-done((bf16[512,512]{1,0:T(8,128)(2,1)S(1)}, bf16[512,512]{1,0:T(8,128)(2,1)S(1)}, u32[]{:S(2)}, u32[]{:S(2)}) %collective-permute-start) | collective-permute-done | bytes 524320 | tf_op jit(solution)/shard_map/ppermute | solution.py:230
  96.4 0.7 collective-permute-start.1
  97.1 4.7 %collective-permute-done.2.refs_4_ = bf16[512,512]{1,0:T(8,128)(2,1)S(1)} collective-permute-done((bf16[512,512]{1,0:T(8,128)(2,1)S(1)}, bf16[512,512]{1,0:T(8,128)(2,1)S(1)}, u32[]{:S(2)}, u32[]{:S(2)}) %collective-permute-start.2) | collective-permute-done | bytes 524320 | tf_op jit(solution)/shard_map/ppermute | solution.py:231
  101.8 1.3 collective-permute-start.3
  103.1 0.0 collective-permute-done.14.refs_2_
  103.1 9.9 %collective-permute-done.16.refs_5_ = bf16[512,512]{1,0:T(8,128)(2,1)S(1)} collective-permute-done((bf16[512,512]{1,0:T(8,128)(2,1)S(1)}, bf16[512,512]{1,0:T(8,128)(2,1)S(1)}, u32[]{:S(2)}, u32[]{:S(2)}) %collective-permute-start.16) | collective-permute-done | bytes 524320 | tf_op jit(solution)/shard_map/ppermute | solution.py:231
  113.0 2.8 %collective-permute-start.17 = (bf16[512,512]{1,0:T(8,128)(2,1)S(1)}, bf16[512,512]{1,0:T(8,128)(2,1)}, u32[]{:S(2)}, u32[]{:S(2)}) collective-permute-start(bf16[512,512]{1,0:T(8,128)(2,1)S(1)} %bitcast.11), channel_id=1, source_target_pairs={{0,1},{1,2},{2,3},{4,5},{5,6},{6,7},{8,9},{9,10},{10,11},{12,13},{... | collective-permute-start | bytes 1572872 | tf_op jit(solution)/shard_map/ppermute | solution.py:230
  115.8 1.3 collective-permute-start.20
  117.1 0.0 collective-permute-done.1.refs_2_
  117.1 7.2 %collective-permute-done.3.refs_5_ = bf16[512,512]{1,0:T(8,128)(2,1)} collective-permute-done((bf16[512,512]{1,0:T(8,128)(2,1)S(1)}, bf16[512,512]{1,0:T(8,128)(2,1)}, u32[]{:S(2)}, u32[]{:S(2)}) %collective-permute-start.3) | collective-permute-done | bytes 524320 | tf_op jit(solution)/shard_map/ppermute | solution.py:231
  124.4 2.8 %collective-permute-start.4 = (bf16[512,512]{1,0:T(8,128)(2,1)S(1)}, bf16[512,512]{1,0:T(8,128)(2,1)}, u32[]{:S(2)}, u32[]{:S(2)}) collective-permute-start(bf16[512,512]{1,0:T(8,128)(2,1)S(1)} %bitcast.8), channel_id=1, source_target_pairs={{0,1},{1,2},{2,3},{4,5},{5,6},{6,7},{8,9},{9,10},{10,11},{12,13},{... | collective-permute-start | bytes 1572872 | tf_op jit(solution)/shard_map/ppermute | solution.py:230
  127.2 1.3 collective-permute-start.7
  128.4 0.7 collective-permute-start.25
  129.1 0.0 collective-permute-done.17.refs_10_.refs_1_
  129.2 1.3 collective-permute-start.26
  130.5 5.1 %collective-permute-done.20.refs_11_.refs_4_ = bf16[512,512]{1,0:T(8,128)(2,1)} collective-permute-done((bf16[512,512]{1,0:T(8,128)(2,1)S(1)}, bf16[512,512]{1,0:T(8,128)(2,1)}, u32[]{:S(2)}, u32[]{:S(2)}) %collective-permute-start.20) | collective-permute-done | bytes 524320 | tf_op jit(solution)/shard_map/ppermute | solution.py:231
  135.6 0.7 collective-permute-start.23
  136.3 1.3 collective-permute-start.24
  137.6 9.2 %collective-permute-done.7.refs_13_.refs_4_ = bf16[512,512]{1,0:T(8,128)(2,1)} collective-permute-done((bf16[512,512]{1,0:T(8,128)(2,1)S(1)}, bf16[512,512]{1,0:T(8,128)(2,1)}, u32[]{:S(2)}, u32[]{:S(2)}) %collective-permute-start.7) | collective-permute-done | bytes 524320 | tf_op jit(solution)/shard_map/ppermute | solution.py:231
  146.8 1.5 collective-permute-start.18
  148.3 1.3 collective-permute-start.21
  149.6 8.4 %collective-permute-done.26.refs_6_ = bf16[512,512]{1,0:T(8,128)(2,1)S(1)} collective-permute-done((bf16[512,512]{1,0:T(8,128)(2,1)S(1)}, bf16[512,512]{1,0:T(8,128)(2,1)S(1)}, u32[]{:S(2)}, u32[]{:S(2)}) %collective-permute-start.26) | collective-permute-done | bytes 524320 | tf_op jit(solution)/shard_map/ppermute | solution.py:231
  158.0 1.4 collective-permute-start.5
  159.5 0.8 copy-done.7
  160.3 1.5 collective-permute-start.8
  161.8 0.0 all-gather.3.cloned.1.call-done.refs_7_
  161.8 0.0 all-gather.5.cloned.1.call-done.refs_8_
  161.8 21.9 %shard_map.38.refs_10_ = bf16[64,128,1024]{2,1,0:T(8,128)(2,1)} custom-call(s32[1]{0:T(128)} %bitcast.own, bf16[512,512]{1,0:T(8,128)(2,1)} %bitcast.20, bf16[512,512]{1,0:T(8,128)(2,1)} %copy-done.13, bf16[512,512]{1,0:T(8,128)(2,1)} %copy-done.15, bf16[512,512]{1,0:T(8,128)(2,1)} %copy-done.17, bf16[512,512]{1,0:T(8,128)(2,1)} %copy-done.14, ...), custom_call_target="tpu_custom_call" | custom-call | flops 12884901888 | bytes 25165824 | tf_op jit(solution)/shard_map/pallas_call | solution.py:154
  183.8 0.7 collective-permute-start.19
  184.5 1.3 collective-permute-start.22
  185.8 0.7 collective-permute-start.6
  186.5 5.2 %collective-permute-done.8.refs_5_ = bf16[512,512]{1,0:T(8,128)(2,1)} collective-permute-done((bf16[512,512]{1,0:T(8,128)(2,1)}, bf16[512,512]{1,0:T(8,128)(2,1)}, u32[]{:S(2)}, u32[]{:S(2)}) %collective-permute-start.8) | collective-permute-done | bytes 524320 | tf_op jit(solution)/shard_map/ppermute | solution.py:231
  191.8 1.7 collective-permute-start.9
  193.5 21.9 %shard_map.39.refs_10_ = bf16[64,128,1024]{2,1,0:T(8,128)(2,1)} custom-call(s32[1]{0:T(128)} %bitcast.own, bf16[512,512]{1,0:T(8,128)(2,1)} %bitcast.16, bf16[512,512]{1,0:T(8,128)(2,1)} %copy-done.4, bf16[512,512]{1,0:T(8,128)(2,1)} %copy-done.6, bf16[512,512]{1,0:T(8,128)(2,1)} %copy-done.7, ...), custom_call_target="tpu_custom_call", output_to_operand_aliasing={{}: (11, {})} | custom-call | flops 12884901888 | bytes 25165824 | tf_op jit(solution)/shard_map/pallas_call | solution.py:154
  215.4 0.8 copy-done.9
  216.2 0.8 copy-done.11
  216.9 22.1 %shard_map.40.refs_10_ = bf16[64,128,1024]{2,1,0:T(8,128)(2,1)} custom-call(s32[1]{0:T(128)} %bitcast.own, bf16[512,512]{1,0:T(8,128)(2,1)} %bitcast.13, bf16[512,512]{1,0:T(8,128)(2,1)} %collective-permute-done.17.refs_10_.refs_1_, bf16[512,512]{1,0:T(8,128)(2,1)} %collective-permute-done.18.refs_2_, ...), custom_call_target="tpu_custom_call", output_to_operand_aliasing={{}: (11, {})} | custom-call | flops 12884901888 | bytes 25165824 | tf_op jit(solution)/shard_map/pallas_call | solution.py:154
  239.1 0.8 copy-done.8
  239.8 0.8 copy-done.10
  240.6 22.1 %shard_map.41 = bf16[64,128,1024]{2,1,0:T(8,128)(2,1)} custom-call(s32[1]{0:T(128)} %bitcast.own, bf16[512,512]{1,0:T(8,128)(2,1)} %bitcast.10, bf16[512,512]{1,0:T(8,128)(2,1)} %collective-permute-done.4.refs_12_.refs_1_, bf16[512,512]{1,0:T(8,128)(2,1)} %collective-permute-done.5.refs_2_, ...), custom_call_target="tpu_custom_call", output_to_operand_aliasing={{}: (11, {})} | custom-call | flops 12884901888 | bytes 25165824 | tf_op jit(solution)/shard_map/pallas_call | solution.py:154
  (44 shorter events, 0.1 us)
Async XLA Ops:
  6.5 155.3 %all-gather.3.cloned.1.call-start = ((), (), s32[]{:S(2)}) async-start(), calls=%async_computation.1 | async-start | bytes 4718592 | tf_op jit(solution)/shard_map/all_gather | solution.py:216
  6.5 1.6 copy-start
  12.7 44.5 %all-to-all-start = ((bf16[8,4,4,16,512]{4,3,2,1,0:T(8,128)(2,1)}), bf16[8,4,4,16,512]{4,3,2,1,0:T(8,128)(2,1)}, u32[]{:S(2)}, u32[]{:S(2)}) async-start(bf16[8,4,4,16,512]{4,3,2,1,0:T(8,128)(2,1)} %copy.8), calls=%async_computation | async-start | bytes 4194304 | tf_op jit(solution)/shard_map/all_to_all | solution.py:212
  17.8 144.0 %all-gather.5.cloned.1.call-start = ((), (), s32[]{:S(2)}) async-start(), calls=%async_computation.2 | async-start | bytes 14155776 | tf_op jit(solution)/shard_map/all_gather | solution.py:216
  17.9 17.1 %collective-permute-start.10 = (bf16[256,1024]{1,0:T(8,128)(2,1)S(1)}, bf16[256,1024]{1,0:T(8,128)(2,1)S(1)}, u32[]{:S(2)}, u32[]{:S(2)}) collective-permute-start(bf16[256,1024]{1,0:T(8,128)(2,1)S(1)} %get-tuple-element.24), channel_id=1, source_target_pairs={{0,1},{1,2},{2,3},{3,0},{4,5},{5,6},{6,7},{7,4},{8,9},{9,10},{10,1... | collective-permute-start | bytes 1572872 | tf_op jit(solution)/shard_map/ppermute | solution.py:208
  20.1 37.0 %collective-permute-start.11 = (bf16[256,1024]{1,0:T(8,128)(2,1)S(1)}, bf16[256,1024]{1,0:T(8,128)(2,1)S(1)}, u32[]{:S(2)}, u32[]{:S(2)}) collective-permute-start(bf16[256,1024]{1,0:T(8,128)(2,1)S(1)} %get-tuple-element.25), channel_id=1, source_target_pairs={{0,2},{1,3},{2,0},{3,1},{4,6},{5,7},{6,4},{7,5},{8,10},{9,11},{10,... | collective-permute-start | bytes 1572872 | tf_op jit(solution)/shard_map/ppermute | solution.py:208
  22.7 34.4 %collective-permute-start.12 = (bf16[256,1024]{1,0:T(8,128)(2,1)S(1)}, bf16[256,1024]{1,0:T(8,128)(2,1)S(1)}, u32[]{:S(2)}, u32[]{:S(2)}) collective-permute-start(bf16[256,1024]{1,0:T(8,128)(2,1)S(1)} %get-tuple-element.26), channel_id=1, source_target_pairs={{0,3},{1,0},{2,1},{3,2},{4,7},{5,4},{6,5},{7,6},{8,11},{9,8},{10,9... | collective-permute-start | bytes 1572872 | tf_op jit(solution)/shard_map/ppermute | solution.py:208
  60.1 99.3 %copy-start.12 = (bf16[8,1,4,16,512]{4,3,2,1,0:T(8,128)(2,1)}, bf16[8,1,4,16,512]{4,3,2,1,0:T(8,128)(2,1)S(1)}, u32[]{:S(2)}) copy-start(bf16[8,1,4,16,512]{4,3,2,1,0:T(8,128)(2,1)S(1)} %get-tuple-element.35) | copy-start | bytes 1572868
  60.1 123.6 %copy-start.1 = (bf16[8,1,4,16,512]{4,3,2,1,0:T(8,128)(2,1)}, bf16[8,1,4,16,512]{4,3,2,1,0:T(8,128)(2,1)S(1)}, u32[]{:S(2)}) copy-start(bf16[8,1,4,16,512]{4,3,2,1,0:T(8,128)(2,1)S(1)} %get-tuple-element.38) | copy-start | bytes 1572868
  60.2 123.6 %copy-start.2 = (bf16[8,1,4,16,512]{4,3,2,1,0:T(8,128)(2,1)}, bf16[8,1,4,16,512]{4,3,2,1,0:T(8,128)(2,1)S(1)}, u32[]{:S(2)}) copy-start(bf16[8,1,4,16,512]{4,3,2,1,0:T(8,128)(2,1)S(1)} %get-tuple-element.36) | copy-start | bytes 1572868
  60.2 123.6 %copy-start.3 = (bf16[8,1,4,16,512]{4,3,2,1,0:T(8,128)(2,1)}, bf16[8,1,4,16,512]{4,3,2,1,0:T(8,128)(2,1)S(1)}, u32[]{:S(2)}) copy-start(bf16[8,1,4,16,512]{4,3,2,1,0:T(8,128)(2,1)S(1)} %get-tuple-element.37) | copy-start | bytes 1572868
  60.2 25.9 %collective-permute-start.13 = (bf16[512,512]{1,0:T(8,128)(2,1)S(1)}, bf16[512,512]{1,0:T(8,128)(2,1)S(1)}, u32[]{:S(2)}, u32[]{:S(2)}) collective-permute-start(bf16[512,512]{1,0:T(8,128)(2,1)S(1)} %bitcast.18), channel_id=1, source_target_pairs={{0,1},{1,2},{2,3},{4,5},{5,6},{6,7},{8,9},{9,10},{10,11},{12,13},{... | collective-permute-start | bytes 1572872 | tf_op jit(solution)/shard_map/ppermute | solution.py:230
  73.8 16.7 %collective-permute-start.15 = (bf16[512,512]{1,0:T(8,128)(2,1)S(1)}, bf16[512,512]{1,0:T(8,128)(2,1)S(1)}, u32[]{:S(2)}, u32[]{:S(2)}) collective-permute-start(bf16[512,512]{1,0:T(8,128)(2,1)S(1)} %bitcast.19), channel_id=1, source_target_pairs={{1,0},{2,1},{3,2},{5,4},{6,5},{7,6},{9,8},{10,9},{11,10},{13,12},{... | collective-permute-start | bytes 1572872 | tf_op jit(solution)/shard_map/ppermute | solution.py:231
  75.1 21.3 %collective-permute-start = (bf16[512,512]{1,0:T(8,128)(2,1)S(1)}, bf16[512,512]{1,0:T(8,128)(2,1)S(1)}, u32[]{:S(2)}, u32[]{:S(2)}) collective-permute-start(bf16[512,512]{1,0:T(8,128)(2,1)S(1)} %bitcast.14), channel_id=1, source_target_pairs={{0,1},{1,2},{2,3},{4,5},{5,6},{6,7},{8,9},{9,10},{10,11},{12,13},{... | collective-permute-start | bytes 1572872 | tf_op jit(solution)/shard_map/ppermute | solution.py:230
  79.7 22.1 %collective-permute-start.2 = (bf16[512,512]{1,0:T(8,128)(2,1)S(1)}, bf16[512,512]{1,0:T(8,128)(2,1)S(1)}, u32[]{:S(2)}, u32[]{:S(2)}) collective-permute-start(bf16[512,512]{1,0:T(8,128)(2,1)S(1)} %bitcast.15), channel_id=1, source_target_pairs={{1,0},{2,1},{3,2},{5,4},{6,5},{7,6},{9,8},{10,9},{11,10},{13,12},{... | collective-permute-start | bytes 1572872 | tf_op jit(solution)/shard_map/ppermute | solution.py:231
  86.1 44.4 %copy-start.13 = (bf16[512,512]{1,0:T(8,128)(2,1)}, bf16[512,512]{1,0:T(8,128)(2,1)S(1)}, u32[]{:S(2)}) copy-start(bf16[512,512]{1,0:T(8,128)(2,1)S(1)} %collective-permute-done.13.refs_1_) | copy-start | bytes 1572868
  86.1 17.0 %collective-permute-start.14 = (bf16[512,512]{1,0:T(8,128)(2,1)S(1)}, bf16[512,512]{1,0:T(8,128)(2,1)S(1)}, u32[]{:S(2)}, u32[]{:S(2)}) collective-permute-start(bf16[512,512]{1,0:T(8,128)(2,1)S(1)} %collective-permute-done.13.refs_1_), channel_id=1, source_target_pairs={{1,2},{2,3},{5,6},{6,7},{9,10},{10,11},{13,14},{14,15},{17,18},{18... | collective-permute-start | bytes 1572872 | tf_op jit(solution)/shard_map/ppermute | solution.py:230
  90.5 68.9 %copy-start.14 = (bf16[512,512]{1,0:T(8,128)(2,1)}, bf16[512,512]{1,0:T(8,128)(2,1)S(1)}, u32[]{:S(2)}) copy-start(bf16[512,512]{1,0:T(8,128)(2,1)S(1)} %collective-permute-done.15.refs_4_) | copy-start | bytes 1572868
  90.5 22.5 %collective-permute-start.16 = (bf16[512,512]{1,0:T(8,128)(2,1)S(1)}, bf16[512,512]{1,0:T(8,128)(2,1)S(1)}, u32[]{:S(2)}, u32[]{:S(2)}) collective-permute-start(bf16[512,512]{1,0:T(8,128)(2,1)S(1)} %collective-permute-done.15.refs_4_), channel_id=1, source_target_pairs={{1,0},{2,1},{5,4},{6,5},{9,8},{10,9},{13,12},{14,13},{17,16},{18,1... | collective-permute-start | bytes 1572872 | tf_op jit(solution)/shard_map/ppermute | solution.py:231
  96.4 87.4 %copy-start.4 = (bf16[512,512]{1,0:T(8,128)(2,1)}, bf16[512,512]{1,0:T(8,128)(2,1)S(1)}, u32[]{:S(2)}) copy-start(bf16[512,512]{1,0:T(8,128)(2,1)S(1)} %collective-permute-done.refs_1_) | copy-start | bytes 1572868
  96.4 20.7 %collective-permute-start.1 = (bf16[512,512]{1,0:T(8,128)(2,1)S(1)}, bf16[512,512]{1,0:T(8,128)(2,1)S(1)}, u32[]{:S(2)}, u32[]{:S(2)}) collective-permute-start(bf16[512,512]{1,0:T(8,128)(2,1)S(1)} %collective-permute-done.refs_1_), channel_id=1, source_target_pairs={{1,2},{2,3},{5,6},{6,7},{9,10},{10,11},{13,14},{14,15},{17,18},{18... | collective-permute-start | bytes 1572872 | tf_op jit(solution)/shard_map/ppermute | solution.py:230
  101.8 82.0 %copy-start.5 = (bf16[512,512]{1,0:T(8,128)(2,1)}, bf16[512,512]{1,0:T(8,128)(2,1)S(1)}, u32[]{:S(2)}) copy-start(bf16[512,512]{1,0:T(8,128)(2,1)S(1)} %collective-permute-done.2.refs_4_) | copy-start | bytes 1572868
  101.8 22.6 %collective-permute-start.3 = (bf16[512,512]{1,0:T(8,128)(2,1)S(1)}, bf16[512,512]{1,0:T(8,128)(2,1)}, u32[]{:S(2)}, u32[]{:S(2)}) collective-permute-start(bf16[512,512]{1,0:T(8,128)(2,1)S(1)} %collective-permute-done.2.refs_4_), channel_id=1, source_target_pairs={{1,0},{2,1},{5,4},{6,5},{9,8},{10,9},{13,12},{14,13},{17,16},{18,1... | collective-permute-start | bytes 1572872 | tf_op jit(solution)/shard_map/ppermute | solution.py:231
  103.1 56.3 %copy-start.15 = (bf16[512,512]{1,0:T(8,128)(2,1)}, bf16[512,512]{1,0:T(8,128)(2,1)S(1)}, u32[]{:S(2)}) copy-start(bf16[512,512]{1,0:T(8,128)(2,1)S(1)} %collective-permute-done.14.refs_2_) | copy-start | bytes 1572868
  113.0 46.4 %copy-start.16 = (bf16[512,512]{1,0:T(8,128)(2,1)}, bf16[512,512]{1,0:T(8,128)(2,1)S(1)}, u32[]{:S(2)}) copy-start(bf16[512,512]{1,0:T(8,128)(2,1)S(1)} %collective-permute-done.16.refs_5_) | copy-start | bytes 1572868
  113.0 16.1 %collective-permute-start.17 = (bf16[512,512]{1,0:T(8,128)(2,1)S(1)}, bf16[512,512]{1,0:T(8,128)(2,1)}, u32[]{:S(2)}, u32[]{:S(2)}) collective-permute-start(bf16[512,512]{1,0:T(8,128)(2,1)S(1)} %bitcast.11), channel_id=1, source_target_pairs={{0,1},{1,2},{2,3},{4,5},{5,6},{6,7},{8,9},{9,10},{10,11},{12,13},{... | collective-permute-start | bytes 1572872 | tf_op jit(solution)/shard_map/ppermute | solution.py:230
  115.8 19.8 %collective-permute-start.20 = (bf16[512,512]{1,0:T(8,128)(2,1)S(1)}, bf16[512,512]{1,0:T(8,128)(2,1)}, u32[]{:S(2)}, u32[]{:S(2)}) collective-permute-start(bf16[512,512]{1,0:T(8,128)(2,1)S(1)} %bitcast.12), channel_id=1, source_target_pairs={{1,0},{2,1},{3,2},{5,4},{6,5},{7,6},{9,8},{10,9},{11,10},{13,12},{... | collective-permute-start | bytes 1572872 | tf_op jit(solution)/shard_map/ppermute | solution.py:231
  117.1 66.7 %copy-start.6 = (bf16[512,512]{1,0:T(8,128)(2,1)}, bf16[512,512]{1,0:T(8,128)(2,1)S(1)}, u32[]{:S(2)}) copy-start(bf16[512,512]{1,0:T(8,128)(2,1)S(1)} %collective-permute-done.1.refs_2_) | copy-start | bytes 1572868
  124.4 11.9 %collective-permute-start.4 = (bf16[512,512]{1,0:T(8,128)(2,1)S(1)}, bf16[512,512]{1,0:T(8,128)(2,1)}, u32[]{:S(2)}, u32[]{:S(2)}) collective-permute-start(bf16[512,512]{1,0:T(8,128)(2,1)S(1)} %bitcast.8), channel_id=1, source_target_pairs={{0,1},{1,2},{2,3},{4,5},{5,6},{6,7},{8,9},{9,10},{10,11},{12,13},{... | collective-permute-start | bytes 1572872 | tf_op jit(solution)/shard_map/ppermute | solution.py:230
  127.2 19.7 %collective-permute-start.7 = (bf16[512,512]{1,0:T(8,128)(2,1)S(1)}, bf16[512,512]{1,0:T(8,128)(2,1)}, u32[]{:S(2)}, u32[]{:S(2)}) collective-permute-start(bf16[512,512]{1,0:T(8,128)(2,1)S(1)} %bitcast.9), channel_id=1, source_target_pairs={{1,0},{2,1},{3,2},{5,4},{6,5},{7,6},{9,8},{10,9},{11,10},{13,12},{... | collective-permute-start | bytes 1572872 | tf_op jit(solution)/shard_map/ppermute | solution.py:231
  128.4 19.9 %collective-permute-start.25 = (bf16[512,512]{1,0:T(8,128)(2,1)S(1)}, bf16[512,512]{1,0:T(8,128)(2,1)S(1)}, u32[]{:S(2)}, u32[]{:S(2)}) collective-permute-start(bf16[512,512]{1,0:T(8,128)(2,1)S(1)} %collective-permute-done.14.refs_2_), channel_id=1, source_target_pairs={{2,3},{6,7},{10,11},{14,15},{18,19},{22,23},{26,27},{30,31}} | collective-permute-start | bytes 1572872 | tf_op jit(solution)/shard_map/ppermute | solution.py:230
  129.2 28.8 %collective-permute-start.26 = (bf16[512,512]{1,0:T(8,128)(2,1)S(1)}, bf16[512,512]{1,0:T(8,128)(2,1)S(1)}, u32[]{:S(2)}, u32[]{:S(2)}) collective-permute-start(bf16[512,512]{1,0:T(8,128)(2,1)S(1)} %collective-permute-done.16.refs_5_), channel_id=1, source_target_pairs={{1,0},{5,4},{9,8},{13,12},{17,16},{21,20},{25,24},{29,28}} | collective-permute-start | bytes 1572872 | tf_op jit(solution)/shard_map/ppermute | solution.py:231
  135.6 23.8 %collective-permute-start.23 = (bf16[512,512]{1,0:T(8,128)(2,1)S(1)}, bf16[512,512]{1,0:T(8,128)(2,1)S(1)}, u32[]{:S(2)}, u32[]{:S(2)}) collective-permute-start(bf16[512,512]{1,0:T(8,128)(2,1)S(1)} %collective-permute-done.1.refs_2_), channel_id=1, source_target_pairs={{2,3},{6,7},{10,11},{14,15},{18,19},{22,23},{26,27},{30,31}} | collective-permute-start | bytes 1572872 | tf_op jit(solution)/shard_map/ppermute | solution.py:230
  136.3 57.2 %collective-permute-start.24 = (bf16[512,512]{1,0:T(8,128)(2,1)}, bf16[512,512]{1,0:T(8,128)(2,1)}, u32[]{:S(2)}, u32[]{:S(2)}) collective-permute-start(bf16[512,512]{1,0:T(8,128)(2,1)} %collective-permute-done.3.refs_5_), channel_id=1, source_target_pairs={{1,0},{5,4},{9,8},{13,12},{17,16},{21,20},{25,24},{29,28}} | collective-permute-start | bytes 1572872 | tf_op jit(solution)/shard_map/ppermute | solution.py:231
  146.8 37.0 %collective-permute-start.18 = (bf16[512,512]{1,0:T(8,128)(2,1)}, bf16[512,512]{1,0:T(8,128)(2,1)}, u32[]{:S(2)}, u32[]{:S(2)}) collective-permute-start(bf16[512,512]{1,0:T(8,128)(2,1)} %collective-permute-done.17.refs_10_.refs_1_), channel_id=1, source_target_pairs={{1,2},{2,3},{5,6},{6,7},{9,10},{10,11},{13,14},{14,15},{17,18},{18... | collective-permute-start | bytes 1572872 | tf_op jit(solution)/shard_map/ppermute | solution.py:230
  148.3 11.1 %copy-start.17 = (bf16[512,512]{1,0:T(8,128)(2,1)}, bf16[512,512]{1,0:T(8,128)(2,1)S(1)}, u32[]{:S(2)}) copy-start(bf16[512,512]{1,0:T(8,128)(2,1)S(1)} %collective-permute-done.25.refs_3_) | copy-start | bytes 1572868
  148.3 36.2 %collective-permute-start.21 = (bf16[512,512]{1,0:T(8,128)(2,1)}, bf16[512,512]{1,0:T(8,128)(2,1)}, u32[]{:S(2)}, u32[]{:S(2)}) collective-permute-start(bf16[512,512]{1,0:T(8,128)(2,1)} %collective-permute-done.20.refs_11_.refs_4_), channel_id=1, source_target_pairs={{1,0},{2,1},{5,4},{6,5},{9,8},{10,9},{13,12},{14,13},{17,16},{18,1... | collective-permute-start | bytes 1572872 | tf_op jit(solution)/shard_map/ppermute | solution.py:231
  158.0 1.5 copy-start.18
  158.0 27.9 %collective-permute-start.5 = (bf16[512,512]{1,0:T(8,128)(2,1)}, bf16[512,512]{1,0:T(8,128)(2,1)}, u32[]{:S(2)}, u32[]{:S(2)}) collective-permute-start(bf16[512,512]{1,0:T(8,128)(2,1)} %collective-permute-done.4.refs_12_.refs_1_), channel_id=1, source_target_pairs={{1,2},{2,3},{5,6},{6,7},{9,10},{10,11},{13,14},{14,15},{17,18},{18... | collective-permute-start | bytes 1572872 | tf_op jit(solution)/shard_map/ppermute | solution.py:230
  159.5 0.8 copy-start.7
  160.3 31.5 %collective-permute-start.8 = (bf16[512,512]{1,0:T(8,128)(2,1)}, bf16[512,512]{1,0:T(8,128)(2,1)}, u32[]{:S(2)}, u32[]{:S(2)}) collective-permute-start(bf16[512,512]{1,0:T(8,128)(2,1)} %collective-permute-done.7.refs_13_.refs_4_), channel_id=1, source_target_pairs={{1,0},{2,1},{5,4},{6,5},{9,8},{10,9},{13,12},{14,13},{17,16},{18,1... | collective-permute-start | bytes 1572872 | tf_op jit(solution)/shard_map/ppermute | solution.py:231
  183.8 31.6 %collective-permute-start.19 = (bf16[512,512]{1,0:T(8,128)(2,1)}, bf16[512,512]{1,0:T(8,128)(2,1)S(1)}, u32[]{:S(2)}, u32[]{:S(2)}) collective-permute-start(bf16[512,512]{1,0:T(8,128)(2,1)} %collective-permute-done.18.refs_2_), channel_id=1, source_target_pairs={{2,3},{6,7},{10,11},{14,15},{18,19},{22,23},{26,27},{30,31}} | collective-permute-start | bytes 1572872 | tf_op jit(solution)/shard_map/ppermute | solution.py:230
  184.5 30.9 %collective-permute-start.22 = (bf16[512,512]{1,0:T(8,128)(2,1)}, bf16[512,512]{1,0:T(8,128)(2,1)S(1)}, u32[]{:S(2)}, u32[]{:S(2)}) collective-permute-start(bf16[512,512]{1,0:T(8,128)(2,1)} %collective-permute-done.21.refs_5_), channel_id=1, source_target_pairs={{1,0},{5,4},{9,8},{13,12},{17,16},{21,20},{25,24},{29,28}} | collective-permute-start | bytes 1572872 | tf_op jit(solution)/shard_map/ppermute | solution.py:231
  185.8 53.2 %collective-permute-start.6 = (bf16[512,512]{1,0:T(8,128)(2,1)}, bf16[512,512]{1,0:T(8,128)(2,1)S(1)}, u32[]{:S(2)}, u32[]{:S(2)}) collective-permute-start(bf16[512,512]{1,0:T(8,128)(2,1)} %collective-permute-done.5.refs_2_), channel_id=1, source_target_pairs={{2,3},{6,7},{10,11},{14,15},{18,19},{22,23},{26,27},{30,31}} | collective-permute-start | bytes 1572872 | tf_op jit(solution)/shard_map/ppermute | solution.py:230
  191.8 47.3 %collective-permute-start.9 = (bf16[512,512]{1,0:T(8,128)(2,1)}, bf16[512,512]{1,0:T(8,128)(2,1)S(1)}, u32[]{:S(2)}, u32[]{:S(2)}) collective-permute-start(bf16[512,512]{1,0:T(8,128)(2,1)} %collective-permute-done.8.refs_5_), channel_id=1, source_target_pairs={{1,0},{5,4},{9,8},{13,12},{17,16},{21,20},{25,24},{29,28}} | collective-permute-start | bytes 1572872 | tf_op jit(solution)/shard_map/ppermute | solution.py:231
  215.4 0.8 copy-start.9
  216.2 0.8 copy-start.11
  239.0 0.8 copy-start.8
  239.8 0.8 copy-start.10
Sparse Core Ops, SparseCore 0:
  9.6 54.9 all-gather.2
  66.5 74.6 all-gather.4

commit v5 on v3

--- a/solution.py
+++ b/solution.py
@@ -44,10 +44,10 @@
 
 def chunk_kernel(own, *refs, parts, occupied, b_local, q):
     t_own, t_right, t_left = refs[0], refs[1:parts], refs[parts:2 * parts - 1]
-    w_refs = refs[2 * parts - 1:3 * parts - 1]
-    ladder_hbm = refs[3 * parts - 1]
+    w_own, w_rest, ladder_hbm = refs[2 * parts - 1:2 * parts + 2]
     out_ref, t_all, w_buf, ladder, pairs, out_buf, t_sem, w_sem, l_sem, out_sem = refs[-10:]
     depth = t_own.shape[1]
+    width = w_own.shape[1]
     count = occupied * occupied
     pitch = count + PAD
     per_part = occupied // parts
@@ -58,7 +58,8 @@
         return pltpu.make_async_copy(src, t_all.at[:, cols], t_sem.at[s])
 
     def w_copy(s, slot):
-        return pltpu.make_async_copy(w_refs[s], w_buf.at[slot], w_sem.at[slot])
+        src = w_rest.at[:, (s - 1) * width:s * width] if s else w_own
+        return pltpu.make_async_copy(src, w_buf.at[slot], w_sem.at[slot])
 
     blocks = [lax.rem(own[0] - s + parts, parts) for s in range(parts)]
     t_copy(t_own, blocks[0], 0).start()
@@ -71,9 +72,7 @@
         def _():
             t_copy(t_left[parts - s - 1], blocks[s], s).start()
     w_copy(0, 0).start()
-    w_copy(1 % parts, 1).start()
     ladder_copy = pltpu.make_async_copy(ladder_hbm, ladder, l_sem)
-    ladder_copy.start()
     for s in range(parts):
         t_copy(t_own, blocks[s], s).wait()
 
@@ -81,6 +80,15 @@
     def _(step):
         slot = lax.rem(step, 2)
         w_copy(0, slot).wait()
+        for s in range(1, parts):
+            @pl.when(step + 1 == s)
+            def _():
+                w_copy(s, s % 2).start()
+
+        @pl.when(step == parts - 1)
+        def _():
+            ladder_copy.start()
+
         j0 = lax.rem(own[0] - step + parts, parts) * per_part
         for tile in range(per_part // wide):
             acc = jnp.dot(
@@ -92,10 +100,6 @@
                         row = i * GROUP + h * 8
                         pairs[pl.ds(h * 8 * pitch + n, 8, stride=pitch), :] = (
                             acc[row:row + 8, k * b_local:(k + 1) * b_local])
-        for s in range(2, parts):
-            @pl.when(step + 2 == s)
-            def _():
-                w_copy(s, slot).start()
 
     ladder_copy.wait()
     steps = GROUP // STEP_A
@@ -130,10 +134,10 @@
 
 
 def chunk_update(own, pieces, panel_w, ladder, out, after, q, a_local, b_local, occupied):
-    parts = len(panel_w)
     rows, depth = pieces[0].shape
     count = occupied * occupied
     k_all, width = panel_w[0].shape
+    parts = 1 + panel_w[1].shape[1] // width
     args = [*pieces, *panel_w, ladder, *after]
     aliases = {}
     if out is not None:
@@ -164,7 +168,7 @@
 
 
 def plain_update(own, pieces, panel_w, ladder, b_local, occupied):
-    parts = len(panel_w)
+    parts = (len(pieces) + 1) // 2
     back = jnp.argsort(lax.rem(own - jnp.arange(parts) + parts, parts))
     rows, depth = pieces[0].shape
     right, left = pieces[1:parts], pieces[parts:]
@@ -197,10 +201,22 @@
     blocks = amplitudes.reshape(i_local, rows, chunks, GROUP, depth).transpose(1, 2, 0, 3, 4)
     blocks = lax.all_to_all(blocks, "row", split_axis=0, concat_axis=0, tiled=True)
 
-    arrived[1:], blocks = lax.optimization_barrier((arrived[1:], blocks))
-    panel_w = [lax.all_gather(part, "row", axis=0, tiled=True) for part in arrived]
-
-    pieces = []
+    per_part = occupied // cols
+    plain = b_local % 128 or WIDE % b_local or depth % 128 or cols < 3 or per_part * b_local % WIDE or chunks < 3
+
+    def update(q, out, after):
+        return chunk_update(own, flat(pieces[q]), panel_w, ladder, out, after, q, a_local, b_local, occupied)
+
+    def flat(sides):
+        right, left = sides
+        return [right[0], *right[1:], *left[1:]]
+
+    rest, _ = lax.optimization_barrier((arrived[1:], blocks))
+    panel_w = [
+        lax.all_gather(part, "row", axis=0, tiled=True) for part in (arrived[0], jnp.concatenate(rest, axis=1))
+    ]
+
+    pieces, out = [], None
     for q in range(0, chunks, 2):
         both = [blocks[:, p].reshape(occupied * GROUP, depth) for p in range(q, min(q + 2, chunks))]
         if q:
@@ -209,23 +225,22 @@
                 both[n], right[middle + 1], left[middle + 1] = lax.optimization_barrier(
                     (both[n], right[middle + 1], left[middle + 1]))
         pair = [([held], [held]) for held in both]
+        final = q + 2 >= chunks and not plain
         for s in range(1, cols):
-            for right, left in pair:
+            if final and s == cols - 1:
+                out = update(0, None, (pair[0][0][-1], pair[0][1][-1]))
+            for n, (right, left) in enumerate(pair):
+                if final and s == cols - 1 and n:
+                    out, right[-1], left[-1] = lax.optimization_barrier((out, right[-1], left[-1]))
                 right.append(lax.ppermute(right[-1], "col", [(c, c + 1) for c in range(s - 1, cols - 1)]))
                 left.append(lax.ppermute(left[-1], "col", [(c + 1, c) for c in range(cols - s)]))
-            if s == 1:
-                started = [got[-1] for sides in pair for got in sides]
         pieces += pair
-    pieces = [[right[0], *right[1:], *left[1:]] for right, left in pieces]
-
-    per_part = occupied // cols
-    if b_local % 128 or WIDE % b_local or depth % 128 or cols < 2 or per_part * b_local % WIDE:
+
+    if plain:
         return jnp.concatenate(
-            [plain_update(own, got, panel_w, ladder, b_local, occupied) for got in pieces], axis=0)
-    out = None
-    for q in range(chunks):
-        after = () if q else started
-        out = chunk_update(own, pieces[q], panel_w, ladder, out, after, q, a_local, b_local, occupied)
+            [plain_update(own, flat(got), panel_w, ladder, b_local, occupied) for got in pieces], axis=0)
+    for q in range(1, chunks):
+        out = update(q, out, ())
     return out
 
 

time: 273 us -> 260 us (0.952)
  waiting for transfers between devices: 110 us -> 99.6 us
    all_gather x4 -> x2, waiting for transfers between devices: 20.1 us -> 0.01 us  [local(): lax.all_gather(part, 'row', axis=0, tiled=True)]
    ppermute x12, waiting for transfers between devices: 45.7 us -> 56.8 us  [local(): lax.ppermute(left[-1], 'col', [(c + 1, c) for c in range(cols - s)])]
    unnamed x46 -> x42, local copies, waits for them, and re-layouts: 6.45 us -> 4.78 us
  transfers between devices with their start and end apart: 32 -> 30, of which waited for: 12 -> 12; matrix products, arithmetic and copies ran while one was open for 2% -> 2% of each run, Pallas kernels for 21% -> 22%
where the time goes in v5:
time: 260 us; the launch traced here: 259 us
  waiting for transfers between devices  99.6 us (38%)
  Pallas kernels  76.3 us (29%)
  starting transfers between devices  58.7 us (23%)
  between operations  13.9 us (5%)
  local copies, waits for them, and re-layouts  9.67 us (4%)
    pallas_call x4, Pallas kernels, chunk_update(): pl.pallas_call(functools.partial(chunk_kernel, parts=parts, occupied=occu...  75 us
    ppermute x12, waiting for transfers between devices, local(): lax.ppermute(left[-1], 'col', [(c + 1, c) for c in range(cols - s)])  56.8 us
    ppermute x3, waiting for transfers between devices, local(): lax.ppermute(arrived[s], 'col', [(c, (c + s) % cols) for c in range(cols)])  33.1 us
    ppermute x12, starting transfers between devices, local(): lax.ppermute(right[-1], 'col', [(c, c + 1) for c in range(s - 1, cols - 1)])  31.7 us
    ppermute x12, starting transfers between devices, local(): lax.ppermute(left[-1], 'col', [(c + 1, c) for c in range(cols - s)])  15.6 us
    ppermute x12, waiting for transfers between devices, local(): lax.ppermute(right[-1], 'col', [(c, c + 1) for c in range(s - 1, cols - 1)])  9.64 us
    ppermute x3, starting transfers between devices, local(): lax.ppermute(arrived[s], 'col', [(c, (c + s) % cols) for c in range(cols)])  6.2 us
  transfers between devices with their start and end apart: 30, of which 12 were waited for; matrix products, arithmetic and copies ran while one was open for 2% of the time, Pallas kernels for 22%

profile of v5, /device:TPU:0, one launch (start us, length us, event | category | flops | bytes accessed | tf_op | source)
XLA Modules:
  0.0 259.4 jit_solution(16751313358619012799)
XLA Ops:
  6.5 1.6 copy-done
  8.1 1.3 shard_map.37
  9.5 0.0 all-gather.3.cloned.1.call-update
  9.5 3.2 %copy.8 = bf16[8,4,4,16,512]{4,3,2,1,0:T(8,128)(2,1)} copy(bf16[8,4,4,16,512]{4,3,1,0,2:T(8,128)(2,1)} %bitcast.17) | data formatting | bytes 4194304 | tf_op jit(solution)/shard_map/transpose | solution.py:201
  12.7 5.2 %all-to-all-start = ((bf16[8,4,4,16,512]{4,3,2,1,0:T(8,128)(2,1)}), bf16[8,4,4,16,512]{4,3,2,1,0:T(8,128)(2,1)}, u32[]{:S(2)}, u32[]{:S(2)}) async-start(bf16[8,4,4,16,512]{4,3,2,1,0:T(8,128)(2,1)} %copy.8), calls=%async_computation | async-start | bytes 4194304 | tf_op jit(solution)/shard_map/all_to_all | solution.py:202
  17.8 0.0 all-gather.5.cloned.1.call-start
  17.9 2.3 collective-permute-start.11
  20.1 2.6 collective-permute-start.12
  22.7 1.3 collective-permute-start.13
  24.1 10.9 %collective-permute-done.11 = bf16[256,1024]{1,0:T(8,128)(2,1)S(1)} collective-permute-done((bf16[256,1024]{1,0:T(8,128)(2,1)S(1)}, bf16[256,1024]{1,0:T(8,128)(2,1)S(1)}, u32[]{:S(2)}, u32[]{:S(2)}) %collective-permute-start.11) | collective-permute-done | bytes 524320 | tf_op jit(solution)/shard_map/ppermute | solution.py:198
  35.0 22.1 %collective-permute-done.12 = bf16[256,1024]{1,0:T(8,128)(2,1)S(1)} collective-permute-done((bf16[256,1024]{1,0:T(8,128)(2,1)S(1)}, bf16[256,1024]{1,0:T(8,128)(2,1)S(1)}, u32[]{:S(2)}, u32[]{:S(2)}) %collective-permute-start.12) | collective-permute-done | bytes 524320 | tf_op jit(solution)/shard_map/ppermute | solution.py:198
  57.1 0.0 collective-permute-done.13
  57.1 0.0 all-to-all-done
  57.1 1.2 pad_maximum_fusion
  58.4 0.0 all-gather.5.cloned.1.call-update
  58.4 1.7 fusion
  60.2 13.6 %collective-permute-start.5 = (bf16[512,512]{1,0:T(8,128)(2,1)S(1)}, bf16[512,512]{1,0:T(8,128)(2,1)S(1)}, u32[]{:S(2)}, u32[]{:S(2)}) collective-permute-start(bf16[512,512]{1,0:T(8,128)(2,1)S(1)} %bitcast.18), channel_id=1, source_target_pairs={{0,1},{1,2},{2,3},{4,5},{5,6},{6,7},{8,9},{9,10},{10,11},{12,13},{... | collective-permute-start | bytes 1572872 | tf_op jit(solution)/shard_map/ppermute | solution.py:235
  73.8 1.3 collective-permute-start.7
  75.1 4.6 %collective-permute-start = (bf16[512,512]{1,0:T(8,128)(2,1)S(1)}, bf16[512,512]{1,0:T(8,128)(2,1)S(1)}, u32[]{:S(2)}, u32[]{:S(2)}) collective-permute-start(bf16[512,512]{1,0:T(8,128)(2,1)S(1)} %bitcast.14), channel_id=1, source_target_pairs={{0,1},{1,2},{2,3},{4,5},{5,6},{6,7},{8,9},{9,10},{10,11},{12,13},{... | collective-permute-start | bytes 1572872 | tf_op jit(solution)/shard_map/ppermute | solution.py:235
  79.7 1.3 collective-permute-start.2
  81.0 5.1 %collective-permute-done.5.refs_1_ = bf16[512,512]{1,0:T(8,128)(2,1)S(1)} collective-permute-done((bf16[512,512]{1,0:T(8,128)(2,1)S(1)}, bf16[512,512]{1,0:T(8,128)(2,1)S(1)}, u32[]{:S(2)}, u32[]{:S(2)}) %collective-permute-start.5) | collective-permute-done | bytes 524320 | tf_op jit(solution)/shard_map/ppermute | solution.py:235
  86.1 0.7 collective-permute-start.6
  86.8 3.8 %collective-permute-done.7.refs_4_ = bf16[512,512]{1,0:T(8,128)(2,1)S(1)} collective-permute-done((bf16[512,512]{1,0:T(8,128)(2,1)S(1)}, bf16[512,512]{1,0:T(8,128)(2,1)S(1)}, u32[]{:S(2)}, u32[]{:S(2)}) %collective-permute-start.7) | collective-permute-done | bytes 524320 | tf_op jit(solution)/shard_map/ppermute | solution.py:236
  90.5 1.3 collective-permute-start.8
  91.8 4.5 %collective-permute-done.refs_1_ = bf16[512,512]{1,0:T(8,128)(2,1)S(1)} collective-permute-done((bf16[512,512]{1,0:T(8,128)(2,1)S(1)}, bf16[512,512]{1,0:T(8,128)(2,1)S(1)}, u32[]{:S(2)}, u32[]{:S(2)}) %collective-permute-start) | collective-permute-done | bytes 524320 | tf_op jit(solution)/shard_map/ppermute | solution.py:235
  96.4 0.7 collective-permute-start.1
  97.1 4.7 %collective-permute-done.2.refs_4_ = bf16[512,512]{1,0:T(8,128)(2,1)S(1)} collective-permute-done((bf16[512,512]{1,0:T(8,128)(2,1)S(1)}, bf16[512,512]{1,0:T(8,128)(2,1)S(1)}, u32[]{:S(2)}, u32[]{:S(2)}) %collective-permute-start.2) | collective-permute-done | bytes 524320 | tf_op jit(solution)/shard_map/ppermute | solution.py:236
  101.8 1.3 collective-permute-start.3
  103.1 9.9 %collective-permute-done.8.refs_5_ = bf16[512,512]{1,0:T(8,128)(2,1)S(1)} collective-permute-done((bf16[512,512]{1,0:T(8,128)(2,1)S(1)}, bf16[512,512]{1,0:T(8,128)(2,1)S(1)}, u32[]{:S(2)}, u32[]{:S(2)}) %collective-permute-start.8) | collective-permute-done | bytes 524320 | tf_op jit(solution)/shard_map/ppermute | solution.py:236
  113.0 2.0 collective-permute-start.14
  115.1 1.3 collective-permute-start.16
  116.4 1.3 collective-permute-start.10
  117.7 6.7 %collective-permute-done.3.refs_5_ = bf16[512,512]{1,0:T(8,128)(2,1)} collective-permute-done((bf16[512,512]{1,0:T(8,128)(2,1)S(1)}, bf16[512,512]{1,0:T(8,128)(2,1)}, u32[]{:S(2)}, u32[]{:S(2)}) %collective-permute-start.3) | collective-permute-done | bytes 524320 | tf_op jit(solution)/shard_map/ppermute | solution.py:236
  124.4 0.7 collective-permute-start.9
  125.0 2.8 %collective-permute-start.4 = (bf16[512,512]{1,0:T(8,128)(2,1)S(1)}, bf16[512,512]{1,0:T(8,128)(2,1)}, u32[]{:S(2)}, u32[]{:S(2)}) collective-permute-start(bf16[512,512]{1,0:T(8,128)(2,1)S(1)} %bitcast.8), channel_id=1, source_target_pairs={{0,1},{1,2},{2,3},{4,5},{5,6},{6,7},{8,9},{9,10},{10,11},{12,13},{... | collective-permute-start | bytes 1572872 | tf_op jit(solution)/shard_map/ppermute | solution.py:235
  127.9 0.0 collective-permute-done.14.refs_1_
  127.9 1.3 collective-permute-start.19
  129.2 6.3 %collective-permute-done.16.refs_4_ = bf16[512,512]{1,0:T(8,128)(2,1)S(1)} collective-permute-done((bf16[512,512]{1,0:T(8,128)(2,1)S(1)}, bf16[512,512]{1,0:T(8,128)(2,1)S(1)}, u32[]{:S(2)}, u32[]{:S(2)}) %collective-permute-start.16) | collective-permute-done | bytes 524320 | tf_op jit(solution)/shard_map/ppermute | solution.py:236
  135.5 1.4 collective-permute-start.15
  136.9 9.8 %collective-permute-done.10.refs_6_ = bf16[512,512]{1,0:T(8,128)(2,1)S(1)} collective-permute-done((bf16[512,512]{1,0:T(8,128)(2,1)S(1)}, bf16[512,512]{1,0:T(8,128)(2,1)S(1)}, u32[]{:S(2)}, u32[]{:S(2)}) %collective-permute-start.10) | collective-permute-done | bytes 524320 | tf_op jit(solution)/shard_map/ppermute | solution.py:236
  146.7 1.3 collective-permute-start.17
  148.0 1.5 collective-permute-start.25
  149.5 0.0 collective-permute-done.4.refs_1_
  149.5 1.3 collective-permute-start.26
  150.8 7.3 %collective-permute-done.19.refs_4_ = bf16[512,512]{1,0:T(8,128)(2,1)} collective-permute-done((bf16[512,512]{1,0:T(8,128)(2,1)S(1)}, bf16[512,512]{1,0:T(8,128)(2,1)}, u32[]{:S(2)}, u32[]{:S(2)}) %collective-permute-start.19) | collective-permute-done | bytes 524320 | tf_op jit(solution)/shard_map/ppermute | solution.py:236
  158.1 1.4 collective-permute-start.18
  159.5 0.0 collective-permute-done.15.refs_10_.refs_2_
  159.5 1.3 collective-permute-start.20
  160.8 8.4 %collective-permute-done.17.refs_11_.refs_5_ = bf16[512,512]{1,0:T(8,128)(2,1)S(1)} collective-permute-done((bf16[512,512]{1,0:T(8,128)(2,1)S(1)}, bf16[512,512]{1,0:T(8,128)(2,1)S(1)}, u32[]{:S(2)}, u32[]{:S(2)}) %collective-permute-start.17) | collective-permute-done | bytes 524320 | tf_op jit(solution)/shard_map/ppermute | solution.py:236
  169.2 0.8 copy-done.9
  170.0 1.5 collective-permute-start.23
  171.5 18.8 %shard_map.38.refs_10_ = bf16[64,128,1024]{2,1,0:T(8,128)(2,1)} custom-call(s32[1]{0:T(128)} %bitcast.own, bf16[512,512]{1,0:T(8,128)(2,1)} %bitcast.20, bf16[512,512]{1,0:T(8,128)(2,1)} %copy-done.15, bf16[512,512]{1,0:T(8,128)(2,1)} %copy-done.17, bf16[512,512]{1,0:T(8,128)(2,1)} %copy-done.20, bf16[512,512]{1,0:T(8,128)(2,1)} %copy-done.16, ...), custom_call_target="tpu_custom_call" | custom-call | flops 12884901888 | bytes 25165824 | tf_op jit(solution)/shard_map/pallas_call | solution.py:148
  190.4 1.3 collective-permute-start.24
  191.7 0.0 collective-permute-done.20.refs_5_
  191.7 0.7 collective-permute-start.21
  192.4 1.5 collective-permute-start.22
  193.9 0.0 collective-permute-done.26.refs_6_
  193.9 18.8 %shard_map.39.refs_10_ = bf16[64,128,1024]{2,1,0:T(8,128)(2,1)} custom-call(s32[1]{0:T(128)} %bitcast.own, bf16[512,512]{1,0:T(8,128)(2,1)} %bitcast.16, bf16[512,512]{1,0:T(8,128)(2,1)} %copy-done.4, bf16[512,512]{1,0:T(8,128)(2,1)} %copy-done.6, bf16[512,512]{1,0:T(8,128)(2,1)} %collective-permute-done.25.refs_3_, ...), custom_call_target="tpu_custom_call", output_to_operand_aliasing={{}: (11, {})} | custom-call | flops 12884901888 | bytes 25165824 | tf_op jit(solution)/shard_map/pallas_call | solution.py:148
  212.6 0.0 collective-permute-done.23.refs_3_
  212.7 0.8 copy-done.13
  213.4 18.7 %shard_map.40.refs_10_ = bf16[64,128,1024]{2,1,0:T(8,128)(2,1)} custom-call(s32[1]{0:T(128)} %bitcast.own, bf16[512,512]{1,0:T(8,128)(2,1)} %bitcast.13, bf16[512,512]{1,0:T(8,128)(2,1)} %copy-done.7, bf16[512,512]{1,0:T(8,128)(2,1)} %collective-permute-done.15.refs_10_.refs_2_, ...), custom_call_target="tpu_custom_call", output_to_operand_aliasing={{}: (11, {})} | custom-call | flops 12884901888 | bytes 25165824 | tf_op jit(solution)/shard_map/pallas_call | solution.py:148
  232.2 0.8 copy-done.11
  233.0 0.8 copy-done.12
  233.8 18.7 %shard_map.41 = bf16[64,128,1024]{2,1,0:T(8,128)(2,1)} custom-call(s32[1]{0:T(128)} %bitcast.own, bf16[512,512]{1,0:T(8,128)(2,1)} %bitcast.10, bf16[512,512]{1,0:T(8,128)(2,1)} %collective-permute-done.4.refs_1_, bf16[512,512]{1,0:T(8,128)(2,1)} %collective-permute-done.18.refs_2_, bf16[512,512]{1,0:T(8,128)(2,1)} %copy-done.11, ...), custom_call_target="tpu_custom_call", output_to_operand_aliasing={{}: (11, {})} | custom-call | flops 12884901888 | bytes 25165824 | tf_op jit(solution)/shard_map/pallas_call | solution.py:148
  (48 shorter events, 0.1 us)
Async XLA Ops:
  6.5 165.0 %all-gather.3.cloned.1.call-start = ((), (), s32[]{:S(2)}) async-start(), calls=%async_computation.1 | async-start | bytes 4718592 | tf_op jit(solution)/shard_map/all_gather | solution.py:216
  6.5 1.6 copy-start
  12.7 44.5 %all-to-all-start = ((bf16[8,4,4,16,512]{4,3,2,1,0:T(8,128)(2,1)}), bf16[8,4,4,16,512]{4,3,2,1,0:T(8,128)(2,1)}, u32[]{:S(2)}, u32[]{:S(2)}) async-start(bf16[8,4,4,16,512]{4,3,2,1,0:T(8,128)(2,1)} %copy.8), calls=%async_computation | async-start | bytes 4194304 | tf_op jit(solution)/shard_map/all_to_all | solution.py:202
  17.8 153.7 %all-gather.5.cloned.1.call-start = ((), (), s32[]{:S(2)}) async-start(), calls=%async_computation.2 | async-start | bytes 14155776 | tf_op jit(solution)/shard_map/all_gather | solution.py:216
  17.9 17.1 %collective-permute-start.11 = (bf16[256,1024]{1,0:T(8,128)(2,1)S(1)}, bf16[256,1024]{1,0:T(8,128)(2,1)S(1)}, u32[]{:S(2)}, u32[]{:S(2)}) collective-permute-start(bf16[256,1024]{1,0:T(8,128)(2,1)S(1)} %get-tuple-element.29), channel_id=1, source_target_pairs={{0,1},{1,2},{2,3},{3,0},{4,5},{5,6},{6,7},{7,4},{8,9},{9,10},{10,1... | collective-permute-start | bytes 1572872 | tf_op jit(solution)/shard_map/ppermute | solution.py:198
  20.1 37.0 %collective-permute-start.12 = (bf16[256,1024]{1,0:T(8,128)(2,1)S(1)}, bf16[256,1024]{1,0:T(8,128)(2,1)S(1)}, u32[]{:S(2)}, u32[]{:S(2)}) collective-permute-start(bf16[256,1024]{1,0:T(8,128)(2,1)S(1)} %get-tuple-element.30), channel_id=1, source_target_pairs={{0,2},{1,3},{2,0},{3,1},{4,6},{5,7},{6,4},{7,5},{8,10},{9,11},{10,... | collective-permute-start | bytes 1572872 | tf_op jit(solution)/shard_map/ppermute | solution.py:198
  22.7 34.4 %collective-permute-start.13 = (bf16[256,1024]{1,0:T(8,128)(2,1)S(1)}, bf16[256,1024]{1,0:T(8,128)(2,1)S(1)}, u32[]{:S(2)}, u32[]{:S(2)}) collective-permute-start(bf16[256,1024]{1,0:T(8,128)(2,1)S(1)} %get-tuple-element.31), channel_id=1, source_target_pairs={{0,3},{1,0},{2,1},{3,2},{4,7},{5,4},{6,5},{7,6},{8,11},{9,8},{10,9... | collective-permute-start | bytes 1572872 | tf_op jit(solution)/shard_map/ppermute | solution.py:198
  60.1 109.1 %copy-start.14 = (bf16[8,1,4,16,512]{4,3,2,1,0:T(8,128)(2,1)}, bf16[8,1,4,16,512]{4,3,2,1,0:T(8,128)(2,1)S(1)}, u32[]{:S(2)}) copy-start(bf16[8,1,4,16,512]{4,3,2,1,0:T(8,128)(2,1)S(1)} %get-tuple-element.42) | copy-start | bytes 1572868
  60.1 130.1 %copy-start.1 = (bf16[8,1,4,16,512]{4,3,2,1,0:T(8,128)(2,1)}, bf16[8,1,4,16,512]{4,3,2,1,0:T(8,128)(2,1)S(1)}, u32[]{:S(2)}) copy-start(bf16[8,1,4,16,512]{4,3,2,1,0:T(8,128)(2,1)S(1)} %get-tuple-element.44) | copy-start | bytes 1572868
  60.2 130.1 %copy-start.2 = (bf16[8,1,4,16,512]{4,3,2,1,0:T(8,128)(2,1)}, bf16[8,1,4,16,512]{4,3,2,1,0:T(8,128)(2,1)S(1)}, u32[]{:S(2)}) copy-start(bf16[8,1,4,16,512]{4,3,2,1,0:T(8,128)(2,1)S(1)} %get-tuple-element.41) | copy-start | bytes 1572868
  60.2 130.1 %copy-start.3 = (bf16[8,1,4,16,512]{4,3,2,1,0:T(8,128)(2,1)}, bf16[8,1,4,16,512]{4,3,2,1,0:T(8,128)(2,1)S(1)}, u32[]{:S(2)}) copy-start(bf16[8,1,4,16,512]{4,3,2,1,0:T(8,128)(2,1)S(1)} %get-tuple-element.43) | copy-start | bytes 1572868
  60.2 25.9 %collective-permute-start.5 = (bf16[512,512]{1,0:T(8,128)(2,1)S(1)}, bf16[512,512]{1,0:T(8,128)(2,1)S(1)}, u32[]{:S(2)}, u32[]{:S(2)}) collective-permute-start(bf16[512,512]{1,0:T(8,128)(2,1)S(1)} %bitcast.18), channel_id=1, source_target_pairs={{0,1},{1,2},{2,3},{4,5},{5,6},{6,7},{8,9},{9,10},{10,11},{12,13},{... | collective-permute-start | bytes 1572872 | tf_op jit(solution)/shard_map/ppermute | solution.py:235
  73.8 16.7 %collective-permute-start.7 = (bf16[512,512]{1,0:T(8,128)(2,1)S(1)}, bf16[512,512]{1,0:T(8,128)(2,1)S(1)}, u32[]{:S(2)}, u32[]{:S(2)}) collective-permute-start(bf16[512,512]{1,0:T(8,128)(2,1)S(1)} %bitcast.19), channel_id=1, source_target_pairs={{1,0},{2,1},{3,2},{5,4},{6,5},{7,6},{9,8},{10,9},{11,10},{13,12},{... | collective-permute-start | bytes 1572872 | tf_op jit(solution)/shard_map/ppermute | solution.py:236
  75.1 21.3 %collective-permute-start = (bf16[512,512]{1,0:T(8,128)(2,1)S(1)}, bf16[512,512]{1,0:T(8,128)(2,1)S(1)}, u32[]{:S(2)}, u32[]{:S(2)}) collective-permute-start(bf16[512,512]{1,0:T(8,128)(2,1)S(1)} %bitcast.14), channel_id=1, source_target_pairs={{0,1},{1,2},{2,3},{4,5},{5,6},{6,7},{8,9},{9,10},{10,11},{12,13},{... | collective-permute-start | bytes 1572872 | tf_op jit(solution)/shard_map/ppermute | solution.py:235
  79.7 22.1 %collective-permute-start.2 = (bf16[512,512]{1,0:T(8,128)(2,1)S(1)}, bf16[512,512]{1,0:T(8,128)(2,1)S(1)}, u32[]{:S(2)}, u32[]{:S(2)}) collective-permute-start(bf16[512,512]{1,0:T(8,128)(2,1)S(1)} %bitcast.15), channel_id=1, source_target_pairs={{1,0},{2,1},{3,2},{5,4},{6,5},{7,6},{9,8},{10,9},{11,10},{13,12},{... | collective-permute-start | bytes 1572872 | tf_op jit(solution)/shard_map/ppermute | solution.py:236
  86.1 26.9 %copy-start.15 = (bf16[512,512]{1,0:T(8,128)(2,1)}, bf16[512,512]{1,0:T(8,128)(2,1)S(1)}, u32[]{:S(2)}) copy-start(bf16[512,512]{1,0:T(8,128)(2,1)S(1)} %collective-permute-done.5.refs_1_) | copy-start | bytes 1572868
  86.1 17.0 %collective-permute-start.6 = (bf16[512,512]{1,0:T(8,128)(2,1)S(1)}, bf16[512,512]{1,0:T(8,128)(2,1)S(1)}, u32[]{:S(2)}, u32[]{:S(2)}) collective-permute-start(bf16[512,512]{1,0:T(8,128)(2,1)S(1)} %collective-permute-done.5.refs_1_), channel_id=1, source_target_pairs={{1,2},{2,3},{5,6},{6,7},{9,10},{10,11},{13,14},{14,15},{17,18},{18... | collective-permute-start | bytes 1572872 | tf_op jit(solution)/shard_map/ppermute | solution.py:235
  90.5 22.5 %copy-start.16 = (bf16[512,512]{1,0:T(8,128)(2,1)}, bf16[512,512]{1,0:T(8,128)(2,1)S(1)}, u32[]{:S(2)}) copy-start(bf16[512,512]{1,0:T(8,128)(2,1)S(1)} %collective-permute-done.7.refs_4_) | copy-start | bytes 1572868
  90.5 22.5 %collective-permute-start.8 = (bf16[512,512]{1,0:T(8,128)(2,1)S(1)}, bf16[512,512]{1,0:T(8,128)(2,1)S(1)}, u32[]{:S(2)}, u32[]{:S(2)}) collective-permute-start(bf16[512,512]{1,0:T(8,128)(2,1)S(1)} %collective-permute-done.7.refs_4_), channel_id=1, source_target_pairs={{1,0},{2,1},{5,4},{6,5},{9,8},{10,9},{13,12},{14,13},{17,16},{18,1... | collective-permute-start | bytes 1572872 | tf_op jit(solution)/shard_map/ppermute | solution.py:236
  96.4 93.9 %copy-start.4 = (bf16[512,512]{1,0:T(8,128)(2,1)}, bf16[512,512]{1,0:T(8,128)(2,1)S(1)}, u32[]{:S(2)}) copy-start(bf16[512,512]{1,0:T(8,128)(2,1)S(1)} %collective-permute-done.refs_1_) | copy-start | bytes 1572868
  96.4 21.3 %collective-permute-start.1 = (bf16[512,512]{1,0:T(8,128)(2,1)S(1)}, bf16[512,512]{1,0:T(8,128)(2,1)S(1)}, u32[]{:S(2)}, u32[]{:S(2)}) collective-permute-start(bf16[512,512]{1,0:T(8,128)(2,1)S(1)} %collective-permute-done.refs_1_), channel_id=1, source_target_pairs={{1,2},{2,3},{5,6},{6,7},{9,10},{10,11},{13,14},{14,15},{17,18},{18... | collective-permute-start | bytes 1572872 | tf_op jit(solution)/shard_map/ppermute | solution.py:235
  101.8 88.5 %copy-start.5 = (bf16[512,512]{1,0:T(8,128)(2,1)}, bf16[512,512]{1,0:T(8,128)(2,1)S(1)}, u32[]{:S(2)}) copy-start(bf16[512,512]{1,0:T(8,128)(2,1)S(1)} %collective-permute-done.2.refs_4_) | copy-start | bytes 1572868
  101.8 22.6 %collective-permute-start.3 = (bf16[512,512]{1,0:T(8,128)(2,1)S(1)}, bf16[512,512]{1,0:T(8,128)(2,1)}, u32[]{:S(2)}, u32[]{:S(2)}) collective-permute-start(bf16[512,512]{1,0:T(8,128)(2,1)S(1)} %collective-permute-done.2.refs_4_), channel_id=1, source_target_pairs={{1,0},{2,1},{5,4},{6,5},{9,8},{10,9},{13,12},{14,13},{17,16},{18,1... | collective-permute-start | bytes 1572872 | tf_op jit(solution)/shard_map/ppermute | solution.py:236
  103.1 66.1 %copy-start.17 = (bf16[512,512]{1,0:T(8,128)(2,1)}, bf16[512,512]{1,0:T(8,128)(2,1)S(1)}, u32[]{:S(2)}) copy-start(bf16[512,512]{1,0:T(8,128)(2,1)S(1)} %collective-permute-done.6.refs_2_) | copy-start | bytes 1572868
  113.0 23.9 %copy-start.18 = (bf16[512,512]{1,0:T(8,128)(2,1)}, bf16[512,512]{1,0:T(8,128)(2,1)S(1)}, u32[]{:S(2)}) copy-start(bf16[512,512]{1,0:T(8,128)(2,1)S(1)} %collective-permute-done.8.refs_5_) | copy-start | bytes 1572868
  113.0 14.8 %collective-permute-start.14 = (bf16[512,512]{1,0:T(8,128)(2,1)S(1)}, bf16[512,512]{1,0:T(8,128)(2,1)S(1)}, u32[]{:S(2)}, u32[]{:S(2)}) collective-permute-start(bf16[512,512]{1,0:T(8,128)(2,1)S(1)} %bitcast.11), channel_id=1, source_target_pairs={{0,1},{1,2},{2,3},{4,5},{5,6},{6,7},{8,9},{9,10},{10,11},{12,13},{... | collective-permute-start | bytes 1572872 | tf_op jit(solution)/shard_map/ppermute | solution.py:235
  115.1 20.4 %collective-permute-start.16 = (bf16[512,512]{1,0:T(8,128)(2,1)S(1)}, bf16[512,512]{1,0:T(8,128)(2,1)S(1)}, u32[]{:S(2)}, u32[]{:S(2)}) collective-permute-start(bf16[512,512]{1,0:T(8,128)(2,1)S(1)} %bitcast.12), channel_id=1, source_target_pairs={{1,0},{2,1},{3,2},{5,4},{6,5},{7,6},{9,8},{10,9},{11,10},{13,12},{... | collective-permute-start | bytes 1572872 | tf_op jit(solution)/shard_map/ppermute | solution.py:236
  116.4 30.4 %collective-permute-start.10 = (bf16[512,512]{1,0:T(8,128)(2,1)S(1)}, bf16[512,512]{1,0:T(8,128)(2,1)S(1)}, u32[]{:S(2)}, u32[]{:S(2)}) collective-permute-start(bf16[512,512]{1,0:T(8,128)(2,1)S(1)} %collective-permute-done.8.refs_5_), channel_id=1, source_target_pairs={{1,0},{5,4},{9,8},{13,12},{17,16},{21,20},{25,24},{29,28}} | collective-permute-start | bytes 1572872 | tf_op jit(solution)/shard_map/ppermute | solution.py:236
  117.7 72.7 %copy-start.6 = (bf16[512,512]{1,0:T(8,128)(2,1)}, bf16[512,512]{1,0:T(8,128)(2,1)S(1)}, u32[]{:S(2)}) copy-start(bf16[512,512]{1,0:T(8,128)(2,1)S(1)} %collective-permute-done.1.refs_2_) | copy-start | bytes 1572868
  124.4 23.7 %collective-permute-start.9 = (bf16[512,512]{1,0:T(8,128)(2,1)S(1)}, bf16[512,512]{1,0:T(8,128)(2,1)S(1)}, u32[]{:S(2)}, u32[]{:S(2)}) collective-permute-start(bf16[512,512]{1,0:T(8,128)(2,1)S(1)} %collective-permute-done.6.refs_2_), channel_id=1, source_target_pairs={{2,3},{6,7},{10,11},{14,15},{18,19},{22,23},{26,27},{30,31}} | collective-permute-start | bytes 1572872 | tf_op jit(solution)/shard_map/ppermute | solution.py:235
  125.0 24.5 %collective-permute-start.4 = (bf16[512,512]{1,0:T(8,128)(2,1)S(1)}, bf16[512,512]{1,0:T(8,128)(2,1)}, u32[]{:S(2)}, u32[]{:S(2)}) collective-permute-start(bf16[512,512]{1,0:T(8,128)(2,1)S(1)} %bitcast.8), channel_id=1, source_target_pairs={{0,1},{1,2},{2,3},{4,5},{5,6},{6,7},{8,9},{9,10},{10,11},{12,13},{... | collective-permute-start | bytes 1572872 | tf_op jit(solution)/shard_map/ppermute | solution.py:235
  127.9 30.2 %copy-start.7 = (bf16[512,512]{1,0:T(8,128)(2,1)}, bf16[512,512]{1,0:T(8,128)(2,1)S(1)}, u32[]{:S(2)}) copy-start(bf16[512,512]{1,0:T(8,128)(2,1)S(1)} %collective-permute-done.14.refs_1_) | copy-start | bytes 1572868
  127.9 30.2 %collective-permute-start.19 = (bf16[512,512]{1,0:T(8,128)(2,1)S(1)}, bf16[512,512]{1,0:T(8,128)(2,1)}, u32[]{:S(2)}, u32[]{:S(2)}) collective-permute-start(bf16[512,512]{1,0:T(8,128)(2,1)S(1)} %bitcast.9), channel_id=1, source_target_pairs={{1,0},{2,1},{3,2},{5,4},{6,5},{7,6},{9,8},{10,9},{11,10},{13,12},{... | collective-permute-start | bytes 1572872 | tf_op jit(solution)/shard_map/ppermute | solution.py:236
  135.5 24.0 %copy-start.8 = (bf16[512,512]{1,0:T(8,128)(2,1)}, bf16[512,512]{1,0:T(8,128)(2,1)S(1)}, u32[]{:S(2)}) copy-start(bf16[512,512]{1,0:T(8,128)(2,1)S(1)} %collective-permute-done.16.refs_4_) | copy-start | bytes 1572868
  135.5 24.0 %collective-permute-start.15 = (bf16[512,512]{1,0:T(8,128)(2,1)S(1)}, bf16[512,512]{1,0:T(8,128)(2,1)}, u32[]{:S(2)}, u32[]{:S(2)}) collective-permute-start(bf16[512,512]{1,0:T(8,128)(2,1)S(1)} %collective-permute-done.14.refs_1_), channel_id=1, source_target_pairs={{1,2},{2,3},{5,6},{6,7},{9,10},{10,11},{13,14},{14,15},{17,18},{18... | collective-permute-start | bytes 1572872 | tf_op jit(solution)/shard_map/ppermute | solution.py:235
  146.7 22.5 %copy-start.19 = (bf16[512,512]{1,0:T(8,128)(2,1)}, bf16[512,512]{1,0:T(8,128)(2,1)S(1)}, u32[]{:S(2)}) copy-start(bf16[512,512]{1,0:T(8,128)(2,1)S(1)} %collective-permute-done.10.refs_6_) | copy-start | bytes 1572868
  146.7 22.5 %collective-permute-start.17 = (bf16[512,512]{1,0:T(8,128)(2,1)S(1)}, bf16[512,512]{1,0:T(8,128)(2,1)S(1)}, u32[]{:S(2)}, u32[]{:S(2)}) collective-permute-start(bf16[512,512]{1,0:T(8,128)(2,1)S(1)} %collective-permute-done.16.refs_4_), channel_id=1, source_target_pairs={{1,0},{2,1},{5,4},{6,5},{9,8},{10,9},{13,12},{14,13},{17,16},{18,1... | collective-permute-start | bytes 1572872 | tf_op jit(solution)/shard_map/ppermute | solution.py:236
  148.0 21.2 %copy-start.20 = (bf16[512,512]{1,0:T(8,128)(2,1)}, bf16[512,512]{1,0:T(8,128)(2,1)S(1)}, u32[]{:S(2)}) copy-start(bf16[512,512]{1,0:T(8,128)(2,1)S(1)} %collective-permute-done.9.refs_3_) | copy-start | bytes 1572868
  148.0 44.3 %collective-permute-start.25 = (bf16[512,512]{1,0:T(8,128)(2,1)S(1)}, bf16[512,512]{1,0:T(8,128)(2,1)}, u32[]{:S(2)}, u32[]{:S(2)}) collective-permute-start(bf16[512,512]{1,0:T(8,128)(2,1)S(1)} %collective-permute-done.1.refs_2_), channel_id=1, source_target_pairs={{2,3},{6,7},{10,11},{14,15},{18,19},{22,23},{26,27},{30,31}} | collective-permute-start | bytes 1572872 | tf_op jit(solution)/shard_map/ppermute | solution.py:235
  149.5 44.4 %collective-permute-start.26 = (bf16[512,512]{1,0:T(8,128)(2,1)}, bf16[512,512]{1,0:T(8,128)(2,1)}, u32[]{:S(2)}, u32[]{:S(2)}) collective-permute-start(bf16[512,512]{1,0:T(8,128)(2,1)} %collective-permute-done.3.refs_5_), channel_id=1, source_target_pairs={{1,0},{5,4},{9,8},{13,12},{17,16},{21,20},{25,24},{29,28}} | collective-permute-start | bytes 1572872 | tf_op jit(solution)/shard_map/ppermute | solution.py:236
  158.1 32.3 %collective-permute-start.18 = (bf16[512,512]{1,0:T(8,128)(2,1)}, bf16[512,512]{1,0:T(8,128)(2,1)}, u32[]{:S(2)}, u32[]{:S(2)}) collective-permute-start(bf16[512,512]{1,0:T(8,128)(2,1)} %collective-permute-done.4.refs_1_), channel_id=1, source_target_pairs={{1,2},{2,3},{5,6},{6,7},{9,10},{10,11},{13,14},{14,15},{17,18},{18... | collective-permute-start | bytes 1572872 | tf_op jit(solution)/shard_map/ppermute | solution.py:235
  159.5 32.2 %collective-permute-start.20 = (bf16[512,512]{1,0:T(8,128)(2,1)}, bf16[512,512]{1,0:T(8,128)(2,1)}, u32[]{:S(2)}, u32[]{:S(2)}) collective-permute-start(bf16[512,512]{1,0:T(8,128)(2,1)} %collective-permute-done.19.refs_4_), channel_id=1, source_target_pairs={{1,0},{2,1},{5,4},{6,5},{9,8},{10,9},{13,12},{14,13},{17,16},{18,1... | collective-permute-start | bytes 1572872 | tf_op jit(solution)/shard_map/ppermute | solution.py:236
  169.2 0.8 copy-start.9
  170.0 42.6 %collective-permute-start.23 = (bf16[512,512]{1,0:T(8,128)(2,1)}, bf16[512,512]{1,0:T(8,128)(2,1)}, u32[]{:S(2)}, u32[]{:S(2)}) collective-permute-start(bf16[512,512]{1,0:T(8,128)(2,1)} %collective-permute-done.15.refs_10_.refs_2_), channel_id=1, source_target_pairs={{2,3},{6,7},{10,11},{14,15},{18,19},{22,23},{26,27},{30,31}} | collective-permute-start | bytes 1572872 | tf_op jit(solution)/shard_map/ppermute | solution.py:235
  171.5 18.9 %copy-start.10 = (bf16[512,512]{1,0:T(8,128)(2,1)S(1)}, bf16[512,512]{1,0:T(8,128)(2,1)}, u32[]{:S(2)}) copy-start(bf16[512,512]{1,0:T(8,128)(2,1)} %copy-done.9) | copy-start | bytes 1572868
  190.4 22.3 %collective-permute-start.24 = (bf16[512,512]{1,0:T(8,128)(2,1)S(1)}, bf16[512,512]{1,0:T(8,128)(2,1)S(1)}, u32[]{:S(2)}, u32[]{:S(2)}) collective-permute-start(bf16[512,512]{1,0:T(8,128)(2,1)S(1)} %copy-done.10), channel_id=1, source_target_pairs={{1,0},{5,4},{9,8},{13,12},{17,16},{21,20},{25,24},{29,28}} | collective-permute-start | bytes 1572872 | tf_op jit(solution)/shard_map/ppermute | solution.py:236
  191.7 40.5 %collective-permute-start.21 = (bf16[512,512]{1,0:T(8,128)(2,1)}, bf16[512,512]{1,0:T(8,128)(2,1)S(1)}, u32[]{:S(2)}, u32[]{:S(2)}) collective-permute-start(bf16[512,512]{1,0:T(8,128)(2,1)} %collective-permute-done.18.refs_2_), channel_id=1, source_target_pairs={{2,3},{6,7},{10,11},{14,15},{18,19},{22,23},{26,27},{30,31}} | collective-permute-start | bytes 1572872 | tf_op jit(solution)/shard_map/ppermute | solution.py:235
  192.4 39.8 %collective-permute-start.22 = (bf16[512,512]{1,0:T(8,128)(2,1)}, bf16[512,512]{1,0:T(8,128)(2,1)S(1)}, u32[]{:S(2)}, u32[]{:S(2)}) collective-permute-start(bf16[512,512]{1,0:T(8,128)(2,1)} %collective-permute-done.20.refs_5_), channel_id=1, source_target_pairs={{1,0},{5,4},{9,8},{13,12},{17,16},{21,20},{25,24},{29,28}} | collective-permute-start | bytes 1572872 | tf_op jit(solution)/shard_map/ppermute | solution.py:236
  212.7 0.8 copy-start.13
  232.2 0.8 copy-start.11
  233.0 0.8 copy-start.12
Sparse Core Ops, SparseCore 0:
  9.6 54.9 all-gather.2
  66.5 74.6 all-gather.4

commit v6 on v5

--- a/solution.py
+++ b/solution.py
@@ -15,31 +15,44 @@
 ANY = pl.BlockSpec(memory_space=pl.ANY)
 
 
-def split_kernel(own, w_ref, *out_refs, j_local, b_local):
-    cols = len(out_refs)
+def cut_kernel(own, t_ref, w_ref, t_out, *refs, j_local, b_local):
+    w_outs, t_sem, w_sem = refs[:-2], refs[-2], refs[-1]
+    cols = len(w_outs)
     for s in range(cols):
         to = lax.rem(own[0] + s, cols)
         for j in range(j_local):
             start = pl.multiple_of((j * cols + to) * b_local, b_local)
-            out_refs[s][:, j * b_local:(j + 1) * b_local] = w_ref[:, pl.ds(start, b_local)]
-
-
-def split_columns(own, couplings, cols, j_local, b_local):
+            pltpu.make_async_copy(
+                w_ref.at[:, pl.ds(start, b_local)], w_outs[s].at[:, j * b_local:(j + 1) * b_local], w_sem.at[s]
+            ).start()
+    for i in range(t_ref.shape[0]):
+        for r in range(t_ref.shape[1]):
+            pltpu.make_async_copy(t_ref.at[i, r], t_out.at[r, :, i], t_sem).start()
+    for s in range(cols):
+        pltpu.make_async_copy(w_outs[s], w_outs[s], w_sem.at[s]).wait()
+    pltpu.make_async_copy(t_out, t_out, t_sem).wait()
+
+
+def cut(own, blocks, couplings, cols, j_local, b_local):
+    i_local, rows, chunks, group, t_depth = blocks.shape
     depth = couplings.shape[0]
-    if b_local % 128:
+    if b_local % 128 or t_depth % 128:
         split = couplings.reshape(depth, j_local, cols, b_local)
-        return [
+        parts = [
             lax.dynamic_index_in_dim(split, lax.rem(own + s, cols), 2, keepdims=False).reshape(depth, -1)
             for s in range(cols)
         ]
+        return [blocks.transpose(1, 2, 0, 3, 4), *parts]
     return pl.pallas_call(
-        functools.partial(split_kernel, j_local=j_local, b_local=b_local),
-        out_shape=[jax.ShapeDtypeStruct((depth, j_local * b_local), couplings.dtype)] * cols,
-        in_specs=[pl.BlockSpec(memory_space=pltpu.SMEM), pl.BlockSpec(memory_space=pltpu.VMEM)],
-        out_specs=[pl.BlockSpec(memory_space=pltpu.VMEM)] * cols,
-        compiler_params=pltpu.CompilerParams(vmem_limit_bytes=24 * 1024 * 1024),
-        cost_estimate=pl.CostEstimate(flops=0, bytes_accessed=4 * couplings.size, transcendentals=0),
-    )(own.reshape(1), couplings)
+        functools.partial(cut_kernel, j_local=j_local, b_local=b_local),
+        out_shape=[jax.ShapeDtypeStruct((rows, chunks, i_local, group, t_depth), blocks.dtype)]
+        + [jax.ShapeDtypeStruct((depth, j_local * b_local), couplings.dtype)] * cols,
+        in_specs=[pl.BlockSpec(memory_space=pltpu.SMEM), ANY, ANY],
+        out_specs=[ANY] * (1 + cols),
+        scratch_shapes=[pltpu.SemaphoreType.DMA, pltpu.SemaphoreType.DMA((cols,))],
+        compiler_params=pltpu.CompilerParams(vmem_limit_bytes=60 * 1024 * 1024),
+        cost_estimate=pl.CostEstimate(flops=0, bytes_accessed=4 * (blocks.size + couplings.size), transcendentals=0),
+    )(own.reshape(1), blocks, couplings)
 
 
 def chunk_kernel(own, *refs, parts, occupied, b_local, q):
@@ -192,29 +205,33 @@
     a_local, b_local = V // rows, V // cols
     own = lax.axis_index("col")
 
-    arrived = list(split_columns(own, couplings, cols, j_local, b_local))
-    arrived[0], amplitudes = lax.optimization_barrier((arrived[0], amplitudes))
+    chunks = a_local // GROUP
+    blocks = amplitudes.reshape(i_local, rows, chunks, GROUP, depth)
+    blocks, *arrived = cut(own, blocks, couplings, cols, j_local, b_local)
     for s in range(1, cols):
         arrived[s] = lax.ppermute(arrived[s], "col", [(c, (c + s) % cols) for c in range(cols)])
-
-    chunks = a_local // GROUP
-    blocks = amplitudes.reshape(i_local, rows, chunks, GROUP, depth).transpose(1, 2, 0, 3, 4)
     blocks = lax.all_to_all(blocks, "row", split_axis=0, concat_axis=0, tiled=True)
-
-    per_part = occupied // cols
-    plain = b_local % 128 or WIDE % b_local or depth % 128 or cols < 3 or per_part * b_local % WIDE or chunks < 3
-
-    def update(q, out, after):
-        return chunk_update(own, flat(pieces[q]), panel_w, ladder, out, after, q, a_local, b_local, occupied)
-
-    def flat(sides):
-        right, left = sides
-        return [right[0], *right[1:], *left[1:]]
 
     rest, _ = lax.optimization_barrier((arrived[1:], blocks))
     panel_w = [
         lax.all_gather(part, "row", axis=0, tiled=True) for part in (arrived[0], jnp.concatenate(rest, axis=1))
     ]
+
+    per_part = occupied // cols
+    plain = (b_local % 128 or WIDE % b_local or depth % 128 or cols < 4
+             or per_part * b_local % WIDE or chunks < 4 or chunks % 2)
+
+    def flat(sides):
+        right, left = sides
+        return [right[0], *right[1:], *left[1:]]
+
+    def update(q, out, after):
+        return chunk_update(own, flat(pieces[q]), panel_w, ladder, out, after, q, a_local, b_local, occupied)
+
+    def hop(sides, s):
+        right, left = sides
+        right.append(lax.ppermute(right[-1], "col", [(c, c + 1) for c in range(s - 1, cols - 1)]))
+        left.append(lax.ppermute(left[-1], "col", [(c + 1, c) for c in range(cols - s)]))
 
     pieces, out = [], None
     for q in range(0, chunks, 2):
@@ -225,21 +242,30 @@
                 both[n], right[middle + 1], left[middle + 1] = lax.optimization_barrier(
                     (both[n], right[middle + 1], left[middle + 1]))
         pair = [([held], [held]) for held in both]
-        final = q + 2 >= chunks and not plain
+        pieces += pair
+        if plain or q + 2 < chunks:
+            for s in range(1, cols):
+                for sides in pair:
+                    hop(sides, s)
+            continue
+        x, y = pair
+        hop(x, 1)
         for s in range(1, cols):
-            if final and s == cols - 1:
-                out = update(0, None, (pair[0][0][-1], pair[0][1][-1]))
-            for n, (right, left) in enumerate(pair):
-                if final and s == cols - 1 and n:
-                    out, right[-1], left[-1] = lax.optimization_barrier((out, right[-1], left[-1]))
-                right.append(lax.ppermute(right[-1], "col", [(c, c + 1) for c in range(s - 1, cols - 1)]))
-                left.append(lax.ppermute(left[-1], "col", [(c + 1, c) for c in range(cols - s)]))
-        pieces += pair
+            if s == cols - 2:
+                out = update(0, None, (x[0][s - 1], x[1][s - 1]))
+                out, x[0][-1], x[1][-1], y[0][-1], y[1][-1] = lax.optimization_barrier(
+                    (out, x[0][-1], x[1][-1], y[0][-1], y[1][-1]))
+            if s == cols - 1:
+                out = update(1, out, ())
+                out, y[0][-1], y[1][-1] = lax.optimization_barrier((out, y[0][-1], y[1][-1]))
+            hop(y, s)
+            if s < cols - 1:
+                hop(x, s + 1)
 
     if plain:
         return jnp.concatenate(
             [plain_update(own, flat(got), panel_w, ladder, b_local, occupied) for got in pieces], axis=0)
-    for q in range(1, chunks):
+    for q in range(2, chunks):
         out = update(q, out, ())
     return out
 

time: 260 us -> 374 us (1.44)
  Pallas kernels: 76.3 us -> 203 us
  waiting for transfers between devices: 99.6 us -> 88.8 us
  local copies, waits for them, and re-layouts: 9.67 us -> 3.45 us
    pallas_call x1, Pallas kernels: 1.34 us -> 128 us  [cut(): pl.pallas_call(functools.partial(cut_kernel, j_local=j_local, b_local=b_l...]
    ppermute x24, waiting for transfers between devices: 66.5 us -> 55.4 us  [the longest x12 55.2 us: hop(): lax.ppermute(left[-1], 'col', [(c + 1, c) for c in range(cols - s)])]
  transfers between devices with their start and end apart: 30 -> 30, of which waited for: 12 -> 11; matrix products, arithmetic and copies ran while one was open for 2% -> 1% of each run, Pallas kernels for 22% -> 15%
where the time goes in v6:
time: 374 us; the launch traced here: 373 us
  Pallas kernels  203 us (54%)
  waiting for transfers between devices  88.8 us (24%)
  starting transfers between devices  61.6 us (16%)
  between operations  13.9 us (4%)
    pallas_call x1, Pallas kernels, cut(): pl.pallas_call(functools.partial(cut_kernel, j_local=j_local, b_local=b_l...  128 us
    pallas_call x4, Pallas kernels, chunk_update(): pl.pallas_call(functools.partial(chunk_kernel, parts=parts, occupied=occu...  75 us
    ppermute x12, waiting for transfers between devices, hop(): lax.ppermute(left[-1], 'col', [(c + 1, c) for c in range(cols - s)])  55.2 us
    ppermute x12, starting transfers between devices, hop(): lax.ppermute(right[-1], 'col', [(c, c + 1) for c in range(s - 1, cols - 1)])  35.2 us
    ppermute x3, waiting for transfers between devices, local(): lax.ppermute(arrived[s], 'col', [(c, (c + s) % cols) for c in range(cols)])  33.4 us
    ppermute x12, starting transfers between devices, hop(): lax.ppermute(left[-1], 'col', [(c + 1, c) for c in range(cols - s)])  15.6 us
  transfers between devices with their start and end apart: 30, of which 11 were waited for; matrix products, arithmetic and copies ran while one was open for 1% of the time, Pallas kernels for 15%

profile of v6, /device:TPU:0, one launch (start us, length us, event | category | flops | bytes accessed | tf_op | source)
XLA Modules:
  0.0 373.3 jit_solution(12540490807071443418)
XLA Ops:
  6.5 128.2 %shard_map.37 = (bf16[8,4,4,16,512]{4,3,2,1,0:T(8,128)(2,1)}, bf16[256,1024]{1,0:T(8,128)(2,1)}, bf16[256,1024]{1,0:T(8,128)(2,1)}, bf16[256,1024]{1,0:T(8,128)(2,1)}, bf16[256,1024]{1,0:T(8,128)(2,1)}) custom-call(s32[1]{0:T(128)} %bitcast.own, bf16[4,8,4,16,512]{4,3,2,1,0:T(8,128)(2,1)} %bitcast.15, bf16[256,4096]{1,0:T(8,128)(2,1)} %w_ref.1), custom_call_target="tpu_custom_call" | custom-call | bytes 8388608 | tf_op jit(solution)/shard_map/pallas_call | solution.py:46
  134.7 0.0 all-gather.3.cloned.1.call-update
  134.8 5.2 %all-to-all-start = ((bf16[8,4,4,16,512]{4,3,2,1,0:T(8,128)(2,1)}), bf16[8,4,4,16,512]{4,3,2,1,0:T(8,128)(2,1)S(1)}, u32[]{:S(2)}, u32[]{:S(2)}) async-start(bf16[8,4,4,16,512]{4,3,2,1,0:T(8,128)(2,1)} %get-tuple-element.27), calls=%async_computation | async-start | bytes 4194304 | tf_op jit(solution)/shard_map/all_to_all | solution.py:213
  140.0 0.0 all-gather.5.cloned.1.call-start
  140.0 1.6 collective-permute-start.10
  141.6 2.6 collective-permute-start.11
  144.2 1.3 collective-permute-start.12
  145.6 11.4 %collective-permute-done.10 = bf16[256,1024]{1,0:T(8,128)(2,1)S(1)} collective-permute-done((bf16[256,1024]{1,0:T(8,128)(2,1)}, bf16[256,1024]{1,0:T(8,128)(2,1)S(1)}, u32[]{:S(2)}, u32[]{:S(2)}) %collective-permute-start.10) | collective-permute-done | bytes 524320 | tf_op jit(solution)/shard_map/ppermute | solution.py:212
  157.0 22.0 %collective-permute-done.11 = bf16[256,1024]{1,0:T(8,128)(2,1)S(1)} collective-permute-done((bf16[256,1024]{1,0:T(8,128)(2,1)}, bf16[256,1024]{1,0:T(8,128)(2,1)S(1)}, u32[]{:S(2)}, u32[]{:S(2)}) %collective-permute-start.11) | collective-permute-done | bytes 524320 | tf_op jit(solution)/shard_map/ppermute | solution.py:212
  178.9 0.0 collective-permute-done.12
  178.9 0.0 all-to-all-done
  179.0 2.3 pad_maximum_fusion
  181.2 0.0 all-gather.5.cloned.1.call-update
  181.3 0.2 fusion
  181.5 1.3 collective-permute-start.6
  182.8 14.4 %collective-permute-start.4 = (bf16[512,512]{1,0:T(8,128)(2,1)S(1)}, bf16[512,512]{1,0:T(8,128)(2,1)S(1)}, u32[]{:S(2)}, u32[]{:S(2)}) collective-permute-start(bf16[512,512]{1,0:T(8,128)(2,1)S(1)} %bitcast.17), channel_id=1, source_target_pairs={{0,1},{1,2},{2,3},{4,5},{5,6},{6,7},{8,9},{9,10},{10,11},{12,13},{... | collective-permute-start | bytes 1572872 | tf_op jit(solution)/shard_map/ppermute | solution.py:233
  197.2 1.3 collective-permute-start.2
  198.5 4.6 %collective-permute-start = (bf16[512,512]{1,0:T(8,128)(2,1)S(1)}, bf16[512,512]{1,0:T(8,128)(2,1)S(1)}, u32[]{:S(2)}, u32[]{:S(2)}) collective-permute-start(bf16[512,512]{1,0:T(8,128)(2,1)S(1)} %bitcast.13), channel_id=1, source_target_pairs={{0,1},{1,2},{2,3},{4,5},{5,6},{6,7},{8,9},{9,10},{10,11},{12,13},{... | collective-permute-start | bytes 1572872 | tf_op jit(solution)/shard_map/ppermute | solution.py:233
  203.1 4.9 %collective-permute-done.6.refs_4_ = bf16[512,512]{1,0:T(8,128)(2,1)S(1)} collective-permute-done((bf16[512,512]{1,0:T(8,128)(2,1)S(1)}, bf16[512,512]{1,0:T(8,128)(2,1)S(1)}, u32[]{:S(2)}, u32[]{:S(2)}) %collective-permute-start.6) | collective-permute-done | bytes 524320 | tf_op jit(solution)/shard_map/ppermute | solution.py:234
  208.0 1.3 collective-permute-start.7
  209.3 0.2 collective-permute-done.4.refs_1_
  209.5 0.7 collective-permute-start.5
  210.2 9.0 %collective-permute-done.2.refs_4_ = bf16[512,512]{1,0:T(8,128)(2,1)S(1)} collective-permute-done((bf16[512,512]{1,0:T(8,128)(2,1)S(1)}, bf16[512,512]{1,0:T(8,128)(2,1)S(1)}, u32[]{:S(2)}, u32[]{:S(2)}) %collective-permute-start.2) | collective-permute-done | bytes 524320 | tf_op jit(solution)/shard_map/ppermute | solution.py:234
  219.2 1.3 collective-permute-start.3
  220.5 0.0 collective-permute-done.refs_1_
  220.5 1.5 collective-permute-start.1
  222.0 8.4 %collective-permute-done.7.refs_5_ = bf16[512,512]{1,0:T(8,128)(2,1)S(1)} collective-permute-done((bf16[512,512]{1,0:T(8,128)(2,1)S(1)}, bf16[512,512]{1,0:T(8,128)(2,1)S(1)}, u32[]{:S(2)}, u32[]{:S(2)}) %collective-permute-start.7) | collective-permute-done | bytes 524320 | tf_op jit(solution)/shard_map/ppermute | solution.py:234
  230.5 0.0 collective-permute-done.5.refs_2_
  230.5 1.3 collective-permute-start.14
  231.8 6.1 %collective-permute-start.13 = (bf16[512,512]{1,0:T(8,128)(2,1)S(1)}, bf16[512,512]{1,0:T(8,128)(2,1)S(1)}, u32[]{:S(2)}, u32[]{:S(2)}) collective-permute-start(bf16[512,512]{1,0:T(8,128)(2,1)S(1)} %bitcast.10), channel_id=1, source_target_pairs={{0,1},{1,2},{2,3},{4,5},{5,6},{6,7},{8,9},{9,10},{10,11},{12,13},{... | collective-permute-start | bytes 1572872 | tf_op jit(solution)/shard_map/ppermute | solution.py:233
  237.9 1.3 collective-permute-start.9
  239.2 2.6 collective-permute-done.3.refs_5_
  241.8 0.7 collective-permute-start.8
  242.5 1.3 collective-permute-start.18
  243.8 20.4 %collective-permute-done.9.refs_6_ = bf16[512,512]{1,0:T(8,128)(2,1)S(1)} collective-permute-done((bf16[512,512]{1,0:T(8,128)(2,1)S(1)}, bf16[512,512]{1,0:T(8,128)(2,1)S(1)}, u32[]{:S(2)}, u32[]{:S(2)}) %collective-permute-start.9) | collective-permute-done | bytes 524320 | tf_op jit(solution)/shard_map/ppermute | solution.py:234
  264.2 2.3 collective-permute-start.17
  266.4 0.0 collective-permute-done.14.refs_11_.refs_4_
  266.4 1.3 collective-permute-start.20
  267.7 0.0 collective-permute-done.13.refs_10_.refs_1_
  267.7 1.5 collective-permute-start.19
  269.2 0.0 collective-permute-done.8.refs_3_
  269.3 1.3 collective-permute-start.16
  270.5 4.9 %collective-permute-done.18.refs_4_ = bf16[512,512]{1,0:T(8,128)(2,1)S(1)} collective-permute-done((bf16[512,512]{1,0:T(8,128)(2,1)S(1)}, bf16[512,512]{1,0:T(8,128)(2,1)S(1)}, u32[]{:S(2)}, u32[]{:S(2)}) %collective-permute-start.18) | collective-permute-done | bytes 524320 | tf_op jit(solution)/shard_map/ppermute | solution.py:234
  275.5 0.8 copy-done.7
  276.2 1.5 collective-permute-start.15
  277.7 18.8 %shard_map.38.refs_10_ = bf16[64,128,1024]{2,1,0:T(8,128)(2,1)} custom-call(s32[1]{0:T(128)} %bitcast.own, bf16[512,512]{1,0:T(8,128)(2,1)} %bitcast.18, bf16[512,512]{1,0:T(8,128)(2,1)} %copy-done.17, bf16[512,512]{1,0:T(8,128)(2,1)} %copy-done.19, bf16[512,512]{1,0:T(8,128)(2,1)} %copy-done.21, bf16[512,512]{1,0:T(8,128)(2,1)} %copy-done.16, ...), custom_call_target="tpu_custom_call" | custom-call | flops 12884901888 | bytes 25165824 | tf_op jit(solution)/shard_map/pallas_call | solution.py:161
  296.6 0.8 collective-permute-done.16.refs_5_
  297.4 0.0 collective-permute-done.15.refs_2_
  297.4 0.7 collective-permute-start.21
  298.1 1.3 collective-permute-start.22
  299.4 0.7 collective-permute-start.25
  300.1 0.0 collective-permute-done.20.refs_6_
  300.1 1.3 collective-permute-start.26
  301.4 18.8 %shard_map.39.refs_10_ = bf16[64,128,1024]{2,1,0:T(8,128)(2,1)} custom-call(s32[1]{0:T(128)} %bitcast.own, bf16[512,512]{1,0:T(8,128)(2,1)} %bitcast.14, bf16[512,512]{1,0:T(8,128)(2,1)} %copy-done.4, bf16[512,512]{1,0:T(8,128)(2,1)} %collective-permute-done.1.refs_2_, ...), custom_call_target="tpu_custom_call", output_to_operand_aliasing={{}: (11, {})} | custom-call | flops 12884901888 | bytes 25165824 | tf_op jit(solution)/shard_map/pallas_call | solution.py:161
  320.2 0.0 collective-permute-done.21.refs_2_
  320.2 0.0 collective-permute-done.22.refs_5_
  320.2 0.7 collective-permute-start.23
  320.9 1.5 collective-permute-start.24
  322.4 4.2 %collective-permute-done.26.refs_6_ = bf16[512,512]{1,0:T(8,128)(2,1)S(1)} collective-permute-done((bf16[512,512]{1,0:T(8,128)(2,1)}, bf16[512,512]{1,0:T(8,128)(2,1)S(1)}, u32[]{:S(2)}, u32[]{:S(2)}) %collective-permute-start.26) | collective-permute-done | bytes 524320 | tf_op jit(solution)/shard_map/ppermute | solution.py:234
  326.6 0.8 copy-done.12
  327.4 18.7 %shard_map.40.refs_10_ = bf16[64,128,1024]{2,1,0:T(8,128)(2,1)} custom-call(s32[1]{0:T(128)} %bitcast.own, bf16[512,512]{1,0:T(8,128)(2,1)} %bitcast.11, bf16[512,512]{1,0:T(8,128)(2,1)} %copy-done.6, bf16[512,512]{1,0:T(8,128)(2,1)} %collective-permute-done.15.refs_2_, bf16[512,512]{1,0:T(8,128)(2,1)} %copy-done.11, ...), custom_call_target="tpu_custom_call", output_to_operand_aliasing={{}: (11, {})} | custom-call | flops 12884901888 | bytes 25165824 | tf_op jit(solution)/shard_map/pallas_call | solution.py:161
  346.2 0.8 copy-done.13
  346.9 0.8 copy-done.14
  347.7 18.7 %shard_map.41 = bf16[64,128,1024]{2,1,0:T(8,128)(2,1)} custom-call(s32[1]{0:T(128)} %bitcast.own, bf16[512,512]{1,0:T(8,128)(2,1)} %bitcast.8, bf16[512,512]{1,0:T(8,128)(2,1)} %collective-permute-done.17.refs_1_, bf16[512,512]{1,0:T(8,128)(2,1)} %copy-done.9, bf16[512,512]{1,0:T(8,128)(2,1)} %copy-done.13, ...), custom_call_target="tpu_custom_call", output_to_operand_aliasing={{}: (11, {})} | custom-call | flops 12884901888 | bytes 25165824 | tf_op jit(solution)/shard_map/pallas_call | solution.py:161
  (49 shorter events, 0.1 us)
Async XLA Ops:
  6.5 271.2 %all-gather.3.cloned.1.call-start = ((), (), s32[]{:S(2)}) async-start(), calls=%async_computation.1 | async-start | bytes 4718592 | tf_op jit(solution)/shard_map/all_gather | solution.py:217
  134.8 44.2 %all-to-all-start = ((bf16[8,4,4,16,512]{4,3,2,1,0:T(8,128)(2,1)}), bf16[8,4,4,16,512]{4,3,2,1,0:T(8,128)(2,1)S(1)}, u32[]{:S(2)}, u32[]{:S(2)}) async-start(bf16[8,4,4,16,512]{4,3,2,1,0:T(8,128)(2,1)} %get-tuple-element.27), calls=%async_computation | async-start | bytes 4194304 | tf_op jit(solution)/shard_map/all_to_all | solution.py:213
  140.0 137.7 %all-gather.5.cloned.1.call-start = ((), (), s32[]{:S(2)}) async-start(), calls=%async_computation.2 | async-start | bytes 14155776 | tf_op jit(solution)/shard_map/all_gather | solution.py:217
  140.0 16.9 %collective-permute-start.10 = (bf16[256,1024]{1,0:T(8,128)(2,1)}, bf16[256,1024]{1,0:T(8,128)(2,1)S(1)}, u32[]{:S(2)}, u32[]{:S(2)}) collective-permute-start(bf16[256,1024]{1,0:T(8,128)(2,1)} %get-tuple-element.32), channel_id=1, source_target_pairs={{0,1},{1,2},{2,3},{3,0},{4,5},{5,6},{6,7},{7,4},{8,9},{9,10},{10,1... | collective-permute-start | bytes 1572872 | tf_op jit(solution)/shard_map/ppermute | solution.py:212
  141.6 37.3 %collective-permute-start.11 = (bf16[256,1024]{1,0:T(8,128)(2,1)}, bf16[256,1024]{1,0:T(8,128)(2,1)S(1)}, u32[]{:S(2)}, u32[]{:S(2)}) collective-permute-start(bf16[256,1024]{1,0:T(8,128)(2,1)} %get-tuple-element.33), channel_id=1, source_target_pairs={{0,2},{1,3},{2,0},{3,1},{4,6},{5,7},{6,4},{7,5},{8,10},{9,11},{10,... | collective-permute-start | bytes 1572872 | tf_op jit(solution)/shard_map/ppermute | solution.py:212
  144.2 34.7 %collective-permute-start.12 = (bf16[256,1024]{1,0:T(8,128)(2,1)}, bf16[256,1024]{1,0:T(8,128)(2,1)}, u32[]{:S(2)}, u32[]{:S(2)}) collective-permute-start(bf16[256,1024]{1,0:T(8,128)(2,1)} %get-tuple-element.34), channel_id=1, source_target_pairs={{0,3},{1,0},{2,1},{3,2},{4,7},{5,4},{6,5},{7,6},{8,11},{9,8},{10,9... | collective-permute-start | bytes 1572872 | tf_op jit(solution)/shard_map/ppermute | solution.py:212
  181.5 93.9 %copy-start.2 = (bf16[8,1,4,16,512]{4,3,2,1,0:T(8,128)(2,1)}, bf16[8,1,4,16,512]{4,3,2,1,0:T(8,128)(2,1)S(1)}, u32[]{:S(2)}) copy-start(bf16[8,1,4,16,512]{4,3,2,1,0:T(8,128)(2,1)S(1)} %get-tuple-element.51) | copy-start | bytes 1572868
  181.5 93.9 %copy-start.15 = (bf16[8,1,4,16,512]{4,3,2,1,0:T(8,128)(2,1)}, bf16[8,1,4,16,512]{4,3,2,1,0:T(8,128)(2,1)S(1)}, u32[]{:S(2)}) copy-start(bf16[8,1,4,16,512]{4,3,2,1,0:T(8,128)(2,1)S(1)} %get-tuple-element.50) | copy-start | bytes 1572868
  181.5 115.0 %copy-start = (bf16[8,1,4,16,512]{4,3,2,1,0:T(8,128)(2,1)}, bf16[8,1,4,16,512]{4,3,2,1,0:T(8,128)(2,1)S(1)}, u32[]{:S(2)}) copy-start(bf16[8,1,4,16,512]{4,3,2,1,0:T(8,128)(2,1)S(1)} %get-tuple-element.52) | copy-start | bytes 1572868
  181.5 115.0 %copy-start.1 = (bf16[8,1,4,16,512]{4,3,2,1,0:T(8,128)(2,1)}, bf16[8,1,4,16,512]{4,3,2,1,0:T(8,128)(2,1)S(1)}, u32[]{:S(2)}) copy-start(bf16[8,1,4,16,512]{4,3,2,1,0:T(8,128)(2,1)S(1)} %get-tuple-element.49) | copy-start | bytes 1572868
  181.5 26.5 %collective-permute-start.6 = (bf16[512,512]{1,0:T(8,128)(2,1)S(1)}, bf16[512,512]{1,0:T(8,128)(2,1)S(1)}, u32[]{:S(2)}, u32[]{:S(2)}) collective-permute-start(bf16[512,512]{1,0:T(8,128)(2,1)S(1)} %bitcast.16), channel_id=1, source_target_pairs={{1,0},{2,1},{3,2},{5,4},{6,5},{7,6},{9,8},{10,9},{11,10},{13,12},{... | collective-permute-start | bytes 1572872 | tf_op jit(solution)/shard_map/ppermute | solution.py:234
  182.8 26.7 %collective-permute-start.4 = (bf16[512,512]{1,0:T(8,128)(2,1)S(1)}, bf16[512,512]{1,0:T(8,128)(2,1)S(1)}, u32[]{:S(2)}, u32[]{:S(2)}) collective-permute-start(bf16[512,512]{1,0:T(8,128)(2,1)S(1)} %bitcast.17), channel_id=1, source_target_pairs={{0,1},{1,2},{2,3},{4,5},{5,6},{6,7},{8,9},{9,10},{10,11},{12,13},{... | collective-permute-start | bytes 1572872 | tf_op jit(solution)/shard_map/ppermute | solution.py:233
  197.2 22.0 %collective-permute-start.2 = (bf16[512,512]{1,0:T(8,128)(2,1)S(1)}, bf16[512,512]{1,0:T(8,128)(2,1)S(1)}, u32[]{:S(2)}, u32[]{:S(2)}) collective-permute-start(bf16[512,512]{1,0:T(8,128)(2,1)S(1)} %bitcast.12), channel_id=1, source_target_pairs={{1,0},{2,1},{3,2},{5,4},{6,5},{7,6},{9,8},{10,9},{11,10},{13,12},{... | collective-permute-start | bytes 1572872 | tf_op jit(solution)/shard_map/ppermute | solution.py:234
  198.5 22.0 %collective-permute-start = (bf16[512,512]{1,0:T(8,128)(2,1)S(1)}, bf16[512,512]{1,0:T(8,128)(2,1)S(1)}, u32[]{:S(2)}, u32[]{:S(2)}) collective-permute-start(bf16[512,512]{1,0:T(8,128)(2,1)S(1)} %bitcast.13), channel_id=1, source_target_pairs={{0,1},{1,2},{2,3},{4,5},{5,6},{6,7},{8,9},{9,10},{10,11},{12,13},{... | collective-permute-start | bytes 1572872 | tf_op jit(solution)/shard_map/ppermute | solution.py:233
  208.0 33.8 %copy-start.16 = (bf16[512,512]{1,0:T(8,128)(2,1)}, bf16[512,512]{1,0:T(8,128)(2,1)S(1)}, u32[]{:S(2)}) copy-start(bf16[512,512]{1,0:T(8,128)(2,1)S(1)} %collective-permute-done.6.refs_4_) | copy-start | bytes 1572868
  208.0 22.5 %collective-permute-start.7 = (bf16[512,512]{1,0:T(8,128)(2,1)S(1)}, bf16[512,512]{1,0:T(8,128)(2,1)S(1)}, u32[]{:S(2)}, u32[]{:S(2)}) collective-permute-start(bf16[512,512]{1,0:T(8,128)(2,1)S(1)} %collective-permute-done.6.refs_4_), channel_id=1, source_target_pairs={{1,0},{2,1},{5,4},{6,5},{9,8},{10,9},{13,12},{14,13},{17,16},{18,1... | collective-permute-start | bytes 1572872 | tf_op jit(solution)/shard_map/ppermute | solution.py:234
  209.5 65.9 %copy-start.17 = (bf16[512,512]{1,0:T(8,128)(2,1)}, bf16[512,512]{1,0:T(8,128)(2,1)S(1)}, u32[]{:S(2)}) copy-start(bf16[512,512]{1,0:T(8,128)(2,1)S(1)} %collective-permute-done.4.refs_1_) | copy-start | bytes 1572868
  209.5 21.0 %collective-permute-start.5 = (bf16[512,512]{1,0:T(8,128)(2,1)S(1)}, bf16[512,512]{1,0:T(8,128)(2,1)S(1)}, u32[]{:S(2)}, u32[]{:S(2)}) collective-permute-start(bf16[512,512]{1,0:T(8,128)(2,1)S(1)} %collective-permute-done.4.refs_1_), channel_id=1, source_target_pairs={{1,2},{2,3},{5,6},{6,7},{9,10},{10,11},{13,14},{14,15},{17,18},{18... | collective-permute-start | bytes 1572872 | tf_op jit(solution)/shard_map/ppermute | solution.py:233
  219.2 77.3 %copy-start.3 = (bf16[512,512]{1,0:T(8,128)(2,1)}, bf16[512,512]{1,0:T(8,128)(2,1)S(1)}, u32[]{:S(2)}) copy-start(bf16[512,512]{1,0:T(8,128)(2,1)S(1)} %collective-permute-done.2.refs_4_) | copy-start | bytes 1572868
  219.2 22.6 %collective-permute-start.3 = (bf16[512,512]{1,0:T(8,128)(2,1)S(1)}, bf16[512,512]{1,0:T(8,128)(2,1)}, u32[]{:S(2)}, u32[]{:S(2)}) collective-permute-start(bf16[512,512]{1,0:T(8,128)(2,1)S(1)} %collective-permute-done.2.refs_4_), channel_id=1, source_target_pairs={{1,0},{2,1},{5,4},{6,5},{9,8},{10,9},{13,12},{14,13},{17,16},{18,1... | collective-permute-start | bytes 1572872 | tf_op jit(solution)/shard_map/ppermute | solution.py:234
  220.5 76.0 %copy-start.4 = (bf16[512,512]{1,0:T(8,128)(2,1)}, bf16[512,512]{1,0:T(8,128)(2,1)S(1)}, u32[]{:S(2)}) copy-start(bf16[512,512]{1,0:T(8,128)(2,1)S(1)} %collective-permute-done.refs_1_) | copy-start | bytes 1572868
  220.5 21.3 %collective-permute-start.1 = (bf16[512,512]{1,0:T(8,128)(2,1)S(1)}, bf16[512,512]{1,0:T(8,128)(2,1)}, u32[]{:S(2)}, u32[]{:S(2)}) collective-permute-start(bf16[512,512]{1,0:T(8,128)(2,1)S(1)} %collective-permute-done.refs_1_), channel_id=1, source_target_pairs={{1,2},{2,3},{5,6},{6,7},{9,10},{10,11},{13,14},{14,15},{17,18},{18... | collective-permute-start | bytes 1572872 | tf_op jit(solution)/shard_map/ppermute | solution.py:233
  230.5 45.0 %copy-start.18 = (bf16[512,512]{1,0:T(8,128)(2,1)}, bf16[512,512]{1,0:T(8,128)(2,1)S(1)}, u32[]{:S(2)}) copy-start(bf16[512,512]{1,0:T(8,128)(2,1)S(1)} %collective-permute-done.7.refs_5_) | copy-start | bytes 1572868
  230.5 45.0 %copy-start.19 = (bf16[512,512]{1,0:T(8,128)(2,1)}, bf16[512,512]{1,0:T(8,128)(2,1)S(1)}, u32[]{:S(2)}) copy-start(bf16[512,512]{1,0:T(8,128)(2,1)S(1)} %collective-permute-done.5.refs_2_) | copy-start | bytes 1572868
  230.5 36.0 %collective-permute-start.14 = (bf16[512,512]{1,0:T(8,128)(2,1)S(1)}, bf16[512,512]{1,0:T(8,128)(2,1)S(1)}, u32[]{:S(2)}, u32[]{:S(2)}) collective-permute-start(bf16[512,512]{1,0:T(8,128)(2,1)S(1)} %bitcast.9), channel_id=1, source_target_pairs={{1,0},{2,1},{3,2},{5,4},{6,5},{7,6},{9,8},{10,9},{11,10},{13,12},{... | collective-permute-start | bytes 1572872 | tf_op jit(solution)/shard_map/ppermute | solution.py:234
  231.8 36.0 %collective-permute-start.13 = (bf16[512,512]{1,0:T(8,128)(2,1)S(1)}, bf16[512,512]{1,0:T(8,128)(2,1)S(1)}, u32[]{:S(2)}, u32[]{:S(2)}) collective-permute-start(bf16[512,512]{1,0:T(8,128)(2,1)S(1)} %bitcast.10), channel_id=1, source_target_pairs={{0,1},{1,2},{2,3},{4,5},{5,6},{6,7},{8,9},{9,10},{10,11},{12,13},{... | collective-permute-start | bytes 1572872 | tf_op jit(solution)/shard_map/ppermute | solution.py:233
  237.9 26.3 %collective-permute-start.9 = (bf16[512,512]{1,0:T(8,128)(2,1)S(1)}, bf16[512,512]{1,0:T(8,128)(2,1)S(1)}, u32[]{:S(2)}, u32[]{:S(2)}) collective-permute-start(bf16[512,512]{1,0:T(8,128)(2,1)S(1)} %collective-permute-done.7.refs_5_), channel_id=1, source_target_pairs={{1,0},{5,4},{9,8},{13,12},{17,16},{21,20},{25,24},{29,28}} | collective-permute-start | bytes 1572872 | tf_op jit(solution)/shard_map/ppermute | solution.py:234
  241.8 27.5 %collective-permute-start.8 = (bf16[512,512]{1,0:T(8,128)(2,1)S(1)}, bf16[512,512]{1,0:T(8,128)(2,1)S(1)}, u32[]{:S(2)}, u32[]{:S(2)}) collective-permute-start(bf16[512,512]{1,0:T(8,128)(2,1)S(1)} %collective-permute-done.5.refs_2_), channel_id=1, source_target_pairs={{2,3},{6,7},{10,11},{14,15},{18,19},{22,23},{26,27},{30,31}} | collective-permute-start | bytes 1572872 | tf_op jit(solution)/shard_map/ppermute | solution.py:233
  242.5 32.9 %collective-permute-start.18 = (bf16[512,512]{1,0:T(8,128)(2,1)S(1)}, bf16[512,512]{1,0:T(8,128)(2,1)S(1)}, u32[]{:S(2)}, u32[]{:S(2)}) collective-permute-start(bf16[512,512]{1,0:T(8,128)(2,1)S(1)} %bitcast.6), channel_id=1, source_target_pairs={{1,0},{2,1},{3,2},{5,4},{6,5},{7,6},{9,8},{10,9},{11,10},{13,12},{... | collective-permute-start | bytes 1572872 | tf_op jit(solution)/shard_map/ppermute | solution.py:234
  264.2 11.3 %copy-start.20 = (bf16[512,512]{1,0:T(8,128)(2,1)}, bf16[512,512]{1,0:T(8,128)(2,1)S(1)}, u32[]{:S(2)}) copy-start(bf16[512,512]{1,0:T(8,128)(2,1)S(1)} %collective-permute-done.9.refs_6_) | copy-start | bytes 1572868
  264.2 32.4 %collective-permute-start.17 = (bf16[512,512]{1,0:T(8,128)(2,1)S(1)}, bf16[512,512]{1,0:T(8,128)(2,1)}, u32[]{:S(2)}, u32[]{:S(2)}) collective-permute-start(bf16[512,512]{1,0:T(8,128)(2,1)S(1)} %bitcast.7), channel_id=1, source_target_pairs={{0,1},{1,2},{2,3},{4,5},{5,6},{6,7},{8,9},{9,10},{10,11},{12,13},{... | collective-permute-start | bytes 1572872 | tf_op jit(solution)/shard_map/ppermute | solution.py:233
  266.4 11.3 %copy-start.5 = (bf16[512,512]{1,0:T(8,128)(2,1)}, bf16[512,512]{1,0:T(8,128)(2,1)S(1)}, u32[]{:S(2)}) copy-start(bf16[512,512]{1,0:T(8,128)(2,1)S(1)} %collective-permute-done.14.refs_11_.refs_4_) | copy-start | bytes 1572868
  266.4 33.6 %collective-permute-start.20 = (bf16[512,512]{1,0:T(8,128)(2,1)}, bf16[512,512]{1,0:T(8,128)(2,1)}, u32[]{:S(2)}, u32[]{:S(2)}) collective-permute-start(bf16[512,512]{1,0:T(8,128)(2,1)} %collective-permute-done.3.refs_5_), channel_id=1, source_target_pairs={{1,0},{5,4},{9,8},{13,12},{17,16},{21,20},{25,24},{29,28}} | collective-permute-start | bytes 1572872 | tf_op jit(solution)/shard_map/ppermute | solution.py:234
  267.7 10.0 %copy-start.6 = (bf16[512,512]{1,0:T(8,128)(2,1)}, bf16[512,512]{1,0:T(8,128)(2,1)S(1)}, u32[]{:S(2)}) copy-start(bf16[512,512]{1,0:T(8,128)(2,1)S(1)} %collective-permute-done.13.refs_10_.refs_1_) | copy-start | bytes 1572868
  267.7 33.6 %collective-permute-start.19 = (bf16[512,512]{1,0:T(8,128)(2,1)}, bf16[512,512]{1,0:T(8,128)(2,1)}, u32[]{:S(2)}, u32[]{:S(2)}) collective-permute-start(bf16[512,512]{1,0:T(8,128)(2,1)} %collective-permute-done.1.refs_2_), channel_id=1, source_target_pairs={{2,3},{6,7},{10,11},{14,15},{18,19},{22,23},{26,27},{30,31}} | collective-permute-start | bytes 1572872 | tf_op jit(solution)/shard_map/ppermute | solution.py:233
  269.3 6.2 %copy-start.21 = (bf16[512,512]{1,0:T(8,128)(2,1)}, bf16[512,512]{1,0:T(8,128)(2,1)S(1)}, u32[]{:S(2)}) copy-start(bf16[512,512]{1,0:T(8,128)(2,1)S(1)} %collective-permute-done.8.refs_3_) | copy-start | bytes 1572868
  269.3 28.1 %collective-permute-start.16 = (bf16[512,512]{1,0:T(8,128)(2,1)S(1)}, bf16[512,512]{1,0:T(8,128)(2,1)}, u32[]{:S(2)}, u32[]{:S(2)}) collective-permute-start(bf16[512,512]{1,0:T(8,128)(2,1)S(1)} %collective-permute-done.14.refs_11_.refs_4_), channel_id=1, source_target_pairs={{1,0},{2,1},{5,4},{6,5},{9,8},{10,9},{13,12},{14,13},{17,16},{18,1... | collective-permute-start | bytes 1572872 | tf_op jit(solution)/shard_map/ppermute | solution.py:234
  275.4 0.8 copy-start.7
  276.2 21.1 %collective-permute-start.15 = (bf16[512,512]{1,0:T(8,128)(2,1)S(1)}, bf16[512,512]{1,0:T(8,128)(2,1)}, u32[]{:S(2)}, u32[]{:S(2)}) collective-permute-start(bf16[512,512]{1,0:T(8,128)(2,1)S(1)} %collective-permute-done.13.refs_10_.refs_1_), channel_id=1, source_target_pairs={{1,2},{2,3},{5,6},{6,7},{9,10},{10,11},{13,14},{14,15},{17,18},{18... | collective-permute-start | bytes 1572872 | tf_op jit(solution)/shard_map/ppermute | solution.py:233
  277.7 20.4 %copy-start.8 = (bf16[512,512]{1,0:T(8,128)(2,1)S(1)}, bf16[512,512]{1,0:T(8,128)(2,1)}, u32[]{:S(2)}) copy-start(bf16[512,512]{1,0:T(8,128)(2,1)} %copy-done.7) | copy-start | bytes 1572868
  297.4 22.8 %collective-permute-start.21 = (bf16[512,512]{1,0:T(8,128)(2,1)}, bf16[512,512]{1,0:T(8,128)(2,1)S(1)}, u32[]{:S(2)}, u32[]{:S(2)}) collective-permute-start(bf16[512,512]{1,0:T(8,128)(2,1)} %collective-permute-done.17.refs_1_), channel_id=1, source_target_pairs={{1,2},{2,3},{5,6},{6,7},{9,10},{10,11},{13,14},{14,15},{17,18},{18... | collective-permute-start | bytes 1572872 | tf_op jit(solution)/shard_map/ppermute | solution.py:233
  298.1 22.1 %collective-permute-start.22 = (bf16[512,512]{1,0:T(8,128)(2,1)S(1)}, bf16[512,512]{1,0:T(8,128)(2,1)S(1)}, u32[]{:S(2)}, u32[]{:S(2)}) collective-permute-start(bf16[512,512]{1,0:T(8,128)(2,1)S(1)} %copy-done.8), channel_id=1, source_target_pairs={{1,0},{2,1},{5,4},{6,5},{9,8},{10,9},{13,12},{14,13},{17,16},{18,1... | collective-permute-start | bytes 1572872 | tf_op jit(solution)/shard_map/ppermute | solution.py:234
  299.4 23.0 %collective-permute-start.25 = (bf16[512,512]{1,0:T(8,128)(2,1)}, bf16[512,512]{1,0:T(8,128)(2,1)S(1)}, u32[]{:S(2)}, u32[]{:S(2)}) collective-permute-start(bf16[512,512]{1,0:T(8,128)(2,1)} %collective-permute-done.15.refs_2_), channel_id=1, source_target_pairs={{2,3},{6,7},{10,11},{14,15},{18,19},{22,23},{26,27},{30,31}} | collective-permute-start | bytes 1572872 | tf_op jit(solution)/shard_map/ppermute | solution.py:233
  300.1 26.5 %collective-permute-start.26 = (bf16[512,512]{1,0:T(8,128)(2,1)}, bf16[512,512]{1,0:T(8,128)(2,1)S(1)}, u32[]{:S(2)}, u32[]{:S(2)}) collective-permute-start(bf16[512,512]{1,0:T(8,128)(2,1)} %collective-permute-done.16.refs_5_), channel_id=1, source_target_pairs={{1,0},{5,4},{9,8},{13,12},{17,16},{21,20},{25,24},{29,28}} | collective-permute-start | bytes 1572872 | tf_op jit(solution)/shard_map/ppermute | solution.py:234
  320.2 25.9 %copy-start.9 = (bf16[512,512]{1,0:T(8,128)(2,1)}, bf16[512,512]{1,0:T(8,128)(2,1)S(1)}, u32[]{:S(2)}) copy-start(bf16[512,512]{1,0:T(8,128)(2,1)S(1)} %collective-permute-done.21.refs_2_) | copy-start | bytes 1572868
  320.2 25.9 %copy-start.10 = (bf16[512,512]{1,0:T(8,128)(2,1)}, bf16[512,512]{1,0:T(8,128)(2,1)S(1)}, u32[]{:S(2)}) copy-start(bf16[512,512]{1,0:T(8,128)(2,1)S(1)} %collective-permute-done.22.refs_5_) | copy-start | bytes 1572868
  320.2 25.9 %collective-permute-start.23 = (bf16[512,512]{1,0:T(8,128)(2,1)S(1)}, bf16[512,512]{1,0:T(8,128)(2,1)S(1)}, u32[]{:S(2)}, u32[]{:S(2)}) collective-permute-start(bf16[512,512]{1,0:T(8,128)(2,1)S(1)} %collective-permute-done.21.refs_2_), channel_id=1, source_target_pairs={{2,3},{6,7},{10,11},{14,15},{18,19},{22,23},{26,27},{30,31}} | collective-permute-start | bytes 1572872 | tf_op jit(solution)/shard_map/ppermute | solution.py:233
  320.9 25.3 %collective-permute-start.24 = (bf16[512,512]{1,0:T(8,128)(2,1)S(1)}, bf16[512,512]{1,0:T(8,128)(2,1)S(1)}, u32[]{:S(2)}, u32[]{:S(2)}) collective-permute-start(bf16[512,512]{1,0:T(8,128)(2,1)S(1)} %collective-permute-done.22.refs_5_), channel_id=1, source_target_pairs={{1,0},{5,4},{9,8},{13,12},{17,16},{21,20},{25,24},{29,28}} | collective-permute-start | bytes 1572872 | tf_op jit(solution)/shard_map/ppermute | solution.py:234
  322.4 4.2 %copy-start.11 = (bf16[512,512]{1,0:T(8,128)(2,1)}, bf16[512,512]{1,0:T(8,128)(2,1)S(1)}, u32[]{:S(2)}) copy-start(bf16[512,512]{1,0:T(8,128)(2,1)S(1)} %collective-permute-done.25.refs_3_) | copy-start | bytes 1572868
  326.6 0.8 copy-start.12
  346.1 0.8 copy-start.13
  346.9 0.8 copy-start.14
Sparse Core Ops, SparseCore 0:
  134.9 50.2 all-gather.2
  187.1 76.9 all-gather.4

commit v7 on v6

--- a/solution.py
+++ b/solution.py
@@ -48,15 +48,16 @@
         out_shape=[jax.ShapeDtypeStruct((rows, chunks, i_local, group, t_depth), blocks.dtype)]
         + [jax.ShapeDtypeStruct((depth, j_local * b_local), couplings.dtype)] * cols,
         in_specs=[pl.BlockSpec(memory_space=pltpu.SMEM), ANY, ANY],
-        out_specs=[ANY] * (1 + cols),
+        out_specs=[pl.BlockSpec(memory_space=pltpu.VMEM)] * (1 + cols),
         scratch_shapes=[pltpu.SemaphoreType.DMA, pltpu.SemaphoreType.DMA((cols,))],
         compiler_params=pltpu.CompilerParams(vmem_limit_bytes=60 * 1024 * 1024),
         cost_estimate=pl.CostEstimate(flops=0, bytes_accessed=4 * (blocks.size + couplings.size), transcendentals=0),
     )(own.reshape(1), blocks, couplings)
 
 
-def chunk_kernel(own, *refs, parts, occupied, b_local, q):
-    t_own, t_right, t_left = refs[0], refs[1:parts], refs[parts:2 * parts - 1]
+def chunk_kernel(own, *refs, starts, parts, occupied, b_local, q):
+    t_refs = [ref.at[pl.ds(start, GROUP * occupied)] for ref, start in zip(refs, starts)]
+    t_own, t_right, t_left = t_refs[0], t_refs[1:parts], t_refs[parts:]
     w_own, w_rest, ladder_hbm = refs[2 * parts - 1:2 * parts + 2]
     out_ref, t_all, w_buf, ladder, pairs, out_buf, t_sem, w_sem, l_sem, out_sem = refs[-10:]
     depth = t_own.shape[1]
@@ -147,11 +148,12 @@
 
 
 def chunk_update(own, pieces, panel_w, ladder, out, after, q, a_local, b_local, occupied):
-    rows, depth = pieces[0].shape
+    arrays, starts = zip(*pieces)
+    rows = GROUP * occupied
     count = occupied * occupied
     k_all, width = panel_w[0].shape
     parts = 1 + panel_w[1].shape[1] // width
-    args = [*pieces, *panel_w, ladder, *after]
+    args = [*arrays, *panel_w, ladder, *after]
     aliases = {}
     if out is not None:
         aliases = {len(args) + 1: 0}
@@ -159,7 +161,7 @@
     flops = 2 * rows * k_all * occupied * b_local + 2 * GROUP * b_local * count * count
     size = parts * k_all * width + count * count + rows * k_all + GROUP * b_local * count
     return pl.pallas_call(
-        functools.partial(chunk_kernel, parts=parts, occupied=occupied, b_local=b_local, q=q),
+        functools.partial(chunk_kernel, starts=starts, parts=parts, occupied=occupied, b_local=b_local, q=q),
         out_shape=jax.ShapeDtypeStruct((a_local, b_local, count), jnp.bfloat16),
         in_specs=[pl.BlockSpec(memory_space=pltpu.SMEM)] + [ANY] * len(args),
         out_specs=ANY,
@@ -226,45 +228,63 @@
         return [right[0], *right[1:], *left[1:]]
 
     def update(q, out, after):
-        return chunk_update(own, flat(pieces[q]), panel_w, ladder, out, after, q, a_local, b_local, occupied)
-
-    def hop(sides, s):
+        blocks = [piece if isinstance(piece, tuple) else (piece, 0) for piece in flat(pieces[q])]
+        return chunk_update(own, blocks, panel_w, ladder, out, after, q, a_local, b_local, occupied)
+
+    def hop(sides, s, direct=False):
         right, left = sides
-        right.append(lax.ppermute(right[-1], "col", [(c, c + 1) for c in range(s - 1, cols - 1)]))
-        left.append(lax.ppermute(left[-1], "col", [(c + 1, c) for c in range(cols - s)]))
-
-    pieces, out = [], None
-    for q in range(0, chunks, 2):
-        both = [blocks[:, p].reshape(occupied * GROUP, depth) for p in range(q, min(q + 2, chunks))]
+        first = 0 if direct else s - 1
+        step = s if direct else 1
+        source = 0 if direct else -1
+        right.append(lax.ppermute(right[source], "col", [(c, c + step) for c in range(first, cols - step)]))
+        left.append(lax.ppermute(left[source], "col", [(c + step, c) for c in range(cols - step - first)]))
+
+    pieces = []
+    for q in range(chunks):
+        held = blocks[:, q].reshape(occupied * GROUP, depth)
+        pieces.append(([held], [held]))
+
+    if plain:
+        for sides in pieces:
+            for s in range(1, cols):
+                hop(sides, s)
+        return jnp.concatenate(
+            [plain_update(own, flat(sides), panel_w, ladder, b_local, occupied) for sides in pieces], axis=0)
+
+    def after(done, sides):
+        right, left = sides
+        done, right[0], left[0] = lax.optimization_barrier((done, right[0], left[0]))
+        return done
+
+    *early, x, y = pieces
+    for q in range(0, len(early), 2):
         if q:
-            middle = (cols - 1) // 2
-            for n, (right, left) in enumerate(pieces[-2:][:len(both)]):
-                both[n], right[middle + 1], left[middle + 1] = lax.optimization_barrier(
-                    (both[n], right[middle + 1], left[middle + 1]))
-        pair = [([held], [held]) for held in both]
-        pieces += pair
-        if plain or q + 2 < chunks:
-            for s in range(1, cols):
-                for sides in pair:
-                    hop(sides, s)
-            continue
-        x, y = pair
-        hop(x, 1)
+            for before, sides in zip(early[q - 2:q], early[q:q + 2]):
+                before[0][-2], before[1][-2] = after((before[0][-2], before[1][-2]), sides)
         for s in range(1, cols):
-            if s == cols - 2:
-                out = update(0, None, (x[0][s - 1], x[1][s - 1]))
-                out, x[0][-1], x[1][-1], y[0][-1], y[1][-1] = lax.optimization_barrier(
-                    (out, x[0][-1], x[1][-1], y[0][-1], y[1][-1]))
-            if s == cols - 1:
-                out = update(1, out, ())
-                out, y[0][-1], y[1][-1] = lax.optimization_barrier((out, y[0][-1], y[1][-1]))
-            hop(y, s)
-            if s < cols - 1:
-                hop(x, s + 1)
-
-    if plain:
-        return jnp.concatenate(
-            [plain_update(own, flat(got), panel_w, ladder, b_local, occupied) for got in pieces], axis=0)
+            for sides in early[q:q + 2]:
+                hop(sides, s)
+    before = early[-2]
+    before[0][-2], before[1][-2] = after((before[0][-2], before[1][-2]), x)
+    for s in range(1, cols - 1):
+        hop(x, s)
+    far = (jnp.concatenate([x[0][0], y[0][0]]),) * 2
+    far = ([far[0]], [far[1]])
+    size = x[0][0].shape[0]
+    out = update(0, None, (x[0][1], x[1][1]))
+    moving = (early[-1][0], early[-1][1], x[0], x[1])
+    out, *ends = after((out, *[side[-1] for side in moving]), far)
+    for side, end in zip(moving, ends):
+        side[-1] = end
+    hop(far, cols - 1, direct=True)
+    for n in (0, 1):
+        x[n].append((far[n][1], 0))
+    out = update(1, out, ())
+    out = after(out, y)
+    for s in range(1, cols - 1):
+        hop(y, s, direct=True)
+    for n in (0, 1):
+        y[n].append((far[n][1], size))
     for q in range(2, chunks):
         out = update(q, out, ())
     return out

time: 374 us -> 257 us (0.69)
  the two profiles are of different devices: /device:TPU:0 before, /device:TPU:19 now
where the time goes in v7:
time: 257 us; the launch traced here: 256 us
  waiting for transfers between devices  80.8 us (31%)
  Pallas kernels  79.3 us (31%)
  starting transfers between devices  78.6 us (31%)
  between operations  13.8 us (5%)
    pallas_call x4, Pallas kernels, chunk_update(): pl.pallas_call(functools.partial(chunk_kernel, starts=starts, parts=parts...  75 us
    ppermute x11, starting transfers between devices, hop(): lax.ppermute(left[source], 'col', [(c + step, c) for c in range(cols - st...  46.3 us
    ppermute x3, waiting for transfers between devices, local(): lax.ppermute(arrived[s], 'col', [(c, (c + s) % cols) for c in range(cols)])  44.2 us
    ppermute x11, waiting for transfers between devices, hop(): lax.ppermute(left[source], 'col', [(c + step, c) for c in range(cols - st...  25.8 us
    ppermute x11, starting transfers between devices, hop(): lax.ppermute(right[source], 'col', [(c, c + step) for c in range(first, c...  25.2 us
    ppermute x11, waiting for transfers between devices, hop(): lax.ppermute(right[source], 'col', [(c, c + step) for c in range(first, c...  10.8 us
  transfers between devices with their start and end apart: 28, of which 13 were waited for; matrix products, arithmetic and copies ran while one was open for 1% of the time, Pallas kernels for 22%

profile of v7, /device:TPU:19, one launch (start us, length us, event | category | flops | bytes accessed | tf_op | source)
XLA Modules:
  0.0 256.1 jit_solution(10405414007704036408)
XLA Ops:
  6.5 4.3 %shard_map.37 = (bf16[8,4,4,16,512]{4,3,2,1,0:T(8,128)(2,1)}, bf16[256,1024]{1,0:T(8,128)(2,1)}, bf16[256,1024]{1,0:T(8,128)(2,1)}, bf16[256,1024]{1,0:T(8,128)(2,1)}, bf16[256,1024]{1,0:T(8,128)(2,1)}) custom-call(s32[1]{0:T(128)} %bitcast.own, bf16[4,8,4,16,512]{4,3,2,1,0:T(8,128)(2,1)} %bitcast.19, bf16[256,4096]{1,0:T(8,128)(2,1)} %w_ref.1), custom_call_target="tpu_custom_call" | custom-call | bytes 8388608 | tf_op jit(solution)/shard_map/pallas_call | solution.py:46
  10.8 0.0 all-gather.3.cloned.1.call-update
  10.9 4.6 %all-to-all-start = ((bf16[8,4,4,16,512]{4,3,2,1,0:T(8,128)(2,1)}), bf16[8,4,4,16,512]{4,3,2,1,0:T(8,128)(2,1)S(1)}, u32[]{:S(2)}, u32[]{:S(2)}) async-start(bf16[8,4,4,16,512]{4,3,2,1,0:T(8,128)(2,1)} %get-tuple-element.27), calls=%async_computation | async-start | bytes 4194304 | tf_op jit(solution)/shard_map/all_to_all | solution.py:215
  15.5 1.3 collective-permute-start.8
  16.8 0.1 collective-permute-start.9
  16.8 1.2 collective-permute-start.10
  18.0 11.0 %collective-permute-done.8 = bf16[256,1024]{1,0:T(8,128)(2,1)S(1)} collective-permute-done((bf16[256,1024]{1,0:T(8,128)(2,1)}, bf16[256,1024]{1,0:T(8,128)(2,1)S(1)}, u32[]{:S(2)}, u32[]{:S(2)}) %collective-permute-start.8) | collective-permute-done | bytes 524320 | tf_op jit(solution)/shard_map/ppermute | solution.py:214
  29.0 21.9 %collective-permute-done.9 = bf16[256,1024]{1,0:T(8,128)(2,1)S(1)} collective-permute-done((bf16[256,1024]{1,0:T(8,128)(2,1)}, bf16[256,1024]{1,0:T(8,128)(2,1)S(1)}, u32[]{:S(2)}, u32[]{:S(2)}) %collective-permute-start.9) | collective-permute-done | bytes 524320 | tf_op jit(solution)/shard_map/ppermute | solution.py:214
  50.9 11.2 %collective-permute-done.10 = bf16[256,1024]{1,0:T(8,128)(2,1)} collective-permute-done((bf16[256,1024]{1,0:T(8,128)(2,1)}, bf16[256,1024]{1,0:T(8,128)(2,1)}, u32[]{:S(2)}, u32[]{:S(2)}) %collective-permute-start.10) | collective-permute-done | bytes 524320 | tf_op jit(solution)/shard_map/ppermute | solution.py:214
  62.2 0.0 all-to-all-done
  62.2 2.3 pad_maximum_fusion
  64.5 0.0 all-gather.5.cloned.1.call-update
  64.5 0.2 fusion
  64.8 4.1 %collective-permute-start.4 = (bf16[512,512]{1,0:T(8,128)(2,1)S(1)}, bf16[512,512]{1,0:T(8,128)(2,1)S(1)}, u32[]{:S(2)}, u32[]{:S(2)}) collective-permute-start(bf16[512,512]{1,0:T(8,128)(2,1)S(1)} %bitcast.20), channel_id=1, source_target_pairs={{1,0},{2,1},{3,2},{5,4},{6,5},{7,6},{9,8},{10,9},{11,10},{13,12},{... | collective-permute-start | bytes 1572872 | tf_op jit(solution)/shard_map/ppermute | solution.py:240
  68.9 1.9 collective-permute-start.2
  70.8 3.4 %collective-permute-start.14 = (bf16[512,512]{1,0:T(8,128)(2,1)S(1)}, bf16[512,512]{1,0:T(8,128)(2,1)S(1)}, u32[]{:S(2)}, u32[]{:S(2)}) collective-permute-start(bf16[512,512]{1,0:T(8,128)(2,1)S(1)} %bitcast.16), channel_id=1, source_target_pairs={{1,0},{2,1},{3,2},{5,4},{6,5},{7,6},{9,8},{10,9},{11,10},{13,12},{... | collective-permute-start | bytes 1572872 | tf_op jit(solution)/shard_map/ppermute | solution.py:240
  74.2 1.9 collective-permute-start
  76.1 3.6 %collective-permute-done.4.refs_4_ = bf16[512,512]{1,0:T(8,128)(2,1)S(1)} collective-permute-done((bf16[512,512]{1,0:T(8,128)(2,1)S(1)}, bf16[512,512]{1,0:T(8,128)(2,1)S(1)}, u32[]{:S(2)}, u32[]{:S(2)}) %collective-permute-start.4) | collective-permute-done | bytes 524320 | tf_op jit(solution)/shard_map/ppermute | solution.py:240
  79.8 4.1 %collective-permute-start.5 = (bf16[512,512]{1,0:T(8,128)(2,1)S(1)}, bf16[512,512]{1,0:T(8,128)(2,1)S(1)}, u32[]{:S(2)}, u32[]{:S(2)}) collective-permute-start(bf16[512,512]{1,0:T(8,128)(2,1)S(1)} %collective-permute-done.4.refs_4_), channel_id=1, source_target_pairs={{1,0},{2,1},{5,4},{6,5},{9,8},{10,9},{13,12},{14,13},{17,16},{18,1... | collective-permute-start | bytes 1572872 | tf_op jit(solution)/shard_map/ppermute | solution.py:240
  83.9 0.0 collective-permute-done.2.refs_1_
  83.9 1.9 collective-permute-start.3
  85.8 5.2 %collective-permute-done.14.refs_4_ = bf16[512,512]{1,0:T(8,128)(2,1)S(1)} collective-permute-done((bf16[512,512]{1,0:T(8,128)(2,1)S(1)}, bf16[512,512]{1,0:T(8,128)(2,1)S(1)}, u32[]{:S(2)}, u32[]{:S(2)}) %collective-permute-start.14) | collective-permute-done | bytes 524320 | tf_op jit(solution)/shard_map/ppermute | solution.py:240
  91.0 4.9 %collective-permute-start.15 = (bf16[512,512]{1,0:T(8,128)(2,1)S(1)}, bf16[512,512]{1,0:T(8,128)(2,1)}, u32[]{:S(2)}, u32[]{:S(2)}) collective-permute-start(bf16[512,512]{1,0:T(8,128)(2,1)S(1)} %collective-permute-done.14.refs_4_), channel_id=1, source_target_pairs={{1,0},{2,1},{5,4},{6,5},{9,8},{10,9},{13,12},{14,13},{17,16},{18,1... | collective-permute-start | bytes 1572872 | tf_op jit(solution)/shard_map/ppermute | solution.py:240
  95.9 0.0 collective-permute-done.refs_1_
  95.9 1.9 collective-permute-start.1
  97.8 4.3 %collective-permute-done.5.refs_5_ = bf16[512,512]{1,0:T(8,128)(2,1)S(1)} collective-permute-done((bf16[512,512]{1,0:T(8,128)(2,1)S(1)}, bf16[512,512]{1,0:T(8,128)(2,1)S(1)}, u32[]{:S(2)}, u32[]{:S(2)}) %collective-permute-start.5) | collective-permute-done | bytes 524320 | tf_op jit(solution)/shard_map/ppermute | solution.py:240
  102.1 3.9 %collective-permute-done.3.refs_2_ = bf16[512,512]{1,0:T(8,128)(2,1)S(1)} collective-permute-done((bf16[512,512]{1,0:T(8,128)(2,1)S(1)}, bf16[512,512]{1,0:T(8,128)(2,1)S(1)}, u32[]{:S(2)}, u32[]{:S(2)}) %collective-permute-start.3) | collective-permute-done | bytes 524320 | tf_op jit(solution)/shard_map/ppermute | solution.py:239
  106.0 0.7 collective-permute-start.7
  106.7 1.9 collective-permute-start.12
  108.6 4.1 %collective-permute-start.11 = (bf16[512,512]{1,0:T(8,128)(2,1)S(1)}, bf16[512,512]{1,0:T(8,128)(2,1)}, u32[]{:S(2)}, u32[]{:S(2)}) collective-permute-start(bf16[512,512]{1,0:T(8,128)(2,1)S(1)} %bitcast.13), channel_id=1, source_target_pairs={{0,1},{1,2},{2,3},{4,5},{5,6},{6,7},{8,9},{9,10},{10,11},{12,13},{... | collective-permute-start | bytes 1572872 | tf_op jit(solution)/shard_map/ppermute | solution.py:239
  112.8 0.6 collective-permute-done.15.refs_5_
  113.4 2.1 collective-permute-start.6
  115.4 0.1 pad_maximum_fusion.1
  115.5 1.7 collective-permute-done.1.refs_2_
  117.3 1.4 collective-permute-start.16
  118.7 0.0 collective-permute-done.7.refs_6_
  118.7 3.1 %collective-permute-start.13 = (bf16[512,512]{1,0:T(8,128)(2,1)}, bf16[512,512]{1,0:T(8,128)(2,1)}, u32[]{:S(2)}, u32[]{:S(2)}) collective-permute-start(bf16[512,512]{1,0:T(8,128)(2,1)} %collective-permute-done.1.refs_2_), channel_id=1, source_target_pairs={{2,3},{6,7},{10,11},{14,15},{18,19},{22,23},{26,27},{30,31}} | collective-permute-start | bytes 1572872 | tf_op jit(solution)/shard_map/ppermute | solution.py:239
  121.8 2.8 %collective-permute-done.12.refs_11_.refs_4_ = bf16[512,512]{1,0:T(8,128)(2,1)} collective-permute-done((bf16[512,512]{1,0:T(8,128)(2,1)S(1)}, bf16[512,512]{1,0:T(8,128)(2,1)}, u32[]{:S(2)}, u32[]{:S(2)}) %collective-permute-start.12) | collective-permute-done | bytes 524320 | tf_op jit(solution)/shard_map/ppermute | solution.py:240
  124.6 14.3 %collective-permute-start.18 = (bf16[512,512]{1,0:T(8,128)(2,1)}, bf16[512,512]{1,0:T(8,128)(2,1)}, u32[]{:S(2)}, u32[]{:S(2)}) collective-permute-start(bf16[512,512]{1,0:T(8,128)(2,1)} %collective-permute-done.12.refs_11_.refs_4_), channel_id=1, source_target_pairs={{1,0},{2,1},{5,4},{6,5},{9,8},{10,9},{13,12},{14,13},{17,16},{18,1... | collective-permute-start | bytes 1572872 | tf_op jit(solution)/shard_map/ppermute | solution.py:240
  138.9 0.0 collective-permute-done.11.refs_10_.refs_1_
  138.9 1.9 collective-permute-start.17
  140.9 0.0 collective-permute-done.6.refs_3_
  140.9 0.0 all-gather.3.cloned.1.call-done.refs_7_
  140.9 0.0 all-gather.5.cloned.1.call-done.refs_8_
  140.9 18.8 %shard_map.38.refs_10_ = bf16[64,128,1024]{2,1,0:T(8,128)(2,1)} custom-call(s32[1]{0:T(128)} %bitcast.own, bf16[512,512]{1,0:T(8,128)(2,1)} %bitcast.22, bf16[512,512]{1,0:T(8,128)(2,1)} %copy-done.9, bf16[512,512]{1,0:T(8,128)(2,1)} %copy-done.11, bf16[512,512]{1,0:T(8,128)(2,1)} %collective-permute-done.6.refs_3_, bf16[512,512]{1,0:T(8,128)(2,1)} %copy-done.8, ...), custom_call_target="tpu_custom_call" | custom-call | flops 12884901888 | bytes 25165824 | tf_op jit(solution)/shard_map/pallas_call | solution.py:163
  159.7 0.0 collective-permute-done.16.refs_6_
  159.7 0.0 collective-permute-done.13.refs_3_
  159.7 0.0 collective-permute-done.18.refs_5_
  159.7 0.6 collective-permute-done.17.refs_2_
  160.3 0.7 collective-permute-start.21
  161.1 0.7 collective-permute-start.24
  161.8 18.8 %shard_map.39.refs_10_ = bf16[64,128,1024]{2,1,0:T(8,128)(2,1)} custom-call(s32[1]{0:T(128)} %bitcast.own, bf16[512,512]{1,0:T(8,128)(2,1)} %bitcast.18, bf16[512,512]{1,0:T(8,128)(2,1)} %copy-done.6, bf16[512,512]{1,0:T(8,128)(2,1)} %collective-permute-done.1.refs_2_, ...), custom_call_target="tpu_custom_call", output_to_operand_aliasing={{}: (11, {})} | custom-call | flops 12884901888 | bytes 25165824 | tf_op jit(solution)/shard_map/pallas_call | solution.py:163
  180.6 8.8 %collective-permute-start.23 = (bf16[512,512]{1,0:T(8,128)(2,1)S(1)}, bf16[512,512]{1,0:T(8,128)(2,1)}, u32[]{:S(2)}, u32[]{:S(2)}) collective-permute-start(bf16[512,512]{1,0:T(8,128)(2,1)S(1)} %bitcast.7), channel_id=1, source_target_pairs={{2,0},{3,1},{6,4},{7,5},{10,8},{11,9},{14,12},{15,13},{18,16},{19,... | collective-permute-start | bytes 1572872 | tf_op jit(solution)/shard_map/ppermute | solution.py:240
  189.3 1.9 collective-permute-start.22
  191.3 1.3 collective-permute-start.20
  192.6 0.0 collective-permute-done.21.refs_3_
  192.6 4.3 %collective-permute-start.19 = (bf16[512,512]{1,0:T(8,128)(2,1)S(1)}, bf16[512,512]{1,0:T(8,128)(2,1)}, u32[]{:S(2)}, u32[]{:S(2)}) collective-permute-start(bf16[512,512]{1,0:T(8,128)(2,1)S(1)} %bitcast.10), channel_id=1, source_target_pairs={{0,1},{1,2},{2,3},{4,5},{5,6},{6,7},{8,9},{9,10},{10,11},{12,13},{... | collective-permute-start | bytes 1572872 | tf_op jit(solution)/shard_map/ppermute | solution.py:239
  196.9 0.0 collective-permute-done.24.refs_6_
  197.0 1.0 copy-done.3
  197.9 18.7 %shard_map.40.refs_10_ = bf16[64,128,1024]{2,1,0:T(8,128)(2,1)} custom-call(s32[1]{0:T(128)} %bitcast.own, bf16[512,512]{1,0:T(8,128)(2,1)} %bitcast.15, bf16[512,512]{1,0:T(8,128)(2,1)} %collective-permute-done.11.refs_10_.refs_1_, bf16[512,512]{1,0:T(8,128)(2,1)} %collective-permute-done.17.refs_2_, ...), custom_call_target="tpu_custom_call", output_to_operand_aliasing={{}: (11, {})} | custom-call | flops 12884901888 | bytes 25165824 | tf_op jit(solution)/shard_map/pallas_call | solution.py:163
  216.7 9.3 %collective-permute-done.22.refs_4_ = bf16[512,512]{1,0:T(8,128)(2,1)} collective-permute-done((bf16[512,512]{1,0:T(8,128)(2,1)S(1)}, bf16[512,512]{1,0:T(8,128)(2,1)}, u32[]{:S(2)}, u32[]{:S(2)}) %collective-permute-start.22) | collective-permute-done | bytes 524320 | tf_op jit(solution)/shard_map/ppermute | solution.py:240
  226.0 0.0 collective-permute-done.20.refs_2_
  226.0 4.6 %collective-permute-done.19.refs_1_ = bf16[512,512]{1,0:T(8,128)(2,1)} collective-permute-done((bf16[512,512]{1,0:T(8,128)(2,1)S(1)}, bf16[512,512]{1,0:T(8,128)(2,1)}, u32[]{:S(2)}, u32[]{:S(2)}) %collective-permute-start.19) | collective-permute-done | bytes 524320 | tf_op jit(solution)/shard_map/ppermute | solution.py:239
  230.5 18.7 %shard_map.41 = bf16[64,128,1024]{2,1,0:T(8,128)(2,1)} custom-call(s32[1]{0:T(128)} %bitcast.own, bf16[512,512]{1,0:T(8,128)(2,1)} %bitcast.11, bf16[512,512]{1,0:T(8,128)(2,1)} %collective-permute-done.19.refs_1_, bf16[512,512]{1,0:T(8,128)(2,1)} %collective-permute-done.20.refs_2_, bf16[1024,512]{1,0:T(8,128)(2,1)} %copy-done.2, ...), custom_call_target="tpu_custom_call", output_to_operand_aliasing={{}: (11, {})} | custom-call | flops 12884901888 | bytes 25165824 | tf_op jit(solution)/shard_map/pallas_call | solution.py:163
  (28 shorter events, 0.1 us)
Async XLA Ops:
  6.5 134.3 %all-gather.3.cloned.1.call-start = ((), (), s32[]{:S(2)}) async-start(), calls=%async_computation.1 | async-start | bytes 4718592 | tf_op jit(solution)/shard_map/all_gather | solution.py:219
  10.9 51.3 %all-to-all-start = ((bf16[8,4,4,16,512]{4,3,2,1,0:T(8,128)(2,1)}), bf16[8,4,4,16,512]{4,3,2,1,0:T(8,128)(2,1)S(1)}, u32[]{:S(2)}, u32[]{:S(2)}) async-start(bf16[8,4,4,16,512]{4,3,2,1,0:T(8,128)(2,1)} %get-tuple-element.27), calls=%async_computation | async-start | bytes 4194304 | tf_op jit(solution)/shard_map/all_to_all | solution.py:215
  15.5 125.5 %all-gather.5.cloned.1.call-start = ((), (), s32[]{:S(2)}) async-start(), calls=%async_computation.2 | async-start | bytes 14155776 | tf_op jit(solution)/shard_map/all_gather | solution.py:219
  15.5 13.6 %collective-permute-start.8 = (bf16[256,1024]{1,0:T(8,128)(2,1)}, bf16[256,1024]{1,0:T(8,128)(2,1)S(1)}, u32[]{:S(2)}, u32[]{:S(2)}) collective-permute-start(bf16[256,1024]{1,0:T(8,128)(2,1)} %get-tuple-element.31), channel_id=1, source_target_pairs={{0,1},{1,2},{2,3},{3,0},{4,5},{5,6},{6,7},{7,4},{8,9},{9,10},{10,1... | collective-permute-start | bytes 1572872 | tf_op jit(solution)/shard_map/ppermute | solution.py:214
  16.8 34.2 %collective-permute-start.9 = (bf16[256,1024]{1,0:T(8,128)(2,1)}, bf16[256,1024]{1,0:T(8,128)(2,1)S(1)}, u32[]{:S(2)}, u32[]{:S(2)}) collective-permute-start(bf16[256,1024]{1,0:T(8,128)(2,1)} %get-tuple-element.32), channel_id=1, source_target_pairs={{0,2},{1,3},{2,0},{3,1},{4,6},{5,7},{6,4},{7,5},{8,10},{9,11},{10,... | collective-permute-start | bytes 1572872 | tf_op jit(solution)/shard_map/ppermute | solution.py:214
  16.8 45.4 %collective-permute-start.10 = (bf16[256,1024]{1,0:T(8,128)(2,1)}, bf16[256,1024]{1,0:T(8,128)(2,1)}, u32[]{:S(2)}, u32[]{:S(2)}) collective-permute-start(bf16[256,1024]{1,0:T(8,128)(2,1)} %get-tuple-element.33), channel_id=1, source_target_pairs={{0,3},{1,0},{2,1},{3,2},{4,7},{5,4},{6,5},{7,6},{8,11},{9,8},{10,9... | collective-permute-start | bytes 1572872 | tf_op jit(solution)/shard_map/ppermute | solution.py:214
  64.7 74.2 %copy-start.4 = (bf16[8,1,4,16,512]{4,3,2,1,0:T(8,128)(2,1)}, bf16[8,1,4,16,512]{4,3,2,1,0:T(8,128)(2,1)S(1)}, u32[]{:S(2)}) copy-start(bf16[8,1,4,16,512]{4,3,2,1,0:T(8,128)(2,1)S(1)} %get-tuple-element.52) | copy-start | bytes 1572868
  64.7 76.1 %copy-start.7 = (bf16[8,1,4,16,512]{4,3,2,1,0:T(8,128)(2,1)}, bf16[8,1,4,16,512]{4,3,2,1,0:T(8,128)(2,1)S(1)}, u32[]{:S(2)}) copy-start(bf16[8,1,4,16,512]{4,3,2,1,0:T(8,128)(2,1)S(1)} %get-tuple-element.51) | copy-start | bytes 1572868
  64.7 94.9 %copy-start.1 = (bf16[8,1,4,16,512]{4,3,2,1,0:T(8,128)(2,1)}, bf16[8,1,4,16,512]{4,3,2,1,0:T(8,128)(2,1)S(1)}, u32[]{:S(2)}) copy-start(bf16[8,1,4,16,512]{4,3,2,1,0:T(8,128)(2,1)S(1)} %get-tuple-element.50) | copy-start | bytes 1572868
  64.7 127.8 %copy-start = (bf16[8,1,4,16,512]{4,3,2,1,0:T(8,128)(2,1)}, bf16[8,1,4,16,512]{4,3,2,1,0:T(8,128)(2,1)S(1)}, u32[]{:S(2)}) copy-start(bf16[8,1,4,16,512]{4,3,2,1,0:T(8,128)(2,1)S(1)} %get-tuple-element.49) | copy-start | bytes 1572868
  64.8 15.0 %collective-permute-start.4 = (bf16[512,512]{1,0:T(8,128)(2,1)S(1)}, bf16[512,512]{1,0:T(8,128)(2,1)S(1)}, u32[]{:S(2)}, u32[]{:S(2)}) collective-permute-start(bf16[512,512]{1,0:T(8,128)(2,1)S(1)} %bitcast.20), channel_id=1, source_target_pairs={{1,0},{2,1},{3,2},{5,4},{6,5},{7,6},{9,8},{10,9},{11,10},{13,12},{... | collective-permute-start | bytes 1572872 | tf_op jit(solution)/shard_map/ppermute | solution.py:240
  68.9 15.0 %collective-permute-start.2 = (bf16[512,512]{1,0:T(8,128)(2,1)S(1)}, bf16[512,512]{1,0:T(8,128)(2,1)S(1)}, u32[]{:S(2)}, u32[]{:S(2)}) collective-permute-start(bf16[512,512]{1,0:T(8,128)(2,1)S(1)} %bitcast.21), channel_id=1, source_target_pairs={{0,1},{1,2},{2,3},{4,5},{5,6},{6,7},{8,9},{9,10},{10,11},{12,13},{... | collective-permute-start | bytes 1572872 | tf_op jit(solution)/shard_map/ppermute | solution.py:239
  70.8 20.2 %collective-permute-start.14 = (bf16[512,512]{1,0:T(8,128)(2,1)S(1)}, bf16[512,512]{1,0:T(8,128)(2,1)S(1)}, u32[]{:S(2)}, u32[]{:S(2)}) collective-permute-start(bf16[512,512]{1,0:T(8,128)(2,1)S(1)} %bitcast.16), channel_id=1, source_target_pairs={{1,0},{2,1},{3,2},{5,4},{6,5},{7,6},{9,8},{10,9},{11,10},{13,12},{... | collective-permute-start | bytes 1572872 | tf_op jit(solution)/shard_map/ppermute | solution.py:240
  74.2 21.7 %collective-permute-start = (bf16[512,512]{1,0:T(8,128)(2,1)S(1)}, bf16[512,512]{1,0:T(8,128)(2,1)S(1)}, u32[]{:S(2)}, u32[]{:S(2)}) collective-permute-start(bf16[512,512]{1,0:T(8,128)(2,1)S(1)} %bitcast.17), channel_id=1, source_target_pairs={{0,1},{1,2},{2,3},{4,5},{5,6},{6,7},{8,9},{9,10},{10,11},{12,13},{... | collective-permute-start | bytes 1572872 | tf_op jit(solution)/shard_map/ppermute | solution.py:239
  79.8 35.7 %copy-start.8 = (bf16[512,512]{1,0:T(8,128)(2,1)}, bf16[512,512]{1,0:T(8,128)(2,1)S(1)}, u32[]{:S(2)}) copy-start(bf16[512,512]{1,0:T(8,128)(2,1)S(1)} %collective-permute-done.4.refs_4_) | copy-start | bytes 1572868
  79.8 22.4 %collective-permute-start.5 = (bf16[512,512]{1,0:T(8,128)(2,1)S(1)}, bf16[512,512]{1,0:T(8,128)(2,1)S(1)}, u32[]{:S(2)}, u32[]{:S(2)}) collective-permute-start(bf16[512,512]{1,0:T(8,128)(2,1)S(1)} %collective-permute-done.4.refs_4_), channel_id=1, source_target_pairs={{1,0},{2,1},{5,4},{6,5},{9,8},{10,9},{13,12},{14,13},{17,16},{18,1... | collective-permute-start | bytes 1572872 | tf_op jit(solution)/shard_map/ppermute | solution.py:240
  83.9 31.5 %copy-start.9 = (bf16[512,512]{1,0:T(8,128)(2,1)}, bf16[512,512]{1,0:T(8,128)(2,1)S(1)}, u32[]{:S(2)}) copy-start(bf16[512,512]{1,0:T(8,128)(2,1)S(1)} %collective-permute-done.2.refs_1_) | copy-start | bytes 1572868
  83.9 22.1 %collective-permute-start.3 = (bf16[512,512]{1,0:T(8,128)(2,1)S(1)}, bf16[512,512]{1,0:T(8,128)(2,1)S(1)}, u32[]{:S(2)}, u32[]{:S(2)}) collective-permute-start(bf16[512,512]{1,0:T(8,128)(2,1)S(1)} %collective-permute-done.2.refs_1_), channel_id=1, source_target_pairs={{1,2},{2,3},{5,6},{6,7},{9,10},{10,11},{13,14},{14,15},{17,18},{18... | collective-permute-start | bytes 1572872 | tf_op jit(solution)/shard_map/ppermute | solution.py:239
  91.0 24.5 %copy-start.5 = (bf16[512,512]{1,0:T(8,128)(2,1)}, bf16[512,512]{1,0:T(8,128)(2,1)S(1)}, u32[]{:S(2)}) copy-start(bf16[512,512]{1,0:T(8,128)(2,1)S(1)} %collective-permute-done.14.refs_4_) | copy-start | bytes 1572868
  91.0 22.4 %collective-permute-start.15 = (bf16[512,512]{1,0:T(8,128)(2,1)S(1)}, bf16[512,512]{1,0:T(8,128)(2,1)}, u32[]{:S(2)}, u32[]{:S(2)}) collective-permute-start(bf16[512,512]{1,0:T(8,128)(2,1)S(1)} %collective-permute-done.14.refs_4_), channel_id=1, source_target_pairs={{1,0},{2,1},{5,4},{6,5},{9,8},{10,9},{13,12},{14,13},{17,16},{18,1... | collective-permute-start | bytes 1572872 | tf_op jit(solution)/shard_map/ppermute | solution.py:240
  95.9 63.8 %copy-start.6 = (bf16[512,512]{1,0:T(8,128)(2,1)}, bf16[512,512]{1,0:T(8,128)(2,1)S(1)}, u32[]{:S(2)}) copy-start(bf16[512,512]{1,0:T(8,128)(2,1)S(1)} %collective-permute-done.refs_1_) | copy-start | bytes 1572868
  95.9 21.3 %collective-permute-start.1 = (bf16[512,512]{1,0:T(8,128)(2,1)S(1)}, bf16[512,512]{1,0:T(8,128)(2,1)}, u32[]{:S(2)}, u32[]{:S(2)}) collective-permute-start(bf16[512,512]{1,0:T(8,128)(2,1)S(1)} %collective-permute-done.refs_1_), channel_id=1, source_target_pairs={{1,2},{2,3},{5,6},{6,7},{9,10},{10,11},{13,14},{14,15},{17,18},{18... | collective-permute-start | bytes 1572872 | tf_op jit(solution)/shard_map/ppermute | solution.py:239
  102.1 38.7 %copy-start.10 = (bf16[512,512]{1,0:T(8,128)(2,1)}, bf16[512,512]{1,0:T(8,128)(2,1)S(1)}, u32[]{:S(2)}) copy-start(bf16[512,512]{1,0:T(8,128)(2,1)S(1)} %collective-permute-done.5.refs_5_) | copy-start | bytes 1572868
  106.0 34.8 %copy-start.11 = (bf16[512,512]{1,0:T(8,128)(2,1)}, bf16[512,512]{1,0:T(8,128)(2,1)S(1)}, u32[]{:S(2)}) copy-start(bf16[512,512]{1,0:T(8,128)(2,1)S(1)} %collective-permute-done.3.refs_2_) | copy-start | bytes 1572868
  106.0 12.7 %collective-permute-start.7 = (bf16[512,512]{1,0:T(8,128)(2,1)S(1)}, bf16[512,512]{1,0:T(8,128)(2,1)S(1)}, u32[]{:S(2)}, u32[]{:S(2)}) collective-permute-start(bf16[512,512]{1,0:T(8,128)(2,1)S(1)} %collective-permute-done.5.refs_5_), channel_id=1, source_target_pairs={{1,0},{5,4},{9,8},{13,12},{17,16},{21,20},{25,24},{29,28}} | collective-permute-start | bytes 1572872 | tf_op jit(solution)/shard_map/ppermute | solution.py:240
  106.7 17.9 %collective-permute-start.12 = (bf16[512,512]{1,0:T(8,128)(2,1)S(1)}, bf16[512,512]{1,0:T(8,128)(2,1)}, u32[]{:S(2)}, u32[]{:S(2)}) collective-permute-start(bf16[512,512]{1,0:T(8,128)(2,1)S(1)} %bitcast.12), channel_id=1, source_target_pairs={{1,0},{2,1},{3,2},{5,4},{6,5},{7,6},{9,8},{10,9},{11,10},{13,12},{... | collective-permute-start | bytes 1572872 | tf_op jit(solution)/shard_map/ppermute | solution.py:240
  108.6 30.2 %collective-permute-start.11 = (bf16[512,512]{1,0:T(8,128)(2,1)S(1)}, bf16[512,512]{1,0:T(8,128)(2,1)}, u32[]{:S(2)}, u32[]{:S(2)}) collective-permute-start(bf16[512,512]{1,0:T(8,128)(2,1)S(1)} %bitcast.13), channel_id=1, source_target_pairs={{0,1},{1,2},{2,3},{4,5},{5,6},{6,7},{8,9},{9,10},{10,11},{12,13},{... | collective-permute-start | bytes 1572872 | tf_op jit(solution)/shard_map/ppermute | solution.py:239
  113.4 27.5 %collective-permute-start.6 = (bf16[512,512]{1,0:T(8,128)(2,1)S(1)}, bf16[512,512]{1,0:T(8,128)(2,1)}, u32[]{:S(2)}, u32[]{:S(2)}) collective-permute-start(bf16[512,512]{1,0:T(8,128)(2,1)S(1)} %collective-permute-done.3.refs_2_), channel_id=1, source_target_pairs={{2,3},{6,7},{10,11},{14,15},{18,19},{22,23},{26,27},{30,31}} | collective-permute-start | bytes 1572872 | tf_op jit(solution)/shard_map/ppermute | solution.py:239
  117.3 42.4 %collective-permute-start.16 = (bf16[512,512]{1,0:T(8,128)(2,1)}, bf16[512,512]{1,0:T(8,128)(2,1)}, u32[]{:S(2)}, u32[]{:S(2)}) collective-permute-start(bf16[512,512]{1,0:T(8,128)(2,1)} %collective-permute-done.15.refs_5_), channel_id=1, source_target_pairs={{1,0},{5,4},{9,8},{13,12},{17,16},{21,20},{25,24},{29,28}} | collective-permute-start | bytes 1572872 | tf_op jit(solution)/shard_map/ppermute | solution.py:240
  118.7 22.1 %copy-start.12 = (bf16[512,512]{1,0:T(8,128)(2,1)}, bf16[512,512]{1,0:T(8,128)(2,1)S(1)}, u32[]{:S(2)}) copy-start(bf16[512,512]{1,0:T(8,128)(2,1)S(1)} %collective-permute-done.7.refs_6_) | copy-start | bytes 1572868
  118.7 41.0 %collective-permute-start.13 = (bf16[512,512]{1,0:T(8,128)(2,1)}, bf16[512,512]{1,0:T(8,128)(2,1)}, u32[]{:S(2)}, u32[]{:S(2)}) collective-permute-start(bf16[512,512]{1,0:T(8,128)(2,1)} %collective-permute-done.1.refs_2_), channel_id=1, source_target_pairs={{2,3},{6,7},{10,11},{14,15},{18,19},{22,23},{26,27},{30,31}} | collective-permute-start | bytes 1572872 | tf_op jit(solution)/shard_map/ppermute | solution.py:239
  124.6 35.1 %collective-permute-start.18 = (bf16[512,512]{1,0:T(8,128)(2,1)}, bf16[512,512]{1,0:T(8,128)(2,1)}, u32[]{:S(2)}, u32[]{:S(2)}) collective-permute-start(bf16[512,512]{1,0:T(8,128)(2,1)} %collective-permute-done.12.refs_11_.refs_4_), channel_id=1, source_target_pairs={{1,0},{2,1},{5,4},{6,5},{9,8},{10,9},{13,12},{14,13},{17,16},{18,1... | collective-permute-start | bytes 1572872 | tf_op jit(solution)/shard_map/ppermute | solution.py:240
  138.9 21.4 %collective-permute-start.17 = (bf16[512,512]{1,0:T(8,128)(2,1)}, bf16[512,512]{1,0:T(8,128)(2,1)}, u32[]{:S(2)}, u32[]{:S(2)}) collective-permute-start(bf16[512,512]{1,0:T(8,128)(2,1)} %collective-permute-done.11.refs_10_.refs_1_), channel_id=1, source_target_pairs={{1,2},{2,3},{5,6},{6,7},{9,10},{10,11},{13,14},{14,15},{17,18},{18... | collective-permute-start | bytes 1572872 | tf_op jit(solution)/shard_map/ppermute | solution.py:239
  160.3 32.2 %collective-permute-start.21 = (bf16[1024,512]{1,0:T(8,128)(2,1)S(1)}, bf16[1024,512]{1,0:T(8,128)(2,1)S(1)}, u32[]{:S(2)}, u32[]{:S(2)}) collective-permute-start(bf16[1024,512]{1,0:T(8,128)(2,1)S(1)} %pad_maximum_fusion.1), channel_id=1, source_target_pairs={{0,3},{4,7},{8,11},{12,15},{16,19},{20,23},{24,27},{28,31}} | collective-permute-start | bytes 3145736 | tf_op jit(solution)/shard_map/ppermute | solution.py:239
  161.1 35.9 %collective-permute-start.24 = (bf16[1024,512]{1,0:T(8,128)(2,1)S(1)}, bf16[1024,512]{1,0:T(8,128)(2,1)S(1)}, u32[]{:S(2)}, u32[]{:S(2)}) collective-permute-start(bf16[1024,512]{1,0:T(8,128)(2,1)S(1)} %pad_maximum_fusion.1), channel_id=1, source_target_pairs={{3,0},{7,4},{11,8},{15,12},{19,16},{23,20},{27,24},{31,28}} | collective-permute-start | bytes 3145736 | tf_op jit(solution)/shard_map/ppermute | solution.py:240
  180.6 36.1 %collective-permute-start.23 = (bf16[512,512]{1,0:T(8,128)(2,1)S(1)}, bf16[512,512]{1,0:T(8,128)(2,1)}, u32[]{:S(2)}, u32[]{:S(2)}) collective-permute-start(bf16[512,512]{1,0:T(8,128)(2,1)S(1)} %bitcast.7), channel_id=1, source_target_pairs={{2,0},{3,1},{6,4},{7,5},{10,8},{11,9},{14,12},{15,13},{18,16},{19,... | collective-permute-start | bytes 1572872 | tf_op jit(solution)/shard_map/ppermute | solution.py:240
  189.3 36.6 %collective-permute-start.22 = (bf16[512,512]{1,0:T(8,128)(2,1)S(1)}, bf16[512,512]{1,0:T(8,128)(2,1)}, u32[]{:S(2)}, u32[]{:S(2)}) collective-permute-start(bf16[512,512]{1,0:T(8,128)(2,1)S(1)} %bitcast.8), channel_id=1, source_target_pairs={{1,0},{2,1},{3,2},{5,4},{6,5},{7,6},{9,8},{10,9},{11,10},{13,12},{... | collective-permute-start | bytes 1572872 | tf_op jit(solution)/shard_map/ppermute | solution.py:240
  191.3 34.7 %collective-permute-start.20 = (bf16[512,512]{1,0:T(8,128)(2,1)S(1)}, bf16[512,512]{1,0:T(8,128)(2,1)}, u32[]{:S(2)}, u32[]{:S(2)}) collective-permute-start(bf16[512,512]{1,0:T(8,128)(2,1)S(1)} %bitcast.9), channel_id=1, source_target_pairs={{0,2},{1,3},{4,6},{5,7},{8,10},{9,11},{12,14},{13,15},{16,18},{17,... | collective-permute-start | bytes 1572872 | tf_op jit(solution)/shard_map/ppermute | solution.py:239
  192.6 4.4 %copy-start.2 = (bf16[1024,512]{1,0:T(8,128)(2,1)}, bf16[1024,512]{1,0:T(8,128)(2,1)S(1)}, u32[]{:S(2)}) copy-start(bf16[1024,512]{1,0:T(8,128)(2,1)S(1)} %collective-permute-done.21.refs_3_) | copy-start | bytes 3145732
  192.6 37.9 %collective-permute-start.19 = (bf16[512,512]{1,0:T(8,128)(2,1)S(1)}, bf16[512,512]{1,0:T(8,128)(2,1)}, u32[]{:S(2)}, u32[]{:S(2)}) collective-permute-start(bf16[512,512]{1,0:T(8,128)(2,1)S(1)} %bitcast.10), channel_id=1, source_target_pairs={{0,1},{1,2},{2,3},{4,5},{5,6},{6,7},{8,9},{9,10},{10,11},{12,13},{... | collective-permute-start | bytes 1572872 | tf_op jit(solution)/shard_map/ppermute | solution.py:239
  196.9 1.0 copy-start.3
Sparse Core Ops, SparseCore 0:
  11.0 48.6 all-gather.2
  64.6 74.2 all-gather.4

commit v8 on v7

--- a/solution.py
+++ b/solution.py
@@ -55,12 +55,11 @@
     )(own.reshape(1), blocks, couplings)
 
 
-def chunk_kernel(own, *refs, starts, parts, occupied, b_local, q):
-    t_refs = [ref.at[pl.ds(start, GROUP * occupied)] for ref, start in zip(refs, starts)]
-    t_own, t_right, t_left = t_refs[0], t_refs[1:parts], t_refs[parts:]
-    w_own, w_rest, ladder_hbm = refs[2 * parts - 1:2 * parts + 2]
+def chunk_kernel(own, *refs, pieces, parts, occupied, b_local, q):
+    t_own, t_right, t_left = refs[0], refs[1:parts], refs[parts:pieces]
+    w_own, w_rest, ladder_hbm = refs[pieces:pieces + 3]
     out_ref, t_all, w_buf, ladder, pairs, out_buf, t_sem, w_sem, l_sem, out_sem = refs[-10:]
-    depth = t_own.shape[1]
+    depth = t_all.shape[1] // parts
     width = w_own.shape[1]
     count = occupied * occupied
     pitch = count + PAD
@@ -76,19 +75,25 @@
         return pltpu.make_async_copy(src, w_buf.at[slot], w_sem.at[slot])
 
     blocks = [lax.rem(own[0] - s + parts, parts) for s in range(parts)]
-    t_copy(t_own, blocks[0], 0).start()
-    for s in range(1, parts):
-        @pl.when(own[0] >= s)
-        def _():
-            t_copy(t_right[s - 1], blocks[s], s).start()
-
-        @pl.when(own[0] < s)
-        def _():
-            t_copy(t_left[parts - s - 1], blocks[s], s).start()
+    if pieces == 1:
+        pltpu.make_async_copy(t_own, t_all, t_sem.at[0]).start()
+    else:
+        t_copy(t_own, blocks[0], 0).start()
+        for s in range(1, parts):
+            @pl.when(own[0] >= s)
+            def _():
+                t_copy(t_right[s - 1], blocks[s], s).start()
+
+            @pl.when(own[0] < s)
+            def _():
+                t_copy(t_left[parts - s - 1], blocks[s], s).start()
     w_copy(0, 0).start()
     ladder_copy = pltpu.make_async_copy(ladder_hbm, ladder, l_sem)
-    for s in range(parts):
-        t_copy(t_own, blocks[s], s).wait()
+    if pieces == 1:
+        pltpu.make_async_copy(t_own, t_all, t_sem.at[0]).wait()
+    else:
+        for s in range(parts):
+            t_copy(t_own, blocks[s], s).wait()
 
     @pl.loop(0, parts)
     def _(step):
@@ -148,12 +153,11 @@
 
 
 def chunk_update(own, pieces, panel_w, ladder, out, after, q, a_local, b_local, occupied):
-    arrays, starts = zip(*pieces)
     rows = GROUP * occupied
     count = occupied * occupied
     k_all, width = panel_w[0].shape
     parts = 1 + panel_w[1].shape[1] // width
-    args = [*arrays, *panel_w, ladder, *after]
+    args = [*pieces, *panel_w, ladder, *after]
     aliases = {}
     if out is not None:
         aliases = {len(args) + 1: 0}
@@ -161,7 +165,7 @@
     flops = 2 * rows * k_all * occupied * b_local + 2 * GROUP * b_local * count * count
     size = parts * k_all * width + count * count + rows * k_all + GROUP * b_local * count
     return pl.pallas_call(
-        functools.partial(chunk_kernel, starts=starts, parts=parts, occupied=occupied, b_local=b_local, q=q),
+        functools.partial(chunk_kernel, pieces=len(pieces), parts=parts, occupied=occupied, b_local=b_local, q=q),
         out_shape=jax.ShapeDtypeStruct((a_local, b_local, count), jnp.bfloat16),
         in_specs=[pl.BlockSpec(memory_space=pltpu.SMEM)] + [ANY] * len(args),
         out_specs=ANY,
@@ -228,7 +232,7 @@
         return [right[0], *right[1:], *left[1:]]
 
     def update(q, out, after):
-        blocks = [piece if isinstance(piece, tuple) else (piece, 0) for piece in flat(pieces[q])]
+        blocks = [last] if q == chunks - 1 else flat(pieces[q])
         return chunk_update(own, blocks, panel_w, ladder, out, after, q, a_local, b_local, occupied)
 
     def hop(sides, s, direct=False):
@@ -264,29 +268,20 @@
         for s in range(1, cols):
             for sides in early[q:q + 2]:
                 hop(sides, s)
+    first = early[0]
+    first[0][1], first[1][1] = after((first[0][1], first[1][1]), y)
+    last = lax.all_gather(y[0][0], "col", axis=1, tiled=True)
+
     before = early[-2]
     before[0][-2], before[1][-2] = after((before[0][-2], before[1][-2]), x)
     for s in range(1, cols - 1):
         hop(x, s)
-    far = (jnp.concatenate([x[0][0], y[0][0]]),) * 2
-    far = ([far[0]], [far[1]])
-    size = x[0][0].shape[0]
-    out = update(0, None, (x[0][1], x[1][1]))
-    moving = (early[-1][0], early[-1][1], x[0], x[1])
-    out, *ends = after((out, *[side[-1] for side in moving]), far)
-    for side, end in zip(moving, ends):
-        side[-1] = end
-    hop(far, cols - 1, direct=True)
-    for n in (0, 1):
-        x[n].append((far[n][1], 0))
-    out = update(1, out, ())
-    out = after(out, y)
-    for s in range(1, cols - 1):
-        hop(y, s, direct=True)
-    for n in (0, 1):
-        y[n].append((far[n][1], size))
-    for q in range(2, chunks):
-        out = update(q, out, ())
+    for sides, n in ((early[-1], -2), (x, 1)):
+        sides[0][n], sides[1][n] = after((sides[0][n], sides[1][n]), x)
+    hop(x, cols - 1, direct=True)
+    out = None
+    for q in range(chunks):
+        out = update(q, out, () if q else (x[0][1], x[1][1]))
     return out
 
 

time: 257 us -> 257 us (level)
  the two profiles are of different devices: /device:TPU:19 before, /device:TPU:0 now
where the time goes in v8:
time: 257 us; the launch traced here: 256 us
  waiting for transfers between devices  107 us (42%)
  Pallas kernels  79.5 us (31%)
  starting transfers between devices  52.5 us (20%)
  between operations  13.4 us (5%)
    pallas_call x4, Pallas kernels, chunk_update(): pl.pallas_call(functools.partial(chunk_kernel, pieces=len(pieces), parts=...  75.3 us
    ppermute x9, waiting for transfers between devices, hop(): lax.ppermute(left[source], 'col', [(c + step, c) for c in range(cols - st...  63.4 us
    ppermute x3, waiting for transfers between devices, local(): lax.ppermute(arrived[s], 'col', [(c, (c + s) % cols) for c in range(cols)])  33.4 us
    ppermute x9, starting transfers between devices, hop(): lax.ppermute(right[source], 'col', [(c, c + step) for c in range(first, c...  29.9 us
    ppermute x9, starting transfers between devices, hop(): lax.ppermute(left[source], 'col', [(c + step, c) for c in range(cols - st...  11.8 us
    ppermute x9, waiting for transfers between devices, hop(): lax.ppermute(right[source], 'col', [(c, c + step) for c in range(first, c...  9.65 us
    ppermute x3, starting transfers between devices, local(): lax.ppermute(arrived[s], 'col', [(c, (c + s) % cols) for c in range(cols)])  5.54 us
    all_to_all x1, starting transfers between devices, local(): lax.all_to_all(blocks, 'row', split_axis=0, concat_axis=0, tiled=True)  5.21 us
  transfers between devices with their start and end apart: 25, of which 12 were waited for; matrix products, arithmetic and copies ran while one was open for 1% of the time, Pallas kernels for 22%

profile of v8, /device:TPU:0, one launch (start us, length us, event | category | flops | bytes accessed | tf_op | source)
XLA Modules:
  0.0 256.1 jit_solution(3185357555251744468)
XLA Ops:
  6.5 0.0 all-gather.6.cloned.1.call-start
  6.5 4.3 %shard_map.37 = (bf16[8,4,4,16,512]{4,3,2,1,0:T(8,128)(2,1)}, bf16[256,1024]{1,0:T(8,128)(2,1)}, bf16[256,1024]{1,0:T(8,128)(2,1)}, bf16[256,1024]{1,0:T(8,128)(2,1)}, bf16[256,1024]{1,0:T(8,128)(2,1)}) custom-call(s32[1]{0:T(128)} %bitcast.own, bf16[4,8,4,16,512]{4,3,2,1,0:T(8,128)(2,1)} %bitcast.14, bf16[256,4096]{1,0:T(8,128)(2,1)} %w_ref.1), custom_call_target="tpu_custom_call" | custom-call | bytes 8388608 | tf_op jit(solution)/shard_map/pallas_call | solution.py:46
  10.8 0.0 all-gather.6.cloned.1.call-update
  10.9 5.2 %all-to-all-start = ((bf16[8,4,4,16,512]{4,3,2,1,0:T(8,128)(2,1)}), bf16[8,4,4,16,512]{4,3,2,1,0:T(8,128)(2,1)S(1)}, u32[]{:S(2)}, u32[]{:S(2)}) async-start(bf16[8,4,4,16,512]{4,3,2,1,0:T(8,128)(2,1)} %get-tuple-element.28), calls=%async_computation | async-start | bytes 4194304 | tf_op jit(solution)/shard_map/all_to_all | solution.py:219
  16.1 0.0 all-gather.8.cloned.1.call-start
  16.1 1.6 collective-permute-start.2
  17.7 2.6 %collective-permute-start.3 = (bf16[256,1024]{1,0:T(8,128)(2,1)}, bf16[256,1024]{1,0:T(8,128)(2,1)S(1)}, u32[]{:S(2)}, u32[]{:S(2)}) collective-permute-start(bf16[256,1024]{1,0:T(8,128)(2,1)} %get-tuple-element.32), channel_id=1, source_target_pairs={{0,2},{1,3},{2,0},{3,1},{4,6},{5,7},{6,4},{7,5},{8,10},{9,11},{10,... | collective-permute-start | bytes 1572872 | tf_op jit(solution)/shard_map/ppermute | solution.py:218
  20.3 1.3 collective-permute-start.4
  21.7 11.4 %collective-permute-done.2 = bf16[256,1024]{1,0:T(8,128)(2,1)S(1)} collective-permute-done((bf16[256,1024]{1,0:T(8,128)(2,1)}, bf16[256,1024]{1,0:T(8,128)(2,1)S(1)}, u32[]{:S(2)}, u32[]{:S(2)}) %collective-permute-start.2) | collective-permute-done | bytes 524320 | tf_op jit(solution)/shard_map/ppermute | solution.py:218
  33.0 22.0 %collective-permute-done.3 = bf16[256,1024]{1,0:T(8,128)(2,1)S(1)} collective-permute-done((bf16[256,1024]{1,0:T(8,128)(2,1)}, bf16[256,1024]{1,0:T(8,128)(2,1)S(1)}, u32[]{:S(2)}, u32[]{:S(2)}) %collective-permute-start.3) | collective-permute-done | bytes 524320 | tf_op jit(solution)/shard_map/ppermute | solution.py:218
  55.0 0.0 collective-permute-done.4
  55.0 0.0 all-to-all-done
  55.0 2.3 pad_maximum_fusion
  57.3 0.0 all-gather.8.cloned.1.call-update
  57.3 0.0 all-gather.4.cloned.1.call-start
  57.4 1.0 fusion
  58.4 13.8 %collective-permute-start = (bf16[512,512]{1,0:T(8,128)(2,1)S(1)}, bf16[512,512]{1,0:T(8,128)(2,1)S(1)}, u32[]{:S(2)}, u32[]{:S(2)}) collective-permute-start(bf16[512,512]{1,0:T(8,128)(2,1)S(1)} %bitcast.16), channel_id=1, source_target_pairs={{0,1},{1,2},{2,3},{4,5},{5,6},{6,7},{8,9},{9,10},{10,11},{12,13},{... | collective-permute-start | bytes 1572872 | tf_op jit(solution)/shard_map/ppermute | solution.py:243
  72.2 1.3 collective-permute-start.1
  73.5 4.6 %collective-permute-start.9 = (bf16[512,512]{1,0:T(8,128)(2,1)S(1)}, bf16[512,512]{1,0:T(8,128)(2,1)S(1)}, u32[]{:S(2)}, u32[]{:S(2)}) collective-permute-start(bf16[512,512]{1,0:T(8,128)(2,1)S(1)} %bitcast.11), channel_id=1, source_target_pairs={{0,1},{1,2},{2,3},{4,5},{5,6},{6,7},{8,9},{9,10},{10,11},{12,13},{... | collective-permute-start | bytes 1572872 | tf_op jit(solution)/shard_map/ppermute | solution.py:243
  78.1 1.3 collective-permute-start.11
  79.4 5.1 %collective-permute-done.refs_1_ = bf16[512,512]{1,0:T(8,128)(2,1)S(1)} collective-permute-done((bf16[512,512]{1,0:T(8,128)(2,1)S(1)}, bf16[512,512]{1,0:T(8,128)(2,1)S(1)}, u32[]{:S(2)}, u32[]{:S(2)}) %collective-permute-start) | collective-permute-done | bytes 524320 | tf_op jit(solution)/shard_map/ppermute | solution.py:243
  84.5 1.5 collective-permute-start.5
  85.9 3.0 %collective-permute-done.1.refs_4_ = bf16[512,512]{1,0:T(8,128)(2,1)S(1)} collective-permute-done((bf16[512,512]{1,0:T(8,128)(2,1)S(1)}, bf16[512,512]{1,0:T(8,128)(2,1)S(1)}, u32[]{:S(2)}, u32[]{:S(2)}) %collective-permute-start.1) | collective-permute-done | bytes 524320 | tf_op jit(solution)/shard_map/ppermute | solution.py:244
  88.9 1.3 collective-permute-start.6
  90.2 4.6 %collective-permute-done.9.refs_1_ = bf16[512,512]{1,0:T(8,128)(2,1)S(1)} collective-permute-done((bf16[512,512]{1,0:T(8,128)(2,1)S(1)}, bf16[512,512]{1,0:T(8,128)(2,1)S(1)}, u32[]{:S(2)}, u32[]{:S(2)}) %collective-permute-start.9) | collective-permute-done | bytes 524320 | tf_op jit(solution)/shard_map/ppermute | solution.py:243
  94.8 0.7 collective-permute-start.10
  95.5 4.7 %collective-permute-done.11.refs_4_ = bf16[512,512]{1,0:T(8,128)(2,1)S(1)} collective-permute-done((bf16[512,512]{1,0:T(8,128)(2,1)S(1)}, bf16[512,512]{1,0:T(8,128)(2,1)S(1)}, u32[]{:S(2)}, u32[]{:S(2)}) %collective-permute-start.11) | collective-permute-done | bytes 524320 | tf_op jit(solution)/shard_map/ppermute | solution.py:244
  100.2 1.3 collective-permute-start.12
  101.4 0.0 collective-permute-done.5.refs_2_
  101.5 10.0 %collective-permute-done.6.refs_5_ = bf16[512,512]{1,0:T(8,128)(2,1)} collective-permute-done((bf16[512,512]{1,0:T(8,128)(2,1)S(1)}, bf16[512,512]{1,0:T(8,128)(2,1)}, u32[]{:S(2)}, u32[]{:S(2)}) %collective-permute-start.6) | collective-permute-done | bytes 524320 | tf_op jit(solution)/shard_map/ppermute | solution.py:244
  111.5 0.0 copy-done.8
  111.5 1.9 collective-permute-start.7
  113.4 1.3 collective-permute-start.8
  114.7 1.5 collective-permute-start.19
  116.2 0.0 collective-permute-done.10.refs_2_
  116.2 1.3 collective-permute-start.20
  117.5 0.0 copy-done.9
  117.5 0.0 all-gather.4.cloned.1.call-update
  117.5 5.2 %collective-permute-done.12.refs_5_ = bf16[512,512]{1,0:T(8,128)(2,1)} collective-permute-done((bf16[512,512]{1,0:T(8,128)(2,1)S(1)}, bf16[512,512]{1,0:T(8,128)(2,1)}, u32[]{:S(2)}, u32[]{:S(2)}) %collective-permute-start.12) | collective-permute-done | bytes 524320 | tf_op jit(solution)/shard_map/ppermute | solution.py:244
  122.7 1.5 collective-permute-start.17
  124.2 0.0 collective-permute-done.7.refs_10_.refs_1_
  124.2 1.3 collective-permute-start.18
  125.5 8.5 %collective-permute-done.8.refs_11_.refs_4_ = bf16[512,512]{1,0:T(8,128)(2,1)} collective-permute-done((bf16[512,512]{1,0:T(8,128)(2,1)S(1)}, bf16[512,512]{1,0:T(8,128)(2,1)}, u32[]{:S(2)}, u32[]{:S(2)}) %collective-permute-start.8) | collective-permute-done | bytes 524320 | tf_op jit(solution)/shard_map/ppermute | solution.py:244
  134.0 3.1 %collective-permute-start.14 = (bf16[512,512]{1,0:T(8,128)(2,1)S(1)}, bf16[512,512]{1,0:T(8,128)(2,1)}, u32[]{:S(2)}, u32[]{:S(2)}) collective-permute-start(bf16[512,512]{1,0:T(8,128)(2,1)S(1)} %bitcast.8), channel_id=1, source_target_pairs={{0,3},{4,7},{8,11},{12,15},{16,19},{20,23},{24,27},{28,31}} | collective-permute-start | bytes 1572872 | tf_op jit(solution)/shard_map/ppermute | solution.py:243
  137.1 0.0 collective-permute-done.19.refs_3_
  137.1 1.3 collective-permute-start.16
  138.4 6.8 %collective-permute-done.20.refs_6_ = bf16[512,512]{1,0:T(8,128)(2,1)} collective-permute-done((bf16[512,512]{1,0:T(8,128)(2,1)}, bf16[512,512]{1,0:T(8,128)(2,1)}, u32[]{:S(2)}, u32[]{:S(2)}) %collective-permute-start.20) | collective-permute-done | bytes 524320 | tf_op jit(solution)/shard_map/ppermute | solution.py:244
  145.2 1.4 collective-permute-start.13
  146.7 19.0 %shard_map.38.refs_10_ = bf16[64,128,1024]{2,1,0:T(8,128)(2,1)} custom-call(s32[1]{0:T(128)} %bitcast.own, bf16[512,512]{1,0:T(8,128)(2,1)} %bitcast.18, bf16[512,512]{1,0:T(8,128)(2,1)} %copy-done.8, bf16[512,512]{1,0:T(8,128)(2,1)} %collective-permute-done.5.refs_2_, bf16[512,512]{1,0:T(8,128)(2,1)} %collective-permute-done.19.refs_3_, ...), custom_call_target="tpu_custom_call" | custom-call | flops 12884901888 | bytes 25165824 | tf_op jit(solution)/shard_map/pallas_call | solution.py:167
  165.7 0.0 copy-done
  165.7 0.0 copy-done.1
  165.7 0.0 copy-done.2
  165.7 0.0 collective-permute-done.17.refs_3_
  165.7 1.5 collective-permute-start.15
  167.2 7.0 %collective-permute-done.18.refs_6_ = bf16[512,512]{1,0:T(8,128)(2,1)} collective-permute-done((bf16[512,512]{1,0:T(8,128)(2,1)}, bf16[512,512]{1,0:T(8,128)(2,1)}, u32[]{:S(2)}, u32[]{:S(2)}) %collective-permute-start.18) | collective-permute-done | bytes 524320 | tf_op jit(solution)/shard_map/ppermute | solution.py:244
  174.2 18.8 %shard_map.39.refs_10_ = bf16[64,128,1024]{2,1,0:T(8,128)(2,1)} custom-call(s32[1]{0:T(128)} %bitcast.own, bf16[512,512]{1,0:T(8,128)(2,1)} %bitcast.13, bf16[512,512]{1,0:T(8,128)(2,1)} %copy-done.2, bf16[512,512]{1,0:T(8,128)(2,1)} %copy-done.5, bf16[512,512]{1,0:T(8,128)(2,1)} %collective-permute-done.17.refs_3_, ...), custom_call_target="tpu_custom_call", output_to_operand_aliasing={{}: (11, {})} | custom-call | flops 12884901888 | bytes 25165824 | tf_op jit(solution)/shard_map/pallas_call | solution.py:167
  193.0 0.0 collective-permute-done.14.refs_3_
  193.0 0.0 collective-permute-done.16.refs_6_
  193.0 0.0 collective-permute-done.13.refs_2_
  193.0 18.3 %collective-permute-done.15.refs_5_ = bf16[512,512]{1,0:T(8,128)(2,1)S(1)} collective-permute-done((bf16[512,512]{1,0:T(8,128)(2,1)}, bf16[512,512]{1,0:T(8,128)(2,1)S(1)}, u32[]{:S(2)}, u32[]{:S(2)}) %collective-permute-start.15) | collective-permute-done | bytes 524320 | tf_op jit(solution)/shard_map/ppermute | solution.py:244
  211.3 0.8 copy-done.6
  212.1 18.7 %shard_map.40.refs_4_ = bf16[64,128,1024]{2,1,0:T(8,128)(2,1)} custom-call(s32[1]{0:T(128)} %bitcast.own, bf16[512,512]{1,0:T(8,128)(2,1)} %bitcast.10, bf16[512,512]{1,0:T(8,128)(2,1)} %copy-done.4, bf16[512,512]{1,0:T(8,128)(2,1)} %collective-permute-done.13.refs_2_, ...), custom_call_target="tpu_custom_call", output_to_operand_aliasing={{}: (11, {})} | custom-call | flops 12884901888 | bytes 25165824 | tf_op jit(solution)/shard_map/pallas_call | solution.py:167
  230.8 0.0 all-gather.4.cloned.1.call-done.refs_0_
  230.8 18.7 %shard_map.41 = bf16[64,128,1024]{2,1,0:T(8,128)(2,1)} custom-call(s32[1]{0:T(128)} %bitcast.own, bf16[512,2048]{1,0:T(8,128)(2,1)} %all-gather.4.cloned.1.call-done.refs_0_, bf16[2048,1024]{1,0:T(8,128)(2,1)} %all-gather.6.cloned.1.call-done.refs_7_.refs_1_, ...), custom_call_target="tpu_custom_call", output_to_operand_aliasing={{}: (5, {})} | custom-call | flops 12884901888 | bytes 25165824 | tf_op jit(solution)/shard_map/pallas_call | solution.py:167
  (16 shorter events, 0.0 us)
Async XLA Ops:
  6.5 140.1 %all-gather.6.cloned.1.call-start = ((), (), s32[]{:S(2)}) async-start(), calls=%async_computation.2 | async-start | bytes 4718592 | tf_op jit(solution)/shard_map/all_gather | solution.py:223
  10.9 44.2 %all-to-all-start = ((bf16[8,4,4,16,512]{4,3,2,1,0:T(8,128)(2,1)}), bf16[8,4,4,16,512]{4,3,2,1,0:T(8,128)(2,1)S(1)}, u32[]{:S(2)}, u32[]{:S(2)}) async-start(bf16[8,4,4,16,512]{4,3,2,1,0:T(8,128)(2,1)} %get-tuple-element.28), calls=%async_computation | async-start | bytes 4194304 | tf_op jit(solution)/shard_map/all_to_all | solution.py:219
  16.1 130.6 %all-gather.8.cloned.1.call-start = ((), (), s32[]{:S(2)}) async-start(), calls=%async_computation.3 | async-start | bytes 14155776 | tf_op jit(solution)/shard_map/all_gather | solution.py:223
  16.1 16.9 %collective-permute-start.2 = (bf16[256,1024]{1,0:T(8,128)(2,1)}, bf16[256,1024]{1,0:T(8,128)(2,1)S(1)}, u32[]{:S(2)}, u32[]{:S(2)}) collective-permute-start(bf16[256,1024]{1,0:T(8,128)(2,1)} %get-tuple-element.31), channel_id=1, source_target_pairs={{0,1},{1,2},{2,3},{3,0},{4,5},{5,6},{6,7},{7,4},{8,9},{9,10},{10,1... | collective-permute-start | bytes 1572872 | tf_op jit(solution)/shard_map/ppermute | solution.py:218
  17.7 37.3 %collective-permute-start.3 = (bf16[256,1024]{1,0:T(8,128)(2,1)}, bf16[256,1024]{1,0:T(8,128)(2,1)S(1)}, u32[]{:S(2)}, u32[]{:S(2)}) collective-permute-start(bf16[256,1024]{1,0:T(8,128)(2,1)} %get-tuple-element.32), channel_id=1, source_target_pairs={{0,2},{1,3},{2,0},{3,1},{4,6},{5,7},{6,4},{7,5},{8,10},{9,11},{10,... | collective-permute-start | bytes 1572872 | tf_op jit(solution)/shard_map/ppermute | solution.py:218
  20.3 34.7 %collective-permute-start.4 = (bf16[256,1024]{1,0:T(8,128)(2,1)}, bf16[256,1024]{1,0:T(8,128)(2,1)}, u32[]{:S(2)}, u32[]{:S(2)}) collective-permute-start(bf16[256,1024]{1,0:T(8,128)(2,1)} %get-tuple-element.33), channel_id=1, source_target_pairs={{0,3},{1,0},{2,1},{3,2},{4,7},{5,4},{6,5},{7,6},{8,11},{9,8},{10,9... | collective-permute-start | bytes 1572872 | tf_op jit(solution)/shard_map/ppermute | solution.py:218
  57.3 173.5 %all-gather.4.cloned.1.call-start = ((), (), s32[]{:S(2)}) async-start(), calls=%async_computation.1 | async-start | bytes 2621440 | tf_op jit(solution)/shard_map/all_gather | solution.py:273
  58.4 57.8 %copy-start.7 = (bf16[8,1,4,16,512]{4,3,2,1,0:T(8,128)(2,1)}, bf16[8,1,4,16,512]{4,3,2,1,0:T(8,128)(2,1)S(1)}, u32[]{:S(2)}) copy-start(bf16[8,1,4,16,512]{4,3,2,1,0:T(8,128)(2,1)S(1)} %get-tuple-element.54) | copy-start | bytes 1572868
  58.4 107.2 %copy-start = (bf16[8,1,4,16,512]{4,3,2,1,0:T(8,128)(2,1)}, bf16[8,1,4,16,512]{4,3,2,1,0:T(8,128)(2,1)S(1)}, u32[]{:S(2)}) copy-start(bf16[8,1,4,16,512]{4,3,2,1,0:T(8,128)(2,1)S(1)} %get-tuple-element.52) | copy-start | bytes 1572868
  58.4 107.2 %copy-start.1 = (bf16[8,1,4,16,512]{4,3,2,1,0:T(8,128)(2,1)}, bf16[8,1,4,16,512]{4,3,2,1,0:T(8,128)(2,1)S(1)}, u32[]{:S(2)}) copy-start(bf16[8,1,4,16,512]{4,3,2,1,0:T(8,128)(2,1)S(1)} %get-tuple-element.51) | copy-start | bytes 1572868
  58.4 26.0 %collective-permute-start = (bf16[512,512]{1,0:T(8,128)(2,1)S(1)}, bf16[512,512]{1,0:T(8,128)(2,1)S(1)}, u32[]{:S(2)}, u32[]{:S(2)}) collective-permute-start(bf16[512,512]{1,0:T(8,128)(2,1)S(1)} %bitcast.16), channel_id=1, source_target_pairs={{0,1},{1,2},{2,3},{4,5},{5,6},{6,7},{8,9},{9,10},{10,11},{12,13},{... | collective-permute-start | bytes 1572872 | tf_op jit(solution)/shard_map/ppermute | solution.py:243
  72.2 16.7 %collective-permute-start.1 = (bf16[512,512]{1,0:T(8,128)(2,1)S(1)}, bf16[512,512]{1,0:T(8,128)(2,1)S(1)}, u32[]{:S(2)}, u32[]{:S(2)}) collective-permute-start(bf16[512,512]{1,0:T(8,128)(2,1)S(1)} %bitcast.17), channel_id=1, source_target_pairs={{1,0},{2,1},{3,2},{5,4},{6,5},{7,6},{9,8},{10,9},{11,10},{13,12},{... | collective-permute-start | bytes 1572872 | tf_op jit(solution)/shard_map/ppermute | solution.py:244
  73.5 21.3 %collective-permute-start.9 = (bf16[512,512]{1,0:T(8,128)(2,1)S(1)}, bf16[512,512]{1,0:T(8,128)(2,1)S(1)}, u32[]{:S(2)}, u32[]{:S(2)}) collective-permute-start(bf16[512,512]{1,0:T(8,128)(2,1)S(1)} %bitcast.11), channel_id=1, source_target_pairs={{0,1},{1,2},{2,3},{4,5},{5,6},{6,7},{8,9},{9,10},{10,11},{12,13},{... | collective-permute-start | bytes 1572872 | tf_op jit(solution)/shard_map/ppermute | solution.py:243
  78.1 22.1 %collective-permute-start.11 = (bf16[512,512]{1,0:T(8,128)(2,1)S(1)}, bf16[512,512]{1,0:T(8,128)(2,1)S(1)}, u32[]{:S(2)}, u32[]{:S(2)}) collective-permute-start(bf16[512,512]{1,0:T(8,128)(2,1)S(1)} %bitcast.12), channel_id=1, source_target_pairs={{1,0},{2,1},{3,2},{5,4},{6,5},{7,6},{9,8},{10,9},{11,10},{13,12},{... | collective-permute-start | bytes 1572872 | tf_op jit(solution)/shard_map/ppermute | solution.py:244
  84.5 27.0 %copy-start.8 = (bf16[512,512]{1,0:T(8,128)(2,1)}, bf16[512,512]{1,0:T(8,128)(2,1)S(1)}, u32[]{:S(2)}) copy-start(bf16[512,512]{1,0:T(8,128)(2,1)S(1)} %collective-permute-done.refs_1_) | copy-start | bytes 1572868
  84.5 17.0 %collective-permute-start.5 = (bf16[512,512]{1,0:T(8,128)(2,1)S(1)}, bf16[512,512]{1,0:T(8,128)(2,1)}, u32[]{:S(2)}, u32[]{:S(2)}) collective-permute-start(bf16[512,512]{1,0:T(8,128)(2,1)S(1)} %collective-permute-done.refs_1_), channel_id=1, source_target_pairs={{1,2},{2,3},{5,6},{6,7},{9,10},{10,11},{13,14},{14,15},{17,18},{18... | collective-permute-start | bytes 1572872 | tf_op jit(solution)/shard_map/ppermute | solution.py:243
  88.9 28.6 %copy-start.9 = (bf16[512,512]{1,0:T(8,128)(2,1)}, bf16[512,512]{1,0:T(8,128)(2,1)S(1)}, u32[]{:S(2)}) copy-start(bf16[512,512]{1,0:T(8,128)(2,1)S(1)} %collective-permute-done.1.refs_4_) | copy-start | bytes 1572868
  88.9 22.6 %collective-permute-start.6 = (bf16[512,512]{1,0:T(8,128)(2,1)S(1)}, bf16[512,512]{1,0:T(8,128)(2,1)}, u32[]{:S(2)}, u32[]{:S(2)}) collective-permute-start(bf16[512,512]{1,0:T(8,128)(2,1)S(1)} %collective-permute-done.1.refs_4_), channel_id=1, source_target_pairs={{1,0},{2,1},{5,4},{6,5},{9,8},{10,9},{13,12},{14,13},{17,16},{18,1... | collective-permute-start | bytes 1572872 | tf_op jit(solution)/shard_map/ppermute | solution.py:244
  94.8 70.9 %copy-start.2 = (bf16[512,512]{1,0:T(8,128)(2,1)}, bf16[512,512]{1,0:T(8,128)(2,1)S(1)}, u32[]{:S(2)}) copy-start(bf16[512,512]{1,0:T(8,128)(2,1)S(1)} %collective-permute-done.9.refs_1_) | copy-start | bytes 1572868
  94.8 21.4 %collective-permute-start.10 = (bf16[512,512]{1,0:T(8,128)(2,1)S(1)}, bf16[512,512]{1,0:T(8,128)(2,1)S(1)}, u32[]{:S(2)}, u32[]{:S(2)}) collective-permute-start(bf16[512,512]{1,0:T(8,128)(2,1)S(1)} %collective-permute-done.9.refs_1_), channel_id=1, source_target_pairs={{1,2},{2,3},{5,6},{6,7},{9,10},{10,11},{13,14},{14,15},{17,18},{18... | collective-permute-start | bytes 1572872 | tf_op jit(solution)/shard_map/ppermute | solution.py:243
  100.2 65.6 %copy-start.3 = (bf16[512,512]{1,0:T(8,128)(2,1)}, bf16[512,512]{1,0:T(8,128)(2,1)S(1)}, u32[]{:S(2)}) copy-start(bf16[512,512]{1,0:T(8,128)(2,1)S(1)} %collective-permute-done.11.refs_4_) | copy-start | bytes 1572868
  100.2 22.6 %collective-permute-start.12 = (bf16[512,512]{1,0:T(8,128)(2,1)S(1)}, bf16[512,512]{1,0:T(8,128)(2,1)}, u32[]{:S(2)}, u32[]{:S(2)}) collective-permute-start(bf16[512,512]{1,0:T(8,128)(2,1)S(1)} %collective-permute-done.11.refs_4_), channel_id=1, source_target_pairs={{1,0},{2,1},{5,4},{6,5},{9,8},{10,9},{13,12},{14,13},{17,16},{18,1... | collective-permute-start | bytes 1572872 | tf_op jit(solution)/shard_map/ppermute | solution.py:244
  111.5 12.7 %collective-permute-start.7 = (bf16[512,512]{1,0:T(8,128)(2,1)S(1)}, bf16[512,512]{1,0:T(8,128)(2,1)S(1)}, u32[]{:S(2)}, u32[]{:S(2)}) collective-permute-start(bf16[512,512]{1,0:T(8,128)(2,1)S(1)} %bitcast.6), channel_id=1, source_target_pairs={{0,1},{1,2},{2,3},{4,5},{5,6},{6,7},{8,9},{9,10},{10,11},{12,13},{... | collective-permute-start | bytes 1572872 | tf_op jit(solution)/shard_map/ppermute | solution.py:243
  113.4 20.5 %collective-permute-start.8 = (bf16[512,512]{1,0:T(8,128)(2,1)S(1)}, bf16[512,512]{1,0:T(8,128)(2,1)}, u32[]{:S(2)}, u32[]{:S(2)}) collective-permute-start(bf16[512,512]{1,0:T(8,128)(2,1)S(1)} %bitcast.7), channel_id=1, source_target_pairs={{1,0},{2,1},{3,2},{5,4},{6,5},{7,6},{9,8},{10,9},{11,10},{13,12},{... | collective-permute-start | bytes 1572872 | tf_op jit(solution)/shard_map/ppermute | solution.py:244
  114.7 22.4 %collective-permute-start.19 = (bf16[512,512]{1,0:T(8,128)(2,1)}, bf16[512,512]{1,0:T(8,128)(2,1)}, u32[]{:S(2)}, u32[]{:S(2)}) collective-permute-start(bf16[512,512]{1,0:T(8,128)(2,1)} %collective-permute-done.5.refs_2_), channel_id=1, source_target_pairs={{2,3},{6,7},{10,11},{14,15},{18,19},{22,23},{26,27},{30,31}} | collective-permute-start | bytes 1572872 | tf_op jit(solution)/shard_map/ppermute | solution.py:243
  116.2 49.5 %copy-start.5 = (bf16[512,512]{1,0:T(8,128)(2,1)}, bf16[512,512]{1,0:T(8,128)(2,1)S(1)}, u32[]{:S(2)}) copy-start(bf16[512,512]{1,0:T(8,128)(2,1)S(1)} %collective-permute-done.10.refs_2_) | copy-start | bytes 1572868
  116.2 29.0 %collective-permute-start.20 = (bf16[512,512]{1,0:T(8,128)(2,1)}, bf16[512,512]{1,0:T(8,128)(2,1)}, u32[]{:S(2)}, u32[]{:S(2)}) collective-permute-start(bf16[512,512]{1,0:T(8,128)(2,1)} %collective-permute-done.6.refs_5_), channel_id=1, source_target_pairs={{1,0},{5,4},{9,8},{13,12},{17,16},{21,20},{25,24},{29,28}} | collective-permute-start | bytes 1572872 | tf_op jit(solution)/shard_map/ppermute | solution.py:244
  122.7 43.0 %collective-permute-start.17 = (bf16[512,512]{1,0:T(8,128)(2,1)S(1)}, bf16[512,512]{1,0:T(8,128)(2,1)}, u32[]{:S(2)}, u32[]{:S(2)}) collective-permute-start(bf16[512,512]{1,0:T(8,128)(2,1)S(1)} %collective-permute-done.10.refs_2_), channel_id=1, source_target_pairs={{2,3},{6,7},{10,11},{14,15},{18,19},{22,23},{26,27},{30,31}} | collective-permute-start | bytes 1572872 | tf_op jit(solution)/shard_map/ppermute | solution.py:243
  124.2 22.5 %copy-start.4 = (bf16[512,512]{1,0:T(8,128)(2,1)}, bf16[512,512]{1,0:T(8,128)(2,1)S(1)}, u32[]{:S(2)}) copy-start(bf16[512,512]{1,0:T(8,128)(2,1)S(1)} %collective-permute-done.7.refs_10_.refs_1_) | copy-start | bytes 1572868
  124.2 50.0 %collective-permute-start.18 = (bf16[512,512]{1,0:T(8,128)(2,1)}, bf16[512,512]{1,0:T(8,128)(2,1)}, u32[]{:S(2)}, u32[]{:S(2)}) collective-permute-start(bf16[512,512]{1,0:T(8,128)(2,1)} %collective-permute-done.12.refs_5_), channel_id=1, source_target_pairs={{1,0},{5,4},{9,8},{13,12},{17,16},{21,20},{25,24},{29,28}} | collective-permute-start | bytes 1572872 | tf_op jit(solution)/shard_map/ppermute | solution.py:244
  134.0 59.0 %collective-permute-start.14 = (bf16[512,512]{1,0:T(8,128)(2,1)S(1)}, bf16[512,512]{1,0:T(8,128)(2,1)}, u32[]{:S(2)}, u32[]{:S(2)}) collective-permute-start(bf16[512,512]{1,0:T(8,128)(2,1)S(1)} %bitcast.8), channel_id=1, source_target_pairs={{0,3},{4,7},{8,11},{12,15},{16,19},{20,23},{24,27},{28,31}} | collective-permute-start | bytes 1572872 | tf_op jit(solution)/shard_map/ppermute | solution.py:243
  137.1 55.9 %collective-permute-start.16 = (bf16[512,512]{1,0:T(8,128)(2,1)S(1)}, bf16[512,512]{1,0:T(8,128)(2,1)}, u32[]{:S(2)}, u32[]{:S(2)}) collective-permute-start(bf16[512,512]{1,0:T(8,128)(2,1)S(1)} %bitcast.9), channel_id=1, source_target_pairs={{3,0},{7,4},{11,8},{15,12},{19,16},{23,20},{27,24},{31,28}} | collective-permute-start | bytes 1572872 | tf_op jit(solution)/shard_map/ppermute | solution.py:244
  145.2 47.8 %collective-permute-start.13 = (bf16[512,512]{1,0:T(8,128)(2,1)S(1)}, bf16[512,512]{1,0:T(8,128)(2,1)}, u32[]{:S(2)}, u32[]{:S(2)}) collective-permute-start(bf16[512,512]{1,0:T(8,128)(2,1)S(1)} %collective-permute-done.7.refs_10_.refs_1_), channel_id=1, source_target_pairs={{1,2},{2,3},{5,6},{6,7},{9,10},{10,11},{13,14},{14,15},{17,18},{18... | collective-permute-start | bytes 1572872 | tf_op jit(solution)/shard_map/ppermute | solution.py:243
  165.7 45.5 %collective-permute-start.15 = (bf16[512,512]{1,0:T(8,128)(2,1)}, bf16[512,512]{1,0:T(8,128)(2,1)S(1)}, u32[]{:S(2)}, u32[]{:S(2)}) collective-permute-start(bf16[512,512]{1,0:T(8,128)(2,1)} %collective-permute-done.8.refs_11_.refs_4_), channel_id=1, source_target_pairs={{1,0},{2,1},{5,4},{6,5},{9,8},{10,9},{13,12},{14,13},{17,16},{18,1... | collective-permute-start | bytes 1572872 | tf_op jit(solution)/shard_map/ppermute | solution.py:244
  211.3 0.8 copy-start.6
Sparse Core Ops, SparseCore 0:
  11.0 50.2 all-gather.5
  63.1 76.9 all-gather.7
  141.7 69.5 all-gather.3

commit v9 on v8

--- a/solution.py
+++ b/solution.py
@@ -55,9 +55,9 @@
     )(own.reshape(1), blocks, couplings)
 
 
-def chunk_kernel(own, *refs, pieces, parts, occupied, b_local, q):
-    t_own, t_right, t_left = refs[0], refs[1:parts], refs[parts:pieces]
-    w_own, w_rest, ladder_hbm = refs[pieces:pieces + 3]
+def chunk_kernel(own, *refs, groups, pieces, parts, occupied, b_local, q):
+    t_refs = [refs[g * pieces:(g + 1) * pieces] for g in range(groups)]
+    w_own, w_rest, ladder_hbm = refs[groups * pieces:groups * pieces + 3]
     out_ref, t_all, w_buf, ladder, pairs, out_buf, t_sem, w_sem, l_sem, out_sem = refs[-10:]
     depth = t_all.shape[1] // parts
     width = w_own.shape[1]
@@ -66,34 +66,39 @@
     per_part = occupied // parts
     wide = WIDE // b_local
 
-    def t_copy(src, block, s):
+    size = GROUP * occupied
+
+    def t_copy(src, g, block, s):
         cols = pl.ds(pl.multiple_of(block * depth, depth), depth)
-        return pltpu.make_async_copy(src, t_all.at[:, cols], t_sem.at[s])
+        return pltpu.make_async_copy(src, t_all.at[g * size:(g + 1) * size, cols], t_sem.at[g, s])
 
     def w_copy(s, slot):
         src = w_rest.at[:, (s - 1) * width:s * width] if s else w_own
         return pltpu.make_async_copy(src, w_buf.at[slot], w_sem.at[slot])
 
     blocks = [lax.rem(own[0] - s + parts, parts) for s in range(parts)]
-    if pieces == 1:
-        pltpu.make_async_copy(t_own, t_all, t_sem.at[0]).start()
-    else:
-        t_copy(t_own, blocks[0], 0).start()
+    for g in range(groups):
+        t_own, t_right, t_left = t_refs[g][0], t_refs[g][1:parts], t_refs[g][parts:]
+        if pieces == 1:
+            pltpu.make_async_copy(t_own, t_all.at[g * size:(g + 1) * size], t_sem.at[g, 0]).start()
+            continue
+        t_copy(t_own, g, blocks[0], 0).start()
         for s in range(1, parts):
             @pl.when(own[0] >= s)
             def _():
-                t_copy(t_right[s - 1], blocks[s], s).start()
+                t_copy(t_right[s - 1], g, blocks[s], s).start()
 
             @pl.when(own[0] < s)
             def _():
-                t_copy(t_left[parts - s - 1], blocks[s], s).start()
+                t_copy(t_left[parts - s - 1], g, blocks[s], s).start()
     w_copy(0, 0).start()
     ladder_copy = pltpu.make_async_copy(ladder_hbm, ladder, l_sem)
-    if pieces == 1:
-        pltpu.make_async_copy(t_own, t_all, t_sem.at[0]).wait()
-    else:
+    for g in range(groups):
+        if pieces == 1:
+            pltpu.make_async_copy(t_refs[g][0], t_all.at[g * size:(g + 1) * size], t_sem.at[g, 0]).wait()
+            continue
         for s in range(parts):
-            t_copy(t_own, blocks[s], s).wait()
+            t_copy(t_refs[g][0], g, blocks[s], s).wait()
 
     @pl.loop(0, parts)
     def _(step):
@@ -115,13 +120,14 @@
             for i in range(occupied):
                 for k in range(wide):
                     n = j0 + (i * occupied + tile * wide + k)
-                    for h in range(GROUP // 8):
-                        row = i * GROUP + h * 8
-                        pairs[pl.ds(h * 8 * pitch + n, 8, stride=pitch), :] = (
-                            acc[row:row + 8, k * b_local:(k + 1) * b_local])
+                    for g in range(groups):
+                        for h in range(0, GROUP, 8):
+                            row = g * size + i * GROUP + h
+                            pairs[pl.ds((g * GROUP + h) * pitch + n, 8, stride=pitch), :] = (
+                                acc[row:row + 8, k * b_local:(k + 1) * b_local])
 
     ladder_copy.wait()
-    steps = GROUP // STEP_A
+    steps = groups * GROUP // STEP_A
 
     def out_copy(step, slot):
         rows = pl.ds(q * GROUP + step * STEP_A, STEP_A)
@@ -152,20 +158,22 @@
         out_copy(step, step % 2).wait()
 
 
-def chunk_update(own, pieces, panel_w, ladder, out, after, q, a_local, b_local, occupied):
-    rows = GROUP * occupied
+def chunk_update(own, chunks, panel_w, ladder, out, q, a_local, b_local, occupied):
+    groups = len(chunks)
+    rows = groups * GROUP * occupied
     count = occupied * occupied
     k_all, width = panel_w[0].shape
     parts = 1 + panel_w[1].shape[1] // width
-    args = [*pieces, *panel_w, ladder, *after]
+    args = [*[piece for pieces in chunks for piece in pieces], *panel_w, ladder]
     aliases = {}
     if out is not None:
         aliases = {len(args) + 1: 0}
         args.append(out)
-    flops = 2 * rows * k_all * occupied * b_local + 2 * GROUP * b_local * count * count
-    size = parts * k_all * width + count * count + rows * k_all + GROUP * b_local * count
+    flops = 2 * rows * k_all * occupied * b_local + 2 * groups * GROUP * b_local * count * count
+    size = parts * k_all * width + count * count + rows * k_all + groups * GROUP * b_local * count
     return pl.pallas_call(
-        functools.partial(chunk_kernel, pieces=len(pieces), parts=parts, occupied=occupied, b_local=b_local, q=q),
+        functools.partial(
+            chunk_kernel, groups=groups, pieces=len(chunks[0]), parts=parts, occupied=occupied, b_local=b_local, q=q),
         out_shape=jax.ShapeDtypeStruct((a_local, b_local, count), jnp.bfloat16),
         in_specs=[pl.BlockSpec(memory_space=pltpu.SMEM)] + [ANY] * len(args),
         out_specs=ANY,
@@ -173,9 +181,9 @@
             pltpu.VMEM((rows, k_all), jnp.bfloat16),
             pltpu.VMEM((2, k_all, width), jnp.bfloat16),
             pltpu.VMEM((count, count), jnp.bfloat16),
-            pltpu.VMEM((GROUP * (count + PAD), b_local), jnp.float32),
+            pltpu.VMEM((groups * GROUP * (count + PAD), b_local), jnp.float32),
             pltpu.VMEM((2, STEP_A, b_local, count), jnp.bfloat16),
-            pltpu.SemaphoreType.DMA((parts,)),
+            pltpu.SemaphoreType.DMA((groups, parts)),
             pltpu.SemaphoreType.DMA((2,)),
             pltpu.SemaphoreType.DMA,
             pltpu.SemaphoreType.DMA((2,)),
@@ -231,10 +239,6 @@
         right, left = sides
         return [right[0], *right[1:], *left[1:]]
 
-    def update(q, out, after):
-        blocks = [last] if q == chunks - 1 else flat(pieces[q])
-        return chunk_update(own, blocks, panel_w, ladder, out, after, q, a_local, b_local, occupied)
-
     def hop(sides, s, direct=False):
         right, left = sides
         first = 0 if direct else s - 1
@@ -276,13 +280,15 @@
     before[0][-2], before[1][-2] = after((before[0][-2], before[1][-2]), x)
     for s in range(1, cols - 1):
         hop(x, s)
-    for sides, n in ((early[-1], -2), (x, 1)):
+    for sides, n in ((early[0], -1), (early[-1], -2), (x, 1)):
         sides[0][n], sides[1][n] = after((sides[0][n], sides[1][n]), x)
     hop(x, cols - 1, direct=True)
+    update = functools.partial(chunk_update, own, a_local=a_local, b_local=b_local, occupied=occupied)
     out = None
-    for q in range(chunks):
-        out = update(q, out, () if q else (x[0][1], x[1][1]))
-    return out
+    for q in range(0, len(early), 2):
+        out = update([flat(sides) for sides in early[q:q + 2]], panel_w, ladder, out, q)
+    out = update([flat(x)], panel_w, ladder, out, len(early))
+    return update([[last]], panel_w, ladder, out, chunks - 1)
 
 
 def solution(mesh):

time: 257 us -> 261 us (1.016)
  waiting for transfers between devices: 107 us -> 115 us
  Pallas kernels: 79.5 us -> 75.5 us
    ppermute x9, waiting for transfers between devices: 63.4 us -> 71.5 us  [hop(): lax.ppermute(left[source], 'col', [(c + step, c) for c in range(cols - st...]
    pallas_call x4 -> x3, Pallas kernels: 75.3 us -> 71.2 us  [chunk_update(): pl.pallas_call(functools.partial(chunk_kernel, groups=groups, pieces=len(...]
  transfers between devices with their start and end apart: 25 -> 25, of which waited for: 12 -> 11; matrix products, arithmetic and copies ran while one was open for 1% -> 1% of each run, Pallas kernels for 22% -> 20%
where the time goes in v9:
time: 261 us; the launch traced here: 260 us
  waiting for transfers between devices  115 us (44%)
  Pallas kernels  75.5 us (29%)
  starting transfers between devices  51.9 us (20%)
  between operations  13.5 us (5%)
    ppermute x9, waiting for transfers between devices, hop(): lax.ppermute(left[source], 'col', [(c + step, c) for c in range(cols - st...  71.5 us
    pallas_call x3, Pallas kernels, chunk_update(): pl.pallas_call(functools.partial(chunk_kernel, groups=groups, pieces=len(...  71.2 us
    ppermute x3, waiting for transfers between devices, local(): lax.ppermute(arrived[s], 'col', [(c, (c + s) % cols) for c in range(cols)])  33.4 us
    ppermute x9, starting transfers between devices, hop(): lax.ppermute(right[source], 'col', [(c, c + step) for c in range(first, c...  29.3 us
    ppermute x9, starting transfers between devices, hop(): lax.ppermute(left[source], 'col', [(c + step, c) for c in range(cols - st...  11.8 us
    ppermute x9, waiting for transfers between devices, hop(): lax.ppermute(right[source], 'col', [(c, c + step) for c in range(first, c...  9.65 us
    ppermute x3, starting transfers between devices, local(): lax.ppermute(arrived[s], 'col', [(c, (c + s) % cols) for c in range(cols)])  5.54 us
  transfers between devices with their start and end apart: 25, of which 11 were waited for; matrix products, arithmetic and copies ran while one was open for 1% of the time, Pallas kernels for 20%

profile of v9, /device:TPU:0, one launch (start us, length us, event | category | flops | bytes accessed | tf_op | source)
XLA Modules:
  0.0 259.9 jit_solution(4619363300872750374)
XLA Ops:
  6.5 4.3 %shard_map.37 = (bf16[8,4,4,16,512]{4,3,2,1,0:T(8,128)(2,1)}, bf16[256,1024]{1,0:T(8,128)(2,1)}, bf16[256,1024]{1,0:T(8,128)(2,1)}, bf16[256,1024]{1,0:T(8,128)(2,1)}, bf16[256,1024]{1,0:T(8,128)(2,1)}) custom-call(s32[1]{0:T(128)} %bitcast.own, bf16[4,8,4,16,512]{4,3,2,1,0:T(8,128)(2,1)} %bitcast.11, bf16[256,4096]{1,0:T(8,128)(2,1)} %w_ref.1), custom_call_target="tpu_custom_call" | custom-call | bytes 8388608 | tf_op jit(solution)/shard_map/pallas_call | solution.py:46
  10.9 0.0 all-gather.6.cloned.1.call-update
  10.9 5.2 %all-to-all-start = ((bf16[8,4,4,16,512]{4,3,2,1,0:T(8,128)(2,1)}), bf16[8,4,4,16,512]{4,3,2,1,0:T(8,128)(2,1)S(1)}, u32[]{:S(2)}, u32[]{:S(2)}) async-start(bf16[8,4,4,16,512]{4,3,2,1,0:T(8,128)(2,1)} %get-tuple-element.32), calls=%async_computation | async-start | bytes 4194304 | tf_op jit(solution)/shard_map/all_to_all | solution.py:227
  16.1 0.0 all-gather.8.cloned.1.call-start
  16.1 1.6 collective-permute-start.2
  17.7 2.6 collective-permute-start.3
  20.3 1.3 collective-permute-start.4
  21.7 11.4 %collective-permute-done.2 = bf16[256,1024]{1,0:T(8,128)(2,1)S(1)} collective-permute-done((bf16[256,1024]{1,0:T(8,128)(2,1)}, bf16[256,1024]{1,0:T(8,128)(2,1)S(1)}, u32[]{:S(2)}, u32[]{:S(2)}) %collective-permute-start.2) | collective-permute-done | bytes 524320 | tf_op jit(solution)/shard_map/ppermute | solution.py:226
  33.1 22.0 %collective-permute-done.3 = bf16[256,1024]{1,0:T(8,128)(2,1)S(1)} collective-permute-done((bf16[256,1024]{1,0:T(8,128)(2,1)}, bf16[256,1024]{1,0:T(8,128)(2,1)S(1)}, u32[]{:S(2)}, u32[]{:S(2)}) %collective-permute-start.3) | collective-permute-done | bytes 524320 | tf_op jit(solution)/shard_map/ppermute | solution.py:226
  55.1 0.0 collective-permute-done.4
  55.1 0.0 all-to-all-done
  55.1 2.3 pad_maximum_fusion
  57.4 0.0 all-gather.8.cloned.1.call-update
  57.4 0.0 all-gather.4.cloned.1.call-start
  57.4 1.0 fusion
  58.4 13.8 %collective-permute-start = (bf16[512,512]{1,0:T(8,128)(2,1)S(1)}, bf16[512,512]{1,0:T(8,128)(2,1)S(1)}, u32[]{:S(2)}, u32[]{:S(2)}) collective-permute-start(bf16[512,512]{1,0:T(8,128)(2,1)S(1)} %bitcast.16), channel_id=1, source_target_pairs={{0,1},{1,2},{2,3},{4,5},{5,6},{6,7},{8,9},{9,10},{10,11},{12,13},{... | collective-permute-start | bytes 1572872 | tf_op jit(solution)/shard_map/ppermute | solution.py:247
  72.2 1.3 collective-permute-start.1
  73.5 4.6 %collective-permute-start.9 = (bf16[512,512]{1,0:T(8,128)(2,1)S(1)}, bf16[512,512]{1,0:T(8,128)(2,1)S(1)}, u32[]{:S(2)}, u32[]{:S(2)}) collective-permute-start(bf16[512,512]{1,0:T(8,128)(2,1)S(1)} %bitcast.13), channel_id=1, source_target_pairs={{0,1},{1,2},{2,3},{4,5},{5,6},{6,7},{8,9},{9,10},{10,11},{12,13},{... | collective-permute-start | bytes 1572872 | tf_op jit(solution)/shard_map/ppermute | solution.py:247
  78.1 1.3 collective-permute-start.11
  79.4 5.1 %collective-permute-done.refs_1_ = bf16[512,512]{1,0:T(8,128)(2,1)S(1)} collective-permute-done((bf16[512,512]{1,0:T(8,128)(2,1)S(1)}, bf16[512,512]{1,0:T(8,128)(2,1)S(1)}, u32[]{:S(2)}, u32[]{:S(2)}) %collective-permute-start) | collective-permute-done | bytes 524320 | tf_op jit(solution)/shard_map/ppermute | solution.py:247
  84.5 0.7 collective-permute-start.5
  85.1 3.8 %collective-permute-done.1.refs_4_ = bf16[512,512]{1,0:T(8,128)(2,1)S(1)} collective-permute-done((bf16[512,512]{1,0:T(8,128)(2,1)S(1)}, bf16[512,512]{1,0:T(8,128)(2,1)S(1)}, u32[]{:S(2)}, u32[]{:S(2)}) %collective-permute-start.1) | collective-permute-done | bytes 524320 | tf_op jit(solution)/shard_map/ppermute | solution.py:248
  88.9 1.3 collective-permute-start.6
  90.2 4.6 %collective-permute-done.9.refs_8_ = bf16[512,512]{1,0:T(8,128)(2,1)S(1)} collective-permute-done((bf16[512,512]{1,0:T(8,128)(2,1)S(1)}, bf16[512,512]{1,0:T(8,128)(2,1)S(1)}, u32[]{:S(2)}, u32[]{:S(2)}) %collective-permute-start.9) | collective-permute-done | bytes 524320 | tf_op jit(solution)/shard_map/ppermute | solution.py:247
  94.8 1.5 collective-permute-start.10
  96.2 3.9 %collective-permute-done.11.refs_11_ = bf16[512,512]{1,0:T(8,128)(2,1)S(1)} collective-permute-done((bf16[512,512]{1,0:T(8,128)(2,1)S(1)}, bf16[512,512]{1,0:T(8,128)(2,1)S(1)}, u32[]{:S(2)}, u32[]{:S(2)}) %collective-permute-start.11) | collective-permute-done | bytes 524320 | tf_op jit(solution)/shard_map/ppermute | solution.py:248
  100.2 1.3 collective-permute-start.12
  101.4 0.0 collective-permute-done.5.refs_2_
  101.5 0.7 collective-permute-start.13
  102.2 9.2 %collective-permute-done.6.refs_5_ = bf16[512,512]{1,0:T(8,128)(2,1)S(1)} collective-permute-done((bf16[512,512]{1,0:T(8,128)(2,1)S(1)}, bf16[512,512]{1,0:T(8,128)(2,1)S(1)}, u32[]{:S(2)}, u32[]{:S(2)}) %collective-permute-start.6) | collective-permute-done | bytes 524320 | tf_op jit(solution)/shard_map/ppermute | solution.py:248
  111.4 1.3 collective-permute-start.14
  112.7 4.6 %collective-permute-start.7 = (bf16[512,512]{1,0:T(8,128)(2,1)S(1)}, bf16[512,512]{1,0:T(8,128)(2,1)S(1)}, u32[]{:S(2)}, u32[]{:S(2)}) collective-permute-start(bf16[512,512]{1,0:T(8,128)(2,1)S(1)} %bitcast.6), channel_id=1, source_target_pairs={{0,1},{1,2},{2,3},{4,5},{5,6},{6,7},{8,9},{9,10},{10,11},{12,13},{... | collective-permute-start | bytes 1572872 | tf_op jit(solution)/shard_map/ppermute | solution.py:247
  117.3 0.0 collective-permute-done.10.refs_9_
  117.3 0.0 copy-done.7
  117.3 1.3 collective-permute-start.8
  118.6 0.0 copy-done.8
  118.6 4.1 %collective-permute-done.12.refs_12_ = bf16[512,512]{1,0:T(8,128)(2,1)} collective-permute-done((bf16[512,512]{1,0:T(8,128)(2,1)S(1)}, bf16[512,512]{1,0:T(8,128)(2,1)}, u32[]{:S(2)}, u32[]{:S(2)}) %collective-permute-start.12) | collective-permute-done | bytes 524320 | tf_op jit(solution)/shard_map/ppermute | solution.py:248
  122.7 1.5 collective-permute-start.19
  124.2 0.0 copy-done.10
  124.2 0.0 collective-permute-done.13.refs_3_
  124.2 1.3 collective-permute-start.20
  125.5 0.0 all-gather.4.cloned.1.call-update
  125.5 8.3 %collective-permute-done.14.refs_6_ = bf16[512,512]{1,0:T(8,128)(2,1)S(1)} collective-permute-done((bf16[512,512]{1,0:T(8,128)(2,1)S(1)}, bf16[512,512]{1,0:T(8,128)(2,1)S(1)}, u32[]{:S(2)}, u32[]{:S(2)}) %collective-permute-start.14) | collective-permute-done | bytes 524320 | tf_op jit(solution)/shard_map/ppermute | solution.py:248
  133.9 0.0 collective-permute-done.7.refs_1_
  133.9 0.0 copy-done.13
  133.9 0.0 copy-start.1
  133.9 11.2 %collective-permute-done.8.refs_4_ = bf16[512,512]{1,0:T(8,128)(2,1)S(1)} collective-permute-done((bf16[512,512]{1,0:T(8,128)(2,1)S(1)}, bf16[512,512]{1,0:T(8,128)(2,1)S(1)}, u32[]{:S(2)}, u32[]{:S(2)}) %collective-permute-start.8) | collective-permute-done | bytes 524320 | tf_op jit(solution)/shard_map/ppermute | solution.py:248
  145.1 1.3 collective-permute-start.16
  146.4 1.3 collective-permute-start.18
  147.7 0.7 collective-permute-start.15
  148.4 0.0 collective-permute-done.19.refs_10_
  148.4 1.5 collective-permute-start.17
  149.9 30.9 %collective-permute-done.20.refs_13_ = bf16[512,512]{1,0:T(8,128)(2,1)} collective-permute-done((bf16[512,512]{1,0:T(8,128)(2,1)}, bf16[512,512]{1,0:T(8,128)(2,1)}, u32[]{:S(2)}, u32[]{:S(2)}) %collective-permute-start.20) | collective-permute-done | bytes 524320 | tf_op jit(solution)/shard_map/ppermute | solution.py:248
  180.8 33.8 %shard_map.38.refs_10_ = bf16[64,128,1024]{2,1,0:T(8,128)(2,1)} custom-call(s32[1]{0:T(128)} %bitcast.own, bf16[512,512]{1,0:T(8,128)(2,1)} %bitcast.18, bf16[512,512]{1,0:T(8,128)(2,1)} %copy-done.8, bf16[512,512]{1,0:T(8,128)(2,1)} %copy-done.12, bf16[512,512]{1,0:T(8,128)(2,1)} %copy-done.14, bf16[512,512]{1,0:T(8,128)(2,1)} %copy-done.9, ...), custom_call_target="tpu_custom_call" | custom-call | flops 25769803776 | bytes 31457280 | tf_op jit(solution)/shard_map/pallas_call | solution.py:174
  214.6 0.0 collective-permute-done.16.refs_3_
  214.7 0.0 collective-permute-done.18.refs_6_
  214.7 0.0 collective-permute-done.15.refs_2_
  214.7 0.0 collective-permute-done.17.refs_5_
  214.7 0.8 copy-done.3
  215.5 0.2 copy-done.4
  215.6 0.2 copy-done.5
  215.8 18.7 %shard_map.39.refs_4_ = bf16[64,128,1024]{2,1,0:T(8,128)(2,1)} custom-call(s32[1]{0:T(128)} %bitcast.own, bf16[512,512]{1,0:T(8,128)(2,1)} %bitcast.10, bf16[512,512]{1,0:T(8,128)(2,1)} %copy-done.1, bf16[512,512]{1,0:T(8,128)(2,1)} %copy-done.5, bf16[512,512]{1,0:T(8,128)(2,1)} %copy-done.3, ...), custom_call_target="tpu_custom_call", output_to_operand_aliasing={{}: (11, {})} | custom-call | flops 12884901888 | bytes 25165824 | tf_op jit(solution)/shard_map/pallas_call | solution.py:174
  234.6 0.0 all-gather.4.cloned.1.call-done.refs_0_
  234.6 18.7 %shard_map.40 = bf16[64,128,1024]{2,1,0:T(8,128)(2,1)} custom-call(s32[1]{0:T(128)} %bitcast.own, bf16[512,2048]{1,0:T(8,128)(2,1)} %all-gather.4.cloned.1.call-done.refs_0_, bf16[2048,1024]{1,0:T(8,128)(2,1)} %all-gather.6.cloned.1.call-done.refs_14_.refs_7_.refs_1_, ...), custom_call_target="tpu_custom_call", output_to_operand_aliasing={{}: (5, {})} | custom-call | flops 12884901888 | bytes 25165824 | tf_op jit(solution)/shard_map/pallas_call | solution.py:174
  (27 shorter events, 0.1 us)
Async XLA Ops:
  6.5 174.3 %all-gather.6.cloned.1.call-start = ((), (), s32[]{:S(2)}) async-start(), calls=%async_computation.2 | async-start | bytes 4718592 | tf_op jit(solution)/shard_map/all_gather | solution.py:231
  10.9 44.2 %all-to-all-start = ((bf16[8,4,4,16,512]{4,3,2,1,0:T(8,128)(2,1)}), bf16[8,4,4,16,512]{4,3,2,1,0:T(8,128)(2,1)S(1)}, u32[]{:S(2)}, u32[]{:S(2)}) async-start(bf16[8,4,4,16,512]{4,3,2,1,0:T(8,128)(2,1)} %get-tuple-element.32), calls=%async_computation | async-start | bytes 4194304 | tf_op jit(solution)/shard_map/all_to_all | solution.py:227
  16.1 164.8 %all-gather.8.cloned.1.call-start = ((), (), s32[]{:S(2)}) async-start(), calls=%async_computation.3 | async-start | bytes 14155776 | tf_op jit(solution)/shard_map/all_gather | solution.py:231
  16.1 16.9 %collective-permute-start.2 = (bf16[256,1024]{1,0:T(8,128)(2,1)}, bf16[256,1024]{1,0:T(8,128)(2,1)S(1)}, u32[]{:S(2)}, u32[]{:S(2)}) collective-permute-start(bf16[256,1024]{1,0:T(8,128)(2,1)} %get-tuple-element.35), channel_id=1, source_target_pairs={{0,1},{1,2},{2,3},{3,0},{4,5},{5,6},{6,7},{7,4},{8,9},{9,10},{10,1... | collective-permute-start | bytes 1572872 | tf_op jit(solution)/shard_map/ppermute | solution.py:226
  17.7 37.3 %collective-permute-start.3 = (bf16[256,1024]{1,0:T(8,128)(2,1)}, bf16[256,1024]{1,0:T(8,128)(2,1)S(1)}, u32[]{:S(2)}, u32[]{:S(2)}) collective-permute-start(bf16[256,1024]{1,0:T(8,128)(2,1)} %get-tuple-element.36), channel_id=1, source_target_pairs={{0,2},{1,3},{2,0},{3,1},{4,6},{5,7},{6,4},{7,5},{8,10},{9,11},{10,... | collective-permute-start | bytes 1572872 | tf_op jit(solution)/shard_map/ppermute | solution.py:226
  20.3 34.7 %collective-permute-start.4 = (bf16[256,1024]{1,0:T(8,128)(2,1)}, bf16[256,1024]{1,0:T(8,128)(2,1)}, u32[]{:S(2)}, u32[]{:S(2)}) collective-permute-start(bf16[256,1024]{1,0:T(8,128)(2,1)} %get-tuple-element.37), channel_id=1, source_target_pairs={{0,3},{1,0},{2,1},{3,2},{4,7},{5,4},{6,5},{7,6},{8,11},{9,8},{10,9... | collective-permute-start | bytes 1572872 | tf_op jit(solution)/shard_map/ppermute | solution.py:226
  57.4 177.2 %all-gather.4.cloned.1.call-start = ((), (), s32[]{:S(2)}) async-start(), calls=%async_computation.1 | async-start | bytes 2621440 | tf_op jit(solution)/shard_map/all_gather | solution.py:277
  58.4 58.9 %copy-start.6 = (bf16[8,1,4,16,512]{4,3,2,1,0:T(8,128)(2,1)}, bf16[8,1,4,16,512]{4,3,2,1,0:T(8,128)(2,1)S(1)}, u32[]{:S(2)}) copy-start(bf16[8,1,4,16,512]{4,3,2,1,0:T(8,128)(2,1)S(1)} %get-tuple-element.59) | copy-start | bytes 1572868
  58.4 58.9 %copy-start.7 = (bf16[8,1,4,16,512]{4,3,2,1,0:T(8,128)(2,1)}, bf16[8,1,4,16,512]{4,3,2,1,0:T(8,128)(2,1)S(1)}, u32[]{:S(2)}) copy-start(bf16[8,1,4,16,512]{4,3,2,1,0:T(8,128)(2,1)S(1)} %get-tuple-element.62) | copy-start | bytes 1572868
  58.4 156.2 %copy-start = (bf16[8,1,4,16,512]{4,3,2,1,0:T(8,128)(2,1)}, bf16[8,1,4,16,512]{4,3,2,1,0:T(8,128)(2,1)S(1)}, u32[]{:S(2)}) copy-start(bf16[8,1,4,16,512]{4,3,2,1,0:T(8,128)(2,1)S(1)} %get-tuple-element.60) | copy-start | bytes 1572868
  58.4 26.0 %collective-permute-start = (bf16[512,512]{1,0:T(8,128)(2,1)S(1)}, bf16[512,512]{1,0:T(8,128)(2,1)S(1)}, u32[]{:S(2)}, u32[]{:S(2)}) collective-permute-start(bf16[512,512]{1,0:T(8,128)(2,1)S(1)} %bitcast.16), channel_id=1, source_target_pairs={{0,1},{1,2},{2,3},{4,5},{5,6},{6,7},{8,9},{9,10},{10,11},{12,13},{... | collective-permute-start | bytes 1572872 | tf_op jit(solution)/shard_map/ppermute | solution.py:247
  72.2 16.7 %collective-permute-start.1 = (bf16[512,512]{1,0:T(8,128)(2,1)S(1)}, bf16[512,512]{1,0:T(8,128)(2,1)S(1)}, u32[]{:S(2)}, u32[]{:S(2)}) collective-permute-start(bf16[512,512]{1,0:T(8,128)(2,1)S(1)} %bitcast.17), channel_id=1, source_target_pairs={{1,0},{2,1},{3,2},{5,4},{6,5},{7,6},{9,8},{10,9},{11,10},{13,12},{... | collective-permute-start | bytes 1572872 | tf_op jit(solution)/shard_map/ppermute | solution.py:248
  73.5 21.3 %collective-permute-start.9 = (bf16[512,512]{1,0:T(8,128)(2,1)S(1)}, bf16[512,512]{1,0:T(8,128)(2,1)S(1)}, u32[]{:S(2)}, u32[]{:S(2)}) collective-permute-start(bf16[512,512]{1,0:T(8,128)(2,1)S(1)} %bitcast.13), channel_id=1, source_target_pairs={{0,1},{1,2},{2,3},{4,5},{5,6},{6,7},{8,9},{9,10},{10,11},{12,13},{... | collective-permute-start | bytes 1572872 | tf_op jit(solution)/shard_map/ppermute | solution.py:247
  78.1 22.1 %collective-permute-start.11 = (bf16[512,512]{1,0:T(8,128)(2,1)S(1)}, bf16[512,512]{1,0:T(8,128)(2,1)S(1)}, u32[]{:S(2)}, u32[]{:S(2)}) collective-permute-start(bf16[512,512]{1,0:T(8,128)(2,1)S(1)} %bitcast.14), channel_id=1, source_target_pairs={{1,0},{2,1},{3,2},{5,4},{6,5},{7,6},{9,8},{10,9},{11,10},{13,12},{... | collective-permute-start | bytes 1572872 | tf_op jit(solution)/shard_map/ppermute | solution.py:248
  84.4 34.2 %copy-start.8 = (bf16[512,512]{1,0:T(8,128)(2,1)}, bf16[512,512]{1,0:T(8,128)(2,1)S(1)}, u32[]{:S(2)}) copy-start(bf16[512,512]{1,0:T(8,128)(2,1)S(1)} %collective-permute-done.refs_1_) | copy-start | bytes 1572868
  84.5 17.0 %collective-permute-start.5 = (bf16[512,512]{1,0:T(8,128)(2,1)S(1)}, bf16[512,512]{1,0:T(8,128)(2,1)S(1)}, u32[]{:S(2)}, u32[]{:S(2)}) collective-permute-start(bf16[512,512]{1,0:T(8,128)(2,1)S(1)} %collective-permute-done.refs_1_), channel_id=1, source_target_pairs={{1,2},{2,3},{5,6},{6,7},{9,10},{10,11},{13,14},{14,15},{17,18},{18... | collective-permute-start | bytes 1572872 | tf_op jit(solution)/shard_map/ppermute | solution.py:247
  88.9 33.8 %copy-start.9 = (bf16[512,512]{1,0:T(8,128)(2,1)}, bf16[512,512]{1,0:T(8,128)(2,1)S(1)}, u32[]{:S(2)}) copy-start(bf16[512,512]{1,0:T(8,128)(2,1)S(1)} %collective-permute-done.1.refs_4_) | copy-start | bytes 1572868
  88.9 22.5 %collective-permute-start.6 = (bf16[512,512]{1,0:T(8,128)(2,1)S(1)}, bf16[512,512]{1,0:T(8,128)(2,1)S(1)}, u32[]{:S(2)}, u32[]{:S(2)}) collective-permute-start(bf16[512,512]{1,0:T(8,128)(2,1)S(1)} %collective-permute-done.1.refs_4_), channel_id=1, source_target_pairs={{1,0},{2,1},{5,4},{6,5},{9,8},{10,9},{13,12},{14,13},{17,16},{18,1... | collective-permute-start | bytes 1572872 | tf_op jit(solution)/shard_map/ppermute | solution.py:248
  94.8 29.4 %copy-start.10 = (bf16[512,512]{1,0:T(8,128)(2,1)}, bf16[512,512]{1,0:T(8,128)(2,1)S(1)}, u32[]{:S(2)}) copy-start(bf16[512,512]{1,0:T(8,128)(2,1)S(1)} %collective-permute-done.9.refs_8_) | copy-start | bytes 1572868
  94.8 22.5 %collective-permute-start.10 = (bf16[512,512]{1,0:T(8,128)(2,1)S(1)}, bf16[512,512]{1,0:T(8,128)(2,1)}, u32[]{:S(2)}, u32[]{:S(2)}) collective-permute-start(bf16[512,512]{1,0:T(8,128)(2,1)S(1)} %collective-permute-done.9.refs_8_), channel_id=1, source_target_pairs={{1,2},{2,3},{5,6},{6,7},{9,10},{10,11},{13,14},{14,15},{17,18},{18... | collective-permute-start | bytes 1572872 | tf_op jit(solution)/shard_map/ppermute | solution.py:247
  100.1 24.0 %copy-start.11 = (bf16[512,512]{1,0:T(8,128)(2,1)}, bf16[512,512]{1,0:T(8,128)(2,1)S(1)}, u32[]{:S(2)}) copy-start(bf16[512,512]{1,0:T(8,128)(2,1)S(1)} %collective-permute-done.11.refs_11_) | copy-start | bytes 1572868
  100.2 22.6 %collective-permute-start.12 = (bf16[512,512]{1,0:T(8,128)(2,1)S(1)}, bf16[512,512]{1,0:T(8,128)(2,1)}, u32[]{:S(2)}, u32[]{:S(2)}) collective-permute-start(bf16[512,512]{1,0:T(8,128)(2,1)S(1)} %collective-permute-done.11.refs_11_), channel_id=1, source_target_pairs={{1,0},{2,1},{5,4},{6,5},{9,8},{10,9},{13,12},{14,13},{17,16},{18,1... | collective-permute-start | bytes 1572872 | tf_op jit(solution)/shard_map/ppermute | solution.py:248
  101.4 24.1 %copy-start.12 = (bf16[512,512]{1,0:T(8,128)(2,1)}, bf16[512,512]{1,0:T(8,128)(2,1)S(1)}, u32[]{:S(2)}) copy-start(bf16[512,512]{1,0:T(8,128)(2,1)S(1)} %collective-permute-done.5.refs_2_) | copy-start | bytes 1572868
  101.5 22.7 %collective-permute-start.13 = (bf16[512,512]{1,0:T(8,128)(2,1)S(1)}, bf16[512,512]{1,0:T(8,128)(2,1)S(1)}, u32[]{:S(2)}, u32[]{:S(2)}) collective-permute-start(bf16[512,512]{1,0:T(8,128)(2,1)S(1)} %collective-permute-done.5.refs_2_), channel_id=1, source_target_pairs={{2,3},{6,7},{10,11},{14,15},{18,19},{22,23},{26,27},{30,31}} | collective-permute-start | bytes 1572872 | tf_op jit(solution)/shard_map/ppermute | solution.py:247
  111.4 22.5 %copy-start.13 = (bf16[512,512]{1,0:T(8,128)(2,1)}, bf16[512,512]{1,0:T(8,128)(2,1)S(1)}, u32[]{:S(2)}) copy-start(bf16[512,512]{1,0:T(8,128)(2,1)S(1)} %collective-permute-done.6.refs_5_) | copy-start | bytes 1572868
  111.4 22.5 %collective-permute-start.14 = (bf16[512,512]{1,0:T(8,128)(2,1)S(1)}, bf16[512,512]{1,0:T(8,128)(2,1)S(1)}, u32[]{:S(2)}, u32[]{:S(2)}) collective-permute-start(bf16[512,512]{1,0:T(8,128)(2,1)S(1)} %collective-permute-done.6.refs_5_), channel_id=1, source_target_pairs={{1,0},{5,4},{9,8},{13,12},{17,16},{21,20},{25,24},{29,28}} | collective-permute-start | bytes 1572872 | tf_op jit(solution)/shard_map/ppermute | solution.py:248
  112.7 21.2 %collective-permute-start.7 = (bf16[512,512]{1,0:T(8,128)(2,1)S(1)}, bf16[512,512]{1,0:T(8,128)(2,1)S(1)}, u32[]{:S(2)}, u32[]{:S(2)}) collective-permute-start(bf16[512,512]{1,0:T(8,128)(2,1)S(1)} %bitcast.6), channel_id=1, source_target_pairs={{0,1},{1,2},{2,3},{4,5},{5,6},{6,7},{8,9},{9,10},{10,11},{12,13},{... | collective-permute-start | bytes 1572872 | tf_op jit(solution)/shard_map/ppermute | solution.py:247
  117.3 27.8 %collective-permute-start.8 = (bf16[512,512]{1,0:T(8,128)(2,1)S(1)}, bf16[512,512]{1,0:T(8,128)(2,1)S(1)}, u32[]{:S(2)}, u32[]{:S(2)}) collective-permute-start(bf16[512,512]{1,0:T(8,128)(2,1)S(1)} %bitcast.7), channel_id=1, source_target_pairs={{1,0},{2,1},{3,2},{5,4},{6,5},{7,6},{9,8},{10,9},{11,10},{13,12},{... | collective-permute-start | bytes 1572872 | tf_op jit(solution)/shard_map/ppermute | solution.py:248
  122.7 25.7 %collective-permute-start.19 = (bf16[512,512]{1,0:T(8,128)(2,1)}, bf16[512,512]{1,0:T(8,128)(2,1)}, u32[]{:S(2)}, u32[]{:S(2)}) collective-permute-start(bf16[512,512]{1,0:T(8,128)(2,1)} %collective-permute-done.10.refs_9_), channel_id=1, source_target_pairs={{2,3},{6,7},{10,11},{14,15},{18,19},{22,23},{26,27},{30,31}} | collective-permute-start | bytes 1572872 | tf_op jit(solution)/shard_map/ppermute | solution.py:247
  124.2 1.3 copy-start.14
  124.2 56.6 %collective-permute-start.20 = (bf16[512,512]{1,0:T(8,128)(2,1)}, bf16[512,512]{1,0:T(8,128)(2,1)}, u32[]{:S(2)}, u32[]{:S(2)}) collective-permute-start(bf16[512,512]{1,0:T(8,128)(2,1)} %collective-permute-done.12.refs_12_), channel_id=1, source_target_pairs={{1,0},{5,4},{9,8},{13,12},{17,16},{21,20},{25,24},{29,28}} | collective-permute-start | bytes 1572872 | tf_op jit(solution)/shard_map/ppermute | solution.py:248
  133.9 11.2 %copy-start.15 = (bf16[512,512]{1,0:T(8,128)(2,1)}, bf16[512,512]{1,0:T(8,128)(2,1)S(1)}, u32[]{:S(2)}) copy-start(bf16[512,512]{1,0:T(8,128)(2,1)S(1)} %collective-permute-done.14.refs_6_) | copy-start | bytes 1572868
  133.9 80.8 %copy-start.1 = (bf16[512,512]{1,0:T(8,128)(2,1)}, bf16[512,512]{1,0:T(8,128)(2,1)S(1)}, u32[]{:S(2)}) copy-start(bf16[512,512]{1,0:T(8,128)(2,1)S(1)} %collective-permute-done.7.refs_1_) | copy-start | bytes 1572868
  145.1 69.5 %copy-start.2 = (bf16[512,512]{1,0:T(8,128)(2,1)}, bf16[512,512]{1,0:T(8,128)(2,1)S(1)}, u32[]{:S(2)}) copy-start(bf16[512,512]{1,0:T(8,128)(2,1)S(1)} %collective-permute-done.8.refs_4_) | copy-start | bytes 1572868
  145.1 69.5 %collective-permute-start.16 = (bf16[512,512]{1,0:T(8,128)(2,1)S(1)}, bf16[512,512]{1,0:T(8,128)(2,1)S(1)}, u32[]{:S(2)}, u32[]{:S(2)}) collective-permute-start(bf16[512,512]{1,0:T(8,128)(2,1)S(1)} %bitcast.8), channel_id=1, source_target_pairs={{0,3},{4,7},{8,11},{12,15},{16,19},{20,23},{24,27},{28,31}} | collective-permute-start | bytes 1572872 | tf_op jit(solution)/shard_map/ppermute | solution.py:247
  146.4 68.2 %collective-permute-start.18 = (bf16[512,512]{1,0:T(8,128)(2,1)S(1)}, bf16[512,512]{1,0:T(8,128)(2,1)S(1)}, u32[]{:S(2)}, u32[]{:S(2)}) collective-permute-start(bf16[512,512]{1,0:T(8,128)(2,1)S(1)} %bitcast.9), channel_id=1, source_target_pairs={{3,0},{7,4},{11,8},{15,12},{19,16},{23,20},{27,24},{31,28}} | collective-permute-start | bytes 1572872 | tf_op jit(solution)/shard_map/ppermute | solution.py:248
  147.7 67.0 %collective-permute-start.15 = (bf16[512,512]{1,0:T(8,128)(2,1)S(1)}, bf16[512,512]{1,0:T(8,128)(2,1)S(1)}, u32[]{:S(2)}, u32[]{:S(2)}) collective-permute-start(bf16[512,512]{1,0:T(8,128)(2,1)S(1)} %collective-permute-done.7.refs_1_), channel_id=1, source_target_pairs={{1,2},{2,3},{5,6},{6,7},{9,10},{10,11},{13,14},{14,15},{17,18},{18... | collective-permute-start | bytes 1572872 | tf_op jit(solution)/shard_map/ppermute | solution.py:247
  148.4 66.3 %collective-permute-start.17 = (bf16[512,512]{1,0:T(8,128)(2,1)S(1)}, bf16[512,512]{1,0:T(8,128)(2,1)}, u32[]{:S(2)}, u32[]{:S(2)}) collective-permute-start(bf16[512,512]{1,0:T(8,128)(2,1)S(1)} %collective-permute-done.8.refs_4_), channel_id=1, source_target_pairs={{1,0},{2,1},{5,4},{6,5},{9,8},{10,9},{13,12},{14,13},{17,16},{18,1... | collective-permute-start | bytes 1572872 | tf_op jit(solution)/shard_map/ppermute | solution.py:248
  214.7 0.8 copy-start.3
  214.7 1.0 copy-start.4
  214.7 1.1 copy-start.5
Sparse Core Ops, SparseCore 0:
  11.0 50.2 all-gather.5
  63.2 76.9 all-gather.7
  141.8 69.7 all-gather.3

commit v10 on v9

--- a/solution.py
+++ b/solution.py
@@ -272,17 +272,15 @@
         for s in range(1, cols):
             for sides in early[q:q + 2]:
                 hop(sides, s)
-    first = early[0]
-    first[0][1], first[1][1] = after((first[0][1], first[1][1]), y)
-    last = lax.all_gather(y[0][0], "col", axis=1, tiled=True)
-
-    before = early[-2]
-    before[0][-2], before[1][-2] = after((before[0][-2], before[1][-2]), x)
+    ends = early[0]
+    ends[0][-1], ends[1][-1] = after((ends[0][-1], ends[1][-1]), x)
     for s in range(1, cols - 1):
         hop(x, s)
-    for sides, n in ((early[0], -1), (early[-1], -2), (x, 1)):
-        sides[0][n], sides[1][n] = after((sides[0][n], sides[1][n]), x)
+    x[0][1], x[1][1] = after((x[0][1], x[1][1]), x)
     hop(x, cols - 1, direct=True)
+    x[0][1], x[1][1] = after((x[0][1], x[1][1]), y)
+    last = lax.all_gather(y[0][0], "col", axis=1, tiled=True)
+
     update = functools.partial(chunk_update, own, a_local=a_local, b_local=b_local, occupied=occupied)
     out = None
     for q in range(0, len(early), 2):

time: 261 us -> 260 us (level)
  starting transfers between devices: 51.9 us -> 37.5 us
  waiting for transfers between devices: 115 us -> 128 us
    ppermute x9, starting transfers between devices: 29.3 us -> 15.8 us  [hop(): lax.ppermute(right[source], 'col', [(c, c + step) for c in range(first, c...]
    ppermute x3, waiting for transfers between devices: 33.4 us -> 44.7 us  [local(): lax.ppermute(arrived[s], 'col', [(c, (c + s) % cols) for c in range(cols)])]
    ppermute x9, waiting for transfers between devices: 71.5 us -> 74.2 us  [hop(): lax.ppermute(left[source], 'col', [(c + step, c) for c in range(cols - st...]
where the time goes in v10:
time: 260 us; the launch traced here: 259 us
  waiting for transfers between devices  128 us (49%)
  Pallas kernels  75.5 us (29%)
  starting transfers between devices  37.5 us (14%)
  between operations  13.5 us (5%)
    ppermute x9, waiting for transfers between devices, hop(): lax.ppermute(left[source], 'col', [(c + step, c) for c in range(cols - st...  74.2 us
    pallas_call x3, Pallas kernels, chunk_update(): pl.pallas_call(functools.partial(chunk_kernel, groups=groups, pieces=len(...  71.2 us
    ppermute x3, waiting for transfers between devices, local(): lax.ppermute(arrived[s], 'col', [(c, (c + s) % cols) for c in range(cols)])  44.7 us
    ppermute x9, starting transfers between devices, hop(): lax.ppermute(right[source], 'col', [(c, c + step) for c in range(first, c...  15.8 us
    ppermute x9, starting transfers between devices, hop(): lax.ppermute(left[source], 'col', [(c + step, c) for c in range(cols - st...  11.8 us
    ppermute x9, waiting for transfers between devices, hop(): lax.ppermute(right[source], 'col', [(c, c + step) for c in range(first, c...  9.49 us
    all_to_all x1, starting transfers between devices, local(): lax.all_to_all(blocks, 'row', split_axis=0, concat_axis=0, tiled=True)  5.21 us
  transfers between devices with their start and end apart: 25, of which 11 were waited for; matrix products, arithmetic and copies ran while one was open for 1% of the time, Pallas kernels for 20%

profile of v10, /device:TPU:0, one launch (start us, length us, event | category | flops | bytes accessed | tf_op | source)
XLA Modules:
  0.0 259.4 jit_solution(16526313421596140165)
XLA Ops:
  6.5 4.3 %shard_map.37 = (bf16[8,4,4,16,512]{4,3,2,1,0:T(8,128)(2,1)}, bf16[256,1024]{1,0:T(8,128)(2,1)}, bf16[256,1024]{1,0:T(8,128)(2,1)}, bf16[256,1024]{1,0:T(8,128)(2,1)}, bf16[256,1024]{1,0:T(8,128)(2,1)}) custom-call(s32[1]{0:T(128)} %bitcast.own, bf16[4,8,4,16,512]{4,3,2,1,0:T(8,128)(2,1)} %bitcast.11, bf16[256,4096]{1,0:T(8,128)(2,1)} %w_ref.1), custom_call_target="tpu_custom_call" | custom-call | bytes 8388608 | tf_op jit(solution)/shard_map/pallas_call | solution.py:46
  10.9 0.0 all-gather.6.cloned.1.call-update
  10.9 5.2 %all-to-all-start = ((bf16[8,4,4,16,512]{4,3,2,1,0:T(8,128)(2,1)}), bf16[8,4,4,16,512]{4,3,2,1,0:T(8,128)(2,1)S(1)}, u32[]{:S(2)}, u32[]{:S(2)}) async-start(bf16[8,4,4,16,512]{4,3,2,1,0:T(8,128)(2,1)} %get-tuple-element.24), calls=%async_computation | async-start | bytes 4194304 | tf_op jit(solution)/shard_map/all_to_all | solution.py:227
  16.1 0.0 all-gather.8.cloned.1.call-start
  16.1 3.6 %collective-permute-start.10 = (bf16[256,1024]{1,0:T(8,128)(2,1)}, bf16[256,1024]{1,0:T(8,128)(2,1)S(1)}, u32[]{:S(2)}, u32[]{:S(2)}) collective-permute-start(bf16[256,1024]{1,0:T(8,128)(2,1)} %get-tuple-element.33), channel_id=1, source_target_pairs={{0,3},{1,0},{2,1},{3,2},{4,7},{5,4},{6,5},{7,6},{8,11},{9,8},{10,9... | collective-permute-start | bytes 1572872 | tf_op jit(solution)/shard_map/ppermute | solution.py:226
  19.8 0.0 collective-permute-start.8
  19.8 1.0 collective-permute-start.9
  20.8 11.6 %collective-permute-done.10 = bf16[256,1024]{1,0:T(8,128)(2,1)S(1)} collective-permute-done((bf16[256,1024]{1,0:T(8,128)(2,1)}, bf16[256,1024]{1,0:T(8,128)(2,1)S(1)}, u32[]{:S(2)}, u32[]{:S(2)}) %collective-permute-start.10) | collective-permute-done | bytes 524320 | tf_op jit(solution)/shard_map/ppermute | solution.py:226
  32.4 12.1 %collective-permute-done.8 = bf16[256,1024]{1,0:T(8,128)(2,1)S(1)} collective-permute-done((bf16[256,1024]{1,0:T(8,128)(2,1)}, bf16[256,1024]{1,0:T(8,128)(2,1)S(1)}, u32[]{:S(2)}, u32[]{:S(2)}) %collective-permute-start.8) | collective-permute-done | bytes 524320 | tf_op jit(solution)/shard_map/ppermute | solution.py:226
  44.5 21.0 %collective-permute-done.9 = bf16[256,1024]{1,0:T(8,128)(2,1)} collective-permute-done((bf16[256,1024]{1,0:T(8,128)(2,1)}, bf16[256,1024]{1,0:T(8,128)(2,1)}, u32[]{:S(2)}, u32[]{:S(2)}) %collective-permute-start.9) | collective-permute-done | bytes 524320 | tf_op jit(solution)/shard_map/ppermute | solution.py:226
  65.5 0.0 all-to-all-done
  65.5 2.3 pad_maximum_fusion
  67.8 0.0 all-gather.8.cloned.1.call-update
  67.8 0.0 all-gather.4.cloned.1.call-start
  67.8 1.0 fusion
  68.8 1.8 collective-permute-start
  70.6 1.3 collective-permute-start.3
  71.9 9.5 %collective-permute-done.refs_1_ = bf16[512,512]{1,0:T(8,128)(2,1)S(1)} collective-permute-done((bf16[512,512]{1,0:T(8,128)(2,1)S(1)}, bf16[512,512]{1,0:T(8,128)(2,1)S(1)}, u32[]{:S(2)}, u32[]{:S(2)}) %collective-permute-start) | collective-permute-done | bytes 524320 | tf_op jit(solution)/shard_map/ppermute | solution.py:247
  81.4 0.7 collective-permute-start.1
  82.1 3.5 %collective-permute-done.3.refs_4_ = bf16[512,512]{1,0:T(8,128)(2,1)S(1)} collective-permute-done((bf16[512,512]{1,0:T(8,128)(2,1)S(1)}, bf16[512,512]{1,0:T(8,128)(2,1)S(1)}, u32[]{:S(2)}, u32[]{:S(2)}) %collective-permute-start.3) | collective-permute-done | bytes 524320 | tf_op jit(solution)/shard_map/ppermute | solution.py:248
  85.5 1.3 collective-permute-start.4
  86.8 4.6 %collective-permute-start.15 = (bf16[512,512]{1,0:T(8,128)(2,1)S(1)}, bf16[512,512]{1,0:T(8,128)(2,1)S(1)}, u32[]{:S(2)}, u32[]{:S(2)}) collective-permute-start(bf16[512,512]{1,0:T(8,128)(2,1)S(1)} %bitcast.13), channel_id=1, source_target_pairs={{0,1},{1,2},{2,3},{4,5},{5,6},{6,7},{8,9},{9,10},{10,11},{12,13},{... | collective-permute-start | bytes 1572872 | tf_op jit(solution)/shard_map/ppermute | solution.py:247
  91.4 1.3 collective-permute-start.18
  92.7 0.0 collective-permute-done.1.refs_2_
  92.7 0.7 collective-permute-start.2
  93.4 8.8 %collective-permute-done.4.refs_5_ = bf16[512,512]{1,0:T(8,128)(2,1)S(1)} collective-permute-done((bf16[512,512]{1,0:T(8,128)(2,1)S(1)}, bf16[512,512]{1,0:T(8,128)(2,1)S(1)}, u32[]{:S(2)}, u32[]{:S(2)}) %collective-permute-start.4) | collective-permute-done | bytes 524320 | tf_op jit(solution)/shard_map/ppermute | solution.py:248
  102.3 1.3 collective-permute-start.5
  103.6 0.0 collective-permute-done.15.refs_8_
  103.6 1.5 collective-permute-start.16
  105.1 8.5 %collective-permute-done.18.refs_11_ = bf16[512,512]{1,0:T(8,128)(2,1)S(1)} collective-permute-done((bf16[512,512]{1,0:T(8,128)(2,1)S(1)}, bf16[512,512]{1,0:T(8,128)(2,1)S(1)}, u32[]{:S(2)}, u32[]{:S(2)}) %collective-permute-start.18) | collective-permute-done | bytes 524320 | tf_op jit(solution)/shard_map/ppermute | solution.py:248
  113.5 1.3 collective-permute-start.19
  114.8 0.0 collective-permute-done.2.refs_3_
  114.8 0.0 copy-start.14
  114.8 9.9 %collective-permute-done.5.refs_6_ = bf16[512,512]{1,0:T(8,128)(2,1)S(1)} collective-permute-done((bf16[512,512]{1,0:T(8,128)(2,1)S(1)}, bf16[512,512]{1,0:T(8,128)(2,1)S(1)}, u32[]{:S(2)}, u32[]{:S(2)}) %collective-permute-start.5) | collective-permute-done | bytes 524320 | tf_op jit(solution)/shard_map/ppermute | solution.py:248
  124.8 1.5 collective-permute-start.6
  126.2 1.3 collective-permute-start.7
  127.5 0.0 collective-permute-done.16.refs_9_
  127.5 1.5 collective-permute-start.17
  129.0 7.1 %collective-permute-done.19.refs_12_ = bf16[512,512]{1,0:T(8,128)(2,1)} collective-permute-done((bf16[512,512]{1,0:T(8,128)(2,1)S(1)}, bf16[512,512]{1,0:T(8,128)(2,1)}, u32[]{:S(2)}, u32[]{:S(2)}) %collective-permute-start.19) | collective-permute-done | bytes 524320 | tf_op jit(solution)/shard_map/ppermute | solution.py:248
  136.1 1.3 collective-permute-start.20
  137.4 0.0 collective-permute-done.6.refs_1_
  137.4 9.8 %collective-permute-done.7.refs_4_ = bf16[512,512]{1,0:T(8,128)(2,1)S(1)} collective-permute-done((bf16[512,512]{1,0:T(8,128)(2,1)S(1)}, bf16[512,512]{1,0:T(8,128)(2,1)S(1)}, u32[]{:S(2)}, u32[]{:S(2)}) %collective-permute-start.7) | collective-permute-done | bytes 524320 | tf_op jit(solution)/shard_map/ppermute | solution.py:248
  147.2 2.9 %collective-permute-start.12 = (bf16[512,512]{1,0:T(8,128)(2,1)S(1)}, bf16[512,512]{1,0:T(8,128)(2,1)S(1)}, u32[]{:S(2)}, u32[]{:S(2)}) collective-permute-start(bf16[512,512]{1,0:T(8,128)(2,1)S(1)} %bitcast.8), channel_id=1, source_target_pairs={{0,3},{4,7},{8,11},{12,15},{16,19},{20,23},{24,27},{28,31}} | collective-permute-start | bytes 1572872 | tf_op jit(solution)/shard_map/ppermute | solution.py:247
  150.2 1.3 collective-permute-start.14
  151.6 0.0 all-gather.4.cloned.1.call-update
  151.6 0.7 collective-permute-start.11
  152.3 0.0 collective-permute-done.17.refs_10_
  152.3 1.5 collective-permute-start.13
  153.8 26.6 %collective-permute-done.20.refs_13_ = bf16[512,512]{1,0:T(8,128)(2,1)} collective-permute-done((bf16[512,512]{1,0:T(8,128)(2,1)}, bf16[512,512]{1,0:T(8,128)(2,1)}, u32[]{:S(2)}, u32[]{:S(2)}) %collective-permute-start.20) | collective-permute-done | bytes 524320 | tf_op jit(solution)/shard_map/ppermute | solution.py:248
  180.4 33.8 %shard_map.38.refs_10_ = bf16[64,128,1024]{2,1,0:T(8,128)(2,1)} custom-call(s32[1]{0:T(128)} %bitcast.own, bf16[512,512]{1,0:T(8,128)(2,1)} %bitcast.18, bf16[512,512]{1,0:T(8,128)(2,1)} %copy-done.8, bf16[512,512]{1,0:T(8,128)(2,1)} %copy-done.10, bf16[512,512]{1,0:T(8,128)(2,1)} %copy-done.14, bf16[512,512]{1,0:T(8,128)(2,1)} %copy-done.9, ...), custom_call_target="tpu_custom_call" | custom-call | flops 25769803776 | bytes 31457280 | tf_op jit(solution)/shard_map/pallas_call | solution.py:174
  214.1 0.0 copy-done
  214.2 0.0 copy-done.1
  214.2 0.0 copy-done.2
  214.2 0.0 collective-permute-done.12.refs_3_
  214.2 0.0 collective-permute-done.14.refs_6_
  214.2 0.0 collective-permute-done.11.refs_2_
  214.2 0.0 copy-start.5
  214.2 0.0 collective-permute-done.13.refs_5_
  214.2 0.8 copy-done.3
  215.0 0.2 copy-done.4
  215.2 0.2 copy-done.5
  215.4 18.7 %shard_map.39.refs_4_ = bf16[64,128,1024]{2,1,0:T(8,128)(2,1)} custom-call(s32[1]{0:T(128)} %bitcast.own, bf16[512,512]{1,0:T(8,128)(2,1)} %bitcast.10, bf16[512,512]{1,0:T(8,128)(2,1)} %copy-done.1, bf16[512,512]{1,0:T(8,128)(2,1)} %copy-done.5, bf16[512,512]{1,0:T(8,128)(2,1)} %copy-done.3, ...), custom_call_target="tpu_custom_call", output_to_operand_aliasing={{}: (11, {})} | custom-call | flops 12884901888 | bytes 25165824 | tf_op jit(solution)/shard_map/pallas_call | solution.py:174
  234.1 0.0 all-gather.4.cloned.1.call-done.refs_0_
  234.1 18.7 %shard_map.40 = bf16[64,128,1024]{2,1,0:T(8,128)(2,1)} custom-call(s32[1]{0:T(128)} %bitcast.own, bf16[512,2048]{1,0:T(8,128)(2,1)} %all-gather.4.cloned.1.call-done.refs_0_, bf16[2048,1024]{1,0:T(8,128)(2,1)} %all-gather.6.cloned.1.call-done.refs_14_.refs_7_.refs_1_, ...), custom_call_target="tpu_custom_call", output_to_operand_aliasing={{}: (5, {})} | custom-call | flops 12884901888 | bytes 25165824 | tf_op jit(solution)/shard_map/pallas_call | solution.py:174
  (27 shorter events, 0.1 us)
Async XLA Ops:
  6.5 173.8 %all-gather.6.cloned.1.call-start = ((), (), s32[]{:S(2)}) async-start(), calls=%async_computation.2 | async-start | bytes 4718592 | tf_op jit(solution)/shard_map/all_gather | solution.py:231
  10.9 54.6 %all-to-all-start = ((bf16[8,4,4,16,512]{4,3,2,1,0:T(8,128)(2,1)}), bf16[8,4,4,16,512]{4,3,2,1,0:T(8,128)(2,1)S(1)}, u32[]{:S(2)}, u32[]{:S(2)}) async-start(bf16[8,4,4,16,512]{4,3,2,1,0:T(8,128)(2,1)} %get-tuple-element.24), calls=%async_computation | async-start | bytes 4194304 | tf_op jit(solution)/shard_map/all_to_all | solution.py:227
  16.1 164.3 %all-gather.8.cloned.1.call-start = ((), (), s32[]{:S(2)}) async-start(), calls=%async_computation.3 | async-start | bytes 14155776 | tf_op jit(solution)/shard_map/all_gather | solution.py:231
  16.1 16.2 %collective-permute-start.10 = (bf16[256,1024]{1,0:T(8,128)(2,1)}, bf16[256,1024]{1,0:T(8,128)(2,1)S(1)}, u32[]{:S(2)}, u32[]{:S(2)}) collective-permute-start(bf16[256,1024]{1,0:T(8,128)(2,1)} %get-tuple-element.33), channel_id=1, source_target_pairs={{0,3},{1,0},{2,1},{3,2},{4,7},{5,4},{6,5},{7,6},{8,11},{9,8},{10,9... | collective-permute-start | bytes 1572872 | tf_op jit(solution)/shard_map/ppermute | solution.py:226
  19.8 24.7 %collective-permute-start.8 = (bf16[256,1024]{1,0:T(8,128)(2,1)}, bf16[256,1024]{1,0:T(8,128)(2,1)S(1)}, u32[]{:S(2)}, u32[]{:S(2)}) collective-permute-start(bf16[256,1024]{1,0:T(8,128)(2,1)} %get-tuple-element.31), channel_id=1, source_target_pairs={{0,1},{1,2},{2,3},{3,0},{4,5},{5,6},{6,7},{7,4},{8,9},{9,10},{10,1... | collective-permute-start | bytes 1572872 | tf_op jit(solution)/shard_map/ppermute | solution.py:226
  19.8 45.7 %collective-permute-start.9 = (bf16[256,1024]{1,0:T(8,128)(2,1)}, bf16[256,1024]{1,0:T(8,128)(2,1)}, u32[]{:S(2)}, u32[]{:S(2)}) collective-permute-start(bf16[256,1024]{1,0:T(8,128)(2,1)} %get-tuple-element.32), channel_id=1, source_target_pairs={{0,2},{1,3},{2,0},{3,1},{4,6},{5,7},{6,4},{7,5},{8,10},{9,11},{10,... | collective-permute-start | bytes 1572872 | tf_op jit(solution)/shard_map/ppermute | solution.py:226
  67.8 166.3 %all-gather.4.cloned.1.call-start = ((), (), s32[]{:S(2)}) async-start(), calls=%async_computation.1 | async-start | bytes 2621440 | tf_op jit(solution)/shard_map/all_gather | solution.py:282
  68.8 78.4 %copy-start.6 = (bf16[8,1,4,16,512]{4,3,2,1,0:T(8,128)(2,1)}, bf16[8,1,4,16,512]{4,3,2,1,0:T(8,128)(2,1)S(1)}, u32[]{:S(2)}) copy-start(bf16[8,1,4,16,512]{4,3,2,1,0:T(8,128)(2,1)S(1)} %get-tuple-element.43) | copy-start | bytes 1572868
  68.8 81.3 %copy-start.7 = (bf16[8,1,4,16,512]{4,3,2,1,0:T(8,128)(2,1)}, bf16[8,1,4,16,512]{4,3,2,1,0:T(8,128)(2,1)S(1)}, u32[]{:S(2)}) copy-start(bf16[8,1,4,16,512]{4,3,2,1,0:T(8,128)(2,1)S(1)} %get-tuple-element.46) | copy-start | bytes 1572868
  68.8 145.3 %copy-start = (bf16[8,1,4,16,512]{4,3,2,1,0:T(8,128)(2,1)}, bf16[8,1,4,16,512]{4,3,2,1,0:T(8,128)(2,1)S(1)}, u32[]{:S(2)}) copy-start(bf16[8,1,4,16,512]{4,3,2,1,0:T(8,128)(2,1)S(1)} %get-tuple-element.45) | copy-start | bytes 1572868
  68.8 12.5 %collective-permute-start = (bf16[512,512]{1,0:T(8,128)(2,1)S(1)}, bf16[512,512]{1,0:T(8,128)(2,1)S(1)}, u32[]{:S(2)}, u32[]{:S(2)}) collective-permute-start(bf16[512,512]{1,0:T(8,128)(2,1)S(1)} %bitcast.16), channel_id=1, source_target_pairs={{0,1},{1,2},{2,3},{4,5},{5,6},{6,7},{8,9},{9,10},{10,11},{12,13},{... | collective-permute-start | bytes 1572872 | tf_op jit(solution)/shard_map/ppermute | solution.py:247
  70.6 14.9 %collective-permute-start.3 = (bf16[512,512]{1,0:T(8,128)(2,1)S(1)}, bf16[512,512]{1,0:T(8,128)(2,1)S(1)}, u32[]{:S(2)}, u32[]{:S(2)}) collective-permute-start(bf16[512,512]{1,0:T(8,128)(2,1)S(1)} %bitcast.17), channel_id=1, source_target_pairs={{1,0},{2,1},{3,2},{5,4},{6,5},{7,6},{9,8},{10,9},{11,10},{13,12},{... | collective-permute-start | bytes 1572872 | tf_op jit(solution)/shard_map/ppermute | solution.py:248
  81.4 70.1 %copy-start.8 = (bf16[512,512]{1,0:T(8,128)(2,1)}, bf16[512,512]{1,0:T(8,128)(2,1)S(1)}, u32[]{:S(2)}) copy-start(bf16[512,512]{1,0:T(8,128)(2,1)S(1)} %collective-permute-done.refs_1_) | copy-start | bytes 1572868
  81.4 11.3 %collective-permute-start.1 = (bf16[512,512]{1,0:T(8,128)(2,1)S(1)}, bf16[512,512]{1,0:T(8,128)(2,1)S(1)}, u32[]{:S(2)}, u32[]{:S(2)}) collective-permute-start(bf16[512,512]{1,0:T(8,128)(2,1)S(1)} %collective-permute-done.refs_1_), channel_id=1, source_target_pairs={{1,2},{2,3},{5,6},{6,7},{9,10},{10,11},{13,14},{14,15},{17,18},{18... | collective-permute-start | bytes 1572872 | tf_op jit(solution)/shard_map/ppermute | solution.py:247
  85.5 66.0 %copy-start.9 = (bf16[512,512]{1,0:T(8,128)(2,1)}, bf16[512,512]{1,0:T(8,128)(2,1)S(1)}, u32[]{:S(2)}) copy-start(bf16[512,512]{1,0:T(8,128)(2,1)S(1)} %collective-permute-done.3.refs_4_) | copy-start | bytes 1572868
  85.5 16.8 %collective-permute-start.4 = (bf16[512,512]{1,0:T(8,128)(2,1)S(1)}, bf16[512,512]{1,0:T(8,128)(2,1)S(1)}, u32[]{:S(2)}, u32[]{:S(2)}) collective-permute-start(bf16[512,512]{1,0:T(8,128)(2,1)S(1)} %collective-permute-done.3.refs_4_), channel_id=1, source_target_pairs={{1,0},{2,1},{5,4},{6,5},{9,8},{10,9},{13,12},{14,13},{17,16},{18,1... | collective-permute-start | bytes 1572872 | tf_op jit(solution)/shard_map/ppermute | solution.py:248
  86.8 16.8 %collective-permute-start.15 = (bf16[512,512]{1,0:T(8,128)(2,1)S(1)}, bf16[512,512]{1,0:T(8,128)(2,1)S(1)}, u32[]{:S(2)}, u32[]{:S(2)}) collective-permute-start(bf16[512,512]{1,0:T(8,128)(2,1)S(1)} %bitcast.13), channel_id=1, source_target_pairs={{0,1},{1,2},{2,3},{4,5},{5,6},{6,7},{8,9},{9,10},{10,11},{12,13},{... | collective-permute-start | bytes 1572872 | tf_op jit(solution)/shard_map/ppermute | solution.py:247
  91.4 22.1 %collective-permute-start.18 = (bf16[512,512]{1,0:T(8,128)(2,1)S(1)}, bf16[512,512]{1,0:T(8,128)(2,1)S(1)}, u32[]{:S(2)}, u32[]{:S(2)}) collective-permute-start(bf16[512,512]{1,0:T(8,128)(2,1)S(1)} %bitcast.14), channel_id=1, source_target_pairs={{1,0},{2,1},{3,2},{5,4},{6,5},{7,6},{9,8},{10,9},{11,10},{13,12},{... | collective-permute-start | bytes 1572872 | tf_op jit(solution)/shard_map/ppermute | solution.py:248
  92.7 58.8 %copy-start.10 = (bf16[512,512]{1,0:T(8,128)(2,1)}, bf16[512,512]{1,0:T(8,128)(2,1)S(1)}, u32[]{:S(2)}) copy-start(bf16[512,512]{1,0:T(8,128)(2,1)S(1)} %collective-permute-done.1.refs_2_) | copy-start | bytes 1572868
  92.7 22.1 %collective-permute-start.2 = (bf16[512,512]{1,0:T(8,128)(2,1)S(1)}, bf16[512,512]{1,0:T(8,128)(2,1)S(1)}, u32[]{:S(2)}, u32[]{:S(2)}) collective-permute-start(bf16[512,512]{1,0:T(8,128)(2,1)S(1)} %collective-permute-done.1.refs_2_), channel_id=1, source_target_pairs={{2,3},{6,7},{10,11},{14,15},{18,19},{22,23},{26,27},{30,31}} | collective-permute-start | bytes 1572872 | tf_op jit(solution)/shard_map/ppermute | solution.py:247
  102.3 49.2 %copy-start.11 = (bf16[512,512]{1,0:T(8,128)(2,1)}, bf16[512,512]{1,0:T(8,128)(2,1)S(1)}, u32[]{:S(2)}) copy-start(bf16[512,512]{1,0:T(8,128)(2,1)S(1)} %collective-permute-done.4.refs_5_) | copy-start | bytes 1572868
  102.3 22.5 %collective-permute-start.5 = (bf16[512,512]{1,0:T(8,128)(2,1)S(1)}, bf16[512,512]{1,0:T(8,128)(2,1)S(1)}, u32[]{:S(2)}, u32[]{:S(2)}) collective-permute-start(bf16[512,512]{1,0:T(8,128)(2,1)S(1)} %collective-permute-done.4.refs_5_), channel_id=1, source_target_pairs={{1,0},{5,4},{9,8},{13,12},{17,16},{21,20},{25,24},{29,28}} | collective-permute-start | bytes 1572872 | tf_op jit(solution)/shard_map/ppermute | solution.py:248
  103.6 47.9 %copy-start.12 = (bf16[512,512]{1,0:T(8,128)(2,1)}, bf16[512,512]{1,0:T(8,128)(2,1)S(1)}, u32[]{:S(2)}) copy-start(bf16[512,512]{1,0:T(8,128)(2,1)S(1)} %collective-permute-done.15.refs_8_) | copy-start | bytes 1572868
  103.6 23.9 %collective-permute-start.16 = (bf16[512,512]{1,0:T(8,128)(2,1)S(1)}, bf16[512,512]{1,0:T(8,128)(2,1)}, u32[]{:S(2)}, u32[]{:S(2)}) collective-permute-start(bf16[512,512]{1,0:T(8,128)(2,1)S(1)} %collective-permute-done.15.refs_8_), channel_id=1, source_target_pairs={{1,2},{2,3},{5,6},{6,7},{9,10},{10,11},{13,14},{14,15},{17,18},{18... | collective-permute-start | bytes 1572872 | tf_op jit(solution)/shard_map/ppermute | solution.py:247
  113.5 38.0 %copy-start.13 = (bf16[512,512]{1,0:T(8,128)(2,1)}, bf16[512,512]{1,0:T(8,128)(2,1)S(1)}, u32[]{:S(2)}) copy-start(bf16[512,512]{1,0:T(8,128)(2,1)S(1)} %collective-permute-done.18.refs_11_) | copy-start | bytes 1572868
  113.5 22.6 %collective-permute-start.19 = (bf16[512,512]{1,0:T(8,128)(2,1)S(1)}, bf16[512,512]{1,0:T(8,128)(2,1)}, u32[]{:S(2)}, u32[]{:S(2)}) collective-permute-start(bf16[512,512]{1,0:T(8,128)(2,1)S(1)} %collective-permute-done.18.refs_11_), channel_id=1, source_target_pairs={{1,0},{2,1},{5,4},{6,5},{9,8},{10,9},{13,12},{14,13},{17,16},{18,1... | collective-permute-start | bytes 1572872 | tf_op jit(solution)/shard_map/ppermute | solution.py:248
  114.8 36.7 %copy-start.14 = (bf16[512,512]{1,0:T(8,128)(2,1)}, bf16[512,512]{1,0:T(8,128)(2,1)S(1)}, u32[]{:S(2)}) copy-start(bf16[512,512]{1,0:T(8,128)(2,1)S(1)} %collective-permute-done.2.refs_3_) | copy-start | bytes 1572868
  124.8 26.8 %copy-start.15 = (bf16[512,512]{1,0:T(8,128)(2,1)}, bf16[512,512]{1,0:T(8,128)(2,1)S(1)}, u32[]{:S(2)}) copy-start(bf16[512,512]{1,0:T(8,128)(2,1)S(1)} %collective-permute-done.5.refs_6_) | copy-start | bytes 1572868
  124.8 12.6 %collective-permute-start.6 = (bf16[512,512]{1,0:T(8,128)(2,1)S(1)}, bf16[512,512]{1,0:T(8,128)(2,1)S(1)}, u32[]{:S(2)}, u32[]{:S(2)}) collective-permute-start(bf16[512,512]{1,0:T(8,128)(2,1)S(1)} %bitcast.6), channel_id=1, source_target_pairs={{0,1},{1,2},{2,3},{4,5},{5,6},{6,7},{8,9},{9,10},{10,11},{12,13},{... | collective-permute-start | bytes 1572872 | tf_op jit(solution)/shard_map/ppermute | solution.py:247
  126.2 21.0 %collective-permute-start.7 = (bf16[512,512]{1,0:T(8,128)(2,1)S(1)}, bf16[512,512]{1,0:T(8,128)(2,1)S(1)}, u32[]{:S(2)}, u32[]{:S(2)}) collective-permute-start(bf16[512,512]{1,0:T(8,128)(2,1)S(1)} %bitcast.7), channel_id=1, source_target_pairs={{1,0},{2,1},{3,2},{5,4},{6,5},{7,6},{9,8},{10,9},{11,10},{13,12},{... | collective-permute-start | bytes 1572872 | tf_op jit(solution)/shard_map/ppermute | solution.py:248
  127.5 24.7 %collective-permute-start.17 = (bf16[512,512]{1,0:T(8,128)(2,1)}, bf16[512,512]{1,0:T(8,128)(2,1)}, u32[]{:S(2)}, u32[]{:S(2)}) collective-permute-start(bf16[512,512]{1,0:T(8,128)(2,1)} %collective-permute-done.16.refs_9_), channel_id=1, source_target_pairs={{2,3},{6,7},{10,11},{14,15},{18,19},{22,23},{26,27},{30,31}} | collective-permute-start | bytes 1572872 | tf_op jit(solution)/shard_map/ppermute | solution.py:247
  136.1 44.3 %collective-permute-start.20 = (bf16[512,512]{1,0:T(8,128)(2,1)}, bf16[512,512]{1,0:T(8,128)(2,1)}, u32[]{:S(2)}, u32[]{:S(2)}) collective-permute-start(bf16[512,512]{1,0:T(8,128)(2,1)} %collective-permute-done.19.refs_12_), channel_id=1, source_target_pairs={{1,0},{5,4},{9,8},{13,12},{17,16},{21,20},{25,24},{29,28}} | collective-permute-start | bytes 1572872 | tf_op jit(solution)/shard_map/ppermute | solution.py:248
  137.4 76.8 %copy-start.1 = (bf16[512,512]{1,0:T(8,128)(2,1)}, bf16[512,512]{1,0:T(8,128)(2,1)S(1)}, u32[]{:S(2)}) copy-start(bf16[512,512]{1,0:T(8,128)(2,1)S(1)} %collective-permute-done.6.refs_1_) | copy-start | bytes 1572868
  147.2 66.9 %copy-start.2 = (bf16[512,512]{1,0:T(8,128)(2,1)}, bf16[512,512]{1,0:T(8,128)(2,1)S(1)}, u32[]{:S(2)}) copy-start(bf16[512,512]{1,0:T(8,128)(2,1)S(1)} %collective-permute-done.7.refs_4_) | copy-start | bytes 1572868
  147.2 67.0 %collective-permute-start.12 = (bf16[512,512]{1,0:T(8,128)(2,1)S(1)}, bf16[512,512]{1,0:T(8,128)(2,1)S(1)}, u32[]{:S(2)}, u32[]{:S(2)}) collective-permute-start(bf16[512,512]{1,0:T(8,128)(2,1)S(1)} %bitcast.8), channel_id=1, source_target_pairs={{0,3},{4,7},{8,11},{12,15},{16,19},{20,23},{24,27},{28,31}} | collective-permute-start | bytes 1572872 | tf_op jit(solution)/shard_map/ppermute | solution.py:247
  150.2 64.0 %collective-permute-start.14 = (bf16[512,512]{1,0:T(8,128)(2,1)S(1)}, bf16[512,512]{1,0:T(8,128)(2,1)S(1)}, u32[]{:S(2)}, u32[]{:S(2)}) collective-permute-start(bf16[512,512]{1,0:T(8,128)(2,1)S(1)} %bitcast.9), channel_id=1, source_target_pairs={{3,0},{7,4},{11,8},{15,12},{19,16},{23,20},{27,24},{31,28}} | collective-permute-start | bytes 1572872 | tf_op jit(solution)/shard_map/ppermute | solution.py:248
  151.6 62.6 %collective-permute-start.11 = (bf16[512,512]{1,0:T(8,128)(2,1)S(1)}, bf16[512,512]{1,0:T(8,128)(2,1)S(1)}, u32[]{:S(2)}, u32[]{:S(2)}) collective-permute-start(bf16[512,512]{1,0:T(8,128)(2,1)S(1)} %collective-permute-done.6.refs_1_), channel_id=1, source_target_pairs={{1,2},{2,3},{5,6},{6,7},{9,10},{10,11},{13,14},{14,15},{17,18},{18... | collective-permute-start | bytes 1572872 | tf_op jit(solution)/shard_map/ppermute | solution.py:247
  152.3 61.9 %collective-permute-start.13 = (bf16[512,512]{1,0:T(8,128)(2,1)S(1)}, bf16[512,512]{1,0:T(8,128)(2,1)}, u32[]{:S(2)}, u32[]{:S(2)}) collective-permute-start(bf16[512,512]{1,0:T(8,128)(2,1)S(1)} %collective-permute-done.7.refs_4_), channel_id=1, source_target_pairs={{1,0},{2,1},{5,4},{6,5},{9,8},{10,9},{13,12},{14,13},{17,16},{18,1... | collective-permute-start | bytes 1572872 | tf_op jit(solution)/shard_map/ppermute | solution.py:248
  214.2 0.8 copy-start.3
  214.2 1.0 copy-start.4
  214.2 1.1 copy-start.5
Sparse Core Ops, SparseCore 0:
  11.0 50.2 all-gather.5
  67.9 72.5 all-gather.7
  151.7 61.0 all-gather.3

commit v11 on v10

--- a/solution.py
+++ b/solution.py
@@ -222,14 +222,17 @@
     chunks = a_local // GROUP
     blocks = amplitudes.reshape(i_local, rows, chunks, GROUP, depth)
     blocks, *arrived = cut(own, blocks, couplings, cols, j_local, b_local)
-    for s in range(1, cols):
+    shifts = sorted(range(1, cols), key=lambda s: min(s, cols - s))
+    for s in shifts:
         arrived[s] = lax.ppermute(arrived[s], "col", [(c, (c + s) % cols) for c in range(cols)])
     blocks = lax.all_to_all(blocks, "row", split_axis=0, concat_axis=0, tiled=True)
 
-    rest, _ = lax.optimization_barrier((arrived[1:], blocks))
-    panel_w = [
-        lax.all_gather(part, "row", axis=0, tiled=True) for part in (arrived[0], jnp.concatenate(rest, axis=1))
-    ]
+    *near, blocks = lax.optimization_barrier((*[arrived[s] for s in shifts[:-1]], blocks))
+    for s, part in zip(shifts, near):
+        arrived[s] = part
+
+    def gather_w(rest):
+        return [lax.all_gather(part, "row", axis=0, tiled=True) for part in (arrived[0], jnp.concatenate(rest, axis=1))]
 
     per_part = occupied // cols
     plain = (b_local % 128 or WIDE % b_local or depth % 128 or cols < 4
@@ -257,7 +260,7 @@
             for s in range(1, cols):
                 hop(sides, s)
         return jnp.concatenate(
-            [plain_update(own, flat(sides), panel_w, ladder, b_local, occupied) for sides in pieces], axis=0)
+            [plain_update(own, flat(sides), gather_w(arrived[1:]), ladder, b_local, occupied) for sides in pieces], axis=0)
 
     def after(done, sides):
         right, left = sides
@@ -272,12 +275,14 @@
         for s in range(1, cols):
             for sides in early[q:q + 2]:
                 hop(sides, s)
-    ends = early[0]
-    ends[0][-1], ends[1][-1] = after((ends[0][-1], ends[1][-1]), x)
-    for s in range(1, cols - 1):
+            if q == 0 and s == 1:
+                right, left = early[0]
+                rest, right[1], left[1] = lax.optimization_barrier((arrived[1:], right[1], left[1]))
+                panel_w = gather_w(rest)
+    right, left = early[-1]
+    right[-2], left[-2] = after((right[-2], left[-2]), x)
+    for s in range(1, cols):
         hop(x, s)
-    x[0][1], x[1][1] = after((x[0][1], x[1][1]), x)
-    hop(x, cols - 1, direct=True)
     x[0][1], x[1][1] = after((x[0][1], x[1][1]), y)
     last = lax.all_gather(y[0][0], "col", axis=1, tiled=True)
 

time: 260 us -> 289 us (1.11)
  waiting for transfers between devices: 128 us -> 148 us
  starting transfers between devices: 37.5 us -> 45.5 us
    ppermute x9, waiting for transfers between devices: 74.2 us -> 98.6 us  [hop(): lax.ppermute(left[source], 'col', [(c + step, c) for c in range(cols - st...]
    ppermute x3, waiting for transfers between devices: 44.7 us -> 29.2 us  [local(): lax.ppermute(arrived[s], 'col', [(c, (c + s) % cols) for c in range(cols)])]
    ppermute x9, starting transfers between devices: 15.8 us -> 23.6 us  [hop(): lax.ppermute(right[source], 'col', [(c, c + step) for c in range(first, c...]
    all_to_all x1, waiting for transfers between devices: 0.01 us -> 5.27 us  [local(): lax.all_to_all(blocks, 'row', split_axis=0, concat_axis=0, tiled=True)]
    ppermute x9, waiting for transfers between devices: 9.49 us -> 14.4 us  [hop(): lax.ppermute(right[source], 'col', [(c, c + step) for c in range(first, c...]
  transfers between devices with their start and end apart: 25 -> 25, of which waited for: 11 -> 14; matrix products, arithmetic and copies ran while one was open for 1% -> 1% of each run, Pallas kernels for 20% -> 18%
where the time goes in v11:
time: 289 us; the launch traced here: 288 us
  waiting for transfers between devices  148 us (51%)
  Pallas kernels  75.5 us (26%)
  starting transfers between devices  45.5 us (16%)
  between operations  13.5 us (5%)
  local copies, waits for them, and re-layouts  3.63 us (1%)
    ppermute x9, waiting for transfers between devices, hop(): lax.ppermute(left[source], 'col', [(c + step, c) for c in range(cols - st...  98.6 us
    pallas_call x3, Pallas kernels, chunk_update(): pl.pallas_call(functools.partial(chunk_kernel, groups=groups, pieces=len(...  71.2 us
    ppermute x3, waiting for transfers between devices, local(): lax.ppermute(arrived[s], 'col', [(c, (c + s) % cols) for c in range(cols)])  29.2 us
    ppermute x9, starting transfers between devices, hop(): lax.ppermute(right[source], 'col', [(c, c + step) for c in range(first, c...  23.6 us
    ppermute x9, waiting for transfers between devices, hop(): lax.ppermute(right[source], 'col', [(c, c + step) for c in range(first, c...  14.4 us
    ppermute x9, starting transfers between devices, hop(): lax.ppermute(left[source], 'col', [(c + step, c) for c in range(cols - st...  11.9 us
  transfers between devices with their start and end apart: 25, of which 14 were waited for; matrix products, arithmetic and copies ran while one was open for 1% of the time, Pallas kernels for 18%

profile of v11, /device:TPU:0, one launch (start us, length us, event | category | flops | bytes accessed | tf_op | source)
XLA Modules:
  0.0 288.5 jit_solution(885109283488208931)
XLA Ops:
  6.5 4.3 %shard_map.37 = (bf16[8,4,4,16,512]{4,3,2,1,0:T(8,128)(2,1)}, bf16[256,1024]{1,0:T(8,128)(2,1)}, bf16[256,1024]{1,0:T(8,128)(2,1)}, bf16[256,1024]{1,0:T(8,128)(2,1)}, bf16[256,1024]{1,0:T(8,128)(2,1)}) custom-call(s32[1]{0:T(128)} %bitcast.own, bf16[4,8,4,16,512]{4,3,2,1,0:T(8,128)(2,1)} %bitcast.9, bf16[256,4096]{1,0:T(8,128)(2,1)} %w_ref.1), custom_call_target="tpu_custom_call" | custom-call | bytes 8388608 | tf_op jit(solution)/shard_map/pallas_call | solution.py:46
  10.8 0.0 all-gather.6.cloned.1.call-update
  10.9 5.3 %all-to-all-start = ((bf16[8,4,4,16,512]{4,3,2,1,0:T(8,128)(2,1)}), bf16[8,4,4,16,512]{4,3,2,1,0:T(8,128)(2,1)S(1)}, u32[]{:S(2)}, u32[]{:S(2)}) async-start(bf16[8,4,4,16,512]{4,3,2,1,0:T(8,128)(2,1)} %get-tuple-element.27), calls=%async_computation | async-start | bytes 4194304 | tf_op jit(solution)/shard_map/all_to_all | solution.py:228
  16.2 0.0 all-gather.8.cloned.1.call-start
  16.2 1.6 collective-permute-start
  17.9 2.2 collective-permute-start.1
  20.1 0.8 collective-permute-start.8
  20.9 12.2 %collective-permute-done = bf16[256,1024]{1,0:T(8,128)(2,1)S(1)} collective-permute-done((bf16[256,1024]{1,0:T(8,128)(2,1)}, bf16[256,1024]{1,0:T(8,128)(2,1)S(1)}, u32[]{:S(2)}, u32[]{:S(2)}) %collective-permute-start) | collective-permute-done | bytes 524320 | tf_op jit(solution)/shard_map/ppermute | solution.py:227
  33.1 10.1 %collective-permute-done.1 = bf16[256,1024]{1,0:T(8,128)(2,1)} collective-permute-done((bf16[256,1024]{1,0:T(8,128)(2,1)S(1)}, bf16[256,1024]{1,0:T(8,128)(2,1)}, u32[]{:S(2)}, u32[]{:S(2)}) %collective-permute-start.1) | collective-permute-done | bytes 524320 | tf_op jit(solution)/shard_map/ppermute | solution.py:227
  43.2 5.3 %all-to-all-done = bf16[8,4,4,16,512]{4,3,2,1,0:T(8,128)(2,1)S(1)} async-done(((bf16[8,4,4,16,512]{4,3,2,1,0:T(8,128)(2,1)}), bf16[8,4,4,16,512]{4,3,2,1,0:T(8,128)(2,1)S(1)}, u32[]{:S(2)}, u32[]{:S(2)}) %all-to-all-start) | async-done | bytes 2097184 | tf_op jit(solution)/shard_map/all_to_all | solution.py:228
  48.5 1.2 fusion
  49.7 1.4 collective-permute-start.10
  51.1 0.0 copy-done.7
  51.1 8.5 %collective-permute-start.9 = (bf16[512,512]{1,0:T(8,128)(2,1)S(1)}, bf16[512,512]{1,0:T(8,128)(2,1)S(1)}, u32[]{:S(2)}, u32[]{:S(2)}) collective-permute-start(bf16[512,512]{1,0:T(8,128)(2,1)S(1)} %bitcast.12), channel_id=1, source_target_pairs={{0,1},{1,2},{2,3},{4,5},{5,6},{6,7},{8,9},{9,10},{10,11},{12,13},{... | collective-permute-start | bytes 1572872 | tf_op jit(solution)/shard_map/ppermute | solution.py:250
  59.6 7.0 %collective-permute-done.8 = bf16[256,1024]{1,0:T(8,128)(2,1)} collective-permute-done((bf16[256,1024]{1,0:T(8,128)(2,1)}, bf16[256,1024]{1,0:T(8,128)(2,1)}, u32[]{:S(2)}, u32[]{:S(2)}) %collective-permute-start.8) | collective-permute-done | bytes 524320 | tf_op jit(solution)/shard_map/ppermute | solution.py:227
  66.5 7.1 %collective-permute-done.10.refs_4_ = bf16[512,512]{1,0:T(8,128)(2,1)S(1)} collective-permute-done((bf16[512,512]{1,0:T(8,128)(2,1)S(1)}, bf16[512,512]{1,0:T(8,128)(2,1)S(1)}, u32[]{:S(2)}, u32[]{:S(2)}) %collective-permute-start.10) | collective-permute-done | bytes 524320 | tf_op jit(solution)/shard_map/ppermute | solution.py:251
  73.7 0.0 collective-permute-done.9.refs_1_
  73.7 2.8 pad_maximum_fusion
  76.5 0.0 all-gather.8.cloned.1.call-update
  76.5 0.0 all-gather.4.cloned.1.call-start
  76.6 6.4 %collective-permute-start.2 = (bf16[512,512]{1,0:T(8,128)(2,1)S(1)}, bf16[512,512]{1,0:T(8,128)(2,1)S(1)}, u32[]{:S(2)}, u32[]{:S(2)}) collective-permute-start(bf16[512,512]{1,0:T(8,128)(2,1)S(1)} %bitcast.15), channel_id=1, source_target_pairs={{0,1},{1,2},{2,3},{4,5},{5,6},{6,7},{8,9},{9,10},{10,11},{12,13},{... | collective-permute-start | bytes 1572872 | tf_op jit(solution)/shard_map/ppermute | solution.py:250
  83.0 1.3 collective-permute-start.4
  84.3 10.1 %collective-permute-done.2.refs_8_ = bf16[512,512]{1,0:T(8,128)(2,1)S(1)} collective-permute-done((bf16[512,512]{1,0:T(8,128)(2,1)S(1)}, bf16[512,512]{1,0:T(8,128)(2,1)S(1)}, u32[]{:S(2)}, u32[]{:S(2)}) %collective-permute-start.2) | collective-permute-done | bytes 524320 | tf_op jit(solution)/shard_map/ppermute | solution.py:250
  94.4 1.5 collective-permute-start.3
  95.9 2.7 collective-permute-done.4.refs_11_
  98.5 1.3 collective-permute-start.5
  99.8 0.7 collective-permute-start.15
  100.5 0.0 collective-permute-done.3.refs_9_
  100.5 12.8 %collective-permute-done.5.refs_12_ = bf16[512,512]{1,0:T(8,128)(2,1)} collective-permute-done((bf16[512,512]{1,0:T(8,128)(2,1)S(1)}, bf16[512,512]{1,0:T(8,128)(2,1)}, u32[]{:S(2)}, u32[]{:S(2)}) %collective-permute-start.5) | collective-permute-done | bytes 524320 | tf_op jit(solution)/shard_map/ppermute | solution.py:251
  113.3 3.0 %collective-permute-start.6 = (bf16[512,512]{1,0:T(8,128)(2,1)S(1)}, bf16[512,512]{1,0:T(8,128)(2,1)S(1)}, u32[]{:S(2)}, u32[]{:S(2)}) collective-permute-start(bf16[512,512]{1,0:T(8,128)(2,1)S(1)} %bitcast.6), channel_id=1, source_target_pairs={{0,1},{1,2},{2,3},{4,5},{5,6},{6,7},{8,9},{9,10},{10,11},{12,13},{... | collective-permute-start | bytes 1572872 | tf_op jit(solution)/shard_map/ppermute | solution.py:250
  116.3 0.0 copy-done
  116.4 1.3 collective-permute-start.7
  117.7 0.0 copy-done.9
  117.7 1.3 collective-permute-start.17
  119.0 0.0 collective-permute-done.15.refs_2_
  119.0 0.7 collective-permute-start.16
  119.7 1.5 collective-permute-start.19
  121.2 4.3 %collective-permute-done.6.refs_1_ = bf16[512,512]{1,0:T(8,128)(2,1)S(1)} collective-permute-done((bf16[512,512]{1,0:T(8,128)(2,1)S(1)}, bf16[512,512]{1,0:T(8,128)(2,1)S(1)}, u32[]{:S(2)}, u32[]{:S(2)}) %collective-permute-start.6) | collective-permute-done | bytes 524320 | tf_op jit(solution)/shard_map/ppermute | solution.py:250
  125.4 0.7 collective-permute-start.11
  126.1 7.0 %collective-permute-done.7.refs_4_ = bf16[512,512]{1,0:T(8,128)(2,1)S(1)} collective-permute-done((bf16[512,512]{1,0:T(8,128)(2,1)S(1)}, bf16[512,512]{1,0:T(8,128)(2,1)S(1)}, u32[]{:S(2)}, u32[]{:S(2)}) %collective-permute-start.7) | collective-permute-done | bytes 524320 | tf_op jit(solution)/shard_map/ppermute | solution.py:251
  133.1 1.3 collective-permute-start.13
  134.4 10.1 %collective-permute-done.17.refs_5_ = bf16[512,512]{1,0:T(8,128)(2,1)} collective-permute-done((bf16[512,512]{1,0:T(8,128)(2,1)S(1)}, bf16[512,512]{1,0:T(8,128)(2,1)}, u32[]{:S(2)}, u32[]{:S(2)}) %collective-permute-start.17) | collective-permute-done | bytes 524320 | tf_op jit(solution)/shard_map/ppermute | solution.py:251
  144.4 1.3 collective-permute-start.18
  145.7 0.0 collective-permute-done.16.refs_3_
  145.8 0.0 copy-start.14
  145.8 0.8 copy-done.14
  146.6 1.3 collective-permute-start.20
  147.8 0.0 all-gather.4.cloned.1.call-update
  147.9 0.0 collective-permute-done.11.refs_2_
  147.9 0.7 collective-permute-start.12
  148.6 7.0 %collective-permute-done.13.refs_5_ = bf16[512,512]{1,0:T(8,128)(2,1)S(1)} collective-permute-done((bf16[512,512]{1,0:T(8,128)(2,1)S(1)}, bf16[512,512]{1,0:T(8,128)(2,1)S(1)}, u32[]{:S(2)}, u32[]{:S(2)}) %collective-permute-start.13) | collective-permute-done | bytes 524320 | tf_op jit(solution)/shard_map/ppermute | solution.py:251
  155.6 1.5 collective-permute-start.14
  157.0 17.4 %collective-permute-done.18.refs_6_ = bf16[512,512]{1,0:T(8,128)(2,1)} collective-permute-done((bf16[512,512]{1,0:T(8,128)(2,1)}, bf16[512,512]{1,0:T(8,128)(2,1)}, u32[]{:S(2)}, u32[]{:S(2)}) %collective-permute-start.18) | collective-permute-done | bytes 524320 | tf_op jit(solution)/shard_map/ppermute | solution.py:251
  174.4 0.0 collective-permute-done.19.refs_10_
  174.5 34.6 %collective-permute-done.20.refs_13_ = bf16[512,512]{1,0:T(8,128)(2,1)} collective-permute-done((bf16[512,512]{1,0:T(8,128)(2,1)}, bf16[512,512]{1,0:T(8,128)(2,1)}, u32[]{:S(2)}, u32[]{:S(2)}) %collective-permute-start.20) | collective-permute-done | bytes 524320 | tf_op jit(solution)/shard_map/ppermute | solution.py:251
  209.0 33.7 %shard_map.38.refs_10_ = bf16[64,128,1024]{2,1,0:T(8,128)(2,1)} custom-call(s32[1]{0:T(128)} %bitcast.own, bf16[512,512]{1,0:T(8,128)(2,1)} %bitcast.13, bf16[512,512]{1,0:T(8,128)(2,1)} %copy-done.10, bf16[512,512]{1,0:T(8,128)(2,1)} %copy-done.13, bf16[512,512]{1,0:T(8,128)(2,1)} %copy-done.14, bf16[512,512]{1,0:T(8,128)(2,1)} %copy-done.9, ...), custom_call_target="tpu_custom_call" | custom-call | flops 25769803776 | bytes 31457280 | tf_op jit(solution)/shard_map/pallas_call | solution.py:174
  242.8 0.0 collective-permute-done.12.refs_3_
  242.8 0.0 copy-start.5
  242.8 0.0 collective-permute-done.14.refs_6_
  242.8 0.8 copy-done.5
  243.6 0.8 copy-done.6
  244.4 18.7 %shard_map.39.refs_4_ = bf16[64,128,1024]{2,1,0:T(8,128)(2,1)} custom-call(s32[1]{0:T(128)} %bitcast.own, bf16[512,512]{1,0:T(8,128)(2,1)} %bitcast.8, bf16[512,512]{1,0:T(8,128)(2,1)} %copy-done.1, bf16[512,512]{1,0:T(8,128)(2,1)} %copy-done.3, bf16[512,512]{1,0:T(8,128)(2,1)} %copy-done.5, ...), custom_call_target="tpu_custom_call", output_to_operand_aliasing={{}: (11, {})} | custom-call | flops 12884901888 | bytes 25165824 | tf_op jit(solution)/shard_map/pallas_call | solution.py:174
  263.2 0.0 all-gather.4.cloned.1.call-done.refs_0_
  263.2 18.7 %shard_map.40 = bf16[64,128,1024]{2,1,0:T(8,128)(2,1)} custom-call(s32[1]{0:T(128)} %bitcast.own, bf16[512,2048]{1,0:T(8,128)(2,1)} %all-gather.4.cloned.1.call-done.refs_0_, bf16[2048,1024]{1,0:T(8,128)(2,1)} %all-gather.6.cloned.1.call-done.refs_14_.refs_7_.refs_1_, ...), custom_call_target="tpu_custom_call", output_to_operand_aliasing={{}: (5, {})} | custom-call | flops 12884901888 | bytes 25165824 | tf_op jit(solution)/shard_map/pallas_call | solution.py:174
  (27 shorter events, 0.0 us)
Async XLA Ops:
  6.5 202.5 %all-gather.6.cloned.1.call-start = ((), (), s32[]{:S(2)}) async-start(), calls=%async_computation.2 | async-start | bytes 4718592 | tf_op jit(solution)/shard_map/all_gather | solution.py:235
  10.9 7.0 %copy-start.15 = (bf16[256,1024]{1,0:T(8,128)(2,1)S(1)}, bf16[256,1024]{1,0:T(8,128)(2,1)}, u32[]{:S(2)}) copy-start(bf16[256,1024]{1,0:T(8,128)(2,1)} %get-tuple-element.26) | copy-start | bytes 1572868
  10.9 37.6 %all-to-all-start = ((bf16[8,4,4,16,512]{4,3,2,1,0:T(8,128)(2,1)}), bf16[8,4,4,16,512]{4,3,2,1,0:T(8,128)(2,1)S(1)}, u32[]{:S(2)}, u32[]{:S(2)}) async-start(bf16[8,4,4,16,512]{4,3,2,1,0:T(8,128)(2,1)} %get-tuple-element.27), calls=%async_computation | async-start | bytes 4194304 | tf_op jit(solution)/shard_map/all_to_all | solution.py:228
  16.2 192.8 %all-gather.8.cloned.1.call-start = ((), (), s32[]{:S(2)}) async-start(), calls=%async_computation.3 | async-start | bytes 14155776 | tf_op jit(solution)/shard_map/all_gather | solution.py:235
  16.2 16.8 %collective-permute-start = (bf16[256,1024]{1,0:T(8,128)(2,1)}, bf16[256,1024]{1,0:T(8,128)(2,1)S(1)}, u32[]{:S(2)}, u32[]{:S(2)}) collective-permute-start(bf16[256,1024]{1,0:T(8,128)(2,1)} %get-tuple-element.25), channel_id=1, source_target_pairs={{0,1},{1,2},{2,3},{3,0},{4,5},{5,6},{6,7},{7,4},{8,9},{9,10},{10,1... | collective-permute-start | bytes 1572872 | tf_op jit(solution)/shard_map/ppermute | solution.py:227
  17.9 25.3 %collective-permute-start.1 = (bf16[256,1024]{1,0:T(8,128)(2,1)S(1)}, bf16[256,1024]{1,0:T(8,128)(2,1)}, u32[]{:S(2)}, u32[]{:S(2)}) collective-permute-start(bf16[256,1024]{1,0:T(8,128)(2,1)S(1)} %copy-done.15), channel_id=1, source_target_pairs={{0,3},{1,0},{2,1},{3,2},{4,7},{5,4},{6,5},{7,6},{8,11},{9,8},{10,9... | collective-permute-start | bytes 1572872 | tf_op jit(solution)/shard_map/ppermute | solution.py:227
  20.1 46.4 %collective-permute-start.8 = (bf16[256,1024]{1,0:T(8,128)(2,1)}, bf16[256,1024]{1,0:T(8,128)(2,1)}, u32[]{:S(2)}, u32[]{:S(2)}) collective-permute-start(bf16[256,1024]{1,0:T(8,128)(2,1)} %get-tuple-element.34), channel_id=1, source_target_pairs={{0,2},{1,3},{2,0},{3,1},{4,6},{5,7},{6,4},{7,5},{8,10},{9,11},{10,... | collective-permute-start | bytes 1572872 | tf_op jit(solution)/shard_map/ppermute | solution.py:227
  49.7 1.4 copy-start.7
  49.7 66.7 %copy-start = (bf16[8,1,4,16,512]{4,3,2,1,0:T(8,128)(2,1)}, bf16[8,1,4,16,512]{4,3,2,1,0:T(8,128)(2,1)S(1)}, u32[]{:S(2)}) copy-start(bf16[8,1,4,16,512]{4,3,2,1,0:T(8,128)(2,1)S(1)} %get-tuple-element.47) | copy-start | bytes 1572868
  49.7 26.9 %copy-start.8 = (bf16[8,1,4,16,512]{4,3,2,1,0:T(8,128)(2,1)S(1)}, bf16[8,1,4,16,512]{4,3,2,1,0:T(8,128)(2,1)}, u32[]{:S(2)}) copy-start(bf16[8,1,4,16,512]{4,3,2,1,0:T(8,128)(2,1)} %get-tuple-element.48) | copy-start | bytes 1572868
  49.7 24.0 %collective-permute-start.10 = (bf16[512,512]{1,0:T(8,128)(2,1)S(1)}, bf16[512,512]{1,0:T(8,128)(2,1)S(1)}, u32[]{:S(2)}, u32[]{:S(2)}) collective-permute-start(bf16[512,512]{1,0:T(8,128)(2,1)S(1)} %bitcast.11), channel_id=1, source_target_pairs={{1,0},{2,1},{3,2},{5,4},{6,5},{7,6},{9,8},{10,9},{11,10},{13,12},{... | collective-permute-start | bytes 1572872 | tf_op jit(solution)/shard_map/ppermute | solution.py:251
  51.1 22.6 %collective-permute-start.9 = (bf16[512,512]{1,0:T(8,128)(2,1)S(1)}, bf16[512,512]{1,0:T(8,128)(2,1)S(1)}, u32[]{:S(2)}, u32[]{:S(2)}) collective-permute-start(bf16[512,512]{1,0:T(8,128)(2,1)S(1)} %bitcast.12), channel_id=1, source_target_pairs={{0,1},{1,2},{2,3},{4,5},{5,6},{6,7},{8,9},{9,10},{10,11},{12,13},{... | collective-permute-start | bytes 1572872 | tf_op jit(solution)/shard_map/ppermute | solution.py:250
  73.7 44.0 %copy-start.9 = (bf16[512,512]{1,0:T(8,128)(2,1)}, bf16[512,512]{1,0:T(8,128)(2,1)S(1)}, u32[]{:S(2)}) copy-start(bf16[512,512]{1,0:T(8,128)(2,1)S(1)} %collective-permute-done.10.refs_4_) | copy-start | bytes 1572868
  73.7 26.1 %copy-start.10 = (bf16[512,512]{1,0:T(8,128)(2,1)}, bf16[512,512]{1,0:T(8,128)(2,1)S(1)}, u32[]{:S(2)}) copy-start(bf16[512,512]{1,0:T(8,128)(2,1)S(1)} %collective-permute-done.9.refs_1_) | copy-start | bytes 1572868
  76.5 186.7 %all-gather.4.cloned.1.call-start = ((), (), s32[]{:S(2)}) async-start(), calls=%async_computation.1 | async-start | bytes 2621440 | tf_op jit(solution)/shard_map/all_gather | solution.py:287
  76.6 17.8 %collective-permute-start.2 = (bf16[512,512]{1,0:T(8,128)(2,1)S(1)}, bf16[512,512]{1,0:T(8,128)(2,1)S(1)}, u32[]{:S(2)}, u32[]{:S(2)}) collective-permute-start(bf16[512,512]{1,0:T(8,128)(2,1)S(1)} %bitcast.15), channel_id=1, source_target_pairs={{0,1},{1,2},{2,3},{4,5},{5,6},{6,7},{8,9},{9,10},{10,11},{12,13},{... | collective-permute-start | bytes 1572872 | tf_op jit(solution)/shard_map/ppermute | solution.py:250
  83.0 15.5 %collective-permute-start.4 = (bf16[512,512]{1,0:T(8,128)(2,1)S(1)}, bf16[512,512]{1,0:T(8,128)(2,1)S(1)}, u32[]{:S(2)}, u32[]{:S(2)}) collective-permute-start(bf16[512,512]{1,0:T(8,128)(2,1)S(1)} %bitcast.16), channel_id=1, source_target_pairs={{1,0},{2,1},{3,2},{5,4},{6,5},{7,6},{9,8},{10,9},{11,10},{13,12},{... | collective-permute-start | bytes 1572872 | tf_op jit(solution)/shard_map/ppermute | solution.py:251
  94.4 19.0 %copy-start.11 = (bf16[512,512]{1,0:T(8,128)(2,1)}, bf16[512,512]{1,0:T(8,128)(2,1)S(1)}, u32[]{:S(2)}) copy-start(bf16[512,512]{1,0:T(8,128)(2,1)S(1)} %collective-permute-done.2.refs_8_) | copy-start | bytes 1572868
  94.4 6.1 %collective-permute-start.3 = (bf16[512,512]{1,0:T(8,128)(2,1)S(1)}, bf16[512,512]{1,0:T(8,128)(2,1)}, u32[]{:S(2)}, u32[]{:S(2)}) collective-permute-start(bf16[512,512]{1,0:T(8,128)(2,1)S(1)} %collective-permute-done.2.refs_8_), channel_id=1, source_target_pairs={{1,2},{2,3},{5,6},{6,7},{9,10},{10,11},{13,14},{14,15},{17,18},{18... | collective-permute-start | bytes 1572872 | tf_op jit(solution)/shard_map/ppermute | solution.py:250
  98.5 45.9 %copy-start.12 = (bf16[512,512]{1,0:T(8,128)(2,1)}, bf16[512,512]{1,0:T(8,128)(2,1)S(1)}, u32[]{:S(2)}) copy-start(bf16[512,512]{1,0:T(8,128)(2,1)S(1)} %collective-permute-done.4.refs_11_) | copy-start | bytes 1572868
  98.5 14.8 %collective-permute-start.5 = (bf16[512,512]{1,0:T(8,128)(2,1)S(1)}, bf16[512,512]{1,0:T(8,128)(2,1)}, u32[]{:S(2)}, u32[]{:S(2)}) collective-permute-start(bf16[512,512]{1,0:T(8,128)(2,1)S(1)} %collective-permute-done.4.refs_11_), channel_id=1, source_target_pairs={{1,0},{2,1},{5,4},{6,5},{9,8},{10,9},{13,12},{14,13},{17,16},{18,1... | collective-permute-start | bytes 1572872 | tf_op jit(solution)/shard_map/ppermute | solution.py:251
  99.8 19.1 %collective-permute-start.15 = (bf16[512,512]{1,0:T(8,128)(2,1)S(1)}, bf16[512,512]{1,0:T(8,128)(2,1)S(1)}, u32[]{:S(2)}, u32[]{:S(2)}) collective-permute-start(bf16[512,512]{1,0:T(8,128)(2,1)S(1)} %collective-permute-done.9.refs_1_), channel_id=1, source_target_pairs={{1,2},{2,3},{5,6},{6,7},{9,10},{10,11},{13,14},{14,15},{17,18},{18... | collective-permute-start | bytes 1572872 | tf_op jit(solution)/shard_map/ppermute | solution.py:250
  113.3 12.1 %collective-permute-start.6 = (bf16[512,512]{1,0:T(8,128)(2,1)S(1)}, bf16[512,512]{1,0:T(8,128)(2,1)S(1)}, u32[]{:S(2)}, u32[]{:S(2)}) collective-permute-start(bf16[512,512]{1,0:T(8,128)(2,1)S(1)} %bitcast.6), channel_id=1, source_target_pairs={{0,1},{1,2},{2,3},{4,5},{5,6},{6,7},{8,9},{9,10},{10,11},{12,13},{... | collective-permute-start | bytes 1572872 | tf_op jit(solution)/shard_map/ppermute | solution.py:250
  116.4 16.8 %collective-permute-start.7 = (bf16[512,512]{1,0:T(8,128)(2,1)S(1)}, bf16[512,512]{1,0:T(8,128)(2,1)S(1)}, u32[]{:S(2)}, u32[]{:S(2)}) collective-permute-start(bf16[512,512]{1,0:T(8,128)(2,1)S(1)} %bitcast.7), channel_id=1, source_target_pairs={{1,0},{2,1},{3,2},{5,4},{6,5},{7,6},{9,8},{10,9},{11,10},{13,12},{... | collective-permute-start | bytes 1572872 | tf_op jit(solution)/shard_map/ppermute | solution.py:251
  117.7 26.8 %collective-permute-start.17 = (bf16[512,512]{1,0:T(8,128)(2,1)S(1)}, bf16[512,512]{1,0:T(8,128)(2,1)}, u32[]{:S(2)}, u32[]{:S(2)}) collective-permute-start(bf16[512,512]{1,0:T(8,128)(2,1)S(1)} %collective-permute-done.10.refs_4_), channel_id=1, source_target_pairs={{1,0},{2,1},{5,4},{6,5},{9,8},{10,9},{13,12},{14,13},{17,16},{18,1... | collective-permute-start | bytes 1572872 | tf_op jit(solution)/shard_map/ppermute | solution.py:251
  119.0 26.8 %copy-start.13 = (bf16[512,512]{1,0:T(8,128)(2,1)}, bf16[512,512]{1,0:T(8,128)(2,1)S(1)}, u32[]{:S(2)}) copy-start(bf16[512,512]{1,0:T(8,128)(2,1)S(1)} %collective-permute-done.15.refs_2_) | copy-start | bytes 1572868
  119.0 26.8 %collective-permute-start.16 = (bf16[512,512]{1,0:T(8,128)(2,1)S(1)}, bf16[512,512]{1,0:T(8,128)(2,1)S(1)}, u32[]{:S(2)}, u32[]{:S(2)}) collective-permute-start(bf16[512,512]{1,0:T(8,128)(2,1)S(1)} %collective-permute-done.15.refs_2_), channel_id=1, source_target_pairs={{2,3},{6,7},{10,11},{14,15},{18,19},{22,23},{26,27},{30,31}} | collective-permute-start | bytes 1572872 | tf_op jit(solution)/shard_map/ppermute | solution.py:250
  119.7 54.8 %collective-permute-start.19 = (bf16[512,512]{1,0:T(8,128)(2,1)}, bf16[512,512]{1,0:T(8,128)(2,1)}, u32[]{:S(2)}, u32[]{:S(2)}) collective-permute-start(bf16[512,512]{1,0:T(8,128)(2,1)} %collective-permute-done.3.refs_9_), channel_id=1, source_target_pairs={{2,3},{6,7},{10,11},{14,15},{18,19},{22,23},{26,27},{30,31}} | collective-permute-start | bytes 1572872 | tf_op jit(solution)/shard_map/ppermute | solution.py:250
  125.4 117.3 %copy-start.1 = (bf16[512,512]{1,0:T(8,128)(2,1)}, bf16[512,512]{1,0:T(8,128)(2,1)S(1)}, u32[]{:S(2)}) copy-start(bf16[512,512]{1,0:T(8,128)(2,1)S(1)} %collective-permute-done.6.refs_1_) | copy-start | bytes 1572868
  125.4 22.4 %collective-permute-start.11 = (bf16[512,512]{1,0:T(8,128)(2,1)S(1)}, bf16[512,512]{1,0:T(8,128)(2,1)S(1)}, u32[]{:S(2)}, u32[]{:S(2)}) collective-permute-start(bf16[512,512]{1,0:T(8,128)(2,1)S(1)} %collective-permute-done.6.refs_1_), channel_id=1, source_target_pairs={{1,2},{2,3},{5,6},{6,7},{9,10},{10,11},{13,14},{14,15},{17,18},{18... | collective-permute-start | bytes 1572872 | tf_op jit(solution)/shard_map/ppermute | solution.py:250
  133.1 109.7 %copy-start.2 = (bf16[512,512]{1,0:T(8,128)(2,1)}, bf16[512,512]{1,0:T(8,128)(2,1)S(1)}, u32[]{:S(2)}) copy-start(bf16[512,512]{1,0:T(8,128)(2,1)S(1)} %collective-permute-done.7.refs_4_) | copy-start | bytes 1572868
  133.1 22.5 %collective-permute-start.13 = (bf16[512,512]{1,0:T(8,128)(2,1)S(1)}, bf16[512,512]{1,0:T(8,128)(2,1)S(1)}, u32[]{:S(2)}, u32[]{:S(2)}) collective-permute-start(bf16[512,512]{1,0:T(8,128)(2,1)S(1)} %collective-permute-done.7.refs_4_), channel_id=1, source_target_pairs={{1,0},{2,1},{5,4},{6,5},{9,8},{10,9},{13,12},{14,13},{17,16},{18,1... | collective-permute-start | bytes 1572872 | tf_op jit(solution)/shard_map/ppermute | solution.py:251
  144.4 30.0 %collective-permute-start.18 = (bf16[512,512]{1,0:T(8,128)(2,1)}, bf16[512,512]{1,0:T(8,128)(2,1)}, u32[]{:S(2)}, u32[]{:S(2)}) collective-permute-start(bf16[512,512]{1,0:T(8,128)(2,1)} %collective-permute-done.17.refs_5_), channel_id=1, source_target_pairs={{1,0},{5,4},{9,8},{13,12},{17,16},{21,20},{25,24},{29,28}} | collective-permute-start | bytes 1572872 | tf_op jit(solution)/shard_map/ppermute | solution.py:251
  145.8 0.8 copy-start.14
  146.6 62.5 %collective-permute-start.20 = (bf16[512,512]{1,0:T(8,128)(2,1)}, bf16[512,512]{1,0:T(8,128)(2,1)}, u32[]{:S(2)}, u32[]{:S(2)}) collective-permute-start(bf16[512,512]{1,0:T(8,128)(2,1)} %collective-permute-done.5.refs_12_), channel_id=1, source_target_pairs={{1,0},{5,4},{9,8},{13,12},{17,16},{21,20},{25,24},{29,28}} | collective-permute-start | bytes 1572872 | tf_op jit(solution)/shard_map/ppermute | solution.py:251
  147.9 94.9 %copy-start.3 = (bf16[512,512]{1,0:T(8,128)(2,1)}, bf16[512,512]{1,0:T(8,128)(2,1)S(1)}, u32[]{:S(2)}) copy-start(bf16[512,512]{1,0:T(8,128)(2,1)S(1)} %collective-permute-done.11.refs_2_) | copy-start | bytes 1572868
  147.9 94.9 %collective-permute-start.12 = (bf16[512,512]{1,0:T(8,128)(2,1)S(1)}, bf16[512,512]{1,0:T(8,128)(2,1)S(1)}, u32[]{:S(2)}, u32[]{:S(2)}) collective-permute-start(bf16[512,512]{1,0:T(8,128)(2,1)S(1)} %collective-permute-done.11.refs_2_), channel_id=1, source_target_pairs={{2,3},{6,7},{10,11},{14,15},{18,19},{22,23},{26,27},{30,31}} | collective-permute-start | bytes 1572872 | tf_op jit(solution)/shard_map/ppermute | solution.py:250
  155.6 87.2 %copy-start.4 = (bf16[512,512]{1,0:T(8,128)(2,1)}, bf16[512,512]{1,0:T(8,128)(2,1)S(1)}, u32[]{:S(2)}) copy-start(bf16[512,512]{1,0:T(8,128)(2,1)S(1)} %collective-permute-done.13.refs_5_) | copy-start | bytes 1572868
  155.6 87.3 %collective-permute-start.14 = (bf16[512,512]{1,0:T(8,128)(2,1)S(1)}, bf16[512,512]{1,0:T(8,128)(2,1)S(1)}, u32[]{:S(2)}, u32[]{:S(2)}) collective-permute-start(bf16[512,512]{1,0:T(8,128)(2,1)S(1)} %collective-permute-done.13.refs_5_), channel_id=1, source_target_pairs={{1,0},{5,4},{9,8},{13,12},{17,16},{21,20},{25,24},{29,28}} | collective-permute-start | bytes 1572872 | tf_op jit(solution)/shard_map/ppermute | solution.py:251
  242.8 0.8 copy-start.5
  243.6 0.8 copy-start.6
Sparse Core Ops, SparseCore 0:
  11.0 50.3 all-gather.5
  76.7 75.1 all-gather.7
  153.5 61.4 all-gather.3

commit v12 on v7

--- a/solution.py
+++ b/solution.py
@@ -276,13 +276,15 @@
     out, *ends = after((out, *[side[-1] for side in moving]), far)
     for side, end in zip(moving, ends):
         side[-1] = end
+    out = after(out, y)
+    hop(y, 1)
     hop(far, cols - 1, direct=True)
     for n in (0, 1):
         x[n].append((far[n][1], 0))
     out = update(1, out, ())
-    out = after(out, y)
-    for s in range(1, cols - 1):
-        hop(y, s, direct=True)
+    out, y[0][-1], y[1][-1] = lax.optimization_barrier((out, y[0][-1], y[1][-1]))
+    for s in range(2, cols - 1):
+        hop(y, s)
     for n in (0, 1):
         y[n].append((far[n][1], size))
     for q in range(2, chunks):

time: 257 us -> 257 us (level)
  the two profiles are of different devices: /device:TPU:19 before, /device:TPU:18 now
where the time goes in v12:
time: 257 us; the launch traced here: 256 us
  Pallas kernels  79.3 us (31%)
  waiting for transfers between devices  78.9 us (31%)
  starting transfers between devices  77.5 us (30%)
  between operations  13.8 us (5%)
  other arithmetic  3.35 us (1%)
  local copies, waits for them, and re-layouts  3.03 us (1%)
    pallas_call x4, Pallas kernels, chunk_update(): pl.pallas_call(functools.partial(chunk_kernel, starts=starts, parts=parts...  75 us
    ppermute x11, starting transfers between devices, hop(): lax.ppermute(left[source], 'col', [(c + step, c) for c in range(cols - st...  47.2 us
    ppermute x3, waiting for transfers between devices, local(): lax.ppermute(arrived[s], 'col', [(c, (c + s) % cols) for c in range(cols)])  43.6 us
    ppermute x11, waiting for transfers between devices, hop(): lax.ppermute(left[source], 'col', [(c + step, c) for c in range(cols - st...  25.2 us
    ppermute x11, starting transfers between devices, hop(): lax.ppermute(right[source], 'col', [(c, c + step) for c in range(first, c...  22.7 us
    ppermute x11, waiting for transfers between devices, hop(): lax.ppermute(right[source], 'col', [(c, c + step) for c in range(first, c...  10.1 us
  transfers between devices with their start and end apart: 28, of which 11 were waited for; matrix products, arithmetic and copies ran while one was open for 1% of the time, Pallas kernels for 22%

profile of v12, /device:TPU:18, one launch (start us, length us, event | category | flops | bytes accessed | tf_op | source)
XLA Modules:
  0.0 255.9 jit_solution(1694417001358096339)
XLA Ops:
  6.5 4.3 %shard_map.37 = (bf16[8,4,4,16,512]{4,3,2,1,0:T(8,128)(2,1)}, bf16[256,1024]{1,0:T(8,128)(2,1)}, bf16[256,1024]{1,0:T(8,128)(2,1)}, bf16[256,1024]{1,0:T(8,128)(2,1)}, bf16[256,1024]{1,0:T(8,128)(2,1)}) custom-call(s32[1]{0:T(128)} %bitcast.own, bf16[4,8,4,16,512]{4,3,2,1,0:T(8,128)(2,1)} %bitcast.17, bf16[256,4096]{1,0:T(8,128)(2,1)} %w_ref.1), custom_call_target="tpu_custom_call" | custom-call | bytes 8388608 | tf_op jit(solution)/shard_map/pallas_call | solution.py:46
  10.8 0.0 all-gather.3.cloned.1.call-update
  10.9 4.3 %all-to-all-start = ((bf16[8,4,4,16,512]{4,3,2,1,0:T(8,128)(2,1)}), bf16[8,4,4,16,512]{4,3,2,1,0:T(8,128)(2,1)S(1)}, u32[]{:S(2)}, u32[]{:S(2)}) async-start(bf16[8,4,4,16,512]{4,3,2,1,0:T(8,128)(2,1)} %get-tuple-element.30), calls=%async_computation | async-start | bytes 4194304 | tf_op jit(solution)/shard_map/all_to_all | solution.py:215
  15.1 1.6 collective-permute-start.6
  16.7 0.3 collective-permute-start.7
  17.0 1.4 collective-permute-start.8
  18.4 34.2 %collective-permute-done.6 = bf16[256,1024]{1,0:T(8,128)(2,1)S(1)} collective-permute-done((bf16[256,1024]{1,0:T(8,128)(2,1)}, bf16[256,1024]{1,0:T(8,128)(2,1)S(1)}, u32[]{:S(2)}, u32[]{:S(2)}) %collective-permute-start.6) | collective-permute-done | bytes 524320 | tf_op jit(solution)/shard_map/ppermute | solution.py:214
  52.6 0.0 collective-permute-done.7
  52.6 9.4 %collective-permute-done.8 = bf16[256,1024]{1,0:T(8,128)(2,1)} collective-permute-done((bf16[256,1024]{1,0:T(8,128)(2,1)}, bf16[256,1024]{1,0:T(8,128)(2,1)}, u32[]{:S(2)}, u32[]{:S(2)}) %collective-permute-start.8) | collective-permute-done | bytes 524320 | tf_op jit(solution)/shard_map/ppermute | solution.py:214
  62.0 0.0 all-to-all-done
  62.0 2.3 pad_maximum_fusion
  64.3 0.0 all-gather.5.cloned.1.call-update
  64.3 0.2 fusion
  64.6 4.4 %collective-permute-start.2 = (bf16[512,512]{1,0:T(8,128)(2,1)S(1)}, bf16[512,512]{1,0:T(8,128)(2,1)S(1)}, u32[]{:S(2)}, u32[]{:S(2)}) collective-permute-start(bf16[512,512]{1,0:T(8,128)(2,1)S(1)} %bitcast.18), channel_id=1, source_target_pairs={{1,0},{2,1},{3,2},{5,4},{6,5},{7,6},{9,8},{10,9},{11,10},{13,12},{... | collective-permute-start | bytes 1572872 | tf_op jit(solution)/shard_map/ppermute | solution.py:240
  69.0 1.9 collective-permute-start
  70.9 3.9 %collective-permute-start.14 = (bf16[512,512]{1,0:T(8,128)(2,1)S(1)}, bf16[512,512]{1,0:T(8,128)(2,1)S(1)}, u32[]{:S(2)}, u32[]{:S(2)}) collective-permute-start(bf16[512,512]{1,0:T(8,128)(2,1)S(1)} %bitcast.14), channel_id=1, source_target_pairs={{1,0},{2,1},{3,2},{5,4},{6,5},{7,6},{9,8},{10,9},{11,10},{13,12},{... | collective-permute-start | bytes 1572872 | tf_op jit(solution)/shard_map/ppermute | solution.py:240
  74.8 1.9 collective-permute-start.11
  76.8 4.5 %collective-permute-done.2.refs_4_ = bf16[512,512]{1,0:T(8,128)(2,1)S(1)} collective-permute-done((bf16[512,512]{1,0:T(8,128)(2,1)S(1)}, bf16[512,512]{1,0:T(8,128)(2,1)S(1)}, u32[]{:S(2)}, u32[]{:S(2)}) %collective-permute-start.2) | collective-permute-done | bytes 524320 | tf_op jit(solution)/shard_map/ppermute | solution.py:240
  81.3 4.4 %collective-permute-start.3 = (bf16[512,512]{1,0:T(8,128)(2,1)S(1)}, bf16[512,512]{1,0:T(8,128)(2,1)S(1)}, u32[]{:S(2)}, u32[]{:S(2)}) collective-permute-start(bf16[512,512]{1,0:T(8,128)(2,1)S(1)} %collective-permute-done.2.refs_4_), channel_id=1, source_target_pairs={{1,0},{2,1},{5,4},{6,5},{9,8},{10,9},{13,12},{14,13},{17,16},{18,1... | collective-permute-start | bytes 1572872 | tf_op jit(solution)/shard_map/ppermute | solution.py:240
  85.7 0.0 collective-permute-done.refs_1_
  85.7 1.9 collective-permute-start.1
  87.6 4.9 %collective-permute-done.14.refs_4_ = bf16[512,512]{1,0:T(8,128)(2,1)S(1)} collective-permute-done((bf16[512,512]{1,0:T(8,128)(2,1)S(1)}, bf16[512,512]{1,0:T(8,128)(2,1)S(1)}, u32[]{:S(2)}, u32[]{:S(2)}) %collective-permute-start.14) | collective-permute-done | bytes 524320 | tf_op jit(solution)/shard_map/ppermute | solution.py:240
  92.5 5.2 %collective-permute-start.15 = (bf16[512,512]{1,0:T(8,128)(2,1)S(1)}, bf16[512,512]{1,0:T(8,128)(2,1)}, u32[]{:S(2)}, u32[]{:S(2)}) collective-permute-start(bf16[512,512]{1,0:T(8,128)(2,1)S(1)} %collective-permute-done.14.refs_4_), channel_id=1, source_target_pairs={{1,0},{2,1},{5,4},{6,5},{9,8},{10,9},{13,12},{14,13},{17,16},{18,1... | collective-permute-start | bytes 1572872 | tf_op jit(solution)/shard_map/ppermute | solution.py:240
  97.7 0.0 collective-permute-done.11.refs_1_
  97.7 1.9 collective-permute-start.12
  99.6 4.1 %collective-permute-done.3.refs_5_ = bf16[512,512]{1,0:T(8,128)(2,1)S(1)} collective-permute-done((bf16[512,512]{1,0:T(8,128)(2,1)S(1)}, bf16[512,512]{1,0:T(8,128)(2,1)S(1)}, u32[]{:S(2)}, u32[]{:S(2)}) %collective-permute-start.3) | collective-permute-done | bytes 524320 | tf_op jit(solution)/shard_map/ppermute | solution.py:240
  103.7 4.4 %collective-permute-done.1.refs_2_ = bf16[512,512]{1,0:T(8,128)(2,1)S(1)} collective-permute-done((bf16[512,512]{1,0:T(8,128)(2,1)S(1)}, bf16[512,512]{1,0:T(8,128)(2,1)S(1)}, u32[]{:S(2)}, u32[]{:S(2)}) %collective-permute-start.1) | collective-permute-done | bytes 524320 | tf_op jit(solution)/shard_map/ppermute | solution.py:239
  108.2 0.7 collective-permute-start.5
  108.9 2.1 collective-permute-start.10
  111.0 3.8 %collective-permute-start.9 = (bf16[512,512]{1,0:T(8,128)(2,1)S(1)}, bf16[512,512]{1,0:T(8,128)(2,1)S(1)}, u32[]{:S(2)}, u32[]{:S(2)}) collective-permute-start(bf16[512,512]{1,0:T(8,128)(2,1)S(1)} %bitcast.11), channel_id=1, source_target_pairs={{0,1},{1,2},{2,3},{4,5},{5,6},{6,7},{8,9},{9,10},{10,11},{12,13},{... | collective-permute-start | bytes 1572872 | tf_op jit(solution)/shard_map/ppermute | solution.py:239
  114.8 0.2 collective-permute-done.15.refs_5_
  115.0 2.1 collective-permute-start.4
  117.0 1.1 pad_maximum_fusion.1
  118.1 1.4 collective-permute-done.12.refs_2_
  119.5 1.5 collective-permute-start.16
  121.0 0.0 collective-permute-done.5.refs_6_
  121.0 2.7 %collective-permute-start.13 = (bf16[512,512]{1,0:T(8,128)(2,1)}, bf16[512,512]{1,0:T(8,128)(2,1)}, u32[]{:S(2)}, u32[]{:S(2)}) collective-permute-start(bf16[512,512]{1,0:T(8,128)(2,1)} %collective-permute-done.12.refs_2_), channel_id=1, source_target_pairs={{2,3},{6,7},{10,11},{14,15},{18,19},{22,23},{26,27},{30,31}} | collective-permute-start | bytes 1572872 | tf_op jit(solution)/shard_map/ppermute | solution.py:239
  123.7 1.5 collective-permute-done.10.refs_11_.refs_4_
  125.3 14.9 %collective-permute-start.18 = (bf16[512,512]{1,0:T(8,128)(2,1)S(1)}, bf16[512,512]{1,0:T(8,128)(2,1)}, u32[]{:S(2)}, u32[]{:S(2)}) collective-permute-start(bf16[512,512]{1,0:T(8,128)(2,1)S(1)} %collective-permute-done.10.refs_11_.refs_4_), channel_id=1, source_target_pairs={{1,0},{2,1},{5,4},{6,5},{9,8},{10,9},{13,12},{14,13},{17,16},{18,1... | collective-permute-start | bytes 1572872 | tf_op jit(solution)/shard_map/ppermute | solution.py:240
  140.1 0.0 collective-permute-done.9.refs_10_.refs_1_
  140.1 1.9 collective-permute-start.17
  142.1 0.0 collective-permute-done.4.refs_3_
  142.1 0.0 all-gather.3.cloned.1.call-done.refs_7_
  142.1 0.0 all-gather.5.cloned.1.call-done.refs_8_
  142.2 18.8 %shard_map.38.refs_10_ = bf16[64,128,1024]{2,1,0:T(8,128)(2,1)} custom-call(s32[1]{0:T(128)} %bitcast.own, bf16[512,512]{1,0:T(8,128)(2,1)} %bitcast.20, bf16[512,512]{1,0:T(8,128)(2,1)} %copy-done.14, bf16[512,512]{1,0:T(8,128)(2,1)} %copy-done.16, bf16[512,512]{1,0:T(8,128)(2,1)} %collective-permute-done.4.refs_3_, bf16[512,512]{1,0:T(8,128)(2,1)} %copy-done.13, ...), custom_call_target="tpu_custom_call" | custom-call | flops 12884901888 | bytes 25165824 | tf_op jit(solution)/shard_map/pallas_call | solution.py:163
  161.0 0.0 collective-permute-done.16.refs_6_
  161.0 0.0 collective-permute-done.18.refs_5_
  161.0 0.0 collective-permute-done.17.refs_2_
  161.0 4.7 %collective-permute-start.20 = (bf16[512,512]{1,0:T(8,128)(2,1)S(1)}, bf16[512,512]{1,0:T(8,128)(2,1)S(1)}, u32[]{:S(2)}, u32[]{:S(2)}) collective-permute-start(bf16[512,512]{1,0:T(8,128)(2,1)S(1)} %bitcast.7), channel_id=1, source_target_pairs={{1,0},{2,1},{3,2},{5,4},{6,5},{7,6},{9,8},{10,9},{11,10},{13,12},{... | collective-permute-start | bytes 1572872 | tf_op jit(solution)/shard_map/ppermute | solution.py:240
  165.7 1.9 collective-permute-start.19
  167.6 0.7 collective-permute-start.22
  168.4 0.7 collective-permute-start.24
  169.1 18.8 %shard_map.39.refs_10_ = bf16[64,128,1024]{2,1,0:T(8,128)(2,1)} custom-call(s32[1]{0:T(128)} %bitcast.own, bf16[512,512]{1,0:T(8,128)(2,1)} %bitcast.16, bf16[512,512]{1,0:T(8,128)(2,1)} %copy-done.6, bf16[512,512]{1,0:T(8,128)(2,1)} %collective-permute-done.12.refs_2_, ...), custom_call_target="tpu_custom_call", output_to_operand_aliasing={{}: (11, {})} | custom-call | flops 12884901888 | bytes 25165824 | tf_op jit(solution)/shard_map/pallas_call | solution.py:163
  187.9 10.0 %collective-permute-done.20.refs_4_ = bf16[512,512]{1,0:T(8,128)(2,1)S(1)} collective-permute-done((bf16[512,512]{1,0:T(8,128)(2,1)S(1)}, bf16[512,512]{1,0:T(8,128)(2,1)S(1)}, u32[]{:S(2)}, u32[]{:S(2)}) %collective-permute-start.20) | collective-permute-done | bytes 524320 | tf_op jit(solution)/shard_map/ppermute | solution.py:240
  197.8 4.2 %collective-permute-done.19.refs_1_ = bf16[512,512]{1,0:T(8,128)(2,1)S(1)} collective-permute-done((bf16[512,512]{1,0:T(8,128)(2,1)S(1)}, bf16[512,512]{1,0:T(8,128)(2,1)S(1)}, u32[]{:S(2)}, u32[]{:S(2)}) %collective-permute-start.19) | collective-permute-done | bytes 524320 | tf_op jit(solution)/shard_map/ppermute | solution.py:239
  202.0 1.9 collective-permute-start.21
  204.0 4.8 %collective-permute-start.23 = (bf16[512,512]{1,0:T(8,128)(2,1)S(1)}, bf16[512,512]{1,0:T(8,128)(2,1)}, u32[]{:S(2)}, u32[]{:S(2)}) collective-permute-start(bf16[512,512]{1,0:T(8,128)(2,1)S(1)} %collective-permute-done.20.refs_4_), channel_id=1, source_target_pairs={{1,0},{2,1},{5,4},{6,5},{9,8},{10,9},{13,12},{14,13},{17,16},{18,1... | collective-permute-start | bytes 1572872 | tf_op jit(solution)/shard_map/ppermute | solution.py:240
  208.7 0.0 collective-permute-done.24.refs_6_
  208.7 1.0 copy-done.2
  209.7 1.0 copy-done.3
  210.7 18.7 %shard_map.40.refs_10_ = bf16[64,128,1024]{2,1,0:T(8,128)(2,1)} custom-call(s32[1]{0:T(128)} %bitcast.own, bf16[512,512]{1,0:T(8,128)(2,1)} %bitcast.13, bf16[512,512]{1,0:T(8,128)(2,1)} %copy-done.8, bf16[512,512]{1,0:T(8,128)(2,1)} %collective-permute-done.17.refs_2_, bf16[1024,512]{1,0:T(8,128)(2,1)} %copy-done.2, ...), custom_call_target="tpu_custom_call", output_to_operand_aliasing={{}: (11, {})} | custom-call | flops 12884901888 | bytes 25165824 | tf_op jit(solution)/shard_map/pallas_call | solution.py:163
  229.5 0.0 collective-permute-done.23.refs_5_
  229.5 0.8 copy-done.11
  230.3 18.7 %shard_map.41 = bf16[64,128,1024]{2,1,0:T(8,128)(2,1)} custom-call(s32[1]{0:T(128)} %bitcast.own, bf16[512,512]{1,0:T(8,128)(2,1)} %bitcast.9, bf16[512,512]{1,0:T(8,128)(2,1)} %copy-done.10, bf16[512,512]{1,0:T(8,128)(2,1)} %copy-done.11, bf16[1024,512]{1,0:T(8,128)(2,1)} %copy-done.2, bf16[512,512]{1,0:T(8,128)(2,1)} %copy-done.9, ...), custom_call_target="tpu_custom_call", output_to_operand_aliasing={{}: (11, {})} | custom-call | flops 12884901888 | bytes 25165824 | tf_op jit(solution)/shard_map/pallas_call | solution.py:163
  (38 shorter events, 0.1 us)
Async XLA Ops:
  6.5 135.6 %all-gather.3.cloned.1.call-start = ((), (), s32[]{:S(2)}) async-start(), calls=%async_computation.1 | async-start | bytes 4718592 | tf_op jit(solution)/shard_map/all_gather | solution.py:219
  10.9 51.1 %all-to-all-start = ((bf16[8,4,4,16,512]{4,3,2,1,0:T(8,128)(2,1)}), bf16[8,4,4,16,512]{4,3,2,1,0:T(8,128)(2,1)S(1)}, u32[]{:S(2)}, u32[]{:S(2)}) async-start(bf16[8,4,4,16,512]{4,3,2,1,0:T(8,128)(2,1)} %get-tuple-element.30), calls=%async_computation | async-start | bytes 4194304 | tf_op jit(solution)/shard_map/all_to_all | solution.py:215
  15.1 127.0 %all-gather.5.cloned.1.call-start = ((), (), s32[]{:S(2)}) async-start(), calls=%async_computation.2 | async-start | bytes 14155776 | tf_op jit(solution)/shard_map/all_gather | solution.py:219
  15.1 37.4 %collective-permute-start.6 = (bf16[256,1024]{1,0:T(8,128)(2,1)}, bf16[256,1024]{1,0:T(8,128)(2,1)S(1)}, u32[]{:S(2)}, u32[]{:S(2)}) collective-permute-start(bf16[256,1024]{1,0:T(8,128)(2,1)} %get-tuple-element.34), channel_id=1, source_target_pairs={{0,1},{1,2},{2,3},{3,0},{4,5},{5,6},{6,7},{7,4},{8,9},{9,10},{10,1... | collective-permute-start | bytes 1572872 | tf_op jit(solution)/shard_map/ppermute | solution.py:214
  16.7 35.9 %collective-permute-start.7 = (bf16[256,1024]{1,0:T(8,128)(2,1)}, bf16[256,1024]{1,0:T(8,128)(2,1)S(1)}, u32[]{:S(2)}, u32[]{:S(2)}) collective-permute-start(bf16[256,1024]{1,0:T(8,128)(2,1)} %get-tuple-element.35), channel_id=1, source_target_pairs={{0,2},{1,3},{2,0},{3,1},{4,6},{5,7},{6,4},{7,5},{8,10},{9,11},{10,... | collective-permute-start | bytes 1572872 | tf_op jit(solution)/shard_map/ppermute | solution.py:214
  17.0 44.9 %collective-permute-start.8 = (bf16[256,1024]{1,0:T(8,128)(2,1)}, bf16[256,1024]{1,0:T(8,128)(2,1)}, u32[]{:S(2)}, u32[]{:S(2)}) collective-permute-start(bf16[256,1024]{1,0:T(8,128)(2,1)} %get-tuple-element.36), channel_id=1, source_target_pairs={{0,3},{1,0},{2,1},{3,2},{4,7},{5,4},{6,5},{7,6},{8,11},{9,8},{10,9... | collective-permute-start | bytes 1572872 | tf_op jit(solution)/shard_map/ppermute | solution.py:214
  64.5 75.6 %copy-start.4 = (bf16[8,1,4,16,512]{4,3,2,1,0:T(8,128)(2,1)}, bf16[8,1,4,16,512]{4,3,2,1,0:T(8,128)(2,1)S(1)}, u32[]{:S(2)}) copy-start(bf16[8,1,4,16,512]{4,3,2,1,0:T(8,128)(2,1)S(1)} %get-tuple-element.56) | copy-start | bytes 1572868
  64.5 77.5 %copy-start.12 = (bf16[8,1,4,16,512]{4,3,2,1,0:T(8,128)(2,1)}, bf16[8,1,4,16,512]{4,3,2,1,0:T(8,128)(2,1)S(1)}, u32[]{:S(2)}) copy-start(bf16[8,1,4,16,512]{4,3,2,1,0:T(8,128)(2,1)S(1)} %get-tuple-element.58) | copy-start | bytes 1572868
  64.6 96.4 %copy-start.1 = (bf16[8,1,4,16,512]{4,3,2,1,0:T(8,128)(2,1)}, bf16[8,1,4,16,512]{4,3,2,1,0:T(8,128)(2,1)S(1)}, u32[]{:S(2)}) copy-start(bf16[8,1,4,16,512]{4,3,2,1,0:T(8,128)(2,1)S(1)} %get-tuple-element.57) | copy-start | bytes 1572868
  64.6 101.1 %copy-start = (bf16[8,1,4,16,512]{4,3,2,1,0:T(8,128)(2,1)}, bf16[8,1,4,16,512]{4,3,2,1,0:T(8,128)(2,1)S(1)}, u32[]{:S(2)}) copy-start(bf16[8,1,4,16,512]{4,3,2,1,0:T(8,128)(2,1)S(1)} %get-tuple-element.55) | copy-start | bytes 1572868
  64.6 16.7 %collective-permute-start.2 = (bf16[512,512]{1,0:T(8,128)(2,1)S(1)}, bf16[512,512]{1,0:T(8,128)(2,1)S(1)}, u32[]{:S(2)}, u32[]{:S(2)}) collective-permute-start(bf16[512,512]{1,0:T(8,128)(2,1)S(1)} %bitcast.18), channel_id=1, source_target_pairs={{1,0},{2,1},{3,2},{5,4},{6,5},{7,6},{9,8},{10,9},{11,10},{13,12},{... | collective-permute-start | bytes 1572872 | tf_op jit(solution)/shard_map/ppermute | solution.py:240
  69.0 16.7 %collective-permute-start = (bf16[512,512]{1,0:T(8,128)(2,1)S(1)}, bf16[512,512]{1,0:T(8,128)(2,1)S(1)}, u32[]{:S(2)}, u32[]{:S(2)}) collective-permute-start(bf16[512,512]{1,0:T(8,128)(2,1)S(1)} %bitcast.19), channel_id=1, source_target_pairs={{0,1},{1,2},{2,3},{4,5},{5,6},{6,7},{8,9},{9,10},{10,11},{12,13},{... | collective-permute-start | bytes 1572872 | tf_op jit(solution)/shard_map/ppermute | solution.py:239
  70.9 21.6 %collective-permute-start.14 = (bf16[512,512]{1,0:T(8,128)(2,1)S(1)}, bf16[512,512]{1,0:T(8,128)(2,1)S(1)}, u32[]{:S(2)}, u32[]{:S(2)}) collective-permute-start(bf16[512,512]{1,0:T(8,128)(2,1)S(1)} %bitcast.14), channel_id=1, source_target_pairs={{1,0},{2,1},{3,2},{5,4},{6,5},{7,6},{9,8},{10,9},{11,10},{13,12},{... | collective-permute-start | bytes 1572872 | tf_op jit(solution)/shard_map/ppermute | solution.py:240
  74.8 22.9 %collective-permute-start.11 = (bf16[512,512]{1,0:T(8,128)(2,1)S(1)}, bf16[512,512]{1,0:T(8,128)(2,1)S(1)}, u32[]{:S(2)}, u32[]{:S(2)}) collective-permute-start(bf16[512,512]{1,0:T(8,128)(2,1)S(1)} %bitcast.15), channel_id=1, source_target_pairs={{0,1},{1,2},{2,3},{4,5},{5,6},{6,7},{8,9},{9,10},{10,11},{12,13},{... | collective-permute-start | bytes 1572872 | tf_op jit(solution)/shard_map/ppermute | solution.py:239
  81.3 26.9 %copy-start.13 = (bf16[512,512]{1,0:T(8,128)(2,1)}, bf16[512,512]{1,0:T(8,128)(2,1)S(1)}, u32[]{:S(2)}) copy-start(bf16[512,512]{1,0:T(8,128)(2,1)S(1)} %collective-permute-done.2.refs_4_) | copy-start | bytes 1572868
  81.3 22.5 %collective-permute-start.3 = (bf16[512,512]{1,0:T(8,128)(2,1)S(1)}, bf16[512,512]{1,0:T(8,128)(2,1)S(1)}, u32[]{:S(2)}, u32[]{:S(2)}) collective-permute-start(bf16[512,512]{1,0:T(8,128)(2,1)S(1)} %collective-permute-done.2.refs_4_), channel_id=1, source_target_pairs={{1,0},{2,1},{5,4},{6,5},{9,8},{10,9},{13,12},{14,13},{17,16},{18,1... | collective-permute-start | bytes 1572872 | tf_op jit(solution)/shard_map/ppermute | solution.py:240
  85.7 23.2 %copy-start.14 = (bf16[512,512]{1,0:T(8,128)(2,1)}, bf16[512,512]{1,0:T(8,128)(2,1)S(1)}, u32[]{:S(2)}) copy-start(bf16[512,512]{1,0:T(8,128)(2,1)S(1)} %collective-permute-done.refs_1_) | copy-start | bytes 1572868
  85.7 22.5 %collective-permute-start.1 = (bf16[512,512]{1,0:T(8,128)(2,1)S(1)}, bf16[512,512]{1,0:T(8,128)(2,1)S(1)}, u32[]{:S(2)}, u32[]{:S(2)}) collective-permute-start(bf16[512,512]{1,0:T(8,128)(2,1)S(1)} %collective-permute-done.refs_1_), channel_id=1, source_target_pairs={{1,2},{2,3},{5,6},{6,7},{9,10},{10,11},{13,14},{14,15},{17,18},{18... | collective-permute-start | bytes 1572872 | tf_op jit(solution)/shard_map/ppermute | solution.py:239
  92.5 68.5 %copy-start.5 = (bf16[512,512]{1,0:T(8,128)(2,1)}, bf16[512,512]{1,0:T(8,128)(2,1)S(1)}, u32[]{:S(2)}) copy-start(bf16[512,512]{1,0:T(8,128)(2,1)S(1)} %collective-permute-done.14.refs_4_) | copy-start | bytes 1572868
  92.5 22.5 %collective-permute-start.15 = (bf16[512,512]{1,0:T(8,128)(2,1)S(1)}, bf16[512,512]{1,0:T(8,128)(2,1)}, u32[]{:S(2)}, u32[]{:S(2)}) collective-permute-start(bf16[512,512]{1,0:T(8,128)(2,1)S(1)} %collective-permute-done.14.refs_4_), channel_id=1, source_target_pairs={{1,0},{2,1},{5,4},{6,5},{9,8},{10,9},{13,12},{14,13},{17,16},{18,1... | collective-permute-start | bytes 1572872 | tf_op jit(solution)/shard_map/ppermute | solution.py:240
  97.7 63.3 %copy-start.6 = (bf16[512,512]{1,0:T(8,128)(2,1)}, bf16[512,512]{1,0:T(8,128)(2,1)S(1)}, u32[]{:S(2)}) copy-start(bf16[512,512]{1,0:T(8,128)(2,1)S(1)} %collective-permute-done.11.refs_1_) | copy-start | bytes 1572868
  97.7 21.8 %collective-permute-start.12 = (bf16[512,512]{1,0:T(8,128)(2,1)S(1)}, bf16[512,512]{1,0:T(8,128)(2,1)}, u32[]{:S(2)}, u32[]{:S(2)}) collective-permute-start(bf16[512,512]{1,0:T(8,128)(2,1)S(1)} %collective-permute-done.11.refs_1_), channel_id=1, source_target_pairs={{1,2},{2,3},{5,6},{6,7},{9,10},{10,11},{13,14},{14,15},{17,18},{18... | collective-permute-start | bytes 1572872 | tf_op jit(solution)/shard_map/ppermute | solution.py:239
  103.7 38.3 %copy-start.15 = (bf16[512,512]{1,0:T(8,128)(2,1)}, bf16[512,512]{1,0:T(8,128)(2,1)S(1)}, u32[]{:S(2)}) copy-start(bf16[512,512]{1,0:T(8,128)(2,1)S(1)} %collective-permute-done.3.refs_5_) | copy-start | bytes 1572868
  108.2 33.9 %copy-start.16 = (bf16[512,512]{1,0:T(8,128)(2,1)}, bf16[512,512]{1,0:T(8,128)(2,1)S(1)}, u32[]{:S(2)}) copy-start(bf16[512,512]{1,0:T(8,128)(2,1)S(1)} %collective-permute-done.1.refs_2_) | copy-start | bytes 1572868
  108.2 12.9 %collective-permute-start.5 = (bf16[512,512]{1,0:T(8,128)(2,1)S(1)}, bf16[512,512]{1,0:T(8,128)(2,1)S(1)}, u32[]{:S(2)}, u32[]{:S(2)}) collective-permute-start(bf16[512,512]{1,0:T(8,128)(2,1)S(1)} %collective-permute-done.3.refs_5_), channel_id=1, source_target_pairs={{1,0},{5,4},{9,8},{13,12},{17,16},{21,20},{25,24},{29,28}} | collective-permute-start | bytes 1572872 | tf_op jit(solution)/shard_map/ppermute | solution.py:240
  108.9 16.4 %collective-permute-start.10 = (bf16[512,512]{1,0:T(8,128)(2,1)S(1)}, bf16[512,512]{1,0:T(8,128)(2,1)S(1)}, u32[]{:S(2)}, u32[]{:S(2)}) collective-permute-start(bf16[512,512]{1,0:T(8,128)(2,1)S(1)} %bitcast.10), channel_id=1, source_target_pairs={{1,0},{2,1},{3,2},{5,4},{6,5},{7,6},{9,8},{10,9},{11,10},{13,12},{... | collective-permute-start | bytes 1572872 | tf_op jit(solution)/shard_map/ppermute | solution.py:240
  111.0 29.2 %collective-permute-start.9 = (bf16[512,512]{1,0:T(8,128)(2,1)S(1)}, bf16[512,512]{1,0:T(8,128)(2,1)S(1)}, u32[]{:S(2)}, u32[]{:S(2)}) collective-permute-start(bf16[512,512]{1,0:T(8,128)(2,1)S(1)} %bitcast.11), channel_id=1, source_target_pairs={{0,1},{1,2},{2,3},{4,5},{5,6},{6,7},{8,9},{9,10},{10,11},{12,13},{... | collective-permute-start | bytes 1572872 | tf_op jit(solution)/shard_map/ppermute | solution.py:239
  115.0 27.1 %collective-permute-start.4 = (bf16[512,512]{1,0:T(8,128)(2,1)S(1)}, bf16[512,512]{1,0:T(8,128)(2,1)}, u32[]{:S(2)}, u32[]{:S(2)}) collective-permute-start(bf16[512,512]{1,0:T(8,128)(2,1)S(1)} %collective-permute-done.1.refs_2_), channel_id=1, source_target_pairs={{2,3},{6,7},{10,11},{14,15},{18,19},{22,23},{26,27},{30,31}} | collective-permute-start | bytes 1572872 | tf_op jit(solution)/shard_map/ppermute | solution.py:239
  119.5 41.5 %collective-permute-start.16 = (bf16[512,512]{1,0:T(8,128)(2,1)}, bf16[512,512]{1,0:T(8,128)(2,1)}, u32[]{:S(2)}, u32[]{:S(2)}) collective-permute-start(bf16[512,512]{1,0:T(8,128)(2,1)} %collective-permute-done.15.refs_5_), channel_id=1, source_target_pairs={{1,0},{5,4},{9,8},{13,12},{17,16},{21,20},{25,24},{29,28}} | collective-permute-start | bytes 1572872 | tf_op jit(solution)/shard_map/ppermute | solution.py:240
  121.0 21.1 %copy-start.17 = (bf16[512,512]{1,0:T(8,128)(2,1)}, bf16[512,512]{1,0:T(8,128)(2,1)S(1)}, u32[]{:S(2)}) copy-start(bf16[512,512]{1,0:T(8,128)(2,1)S(1)} %collective-permute-done.5.refs_6_) | copy-start | bytes 1572868
  121.0 39.9 %collective-permute-start.13 = (bf16[512,512]{1,0:T(8,128)(2,1)}, bf16[512,512]{1,0:T(8,128)(2,1)}, u32[]{:S(2)}, u32[]{:S(2)}) collective-permute-start(bf16[512,512]{1,0:T(8,128)(2,1)} %collective-permute-done.12.refs_2_), channel_id=1, source_target_pairs={{2,3},{6,7},{10,11},{14,15},{18,19},{22,23},{26,27},{30,31}} | collective-permute-start | bytes 1572872 | tf_op jit(solution)/shard_map/ppermute | solution.py:239
  125.3 16.9 %copy-start.7 = (bf16[512,512]{1,0:T(8,128)(2,1)}, bf16[512,512]{1,0:T(8,128)(2,1)S(1)}, u32[]{:S(2)}) copy-start(bf16[512,512]{1,0:T(8,128)(2,1)S(1)} %collective-permute-done.10.refs_11_.refs_4_) | copy-start | bytes 1572868
  125.3 35.7 %collective-permute-start.18 = (bf16[512,512]{1,0:T(8,128)(2,1)S(1)}, bf16[512,512]{1,0:T(8,128)(2,1)}, u32[]{:S(2)}, u32[]{:S(2)}) collective-permute-start(bf16[512,512]{1,0:T(8,128)(2,1)S(1)} %collective-permute-done.10.refs_11_.refs_4_), channel_id=1, source_target_pairs={{1,0},{2,1},{5,4},{6,5},{9,8},{10,9},{13,12},{14,13},{17,16},{18,1... | collective-permute-start | bytes 1572872 | tf_op jit(solution)/shard_map/ppermute | solution.py:240
  140.1 2.0 copy-start.8
  140.1 20.9 %collective-permute-start.17 = (bf16[512,512]{1,0:T(8,128)(2,1)S(1)}, bf16[512,512]{1,0:T(8,128)(2,1)}, u32[]{:S(2)}, u32[]{:S(2)}) collective-permute-start(bf16[512,512]{1,0:T(8,128)(2,1)S(1)} %collective-permute-done.9.refs_10_.refs_1_), channel_id=1, source_target_pairs={{1,2},{2,3},{5,6},{6,7},{9,10},{10,11},{13,14},{14,15},{17,18},{18... | collective-permute-start | bytes 1572872 | tf_op jit(solution)/shard_map/ppermute | solution.py:239
  161.0 36.8 %collective-permute-start.20 = (bf16[512,512]{1,0:T(8,128)(2,1)S(1)}, bf16[512,512]{1,0:T(8,128)(2,1)S(1)}, u32[]{:S(2)}, u32[]{:S(2)}) collective-permute-start(bf16[512,512]{1,0:T(8,128)(2,1)S(1)} %bitcast.7), channel_id=1, source_target_pairs={{1,0},{2,1},{3,2},{5,4},{6,5},{7,6},{9,8},{10,9},{11,10},{13,12},{... | collective-permute-start | bytes 1572872 | tf_op jit(solution)/shard_map/ppermute | solution.py:240
  165.7 36.3 %collective-permute-start.19 = (bf16[512,512]{1,0:T(8,128)(2,1)S(1)}, bf16[512,512]{1,0:T(8,128)(2,1)S(1)}, u32[]{:S(2)}, u32[]{:S(2)}) collective-permute-start(bf16[512,512]{1,0:T(8,128)(2,1)S(1)} %bitcast.8), channel_id=1, source_target_pairs={{0,1},{1,2},{2,3},{4,5},{5,6},{6,7},{8,9},{9,10},{10,11},{12,13},{... | collective-permute-start | bytes 1572872 | tf_op jit(solution)/shard_map/ppermute | solution.py:239
  167.6 41.1 %collective-permute-start.22 = (bf16[1024,512]{1,0:T(8,128)(2,1)}, bf16[1024,512]{1,0:T(8,128)(2,1)S(1)}, u32[]{:S(2)}, u32[]{:S(2)}) collective-permute-start(bf16[1024,512]{1,0:T(8,128)(2,1)} %pad_maximum_fusion.1), channel_id=1, source_target_pairs={{0,3},{4,7},{8,11},{12,15},{16,19},{20,23},{24,27},{28,31}} | collective-permute-start | bytes 3145736 | tf_op jit(solution)/shard_map/ppermute | solution.py:239
  168.4 40.4 %collective-permute-start.24 = (bf16[1024,512]{1,0:T(8,128)(2,1)}, bf16[1024,512]{1,0:T(8,128)(2,1)S(1)}, u32[]{:S(2)}, u32[]{:S(2)}) collective-permute-start(bf16[1024,512]{1,0:T(8,128)(2,1)} %pad_maximum_fusion.1), channel_id=1, source_target_pairs={{3,0},{7,4},{11,8},{15,12},{19,16},{23,20},{27,24},{31,28}} | collective-permute-start | bytes 3145736 | tf_op jit(solution)/shard_map/ppermute | solution.py:240
  197.8 31.6 %copy-start.9 = (bf16[512,512]{1,0:T(8,128)(2,1)}, bf16[512,512]{1,0:T(8,128)(2,1)S(1)}, u32[]{:S(2)}) copy-start(bf16[512,512]{1,0:T(8,128)(2,1)S(1)} %collective-permute-done.20.refs_4_) | copy-start | bytes 1572868
  202.0 27.4 %copy-start.10 = (bf16[512,512]{1,0:T(8,128)(2,1)}, bf16[512,512]{1,0:T(8,128)(2,1)S(1)}, u32[]{:S(2)}) copy-start(bf16[512,512]{1,0:T(8,128)(2,1)S(1)} %collective-permute-done.19.refs_1_) | copy-start | bytes 1572868
  202.0 27.4 %collective-permute-start.21 = (bf16[512,512]{1,0:T(8,128)(2,1)S(1)}, bf16[512,512]{1,0:T(8,128)(2,1)S(1)}, u32[]{:S(2)}, u32[]{:S(2)}) collective-permute-start(bf16[512,512]{1,0:T(8,128)(2,1)S(1)} %collective-permute-done.19.refs_1_), channel_id=1, source_target_pairs={{1,2},{2,3},{5,6},{6,7},{9,10},{10,11},{13,14},{14,15},{17,18},{18... | collective-permute-start | bytes 1572872 | tf_op jit(solution)/shard_map/ppermute | solution.py:239
  204.0 25.5 %collective-permute-start.23 = (bf16[512,512]{1,0:T(8,128)(2,1)S(1)}, bf16[512,512]{1,0:T(8,128)(2,1)}, u32[]{:S(2)}, u32[]{:S(2)}) collective-permute-start(bf16[512,512]{1,0:T(8,128)(2,1)S(1)} %collective-permute-done.20.refs_4_), channel_id=1, source_target_pairs={{1,0},{2,1},{5,4},{6,5},{9,8},{10,9},{13,12},{14,13},{17,16},{18,1... | collective-permute-start | bytes 1572872 | tf_op jit(solution)/shard_map/ppermute | solution.py:240
  208.7 1.0 copy-start.2
  209.7 1.0 copy-start.3
  229.5 0.8 copy-start.11
Sparse Core Ops, SparseCore 0:
  11.0 48.2 all-gather.2
  64.4 74.0 all-gather.4

commit v13 on v12

--- a/solution.py
+++ b/solution.py
@@ -228,7 +228,7 @@
         return [right[0], *right[1:], *left[1:]]
 
     def update(q, out, after):
-        blocks = [piece if isinstance(piece, tuple) else (piece, 0) for piece in flat(pieces[q])]
+        blocks = [(piece, 0) for piece in flat(pieces[q])]
         return chunk_update(own, blocks, panel_w, ladder, out, after, q, a_local, b_local, occupied)
 
     def hop(sides, s, direct=False):
@@ -268,25 +268,20 @@
     before[0][-2], before[1][-2] = after((before[0][-2], before[1][-2]), x)
     for s in range(1, cols - 1):
         hop(x, s)
-    far = (jnp.concatenate([x[0][0], y[0][0]]),) * 2
-    far = ([far[0]], [far[1]])
-    size = x[0][0].shape[0]
     out = update(0, None, (x[0][1], x[1][1]))
     moving = (early[-1][0], early[-1][1], x[0], x[1])
-    out, *ends = after((out, *[side[-1] for side in moving]), far)
+    out, *ends = after((out, *[side[-1] for side in moving]), x)
     for side, end in zip(moving, ends):
         side[-1] = end
+    hop(x, cols - 1, direct=True)
     out = after(out, y)
     hop(y, 1)
-    hop(far, cols - 1, direct=True)
-    for n in (0, 1):
-        x[n].append((far[n][1], 0))
     out = update(1, out, ())
-    out, y[0][-1], y[1][-1] = lax.optimization_barrier((out, y[0][-1], y[1][-1]))
+    out, y[0][-1], y[1][-1], y[0][0], y[1][0] = lax.optimization_barrier(
+        (out, y[0][-1], y[1][-1], y[0][0], y[1][0]))
     for s in range(2, cols - 1):
         hop(y, s)
-    for n in (0, 1):
-        y[n].append((far[n][1], size))
+    hop(y, cols - 1, direct=True)
     for q in range(2, chunks):
         out = update(q, out, ())
     return out

time: 257 us -> 251 us (0.977)
  the two profiles are of different devices: /device:TPU:18 before, /device:TPU:0 now
where the time goes in v13:
time: 251 us
  waiting for transfers between devices  96.6 us (38%)
  Pallas kernels  79.3 us (32%)
  starting transfers between devices  57.4 us (23%)
  between operations  13.9 us (6%)
    pallas_call x4, Pallas kernels, chunk_update(): pl.pallas_call(functools.partial(chunk_kernel, starts=starts, parts=parts...  75 us
    ppermute x3, waiting for transfers between devices, local(): lax.ppermute(arrived[s], 'col', [(c, (c + s) % cols) for c in range(cols)])  44.7 us
    ppermute x12, waiting for transfers between devices, hop(): lax.ppermute(left[source], 'col', [(c + step, c) for c in range(cols - st...  42.7 us
    ppermute x12, starting transfers between devices, hop(): lax.ppermute(right[source], 'col', [(c, c + step) for c in range(first, c...  31.9 us
    ppermute x12, starting transfers between devices, hop(): lax.ppermute(left[source], 'col', [(c + step, c) for c in range(cols - st...  15.6 us
    ppermute x12, waiting for transfers between devices, hop(): lax.ppermute(right[source], 'col', [(c, c + step) for c in range(first, c...  9.13 us
    all_to_all x1, starting transfers between devices, local(): lax.all_to_all(blocks, 'row', split_axis=0, concat_axis=0, tiled=True)  5.21 us
  transfers between devices with their start and end apart: 30, of which 13 were waited for; matrix products, arithmetic and copies ran while one was open for 1% of the time, Pallas kernels for 22%

profile of v13, /device:TPU:0, one launch (start us, length us, event | category | flops | bytes accessed | tf_op | source)
XLA Modules:
  0.0 250.5 jit_solution(15137425956671279982)
XLA Ops:
  6.5 4.3 %shard_map.37 = (bf16[8,4,4,16,512]{4,3,2,1,0:T(8,128)(2,1)}, bf16[256,1024]{1,0:T(8,128)(2,1)}, bf16[256,1024]{1,0:T(8,128)(2,1)}, bf16[256,1024]{1,0:T(8,128)(2,1)}, bf16[256,1024]{1,0:T(8,128)(2,1)}) custom-call(s32[1]{0:T(128)} %bitcast.own, bf16[4,8,4,16,512]{4,3,2,1,0:T(8,128)(2,1)} %bitcast.19, bf16[256,4096]{1,0:T(8,128)(2,1)} %w_ref.1), custom_call_target="tpu_custom_call" | custom-call | bytes 8388608 | tf_op jit(solution)/shard_map/pallas_call | solution.py:46
  10.8 0.0 all-gather.3.cloned.1.call-update
  10.9 5.2 %all-to-all-start = ((bf16[8,4,4,16,512]{4,3,2,1,0:T(8,128)(2,1)}), bf16[8,4,4,16,512]{4,3,2,1,0:T(8,128)(2,1)S(1)}, u32[]{:S(2)}, u32[]{:S(2)}) async-start(bf16[8,4,4,16,512]{4,3,2,1,0:T(8,128)(2,1)} %get-tuple-element.32), calls=%async_computation | async-start | bytes 4194304 | tf_op jit(solution)/shard_map/all_to_all | solution.py:215
  16.1 0.0 all-gather.5.cloned.1.call-start
  16.1 3.6 %collective-permute-start.10 = (bf16[256,1024]{1,0:T(8,128)(2,1)}, bf16[256,1024]{1,0:T(8,128)(2,1)S(1)}, u32[]{:S(2)}, u32[]{:S(2)}) collective-permute-start(bf16[256,1024]{1,0:T(8,128)(2,1)} %get-tuple-element.38), channel_id=1, source_target_pairs={{0,3},{1,0},{2,1},{3,2},{4,7},{5,4},{6,5},{7,6},{8,11},{9,8},{10,9... | collective-permute-start | bytes 1572872 | tf_op jit(solution)/shard_map/ppermute | solution.py:214
  19.8 0.0 collective-permute-start.8
  19.8 1.0 collective-permute-start.9
  20.8 11.6 %collective-permute-done.10 = bf16[256,1024]{1,0:T(8,128)(2,1)S(1)} collective-permute-done((bf16[256,1024]{1,0:T(8,128)(2,1)}, bf16[256,1024]{1,0:T(8,128)(2,1)S(1)}, u32[]{:S(2)}, u32[]{:S(2)}) %collective-permute-start.10) | collective-permute-done | bytes 524320 | tf_op jit(solution)/shard_map/ppermute | solution.py:214
  32.4 12.1 %collective-permute-done.8 = bf16[256,1024]{1,0:T(8,128)(2,1)S(1)} collective-permute-done((bf16[256,1024]{1,0:T(8,128)(2,1)}, bf16[256,1024]{1,0:T(8,128)(2,1)S(1)}, u32[]{:S(2)}, u32[]{:S(2)}) %collective-permute-start.8) | collective-permute-done | bytes 524320 | tf_op jit(solution)/shard_map/ppermute | solution.py:214
  44.5 21.0 %collective-permute-done.9 = bf16[256,1024]{1,0:T(8,128)(2,1)} collective-permute-done((bf16[256,1024]{1,0:T(8,128)(2,1)}, bf16[256,1024]{1,0:T(8,128)(2,1)}, u32[]{:S(2)}, u32[]{:S(2)}) %collective-permute-start.9) | collective-permute-done | bytes 524320 | tf_op jit(solution)/shard_map/ppermute | solution.py:214
  65.4 0.0 all-to-all-done
  65.4 2.3 pad_maximum_fusion
  67.7 0.0 all-gather.5.cloned.1.call-update
  67.8 0.2 fusion
  68.0 1.8 collective-permute-start.2
  69.8 1.3 collective-permute-start.4
  71.1 4.6 %collective-permute-start = (bf16[512,512]{1,0:T(8,128)(2,1)S(1)}, bf16[512,512]{1,0:T(8,128)(2,1)S(1)}, u32[]{:S(2)}, u32[]{:S(2)}) collective-permute-start(bf16[512,512]{1,0:T(8,128)(2,1)S(1)} %bitcast.16), channel_id=1, source_target_pairs={{0,1},{1,2},{2,3},{4,5},{5,6},{6,7},{8,9},{9,10},{10,11},{12,13},{... | collective-permute-start | bytes 1572872 | tf_op jit(solution)/shard_map/ppermute | solution.py:239
  75.7 1.3 collective-permute-start.14
  77.0 5.1 %collective-permute-done.2.refs_1_ = bf16[512,512]{1,0:T(8,128)(2,1)S(1)} collective-permute-done((bf16[512,512]{1,0:T(8,128)(2,1)S(1)}, bf16[512,512]{1,0:T(8,128)(2,1)S(1)}, u32[]{:S(2)}, u32[]{:S(2)}) %collective-permute-start.2) | collective-permute-done | bytes 524320 | tf_op jit(solution)/shard_map/ppermute | solution.py:239
  82.1 0.7 collective-permute-start.3
  82.8 3.7 %collective-permute-done.4.refs_4_ = bf16[512,512]{1,0:T(8,128)(2,1)S(1)} collective-permute-done((bf16[512,512]{1,0:T(8,128)(2,1)S(1)}, bf16[512,512]{1,0:T(8,128)(2,1)S(1)}, u32[]{:S(2)}, u32[]{:S(2)}) %collective-permute-start.4) | collective-permute-done | bytes 524320 | tf_op jit(solution)/shard_map/ppermute | solution.py:240
  86.5 1.3 collective-permute-start.5
  87.8 4.0 %collective-permute-done.refs_1_ = bf16[512,512]{1,0:T(8,128)(2,1)S(1)} collective-permute-done((bf16[512,512]{1,0:T(8,128)(2,1)S(1)}, bf16[512,512]{1,0:T(8,128)(2,1)S(1)}, u32[]{:S(2)}, u32[]{:S(2)}) %collective-permute-start) | collective-permute-done | bytes 524320 | tf_op jit(solution)/shard_map/ppermute | solution.py:239
  91.8 1.5 collective-permute-start.1
  93.3 4.5 %collective-permute-done.14.refs_4_ = bf16[512,512]{1,0:T(8,128)(2,1)S(1)} collective-permute-done((bf16[512,512]{1,0:T(8,128)(2,1)S(1)}, bf16[512,512]{1,0:T(8,128)(2,1)S(1)}, u32[]{:S(2)}, u32[]{:S(2)}) %collective-permute-start.14) | collective-permute-done | bytes 524320 | tf_op jit(solution)/shard_map/ppermute | solution.py:240
  97.8 1.3 collective-permute-start.15
  99.1 0.0 collective-permute-done.3.refs_2_
  99.1 9.9 %collective-permute-done.5.refs_5_ = bf16[512,512]{1,0:T(8,128)(2,1)S(1)} collective-permute-done((bf16[512,512]{1,0:T(8,128)(2,1)S(1)}, bf16[512,512]{1,0:T(8,128)(2,1)S(1)}, u32[]{:S(2)}, u32[]{:S(2)}) %collective-permute-start.5) | collective-permute-done | bytes 524320 | tf_op jit(solution)/shard_map/ppermute | solution.py:240
  109.0 3.8 %collective-permute-start.11 = (bf16[512,512]{1,0:T(8,128)(2,1)S(1)}, bf16[512,512]{1,0:T(8,128)(2,1)S(1)}, u32[]{:S(2)}, u32[]{:S(2)}) collective-permute-start(bf16[512,512]{1,0:T(8,128)(2,1)S(1)} %bitcast.11), channel_id=1, source_target_pairs={{0,1},{1,2},{2,3},{4,5},{5,6},{6,7},{8,9},{9,10},{10,11},{12,13},{... | collective-permute-start | bytes 1572872 | tf_op jit(solution)/shard_map/ppermute | solution.py:239
  112.8 1.3 collective-permute-start.12
  114.2 0.7 collective-permute-start.6
  114.9 0.0 collective-permute-done.1.refs_2_
  114.9 1.3 collective-permute-start.7
  116.2 4.2 %collective-permute-done.15.refs_5_ = bf16[512,512]{1,0:T(8,128)(2,1)} collective-permute-done((bf16[512,512]{1,0:T(8,128)(2,1)S(1)}, bf16[512,512]{1,0:T(8,128)(2,1)}, u32[]{:S(2)}, u32[]{:S(2)}) %collective-permute-start.15) | collective-permute-done | bytes 524320 | tf_op jit(solution)/shard_map/ppermute | solution.py:240
  120.4 1.5 collective-permute-start.13
  121.8 0.0 collective-permute-done.11.refs_10_.refs_1_
  121.8 1.3 collective-permute-start.16
  123.1 8.4 %collective-permute-done.12.refs_11_.refs_4_ = bf16[512,512]{1,0:T(8,128)(2,1)S(1)} collective-permute-done((bf16[512,512]{1,0:T(8,128)(2,1)S(1)}, bf16[512,512]{1,0:T(8,128)(2,1)S(1)}, u32[]{:S(2)}, u32[]{:S(2)}) %collective-permute-start.12) | collective-permute-done | bytes 524320 | tf_op jit(solution)/shard_map/ppermute | solution.py:240
  131.5 1.5 collective-permute-start.17
  132.9 0.0 collective-permute-done.6.refs_3_
  133.0 1.3 collective-permute-start.18
  134.3 8.5 %collective-permute-done.7.refs_6_ = bf16[512,512]{1,0:T(8,128)(2,1)} collective-permute-done((bf16[512,512]{1,0:T(8,128)(2,1)S(1)}, bf16[512,512]{1,0:T(8,128)(2,1)}, u32[]{:S(2)}, u32[]{:S(2)}) %collective-permute-start.7) | collective-permute-done | bytes 524320 | tf_op jit(solution)/shard_map/ppermute | solution.py:240
  142.8 18.8 %shard_map.38.refs_10_ = bf16[64,128,1024]{2,1,0:T(8,128)(2,1)} custom-call(s32[1]{0:T(128)} %bitcast.own, bf16[512,512]{1,0:T(8,128)(2,1)} %bitcast.22, bf16[512,512]{1,0:T(8,128)(2,1)} %copy-done.13, bf16[512,512]{1,0:T(8,128)(2,1)} %copy-done.15, bf16[512,512]{1,0:T(8,128)(2,1)} %copy-done.17, bf16[512,512]{1,0:T(8,128)(2,1)} %copy-done.14, ...), custom_call_target="tpu_custom_call" | custom-call | flops 12884901888 | bytes 25165824 | tf_op jit(solution)/shard_map/pallas_call | solution.py:163
  161.6 0.0 collective-permute-done.13.refs_3_
  161.6 0.0 collective-permute-done.16.refs_6_
  161.6 0.0 collective-permute-done.17.refs_2_
  161.6 1.8 collective-permute-done.18.refs_5_
  163.5 1.4 collective-permute-start.19
  164.8 1.3 collective-permute-start.20
  166.1 6.1 %collective-permute-start.25 = (bf16[512,512]{1,0:T(8,128)(2,1)S(1)}, bf16[512,512]{1,0:T(8,128)(2,1)S(1)}, u32[]{:S(2)}, u32[]{:S(2)}) collective-permute-start(bf16[512,512]{1,0:T(8,128)(2,1)S(1)} %bitcast.13), channel_id=1, source_target_pairs={{0,3},{4,7},{8,11},{12,15},{16,19},{20,23},{24,27},{28,31}} | collective-permute-start | bytes 1572872 | tf_op jit(solution)/shard_map/ppermute | solution.py:239
  172.3 1.3 collective-permute-start.26
  173.6 18.7 %shard_map.39.refs_10_ = bf16[64,128,1024]{2,1,0:T(8,128)(2,1)} custom-call(s32[1]{0:T(128)} %bitcast.own, bf16[512,512]{1,0:T(8,128)(2,1)} %bitcast.18, bf16[512,512]{1,0:T(8,128)(2,1)} %copy-done.3, bf16[512,512]{1,0:T(8,128)(2,1)} %collective-permute-done.1.refs_2_, ...), custom_call_target="tpu_custom_call", output_to_operand_aliasing={{}: (11, {})} | custom-call | flops 12884901888 | bytes 25165824 | tf_op jit(solution)/shard_map/pallas_call | solution.py:163
  192.3 0.0 collective-permute-done.19.refs_1_
  192.4 0.0 collective-permute-done.20.refs_4_
  192.4 0.7 collective-permute-start.21
  193.1 7.8 %collective-permute-start.22 = (bf16[512,512]{1,0:T(8,128)(2,1)S(1)}, bf16[512,512]{1,0:T(8,128)(2,1)}, u32[]{:S(2)}, u32[]{:S(2)}) collective-permute-start(bf16[512,512]{1,0:T(8,128)(2,1)S(1)} %bitcast.8), channel_id=1, source_target_pairs={{0,3},{4,7},{8,11},{12,15},{16,19},{20,23},{24,27},{28,31}} | collective-permute-start | bytes 1572872 | tf_op jit(solution)/shard_map/ppermute | solution.py:239
  200.9 1.3 collective-permute-start.23
  202.2 1.5 collective-permute-start.24
  203.7 0.0 collective-permute-done.26.refs_6_
  203.7 0.8 copy-done.11
  204.5 18.7 %shard_map.40.refs_10_ = bf16[64,128,1024]{2,1,0:T(8,128)(2,1)} custom-call(s32[1]{0:T(128)} %bitcast.own, bf16[512,512]{1,0:T(8,128)(2,1)} %bitcast.15, bf16[512,512]{1,0:T(8,128)(2,1)} %copy-done.5, bf16[512,512]{1,0:T(8,128)(2,1)} %collective-permute-done.17.refs_2_, bf16[512,512]{1,0:T(8,128)(2,1)} %copy-done.9, ...), custom_call_target="tpu_custom_call", output_to_operand_aliasing={{}: (11, {})} | custom-call | flops 12884901888 | bytes 25165824 | tf_op jit(solution)/shard_map/pallas_call | solution.py:163
  223.2 0.0 collective-permute-done.21.refs_2_
  223.3 1.6 collective-permute-done.23.refs_5_
  224.9 18.7 %shard_map.41 = bf16[64,128,1024]{2,1,0:T(8,128)(2,1)} custom-call(s32[1]{0:T(128)} %bitcast.own, bf16[512,512]{1,0:T(8,128)(2,1)} %bitcast.10, bf16[512,512]{1,0:T(8,128)(2,1)} %copy-done.7, bf16[512,512]{1,0:T(8,128)(2,1)} %copy-done.10, bf16[512,512]{1,0:T(8,128)(2,1)} %collective-permute-done.22.refs_3_, ...), custom_call_target="tpu_custom_call", output_to_operand_aliasing={{}: (11, {})} | custom-call | flops 12884901888 | bytes 25165824 | tf_op jit(solution)/shard_map/pallas_call | solution.py:163
  (41 shorter events, 0.1 us)
Async XLA Ops:
  6.5 136.3 %all-gather.3.cloned.1.call-start = ((), (), s32[]{:S(2)}) async-start(), calls=%async_computation.1 | async-start | bytes 4718592 | tf_op jit(solution)/shard_map/all_gather | solution.py:219
  10.9 54.6 %all-to-all-start = ((bf16[8,4,4,16,512]{4,3,2,1,0:T(8,128)(2,1)}), bf16[8,4,4,16,512]{4,3,2,1,0:T(8,128)(2,1)S(1)}, u32[]{:S(2)}, u32[]{:S(2)}) async-start(bf16[8,4,4,16,512]{4,3,2,1,0:T(8,128)(2,1)} %get-tuple-element.32), calls=%async_computation | async-start | bytes 4194304 | tf_op jit(solution)/shard_map/all_to_all | solution.py:215
  16.1 126.8 %all-gather.5.cloned.1.call-start = ((), (), s32[]{:S(2)}) async-start(), calls=%async_computation.2 | async-start | bytes 14155776 | tf_op jit(solution)/shard_map/all_gather | solution.py:219
  16.1 16.2 %collective-permute-start.10 = (bf16[256,1024]{1,0:T(8,128)(2,1)}, bf16[256,1024]{1,0:T(8,128)(2,1)S(1)}, u32[]{:S(2)}, u32[]{:S(2)}) collective-permute-start(bf16[256,1024]{1,0:T(8,128)(2,1)} %get-tuple-element.38), channel_id=1, source_target_pairs={{0,3},{1,0},{2,1},{3,2},{4,7},{5,4},{6,5},{7,6},{8,11},{9,8},{10,9... | collective-permute-start | bytes 1572872 | tf_op jit(solution)/shard_map/ppermute | solution.py:214
  19.8 24.7 %collective-permute-start.8 = (bf16[256,1024]{1,0:T(8,128)(2,1)}, bf16[256,1024]{1,0:T(8,128)(2,1)S(1)}, u32[]{:S(2)}, u32[]{:S(2)}) collective-permute-start(bf16[256,1024]{1,0:T(8,128)(2,1)} %get-tuple-element.36), channel_id=1, source_target_pairs={{0,1},{1,2},{2,3},{3,0},{4,5},{5,6},{6,7},{7,4},{8,9},{9,10},{10,1... | collective-permute-start | bytes 1572872 | tf_op jit(solution)/shard_map/ppermute | solution.py:214
  19.8 45.7 %collective-permute-start.9 = (bf16[256,1024]{1,0:T(8,128)(2,1)}, bf16[256,1024]{1,0:T(8,128)(2,1)}, u32[]{:S(2)}, u32[]{:S(2)}) collective-permute-start(bf16[256,1024]{1,0:T(8,128)(2,1)} %get-tuple-element.37), channel_id=1, source_target_pairs={{0,2},{1,3},{2,0},{3,1},{4,6},{5,7},{6,4},{7,5},{8,10},{9,11},{10,... | collective-permute-start | bytes 1572872 | tf_op jit(solution)/shard_map/ppermute | solution.py:214
  68.0 63.5 %copy-start.2 = (bf16[8,1,4,16,512]{4,3,2,1,0:T(8,128)(2,1)}, bf16[8,1,4,16,512]{4,3,2,1,0:T(8,128)(2,1)S(1)}, u32[]{:S(2)}) copy-start(bf16[8,1,4,16,512]{4,3,2,1,0:T(8,128)(2,1)S(1)} %get-tuple-element.62) | copy-start | bytes 1572868
  68.0 65.0 %copy-start.12 = (bf16[8,1,4,16,512]{4,3,2,1,0:T(8,128)(2,1)}, bf16[8,1,4,16,512]{4,3,2,1,0:T(8,128)(2,1)S(1)}, u32[]{:S(2)}) copy-start(bf16[8,1,4,16,512]{4,3,2,1,0:T(8,128)(2,1)S(1)} %get-tuple-element.61) | copy-start | bytes 1572868
  68.0 104.3 %copy-start.1 = (bf16[8,1,4,16,512]{4,3,2,1,0:T(8,128)(2,1)}, bf16[8,1,4,16,512]{4,3,2,1,0:T(8,128)(2,1)S(1)}, u32[]{:S(2)}) copy-start(bf16[8,1,4,16,512]{4,3,2,1,0:T(8,128)(2,1)S(1)} %get-tuple-element.60) | copy-start | bytes 1572868
  68.0 134.2 %copy-start = (bf16[8,1,4,16,512]{4,3,2,1,0:T(8,128)(2,1)}, bf16[8,1,4,16,512]{4,3,2,1,0:T(8,128)(2,1)S(1)}, u32[]{:S(2)}) copy-start(bf16[8,1,4,16,512]{4,3,2,1,0:T(8,128)(2,1)S(1)} %get-tuple-element.59) | copy-start | bytes 1572868
  68.0 14.1 %collective-permute-start.2 = (bf16[512,512]{1,0:T(8,128)(2,1)S(1)}, bf16[512,512]{1,0:T(8,128)(2,1)S(1)}, u32[]{:S(2)}, u32[]{:S(2)}) collective-permute-start(bf16[512,512]{1,0:T(8,128)(2,1)S(1)} %bitcast.20), channel_id=1, source_target_pairs={{0,1},{1,2},{2,3},{4,5},{5,6},{6,7},{8,9},{9,10},{10,11},{12,13},{... | collective-permute-start | bytes 1572872 | tf_op jit(solution)/shard_map/ppermute | solution.py:239
  69.8 16.8 %collective-permute-start.4 = (bf16[512,512]{1,0:T(8,128)(2,1)S(1)}, bf16[512,512]{1,0:T(8,128)(2,1)S(1)}, u32[]{:S(2)}, u32[]{:S(2)}) collective-permute-start(bf16[512,512]{1,0:T(8,128)(2,1)S(1)} %bitcast.21), channel_id=1, source_target_pairs={{1,0},{2,1},{3,2},{5,4},{6,5},{7,6},{9,8},{10,9},{11,10},{13,12},{... | collective-permute-start | bytes 1572872 | tf_op jit(solution)/shard_map/ppermute | solution.py:240
  71.1 20.7 %collective-permute-start = (bf16[512,512]{1,0:T(8,128)(2,1)S(1)}, bf16[512,512]{1,0:T(8,128)(2,1)S(1)}, u32[]{:S(2)}, u32[]{:S(2)}) collective-permute-start(bf16[512,512]{1,0:T(8,128)(2,1)S(1)} %bitcast.16), channel_id=1, source_target_pairs={{0,1},{1,2},{2,3},{4,5},{5,6},{6,7},{8,9},{9,10},{10,11},{12,13},{... | collective-permute-start | bytes 1572872 | tf_op jit(solution)/shard_map/ppermute | solution.py:239
  75.7 22.1 %collective-permute-start.14 = (bf16[512,512]{1,0:T(8,128)(2,1)S(1)}, bf16[512,512]{1,0:T(8,128)(2,1)S(1)}, u32[]{:S(2)}, u32[]{:S(2)}) collective-permute-start(bf16[512,512]{1,0:T(8,128)(2,1)S(1)} %bitcast.17), channel_id=1, source_target_pairs={{1,0},{2,1},{3,2},{5,4},{6,5},{7,6},{9,8},{10,9},{11,10},{13,12},{... | collective-permute-start | bytes 1572872 | tf_op jit(solution)/shard_map/ppermute | solution.py:240
  82.1 50.8 %copy-start.13 = (bf16[512,512]{1,0:T(8,128)(2,1)}, bf16[512,512]{1,0:T(8,128)(2,1)S(1)}, u32[]{:S(2)}) copy-start(bf16[512,512]{1,0:T(8,128)(2,1)S(1)} %collective-permute-done.2.refs_1_) | copy-start | bytes 1572868
  82.1 17.0 %collective-permute-start.3 = (bf16[512,512]{1,0:T(8,128)(2,1)S(1)}, bf16[512,512]{1,0:T(8,128)(2,1)S(1)}, u32[]{:S(2)}, u32[]{:S(2)}) collective-permute-start(bf16[512,512]{1,0:T(8,128)(2,1)S(1)} %collective-permute-done.2.refs_1_), channel_id=1, source_target_pairs={{1,2},{2,3},{5,6},{6,7},{9,10},{10,11},{13,14},{14,15},{17,18},{18... | collective-permute-start | bytes 1572872 | tf_op jit(solution)/shard_map/ppermute | solution.py:239
  86.5 47.7 %copy-start.14 = (bf16[512,512]{1,0:T(8,128)(2,1)}, bf16[512,512]{1,0:T(8,128)(2,1)S(1)}, u32[]{:S(2)}) copy-start(bf16[512,512]{1,0:T(8,128)(2,1)S(1)} %collective-permute-done.4.refs_4_) | copy-start | bytes 1572868
  86.5 22.5 %collective-permute-start.5 = (bf16[512,512]{1,0:T(8,128)(2,1)S(1)}, bf16[512,512]{1,0:T(8,128)(2,1)S(1)}, u32[]{:S(2)}, u32[]{:S(2)}) collective-permute-start(bf16[512,512]{1,0:T(8,128)(2,1)S(1)} %collective-permute-done.4.refs_4_), channel_id=1, source_target_pairs={{1,0},{2,1},{5,4},{6,5},{9,8},{10,9},{13,12},{14,13},{17,16},{18,1... | collective-permute-start | bytes 1572872 | tf_op jit(solution)/shard_map/ppermute | solution.py:240
  91.8 69.8 %copy-start.3 = (bf16[512,512]{1,0:T(8,128)(2,1)}, bf16[512,512]{1,0:T(8,128)(2,1)S(1)}, u32[]{:S(2)}) copy-start(bf16[512,512]{1,0:T(8,128)(2,1)S(1)} %collective-permute-done.refs_1_) | copy-start | bytes 1572868
  91.8 23.1 %collective-permute-start.1 = (bf16[512,512]{1,0:T(8,128)(2,1)S(1)}, bf16[512,512]{1,0:T(8,128)(2,1)}, u32[]{:S(2)}, u32[]{:S(2)}) collective-permute-start(bf16[512,512]{1,0:T(8,128)(2,1)S(1)} %collective-permute-done.refs_1_), channel_id=1, source_target_pairs={{1,2},{2,3},{5,6},{6,7},{9,10},{10,11},{13,14},{14,15},{17,18},{18... | collective-permute-start | bytes 1572872 | tf_op jit(solution)/shard_map/ppermute | solution.py:239
  97.8 63.8 %copy-start.4 = (bf16[512,512]{1,0:T(8,128)(2,1)}, bf16[512,512]{1,0:T(8,128)(2,1)S(1)}, u32[]{:S(2)}) copy-start(bf16[512,512]{1,0:T(8,128)(2,1)S(1)} %collective-permute-done.14.refs_4_) | copy-start | bytes 1572868
  97.8 22.6 %collective-permute-start.15 = (bf16[512,512]{1,0:T(8,128)(2,1)S(1)}, bf16[512,512]{1,0:T(8,128)(2,1)}, u32[]{:S(2)}, u32[]{:S(2)}) collective-permute-start(bf16[512,512]{1,0:T(8,128)(2,1)S(1)} %collective-permute-done.14.refs_4_), channel_id=1, source_target_pairs={{1,0},{2,1},{5,4},{6,5},{9,8},{10,9},{13,12},{14,13},{17,16},{18,1... | collective-permute-start | bytes 1572872 | tf_op jit(solution)/shard_map/ppermute | solution.py:240
  99.1 35.2 %copy-start.15 = (bf16[512,512]{1,0:T(8,128)(2,1)}, bf16[512,512]{1,0:T(8,128)(2,1)S(1)}, u32[]{:S(2)}) copy-start(bf16[512,512]{1,0:T(8,128)(2,1)S(1)} %collective-permute-done.3.refs_2_) | copy-start | bytes 1572868
  109.0 25.3 %copy-start.16 = (bf16[512,512]{1,0:T(8,128)(2,1)}, bf16[512,512]{1,0:T(8,128)(2,1)S(1)}, u32[]{:S(2)}) copy-start(bf16[512,512]{1,0:T(8,128)(2,1)S(1)} %collective-permute-done.5.refs_5_) | copy-start | bytes 1572868
  109.0 12.8 %collective-permute-start.11 = (bf16[512,512]{1,0:T(8,128)(2,1)S(1)}, bf16[512,512]{1,0:T(8,128)(2,1)S(1)}, u32[]{:S(2)}, u32[]{:S(2)}) collective-permute-start(bf16[512,512]{1,0:T(8,128)(2,1)S(1)} %bitcast.11), channel_id=1, source_target_pairs={{0,1},{1,2},{2,3},{4,5},{5,6},{6,7},{8,9},{9,10},{10,11},{12,13},{... | collective-permute-start | bytes 1572872 | tf_op jit(solution)/shard_map/ppermute | solution.py:239
  112.8 18.6 %collective-permute-start.12 = (bf16[512,512]{1,0:T(8,128)(2,1)S(1)}, bf16[512,512]{1,0:T(8,128)(2,1)S(1)}, u32[]{:S(2)}, u32[]{:S(2)}) collective-permute-start(bf16[512,512]{1,0:T(8,128)(2,1)S(1)} %bitcast.12), channel_id=1, source_target_pairs={{1,0},{2,1},{3,2},{5,4},{6,5},{7,6},{9,8},{10,9},{11,10},{13,12},{... | collective-permute-start | bytes 1572872 | tf_op jit(solution)/shard_map/ppermute | solution.py:240
  114.2 18.8 %collective-permute-start.6 = (bf16[512,512]{1,0:T(8,128)(2,1)S(1)}, bf16[512,512]{1,0:T(8,128)(2,1)S(1)}, u32[]{:S(2)}, u32[]{:S(2)}) collective-permute-start(bf16[512,512]{1,0:T(8,128)(2,1)S(1)} %collective-permute-done.3.refs_2_), channel_id=1, source_target_pairs={{2,3},{6,7},{10,11},{14,15},{18,19},{22,23},{26,27},{30,31}} | collective-permute-start | bytes 1572872 | tf_op jit(solution)/shard_map/ppermute | solution.py:239
  114.9 28.0 %collective-permute-start.7 = (bf16[512,512]{1,0:T(8,128)(2,1)S(1)}, bf16[512,512]{1,0:T(8,128)(2,1)}, u32[]{:S(2)}, u32[]{:S(2)}) collective-permute-start(bf16[512,512]{1,0:T(8,128)(2,1)S(1)} %collective-permute-done.5.refs_5_), channel_id=1, source_target_pairs={{1,0},{5,4},{9,8},{13,12},{17,16},{21,20},{25,24},{29,28}} | collective-permute-start | bytes 1572872 | tf_op jit(solution)/shard_map/ppermute | solution.py:240
  120.4 41.3 %collective-permute-start.13 = (bf16[512,512]{1,0:T(8,128)(2,1)}, bf16[512,512]{1,0:T(8,128)(2,1)}, u32[]{:S(2)}, u32[]{:S(2)}) collective-permute-start(bf16[512,512]{1,0:T(8,128)(2,1)} %collective-permute-done.1.refs_2_), channel_id=1, source_target_pairs={{2,3},{6,7},{10,11},{14,15},{18,19},{22,23},{26,27},{30,31}} | collective-permute-start | bytes 1572872 | tf_op jit(solution)/shard_map/ppermute | solution.py:239
  121.8 21.0 %copy-start.5 = (bf16[512,512]{1,0:T(8,128)(2,1)}, bf16[512,512]{1,0:T(8,128)(2,1)S(1)}, u32[]{:S(2)}) copy-start(bf16[512,512]{1,0:T(8,128)(2,1)S(1)} %collective-permute-done.11.refs_10_.refs_1_) | copy-start | bytes 1572868
  121.8 39.8 %collective-permute-start.16 = (bf16[512,512]{1,0:T(8,128)(2,1)}, bf16[512,512]{1,0:T(8,128)(2,1)}, u32[]{:S(2)}, u32[]{:S(2)}) collective-permute-start(bf16[512,512]{1,0:T(8,128)(2,1)} %collective-permute-done.15.refs_5_), channel_id=1, source_target_pairs={{1,0},{5,4},{9,8},{13,12},{17,16},{21,20},{25,24},{29,28}} | collective-permute-start | bytes 1572872 | tf_op jit(solution)/shard_map/ppermute | solution.py:240
  131.5 11.3 %copy-start.6 = (bf16[512,512]{1,0:T(8,128)(2,1)}, bf16[512,512]{1,0:T(8,128)(2,1)S(1)}, u32[]{:S(2)}) copy-start(bf16[512,512]{1,0:T(8,128)(2,1)S(1)} %collective-permute-done.12.refs_11_.refs_4_) | copy-start | bytes 1572868
  131.5 30.2 %collective-permute-start.17 = (bf16[512,512]{1,0:T(8,128)(2,1)S(1)}, bf16[512,512]{1,0:T(8,128)(2,1)}, u32[]{:S(2)}, u32[]{:S(2)}) collective-permute-start(bf16[512,512]{1,0:T(8,128)(2,1)S(1)} %collective-permute-done.11.refs_10_.refs_1_), channel_id=1, source_target_pairs={{1,2},{2,3},{5,6},{6,7},{9,10},{10,11},{13,14},{14,15},{17,18},{18... | collective-permute-start | bytes 1572872 | tf_op jit(solution)/shard_map/ppermute | solution.py:239
  133.0 1.3 copy-start.17
  133.0 30.5 %collective-permute-start.18 = (bf16[512,512]{1,0:T(8,128)(2,1)S(1)}, bf16[512,512]{1,0:T(8,128)(2,1)}, u32[]{:S(2)}, u32[]{:S(2)}) collective-permute-start(bf16[512,512]{1,0:T(8,128)(2,1)S(1)} %collective-permute-done.12.refs_11_.refs_4_), channel_id=1, source_target_pairs={{1,0},{2,1},{5,4},{6,5},{9,8},{10,9},{13,12},{14,13},{17,16},{18,1... | collective-permute-start | bytes 1572872 | tf_op jit(solution)/shard_map/ppermute | solution.py:240
  163.5 28.9 %collective-permute-start.19 = (bf16[512,512]{1,0:T(8,128)(2,1)S(1)}, bf16[512,512]{1,0:T(8,128)(2,1)S(1)}, u32[]{:S(2)}, u32[]{:S(2)}) collective-permute-start(bf16[512,512]{1,0:T(8,128)(2,1)S(1)} %bitcast.6), channel_id=1, source_target_pairs={{0,1},{1,2},{2,3},{4,5},{5,6},{6,7},{8,9},{9,10},{10,11},{12,13},{... | collective-permute-start | bytes 1572872 | tf_op jit(solution)/shard_map/ppermute | solution.py:239
  164.8 27.5 %collective-permute-start.20 = (bf16[512,512]{1,0:T(8,128)(2,1)S(1)}, bf16[512,512]{1,0:T(8,128)(2,1)S(1)}, u32[]{:S(2)}, u32[]{:S(2)}) collective-permute-start(bf16[512,512]{1,0:T(8,128)(2,1)S(1)} %bitcast.7), channel_id=1, source_target_pairs={{1,0},{2,1},{3,2},{5,4},{6,5},{7,6},{9,8},{10,9},{11,10},{13,12},{... | collective-permute-start | bytes 1572872 | tf_op jit(solution)/shard_map/ppermute | solution.py:240
  166.1 36.0 %collective-permute-start.25 = (bf16[512,512]{1,0:T(8,128)(2,1)S(1)}, bf16[512,512]{1,0:T(8,128)(2,1)S(1)}, u32[]{:S(2)}, u32[]{:S(2)}) collective-permute-start(bf16[512,512]{1,0:T(8,128)(2,1)S(1)} %bitcast.13), channel_id=1, source_target_pairs={{0,3},{4,7},{8,11},{12,15},{16,19},{20,23},{24,27},{28,31}} | collective-permute-start | bytes 1572872 | tf_op jit(solution)/shard_map/ppermute | solution.py:239
  172.3 31.4 %collective-permute-start.26 = (bf16[512,512]{1,0:T(8,128)(2,1)S(1)}, bf16[512,512]{1,0:T(8,128)(2,1)S(1)}, u32[]{:S(2)}, u32[]{:S(2)}) collective-permute-start(bf16[512,512]{1,0:T(8,128)(2,1)S(1)} %bitcast.14), channel_id=1, source_target_pairs={{3,0},{7,4},{11,8},{15,12},{19,16},{23,20},{27,24},{31,28}} | collective-permute-start | bytes 1572872 | tf_op jit(solution)/shard_map/ppermute | solution.py:240
  192.4 30.9 %copy-start.7 = (bf16[512,512]{1,0:T(8,128)(2,1)}, bf16[512,512]{1,0:T(8,128)(2,1)S(1)}, u32[]{:S(2)}) copy-start(bf16[512,512]{1,0:T(8,128)(2,1)S(1)} %collective-permute-done.19.refs_1_) | copy-start | bytes 1572868
  192.4 30.9 %copy-start.8 = (bf16[512,512]{1,0:T(8,128)(2,1)}, bf16[512,512]{1,0:T(8,128)(2,1)S(1)}, u32[]{:S(2)}) copy-start(bf16[512,512]{1,0:T(8,128)(2,1)S(1)} %collective-permute-done.20.refs_4_) | copy-start | bytes 1572868
  192.4 30.9 %collective-permute-start.21 = (bf16[512,512]{1,0:T(8,128)(2,1)S(1)}, bf16[512,512]{1,0:T(8,128)(2,1)S(1)}, u32[]{:S(2)}, u32[]{:S(2)}) collective-permute-start(bf16[512,512]{1,0:T(8,128)(2,1)S(1)} %collective-permute-done.19.refs_1_), channel_id=1, source_target_pairs={{1,2},{2,3},{5,6},{6,7},{9,10},{10,11},{13,14},{14,15},{17,18},{18... | collective-permute-start | bytes 1572872 | tf_op jit(solution)/shard_map/ppermute | solution.py:239
  193.1 30.2 %collective-permute-start.22 = (bf16[512,512]{1,0:T(8,128)(2,1)S(1)}, bf16[512,512]{1,0:T(8,128)(2,1)}, u32[]{:S(2)}, u32[]{:S(2)}) collective-permute-start(bf16[512,512]{1,0:T(8,128)(2,1)S(1)} %bitcast.8), channel_id=1, source_target_pairs={{0,3},{4,7},{8,11},{12,15},{16,19},{20,23},{24,27},{28,31}} | collective-permute-start | bytes 1572872 | tf_op jit(solution)/shard_map/ppermute | solution.py:239
  200.9 24.1 %collective-permute-start.23 = (bf16[512,512]{1,0:T(8,128)(2,1)S(1)}, bf16[512,512]{1,0:T(8,128)(2,1)}, u32[]{:S(2)}, u32[]{:S(2)}) collective-permute-start(bf16[512,512]{1,0:T(8,128)(2,1)S(1)} %collective-permute-done.20.refs_4_), channel_id=1, source_target_pairs={{1,0},{2,1},{5,4},{6,5},{9,8},{10,9},{13,12},{14,13},{17,16},{18,1... | collective-permute-start | bytes 1572872 | tf_op jit(solution)/shard_map/ppermute | solution.py:240
  202.2 1.5 copy-start.9
  202.2 22.7 %collective-permute-start.24 = (bf16[512,512]{1,0:T(8,128)(2,1)S(1)}, bf16[512,512]{1,0:T(8,128)(2,1)}, u32[]{:S(2)}, u32[]{:S(2)}) collective-permute-start(bf16[512,512]{1,0:T(8,128)(2,1)S(1)} %bitcast.9), channel_id=1, source_target_pairs={{3,0},{7,4},{11,8},{15,12},{19,16},{23,20},{27,24},{31,28}} | collective-permute-start | bytes 1572872 | tf_op jit(solution)/shard_map/ppermute | solution.py:240
  203.7 0.8 copy-start.11
  223.3 1.7 copy-start.10
Sparse Core Ops, SparseCore 0:
  11.0 50.2 all-gather.2
  67.9 72.5 all-gather.4

commit v14 on v13

--- a/solution.py
+++ b/solution.py
@@ -273,7 +273,7 @@
     out, *ends = after((out, *[side[-1] for side in moving]), x)
     for side, end in zip(moving, ends):
         side[-1] = end
-    hop(x, cols - 1, direct=True)
+    hop(x, cols - 1)
     out = after(out, y)
     hop(y, 1)
     out = update(1, out, ())

time: 251 us -> 245 us (0.976)
  starting transfers between devices: 57.4 us -> 50.9 us
    ppermute x12, starting transfers between devices: 31.9 us -> 25.4 us  [hop(): lax.ppermute(right[source], 'col', [(c, c + step) for c in range(first, c...]
  transfers between devices with their start and end apart: 30 -> 30, of which waited for: 13 -> 13; matrix products, arithmetic and copies ran while one was open for 1% -> 1% of each run, Pallas kernels for 22% -> 23%
where the time goes in v14:
time: 245 us
  waiting for transfers between devices  97.2 us (40%)
  Pallas kernels  79.3 us (32%)
  starting transfers between devices  50.9 us (21%)
  between operations  13.9 us (6%)
    pallas_call x4, Pallas kernels, chunk_update(): pl.pallas_call(functools.partial(chunk_kernel, starts=starts, parts=parts...  75 us
    ppermute x3, waiting for transfers between devices, local(): lax.ppermute(arrived[s], 'col', [(c, (c + s) % cols) for c in range(cols)])  44.7 us
    ppermute x12, waiting for transfers between devices, hop(): lax.ppermute(left[source], 'col', [(c + step, c) for c in range(cols - st...  43.3 us
    ppermute x12, starting transfers between devices, hop(): lax.ppermute(right[source], 'col', [(c, c + step) for c in range(first, c...  25.4 us
    ppermute x12, starting transfers between devices, hop(): lax.ppermute(left[source], 'col', [(c + step, c) for c in range(cols - st...  15.7 us
    ppermute x12, waiting for transfers between devices, hop(): lax.ppermute(right[source], 'col', [(c, c + step) for c in range(first, c...  9.13 us
    all_to_all x1, starting transfers between devices, local(): lax.all_to_all(blocks, 'row', split_axis=0, concat_axis=0, tiled=True)  5.21 us
  transfers between devices with their start and end apart: 30, of which 13 were waited for; matrix products, arithmetic and copies ran while one was open for 1% of the time, Pallas kernels for 23%

profile of v14, /device:TPU:0, one launch (start us, length us, event | category | flops | bytes accessed | tf_op | source)
XLA Modules:
  0.0 244.6 jit_solution(10749010595833684798)
XLA Ops:
  6.5 4.3 %shard_map.37 = (bf16[8,4,4,16,512]{4,3,2,1,0:T(8,128)(2,1)}, bf16[256,1024]{1,0:T(8,128)(2,1)}, bf16[256,1024]{1,0:T(8,128)(2,1)}, bf16[256,1024]{1,0:T(8,128)(2,1)}, bf16[256,1024]{1,0:T(8,128)(2,1)}) custom-call(s32[1]{0:T(128)} %bitcast.own, bf16[4,8,4,16,512]{4,3,2,1,0:T(8,128)(2,1)} %bitcast.17, bf16[256,4096]{1,0:T(8,128)(2,1)} %w_ref.1), custom_call_target="tpu_custom_call" | custom-call | bytes 8388608 | tf_op jit(solution)/shard_map/pallas_call | solution.py:46
  10.8 0.0 all-gather.3.cloned.1.call-update
  10.9 5.2 %all-to-all-start = ((bf16[8,4,4,16,512]{4,3,2,1,0:T(8,128)(2,1)}), bf16[8,4,4,16,512]{4,3,2,1,0:T(8,128)(2,1)S(1)}, u32[]{:S(2)}, u32[]{:S(2)}) async-start(bf16[8,4,4,16,512]{4,3,2,1,0:T(8,128)(2,1)} %get-tuple-element.31), calls=%async_computation | async-start | bytes 4194304 | tf_op jit(solution)/shard_map/all_to_all | solution.py:215
  16.1 0.0 all-gather.5.cloned.1.call-start
  16.1 3.6 %collective-permute-start.10 = (bf16[256,1024]{1,0:T(8,128)(2,1)}, bf16[256,1024]{1,0:T(8,128)(2,1)S(1)}, u32[]{:S(2)}, u32[]{:S(2)}) collective-permute-start(bf16[256,1024]{1,0:T(8,128)(2,1)} %get-tuple-element.37), channel_id=1, source_target_pairs={{0,3},{1,0},{2,1},{3,2},{4,7},{5,4},{6,5},{7,6},{8,11},{9,8},{10,9... | collective-permute-start | bytes 1572872 | tf_op jit(solution)/shard_map/ppermute | solution.py:214
  19.7 0.0 collective-permute-start.8
  19.8 1.0 collective-permute-start.9
  20.8 11.6 %collective-permute-done.10 = bf16[256,1024]{1,0:T(8,128)(2,1)S(1)} collective-permute-done((bf16[256,1024]{1,0:T(8,128)(2,1)}, bf16[256,1024]{1,0:T(8,128)(2,1)S(1)}, u32[]{:S(2)}, u32[]{:S(2)}) %collective-permute-start.10) | collective-permute-done | bytes 524320 | tf_op jit(solution)/shard_map/ppermute | solution.py:214
  32.4 12.1 %collective-permute-done.8 = bf16[256,1024]{1,0:T(8,128)(2,1)S(1)} collective-permute-done((bf16[256,1024]{1,0:T(8,128)(2,1)}, bf16[256,1024]{1,0:T(8,128)(2,1)S(1)}, u32[]{:S(2)}, u32[]{:S(2)}) %collective-permute-start.8) | collective-permute-done | bytes 524320 | tf_op jit(solution)/shard_map/ppermute | solution.py:214
  44.4 21.0 %collective-permute-done.9 = bf16[256,1024]{1,0:T(8,128)(2,1)} collective-permute-done((bf16[256,1024]{1,0:T(8,128)(2,1)}, bf16[256,1024]{1,0:T(8,128)(2,1)}, u32[]{:S(2)}, u32[]{:S(2)}) %collective-permute-start.9) | collective-permute-done | bytes 524320 | tf_op jit(solution)/shard_map/ppermute | solution.py:214
  65.4 0.0 all-to-all-done
  65.4 2.3 pad_maximum_fusion
  67.7 0.0 all-gather.5.cloned.1.call-update
  67.8 0.2 fusion
  68.0 1.8 collective-permute-start.2
  69.8 1.3 collective-permute-start.4
  71.1 4.6 %collective-permute-start = (bf16[512,512]{1,0:T(8,128)(2,1)S(1)}, bf16[512,512]{1,0:T(8,128)(2,1)S(1)}, u32[]{:S(2)}, u32[]{:S(2)}) collective-permute-start(bf16[512,512]{1,0:T(8,128)(2,1)S(1)} %bitcast.14), channel_id=1, source_target_pairs={{0,1},{1,2},{2,3},{4,5},{5,6},{6,7},{8,9},{9,10},{10,11},{12,13},{... | collective-permute-start | bytes 1572872 | tf_op jit(solution)/shard_map/ppermute | solution.py:239
  75.7 1.3 collective-permute-start.14
  77.0 5.1 %collective-permute-done.2.refs_1_ = bf16[512,512]{1,0:T(8,128)(2,1)S(1)} collective-permute-done((bf16[512,512]{1,0:T(8,128)(2,1)S(1)}, bf16[512,512]{1,0:T(8,128)(2,1)S(1)}, u32[]{:S(2)}, u32[]{:S(2)}) %collective-permute-start.2) | collective-permute-done | bytes 524320 | tf_op jit(solution)/shard_map/ppermute | solution.py:239
  82.1 0.7 collective-permute-start.3
  82.8 3.7 %collective-permute-done.4.refs_4_ = bf16[512,512]{1,0:T(8,128)(2,1)S(1)} collective-permute-done((bf16[512,512]{1,0:T(8,128)(2,1)S(1)}, bf16[512,512]{1,0:T(8,128)(2,1)S(1)}, u32[]{:S(2)}, u32[]{:S(2)}) %collective-permute-start.4) | collective-permute-done | bytes 524320 | tf_op jit(solution)/shard_map/ppermute | solution.py:240
  86.6 1.3 collective-permute-start.5
  87.8 4.0 %collective-permute-done.refs_1_ = bf16[512,512]{1,0:T(8,128)(2,1)S(1)} collective-permute-done((bf16[512,512]{1,0:T(8,128)(2,1)S(1)}, bf16[512,512]{1,0:T(8,128)(2,1)S(1)}, u32[]{:S(2)}, u32[]{:S(2)}) %collective-permute-start) | collective-permute-done | bytes 524320 | tf_op jit(solution)/shard_map/ppermute | solution.py:239
  91.8 1.4 collective-permute-start.1
  93.3 4.5 %collective-permute-done.14.refs_4_ = bf16[512,512]{1,0:T(8,128)(2,1)S(1)} collective-permute-done((bf16[512,512]{1,0:T(8,128)(2,1)S(1)}, bf16[512,512]{1,0:T(8,128)(2,1)S(1)}, u32[]{:S(2)}, u32[]{:S(2)}) %collective-permute-start.14) | collective-permute-done | bytes 524320 | tf_op jit(solution)/shard_map/ppermute | solution.py:240
  97.8 1.3 collective-permute-start.15
  99.1 0.0 collective-permute-done.3.refs_2_
  99.1 9.9 %collective-permute-done.5.refs_5_ = bf16[512,512]{1,0:T(8,128)(2,1)S(1)} collective-permute-done((bf16[512,512]{1,0:T(8,128)(2,1)S(1)}, bf16[512,512]{1,0:T(8,128)(2,1)S(1)}, u32[]{:S(2)}, u32[]{:S(2)}) %collective-permute-start.5) | collective-permute-done | bytes 524320 | tf_op jit(solution)/shard_map/ppermute | solution.py:240
  109.0 3.8 %collective-permute-start.11 = (bf16[512,512]{1,0:T(8,128)(2,1)S(1)}, bf16[512,512]{1,0:T(8,128)(2,1)S(1)}, u32[]{:S(2)}, u32[]{:S(2)}) collective-permute-start(bf16[512,512]{1,0:T(8,128)(2,1)S(1)} %bitcast.11), channel_id=1, source_target_pairs={{0,1},{1,2},{2,3},{4,5},{5,6},{6,7},{8,9},{9,10},{10,11},{12,13},{... | collective-permute-start | bytes 1572872 | tf_op jit(solution)/shard_map/ppermute | solution.py:239
  112.9 1.3 collective-permute-start.12
  114.2 0.7 collective-permute-start.6
  114.9 1.3 collective-permute-start.7
  116.2 4.2 %collective-permute-done.15.refs_5_ = bf16[512,512]{1,0:T(8,128)(2,1)} collective-permute-done((bf16[512,512]{1,0:T(8,128)(2,1)S(1)}, bf16[512,512]{1,0:T(8,128)(2,1)}, u32[]{:S(2)}, u32[]{:S(2)}) %collective-permute-start.15) | collective-permute-done | bytes 524320 | tf_op jit(solution)/shard_map/ppermute | solution.py:240
  120.4 1.5 collective-permute-start.13
  121.8 0.0 collective-permute-done.11.refs_10_.refs_1_
  121.8 1.3 collective-permute-start.16
  123.1 8.4 %collective-permute-done.12.refs_11_.refs_4_ = bf16[512,512]{1,0:T(8,128)(2,1)S(1)} collective-permute-done((bf16[512,512]{1,0:T(8,128)(2,1)S(1)}, bf16[512,512]{1,0:T(8,128)(2,1)S(1)}, u32[]{:S(2)}, u32[]{:S(2)}) %collective-permute-start.12) | collective-permute-done | bytes 524320 | tf_op jit(solution)/shard_map/ppermute | solution.py:240
  131.5 1.4 collective-permute-start.17
  133.0 1.3 collective-permute-start.18
  134.3 8.5 %collective-permute-done.7.refs_6_ = bf16[512,512]{1,0:T(8,128)(2,1)} collective-permute-done((bf16[512,512]{1,0:T(8,128)(2,1)S(1)}, bf16[512,512]{1,0:T(8,128)(2,1)}, u32[]{:S(2)}, u32[]{:S(2)}) %collective-permute-start.7) | collective-permute-done | bytes 524320 | tf_op jit(solution)/shard_map/ppermute | solution.py:240
  142.8 18.8 %shard_map.38.refs_10_ = bf16[64,128,1024]{2,1,0:T(8,128)(2,1)} custom-call(s32[1]{0:T(128)} %bitcast.own, bf16[512,512]{1,0:T(8,128)(2,1)} %bitcast.20, bf16[512,512]{1,0:T(8,128)(2,1)} %copy-done.14, bf16[512,512]{1,0:T(8,128)(2,1)} %copy-done.16, bf16[512,512]{1,0:T(8,128)(2,1)} %copy-done.18, bf16[512,512]{1,0:T(8,128)(2,1)} %copy-done.15, ...), custom_call_target="tpu_custom_call" | custom-call | flops 12884901888 | bytes 25165824 | tf_op jit(solution)/shard_map/pallas_call | solution.py:163
  161.6 0.0 collective-permute-done.13.refs_3_
  161.7 0.0 collective-permute-done.17.refs_2_
  161.7 1.8 collective-permute-done.18.refs_5_
  163.5 1.4 collective-permute-start.19
  164.8 1.3 collective-permute-start.20
  166.1 0.7 collective-permute-start.25
  166.8 1.3 collective-permute-start.26
  168.1 18.8 %shard_map.39.refs_10_ = bf16[64,128,1024]{2,1,0:T(8,128)(2,1)} custom-call(s32[1]{0:T(128)} %bitcast.own, bf16[512,512]{1,0:T(8,128)(2,1)} %bitcast.16, bf16[512,512]{1,0:T(8,128)(2,1)} %copy-done.3, bf16[512,512]{1,0:T(8,128)(2,1)} %collective-permute-done.1.refs_2_, ...), custom_call_target="tpu_custom_call", output_to_operand_aliasing={{}: (11, {})} | custom-call | flops 12884901888 | bytes 25165824 | tf_op jit(solution)/shard_map/pallas_call | solution.py:163
  186.9 0.0 collective-permute-done.19.refs_1_
  186.9 0.0 collective-permute-done.20.refs_4_
  186.9 0.7 collective-permute-start.21
  187.6 6.7 %collective-permute-start.22 = (bf16[512,512]{1,0:T(8,128)(2,1)S(1)}, bf16[512,512]{1,0:T(8,128)(2,1)S(1)}, u32[]{:S(2)}, u32[]{:S(2)}) collective-permute-start(bf16[512,512]{1,0:T(8,128)(2,1)S(1)} %bitcast.8), channel_id=1, source_target_pairs={{0,3},{4,7},{8,11},{12,15},{16,19},{20,23},{24,27},{28,31}} | collective-permute-start | bytes 1572872 | tf_op jit(solution)/shard_map/ppermute | solution.py:239
  194.4 1.3 collective-permute-start.23
  195.7 0.0 collective-permute-done.25.refs_3_
  195.7 1.5 collective-permute-start.24
  197.2 0.0 collective-permute-done.26.refs_6_
  197.2 0.8 copy-done.11
  198.0 18.7 %shard_map.40.refs_10_ = bf16[64,128,1024]{2,1,0:T(8,128)(2,1)} custom-call(s32[1]{0:T(128)} %bitcast.own, bf16[512,512]{1,0:T(8,128)(2,1)} %bitcast.13, bf16[512,512]{1,0:T(8,128)(2,1)} %copy-done.5, bf16[512,512]{1,0:T(8,128)(2,1)} %collective-permute-done.17.refs_2_, bf16[512,512]{1,0:T(8,128)(2,1)} %copy-done.9, ...), custom_call_target="tpu_custom_call", output_to_operand_aliasing={{}: (11, {})} | custom-call | flops 12884901888 | bytes 25165824 | tf_op jit(solution)/shard_map/pallas_call | solution.py:163
  216.8 0.0 collective-permute-done.21.refs_2_
  216.8 0.0 collective-permute-done.22.refs_3_
  216.8 2.2 collective-permute-done.23.refs_5_
  219.0 0.0 collective-permute-done.24.refs_6_
  219.0 18.7 %shard_map.41 = bf16[64,128,1024]{2,1,0:T(8,128)(2,1)} custom-call(s32[1]{0:T(128)} %bitcast.own, bf16[512,512]{1,0:T(8,128)(2,1)} %bitcast.10, bf16[512,512]{1,0:T(8,128)(2,1)} %copy-done.7, bf16[512,512]{1,0:T(8,128)(2,1)} %copy-done.10, bf16[512,512]{1,0:T(8,128)(2,1)} %copy-done.12, bf16[512,512]{1,0:T(8,128)(2,1)} %copy-done.8, ...), custom_call_target="tpu_custom_call", output_to_operand_aliasing={{}: (11, {})} | custom-call | flops 12884901888 | bytes 25165824 | tf_op jit(solution)/shard_map/pallas_call | solution.py:163
  (43 shorter events, 0.1 us)
Async XLA Ops:
  6.5 136.3 %all-gather.3.cloned.1.call-start = ((), (), s32[]{:S(2)}) async-start(), calls=%async_computation.1 | async-start | bytes 4718592 | tf_op jit(solution)/shard_map/all_gather | solution.py:219
  10.9 54.6 %all-to-all-start = ((bf16[8,4,4,16,512]{4,3,2,1,0:T(8,128)(2,1)}), bf16[8,4,4,16,512]{4,3,2,1,0:T(8,128)(2,1)S(1)}, u32[]{:S(2)}, u32[]{:S(2)}) async-start(bf16[8,4,4,16,512]{4,3,2,1,0:T(8,128)(2,1)} %get-tuple-element.31), calls=%async_computation | async-start | bytes 4194304 | tf_op jit(solution)/shard_map/all_to_all | solution.py:215
  16.1 126.8 %all-gather.5.cloned.1.call-start = ((), (), s32[]{:S(2)}) async-start(), calls=%async_computation.2 | async-start | bytes 14155776 | tf_op jit(solution)/shard_map/all_gather | solution.py:219
  16.1 16.2 %collective-permute-start.10 = (bf16[256,1024]{1,0:T(8,128)(2,1)}, bf16[256,1024]{1,0:T(8,128)(2,1)S(1)}, u32[]{:S(2)}, u32[]{:S(2)}) collective-permute-start(bf16[256,1024]{1,0:T(8,128)(2,1)} %get-tuple-element.37), channel_id=1, source_target_pairs={{0,3},{1,0},{2,1},{3,2},{4,7},{5,4},{6,5},{7,6},{8,11},{9,8},{10,9... | collective-permute-start | bytes 1572872 | tf_op jit(solution)/shard_map/ppermute | solution.py:214
  19.7 24.7 %collective-permute-start.8 = (bf16[256,1024]{1,0:T(8,128)(2,1)}, bf16[256,1024]{1,0:T(8,128)(2,1)S(1)}, u32[]{:S(2)}, u32[]{:S(2)}) collective-permute-start(bf16[256,1024]{1,0:T(8,128)(2,1)} %get-tuple-element.35), channel_id=1, source_target_pairs={{0,1},{1,2},{2,3},{3,0},{4,5},{5,6},{6,7},{7,4},{8,9},{9,10},{10,1... | collective-permute-start | bytes 1572872 | tf_op jit(solution)/shard_map/ppermute | solution.py:214
  19.8 45.7 %collective-permute-start.9 = (bf16[256,1024]{1,0:T(8,128)(2,1)}, bf16[256,1024]{1,0:T(8,128)(2,1)}, u32[]{:S(2)}, u32[]{:S(2)}) collective-permute-start(bf16[256,1024]{1,0:T(8,128)(2,1)} %get-tuple-element.36), channel_id=1, source_target_pairs={{0,2},{1,3},{2,0},{3,1},{4,6},{5,7},{6,4},{7,5},{8,10},{9,11},{10,... | collective-permute-start | bytes 1572872 | tf_op jit(solution)/shard_map/ppermute | solution.py:214
  68.0 63.5 %copy-start.2 = (bf16[8,1,4,16,512]{4,3,2,1,0:T(8,128)(2,1)}, bf16[8,1,4,16,512]{4,3,2,1,0:T(8,128)(2,1)S(1)}, u32[]{:S(2)}) copy-start(bf16[8,1,4,16,512]{4,3,2,1,0:T(8,128)(2,1)S(1)} %get-tuple-element.60) | copy-start | bytes 1572868
  68.0 65.0 %copy-start.13 = (bf16[8,1,4,16,512]{4,3,2,1,0:T(8,128)(2,1)}, bf16[8,1,4,16,512]{4,3,2,1,0:T(8,128)(2,1)S(1)}, u32[]{:S(2)}) copy-start(bf16[8,1,4,16,512]{4,3,2,1,0:T(8,128)(2,1)S(1)} %get-tuple-element.59) | copy-start | bytes 1572868
  68.0 93.6 %copy-start.1 = (bf16[8,1,4,16,512]{4,3,2,1,0:T(8,128)(2,1)}, bf16[8,1,4,16,512]{4,3,2,1,0:T(8,128)(2,1)S(1)}, u32[]{:S(2)}) copy-start(bf16[8,1,4,16,512]{4,3,2,1,0:T(8,128)(2,1)S(1)} %get-tuple-element.58) | copy-start | bytes 1572868
  68.0 127.7 %copy-start = (bf16[8,1,4,16,512]{4,3,2,1,0:T(8,128)(2,1)}, bf16[8,1,4,16,512]{4,3,2,1,0:T(8,128)(2,1)S(1)}, u32[]{:S(2)}) copy-start(bf16[8,1,4,16,512]{4,3,2,1,0:T(8,128)(2,1)S(1)} %get-tuple-element.57) | copy-start | bytes 1572868
  68.0 14.1 %collective-permute-start.2 = (bf16[512,512]{1,0:T(8,128)(2,1)S(1)}, bf16[512,512]{1,0:T(8,128)(2,1)S(1)}, u32[]{:S(2)}, u32[]{:S(2)}) collective-permute-start(bf16[512,512]{1,0:T(8,128)(2,1)S(1)} %bitcast.18), channel_id=1, source_target_pairs={{0,1},{1,2},{2,3},{4,5},{5,6},{6,7},{8,9},{9,10},{10,11},{12,13},{... | collective-permute-start | bytes 1572872 | tf_op jit(solution)/shard_map/ppermute | solution.py:239
  69.8 16.8 %collective-permute-start.4 = (bf16[512,512]{1,0:T(8,128)(2,1)S(1)}, bf16[512,512]{1,0:T(8,128)(2,1)S(1)}, u32[]{:S(2)}, u32[]{:S(2)}) collective-permute-start(bf16[512,512]{1,0:T(8,128)(2,1)S(1)} %bitcast.19), channel_id=1, source_target_pairs={{1,0},{2,1},{3,2},{5,4},{6,5},{7,6},{9,8},{10,9},{11,10},{13,12},{... | collective-permute-start | bytes 1572872 | tf_op jit(solution)/shard_map/ppermute | solution.py:240
  71.1 20.7 %collective-permute-start = (bf16[512,512]{1,0:T(8,128)(2,1)S(1)}, bf16[512,512]{1,0:T(8,128)(2,1)S(1)}, u32[]{:S(2)}, u32[]{:S(2)}) collective-permute-start(bf16[512,512]{1,0:T(8,128)(2,1)S(1)} %bitcast.14), channel_id=1, source_target_pairs={{0,1},{1,2},{2,3},{4,5},{5,6},{6,7},{8,9},{9,10},{10,11},{12,13},{... | collective-permute-start | bytes 1572872 | tf_op jit(solution)/shard_map/ppermute | solution.py:239
  75.7 22.1 %collective-permute-start.14 = (bf16[512,512]{1,0:T(8,128)(2,1)S(1)}, bf16[512,512]{1,0:T(8,128)(2,1)S(1)}, u32[]{:S(2)}, u32[]{:S(2)}) collective-permute-start(bf16[512,512]{1,0:T(8,128)(2,1)S(1)} %bitcast.15), channel_id=1, source_target_pairs={{1,0},{2,1},{3,2},{5,4},{6,5},{7,6},{9,8},{10,9},{11,10},{13,12},{... | collective-permute-start | bytes 1572872 | tf_op jit(solution)/shard_map/ppermute | solution.py:240
  82.1 50.8 %copy-start.14 = (bf16[512,512]{1,0:T(8,128)(2,1)}, bf16[512,512]{1,0:T(8,128)(2,1)S(1)}, u32[]{:S(2)}) copy-start(bf16[512,512]{1,0:T(8,128)(2,1)S(1)} %collective-permute-done.2.refs_1_) | copy-start | bytes 1572868
  82.1 17.0 %collective-permute-start.3 = (bf16[512,512]{1,0:T(8,128)(2,1)S(1)}, bf16[512,512]{1,0:T(8,128)(2,1)S(1)}, u32[]{:S(2)}, u32[]{:S(2)}) collective-permute-start(bf16[512,512]{1,0:T(8,128)(2,1)S(1)} %collective-permute-done.2.refs_1_), channel_id=1, source_target_pairs={{1,2},{2,3},{5,6},{6,7},{9,10},{10,11},{13,14},{14,15},{17,18},{18... | collective-permute-start | bytes 1572872 | tf_op jit(solution)/shard_map/ppermute | solution.py:239
  86.6 47.7 %copy-start.15 = (bf16[512,512]{1,0:T(8,128)(2,1)}, bf16[512,512]{1,0:T(8,128)(2,1)S(1)}, u32[]{:S(2)}) copy-start(bf16[512,512]{1,0:T(8,128)(2,1)S(1)} %collective-permute-done.4.refs_4_) | copy-start | bytes 1572868
  86.6 22.5 %collective-permute-start.5 = (bf16[512,512]{1,0:T(8,128)(2,1)S(1)}, bf16[512,512]{1,0:T(8,128)(2,1)S(1)}, u32[]{:S(2)}, u32[]{:S(2)}) collective-permute-start(bf16[512,512]{1,0:T(8,128)(2,1)S(1)} %collective-permute-done.4.refs_4_), channel_id=1, source_target_pairs={{1,0},{2,1},{5,4},{6,5},{9,8},{10,9},{13,12},{14,13},{17,16},{18,1... | collective-permute-start | bytes 1572872 | tf_op jit(solution)/shard_map/ppermute | solution.py:240
  91.8 69.8 %copy-start.3 = (bf16[512,512]{1,0:T(8,128)(2,1)}, bf16[512,512]{1,0:T(8,128)(2,1)S(1)}, u32[]{:S(2)}) copy-start(bf16[512,512]{1,0:T(8,128)(2,1)S(1)} %collective-permute-done.refs_1_) | copy-start | bytes 1572868
  91.8 23.1 %collective-permute-start.1 = (bf16[512,512]{1,0:T(8,128)(2,1)S(1)}, bf16[512,512]{1,0:T(8,128)(2,1)}, u32[]{:S(2)}, u32[]{:S(2)}) collective-permute-start(bf16[512,512]{1,0:T(8,128)(2,1)S(1)} %collective-permute-done.refs_1_), channel_id=1, source_target_pairs={{1,2},{2,3},{5,6},{6,7},{9,10},{10,11},{13,14},{14,15},{17,18},{18... | collective-permute-start | bytes 1572872 | tf_op jit(solution)/shard_map/ppermute | solution.py:239
  97.8 63.8 %copy-start.4 = (bf16[512,512]{1,0:T(8,128)(2,1)}, bf16[512,512]{1,0:T(8,128)(2,1)S(1)}, u32[]{:S(2)}) copy-start(bf16[512,512]{1,0:T(8,128)(2,1)S(1)} %collective-permute-done.14.refs_4_) | copy-start | bytes 1572868
  97.8 22.6 %collective-permute-start.15 = (bf16[512,512]{1,0:T(8,128)(2,1)S(1)}, bf16[512,512]{1,0:T(8,128)(2,1)}, u32[]{:S(2)}, u32[]{:S(2)}) collective-permute-start(bf16[512,512]{1,0:T(8,128)(2,1)S(1)} %collective-permute-done.14.refs_4_), channel_id=1, source_target_pairs={{1,0},{2,1},{5,4},{6,5},{9,8},{10,9},{13,12},{14,13},{17,16},{18,1... | collective-permute-start | bytes 1572872 | tf_op jit(solution)/shard_map/ppermute | solution.py:240
  99.1 35.2 %copy-start.16 = (bf16[512,512]{1,0:T(8,128)(2,1)}, bf16[512,512]{1,0:T(8,128)(2,1)S(1)}, u32[]{:S(2)}) copy-start(bf16[512,512]{1,0:T(8,128)(2,1)S(1)} %collective-permute-done.3.refs_2_) | copy-start | bytes 1572868
  109.0 25.3 %copy-start.17 = (bf16[512,512]{1,0:T(8,128)(2,1)}, bf16[512,512]{1,0:T(8,128)(2,1)S(1)}, u32[]{:S(2)}) copy-start(bf16[512,512]{1,0:T(8,128)(2,1)S(1)} %collective-permute-done.5.refs_5_) | copy-start | bytes 1572868
  109.0 12.8 %collective-permute-start.11 = (bf16[512,512]{1,0:T(8,128)(2,1)S(1)}, bf16[512,512]{1,0:T(8,128)(2,1)S(1)}, u32[]{:S(2)}, u32[]{:S(2)}) collective-permute-start(bf16[512,512]{1,0:T(8,128)(2,1)S(1)} %bitcast.11), channel_id=1, source_target_pairs={{0,1},{1,2},{2,3},{4,5},{5,6},{6,7},{8,9},{9,10},{10,11},{12,13},{... | collective-permute-start | bytes 1572872 | tf_op jit(solution)/shard_map/ppermute | solution.py:239
  112.9 18.6 %collective-permute-start.12 = (bf16[512,512]{1,0:T(8,128)(2,1)S(1)}, bf16[512,512]{1,0:T(8,128)(2,1)S(1)}, u32[]{:S(2)}, u32[]{:S(2)}) collective-permute-start(bf16[512,512]{1,0:T(8,128)(2,1)S(1)} %bitcast.12), channel_id=1, source_target_pairs={{1,0},{2,1},{3,2},{5,4},{6,5},{7,6},{9,8},{10,9},{11,10},{13,12},{... | collective-permute-start | bytes 1572872 | tf_op jit(solution)/shard_map/ppermute | solution.py:240
  114.2 18.8 %collective-permute-start.6 = (bf16[512,512]{1,0:T(8,128)(2,1)S(1)}, bf16[512,512]{1,0:T(8,128)(2,1)S(1)}, u32[]{:S(2)}, u32[]{:S(2)}) collective-permute-start(bf16[512,512]{1,0:T(8,128)(2,1)S(1)} %collective-permute-done.3.refs_2_), channel_id=1, source_target_pairs={{2,3},{6,7},{10,11},{14,15},{18,19},{22,23},{26,27},{30,31}} | collective-permute-start | bytes 1572872 | tf_op jit(solution)/shard_map/ppermute | solution.py:239
  114.9 28.0 %collective-permute-start.7 = (bf16[512,512]{1,0:T(8,128)(2,1)S(1)}, bf16[512,512]{1,0:T(8,128)(2,1)}, u32[]{:S(2)}, u32[]{:S(2)}) collective-permute-start(bf16[512,512]{1,0:T(8,128)(2,1)S(1)} %collective-permute-done.5.refs_5_), channel_id=1, source_target_pairs={{1,0},{5,4},{9,8},{13,12},{17,16},{21,20},{25,24},{29,28}} | collective-permute-start | bytes 1572872 | tf_op jit(solution)/shard_map/ppermute | solution.py:240
  120.4 41.3 %collective-permute-start.13 = (bf16[512,512]{1,0:T(8,128)(2,1)}, bf16[512,512]{1,0:T(8,128)(2,1)}, u32[]{:S(2)}, u32[]{:S(2)}) collective-permute-start(bf16[512,512]{1,0:T(8,128)(2,1)} %collective-permute-done.1.refs_2_), channel_id=1, source_target_pairs={{2,3},{6,7},{10,11},{14,15},{18,19},{22,23},{26,27},{30,31}} | collective-permute-start | bytes 1572872 | tf_op jit(solution)/shard_map/ppermute | solution.py:239
  121.8 21.0 %copy-start.5 = (bf16[512,512]{1,0:T(8,128)(2,1)}, bf16[512,512]{1,0:T(8,128)(2,1)S(1)}, u32[]{:S(2)}) copy-start(bf16[512,512]{1,0:T(8,128)(2,1)S(1)} %collective-permute-done.11.refs_10_.refs_1_) | copy-start | bytes 1572868
  121.8 39.8 %collective-permute-start.16 = (bf16[512,512]{1,0:T(8,128)(2,1)}, bf16[512,512]{1,0:T(8,128)(2,1)}, u32[]{:S(2)}, u32[]{:S(2)}) collective-permute-start(bf16[512,512]{1,0:T(8,128)(2,1)} %collective-permute-done.15.refs_5_), channel_id=1, source_target_pairs={{1,0},{5,4},{9,8},{13,12},{17,16},{21,20},{25,24},{29,28}} | collective-permute-start | bytes 1572872 | tf_op jit(solution)/shard_map/ppermute | solution.py:240
  131.5 11.3 %copy-start.6 = (bf16[512,512]{1,0:T(8,128)(2,1)}, bf16[512,512]{1,0:T(8,128)(2,1)S(1)}, u32[]{:S(2)}) copy-start(bf16[512,512]{1,0:T(8,128)(2,1)S(1)} %collective-permute-done.12.refs_11_.refs_4_) | copy-start | bytes 1572868
  131.5 30.2 %collective-permute-start.17 = (bf16[512,512]{1,0:T(8,128)(2,1)S(1)}, bf16[512,512]{1,0:T(8,128)(2,1)}, u32[]{:S(2)}, u32[]{:S(2)}) collective-permute-start(bf16[512,512]{1,0:T(8,128)(2,1)S(1)} %collective-permute-done.11.refs_10_.refs_1_), channel_id=1, source_target_pairs={{1,2},{2,3},{5,6},{6,7},{9,10},{10,11},{13,14},{14,15},{17,18},{18... | collective-permute-start | bytes 1572872 | tf_op jit(solution)/shard_map/ppermute | solution.py:239
  133.0 1.3 copy-start.18
  133.0 30.5 %collective-permute-start.18 = (bf16[512,512]{1,0:T(8,128)(2,1)S(1)}, bf16[512,512]{1,0:T(8,128)(2,1)}, u32[]{:S(2)}, u32[]{:S(2)}) collective-permute-start(bf16[512,512]{1,0:T(8,128)(2,1)S(1)} %collective-permute-done.12.refs_11_.refs_4_), channel_id=1, source_target_pairs={{1,0},{2,1},{5,4},{6,5},{9,8},{10,9},{13,12},{14,13},{17,16},{18,1... | collective-permute-start | bytes 1572872 | tf_op jit(solution)/shard_map/ppermute | solution.py:240
  163.5 23.4 %collective-permute-start.19 = (bf16[512,512]{1,0:T(8,128)(2,1)S(1)}, bf16[512,512]{1,0:T(8,128)(2,1)S(1)}, u32[]{:S(2)}, u32[]{:S(2)}) collective-permute-start(bf16[512,512]{1,0:T(8,128)(2,1)S(1)} %bitcast.6), channel_id=1, source_target_pairs={{0,1},{1,2},{2,3},{4,5},{5,6},{6,7},{8,9},{9,10},{10,11},{12,13},{... | collective-permute-start | bytes 1572872 | tf_op jit(solution)/shard_map/ppermute | solution.py:239
  164.8 22.1 %collective-permute-start.20 = (bf16[512,512]{1,0:T(8,128)(2,1)S(1)}, bf16[512,512]{1,0:T(8,128)(2,1)S(1)}, u32[]{:S(2)}, u32[]{:S(2)}) collective-permute-start(bf16[512,512]{1,0:T(8,128)(2,1)S(1)} %bitcast.7), channel_id=1, source_target_pairs={{1,0},{2,1},{3,2},{5,4},{6,5},{7,6},{9,8},{10,9},{11,10},{13,12},{... | collective-permute-start | bytes 1572872 | tf_op jit(solution)/shard_map/ppermute | solution.py:240
  166.1 29.6 %collective-permute-start.25 = (bf16[512,512]{1,0:T(8,128)(2,1)}, bf16[512,512]{1,0:T(8,128)(2,1)S(1)}, u32[]{:S(2)}, u32[]{:S(2)}) collective-permute-start(bf16[512,512]{1,0:T(8,128)(2,1)} %collective-permute-done.17.refs_2_), channel_id=1, source_target_pairs={{2,3},{6,7},{10,11},{14,15},{18,19},{22,23},{26,27},{30,31}} | collective-permute-start | bytes 1572872 | tf_op jit(solution)/shard_map/ppermute | solution.py:239
  166.8 30.4 %collective-permute-start.26 = (bf16[512,512]{1,0:T(8,128)(2,1)}, bf16[512,512]{1,0:T(8,128)(2,1)S(1)}, u32[]{:S(2)}, u32[]{:S(2)}) collective-permute-start(bf16[512,512]{1,0:T(8,128)(2,1)} %collective-permute-done.18.refs_5_), channel_id=1, source_target_pairs={{1,0},{5,4},{9,8},{13,12},{17,16},{21,20},{25,24},{29,28}} | collective-permute-start | bytes 1572872 | tf_op jit(solution)/shard_map/ppermute | solution.py:240
  186.9 29.8 %copy-start.7 = (bf16[512,512]{1,0:T(8,128)(2,1)}, bf16[512,512]{1,0:T(8,128)(2,1)S(1)}, u32[]{:S(2)}) copy-start(bf16[512,512]{1,0:T(8,128)(2,1)S(1)} %collective-permute-done.19.refs_1_) | copy-start | bytes 1572868
  186.9 29.8 %copy-start.8 = (bf16[512,512]{1,0:T(8,128)(2,1)}, bf16[512,512]{1,0:T(8,128)(2,1)S(1)}, u32[]{:S(2)}) copy-start(bf16[512,512]{1,0:T(8,128)(2,1)S(1)} %collective-permute-done.20.refs_4_) | copy-start | bytes 1572868
  186.9 29.8 %collective-permute-start.21 = (bf16[512,512]{1,0:T(8,128)(2,1)S(1)}, bf16[512,512]{1,0:T(8,128)(2,1)S(1)}, u32[]{:S(2)}, u32[]{:S(2)}) collective-permute-start(bf16[512,512]{1,0:T(8,128)(2,1)S(1)} %collective-permute-done.19.refs_1_), channel_id=1, source_target_pairs={{1,2},{2,3},{5,6},{6,7},{9,10},{10,11},{13,14},{14,15},{17,18},{18... | collective-permute-start | bytes 1572872 | tf_op jit(solution)/shard_map/ppermute | solution.py:239
  187.6 29.2 %collective-permute-start.22 = (bf16[512,512]{1,0:T(8,128)(2,1)S(1)}, bf16[512,512]{1,0:T(8,128)(2,1)S(1)}, u32[]{:S(2)}, u32[]{:S(2)}) collective-permute-start(bf16[512,512]{1,0:T(8,128)(2,1)S(1)} %bitcast.8), channel_id=1, source_target_pairs={{0,3},{4,7},{8,11},{12,15},{16,19},{20,23},{24,27},{28,31}} | collective-permute-start | bytes 1572872 | tf_op jit(solution)/shard_map/ppermute | solution.py:239
  194.4 24.6 %collective-permute-start.23 = (bf16[512,512]{1,0:T(8,128)(2,1)S(1)}, bf16[512,512]{1,0:T(8,128)(2,1)}, u32[]{:S(2)}, u32[]{:S(2)}) collective-permute-start(bf16[512,512]{1,0:T(8,128)(2,1)S(1)} %collective-permute-done.20.refs_4_), channel_id=1, source_target_pairs={{1,0},{2,1},{5,4},{6,5},{9,8},{10,9},{13,12},{14,13},{17,16},{18,1... | collective-permute-start | bytes 1572872 | tf_op jit(solution)/shard_map/ppermute | solution.py:240
  195.7 1.5 copy-start.9
  195.7 23.3 %collective-permute-start.24 = (bf16[512,512]{1,0:T(8,128)(2,1)S(1)}, bf16[512,512]{1,0:T(8,128)(2,1)}, u32[]{:S(2)}, u32[]{:S(2)}) collective-permute-start(bf16[512,512]{1,0:T(8,128)(2,1)S(1)} %bitcast.9), channel_id=1, source_target_pairs={{3,0},{7,4},{11,8},{15,12},{19,16},{23,20},{27,24},{31,28}} | collective-permute-start | bytes 1572872 | tf_op jit(solution)/shard_map/ppermute | solution.py:240
  197.2 0.8 copy-start.11
  216.8 2.2 copy-start.10
  216.8 2.2 copy-start.12
Sparse Core Ops, SparseCore 0:
  11.0 50.2 all-gather.2
  67.9 72.5 all-gather.4

commit v15 on v14

--- a/solution.py
+++ b/solution.py
@@ -281,7 +281,9 @@
         (out, y[0][-1], y[1][-1], y[0][0], y[1][0]))
     for s in range(2, cols - 1):
         hop(y, s)
-    hop(y, cols - 1, direct=True)
+    far = lax.ppermute(y[0][0], "col", [(0, cols - 1), (cols - 1, 0)])
+    y[0].append(far)
+    y[1].append(far)
     for q in range(2, chunks):
         out = update(q, out, ())
     return out

time: 245 us -> 246 us (level)
  waiting for transfers between devices: 97.2 us -> 77.6 us
  starting transfers between devices: 50.9 us -> 68.6 us
    ppermute x3, waiting for transfers between devices: 44.7 us -> 33.4 us  [local(): lax.ppermute(arrived[s], 'col', [(c, (c + s) % cols) for c in range(cols)])]
    ppermute x12 -> x11, starting transfers between devices: 25.4 us -> 35.3 us  [hop(): lax.ppermute(right[source], 'col', [(c, c + step) for c in range(first, c...]
    ppermute x12 -> x11, waiting for transfers between devices: 9.13 us -> 0.23 us  [hop(): lax.ppermute(right[source], 'col', [(c, c + step) for c in range(first, c...]
    ppermute x0 -> x1, starting transfers between devices: none -> 8.17 us  [local(): far = lax.ppermute(y[0][0], 'col', [(0, cols - 1), (cols - 1, 0)])]
    ppermute x12 -> x11, starting transfers between devices: 15.7 us -> 14.3 us  [hop(): lax.ppermute(left[source], 'col', [(c + step, c) for c in range(cols - st...]
    ppermute x12 -> x11, waiting for transfers between devices: 43.3 us -> 43.9 us  [hop(): lax.ppermute(left[source], 'col', [(c + step, c) for c in range(cols - st...]
  transfers between devices with their start and end apart: 30 -> 29, of which waited for: 13 -> 10; matrix products, arithmetic and copies ran while one was open for 1% -> 1% of each run, Pallas kernels for 23% -> 23%
where the time goes in v15:
time: 246 us; the launch traced here: 245 us
  Pallas kernels  79.3 us (32%)
  waiting for transfers between devices  77.6 us (32%)
  starting transfers between devices  68.6 us (28%)
  between operations  13.9 us (6%)
  local copies, waits for them, and re-layouts  2.85 us (1%)
    pallas_call x4, Pallas kernels, chunk_update(): pl.pallas_call(functools.partial(chunk_kernel, starts=starts, parts=parts...  75 us
    ppermute x11, waiting for transfers between devices, hop(): lax.ppermute(left[source], 'col', [(c + step, c) for c in range(cols - st...  43.9 us
    ppermute x11, starting transfers between devices, hop(): lax.ppermute(right[source], 'col', [(c, c + step) for c in range(first, c...  35.3 us
    ppermute x3, waiting for transfers between devices, local(): lax.ppermute(arrived[s], 'col', [(c, (c + s) % cols) for c in range(cols)])  33.4 us
    ppermute x11, starting transfers between devices, hop(): lax.ppermute(left[source], 'col', [(c + step, c) for c in range(cols - st...  14.3 us
    ppermute x1, starting transfers between devices, local(): far = lax.ppermute(y[0][0], 'col', [(0, cols - 1), (cols - 1, 0)])  8.17 us
    ppermute x3, starting transfers between devices, local(): lax.ppermute(arrived[s], 'col', [(c, (c + s) % cols) for c in range(cols)])  5.54 us
    all_to_all x1, starting transfers between devices, local(): lax.all_to_all(blocks, 'row', split_axis=0, concat_axis=0, tiled=True)  5.21 us
  transfers between devices with their start and end apart: 29, of which 10 were waited for; matrix products, arithmetic and copies ran while one was open for 1% of the time, Pallas kernels for 23%

profile of v15, /device:TPU:0, one launch (start us, length us, event | category | flops | bytes accessed | tf_op | source)
XLA Modules:
  0.0 244.6 jit_solution(15965904342766133252)
XLA Ops:
  6.5 4.3 %shard_map.37 = (bf16[8,4,4,16,512]{4,3,2,1,0:T(8,128)(2,1)}, bf16[256,1024]{1,0:T(8,128)(2,1)}, bf16[256,1024]{1,0:T(8,128)(2,1)}, bf16[256,1024]{1,0:T(8,128)(2,1)}, bf16[256,1024]{1,0:T(8,128)(2,1)}) custom-call(s32[1]{0:T(128)} %bitcast.own, bf16[4,8,4,16,512]{4,3,2,1,0:T(8,128)(2,1)} %bitcast.16, bf16[256,4096]{1,0:T(8,128)(2,1)} %w_ref.1), custom_call_target="tpu_custom_call" | custom-call | bytes 8388608 | tf_op jit(solution)/shard_map/pallas_call | solution.py:46
  10.8 0.0 all-gather.3.cloned.1.call-update
  10.9 5.2 %all-to-all-start = ((bf16[8,4,4,16,512]{4,3,2,1,0:T(8,128)(2,1)}), bf16[8,4,4,16,512]{4,3,2,1,0:T(8,128)(2,1)S(1)}, u32[]{:S(2)}, u32[]{:S(2)}) async-start(bf16[8,4,4,16,512]{4,3,2,1,0:T(8,128)(2,1)} %get-tuple-element.30), calls=%async_computation | async-start | bytes 4194304 | tf_op jit(solution)/shard_map/all_to_all | solution.py:215
  16.1 0.0 all-gather.5.cloned.1.call-start
  16.1 1.6 collective-permute-start.8
  17.7 2.6 %collective-permute-start.9 = (bf16[256,1024]{1,0:T(8,128)(2,1)}, bf16[256,1024]{1,0:T(8,128)(2,1)S(1)}, u32[]{:S(2)}, u32[]{:S(2)}) collective-permute-start(bf16[256,1024]{1,0:T(8,128)(2,1)} %get-tuple-element.35), channel_id=1, source_target_pairs={{0,2},{1,3},{2,0},{3,1},{4,6},{5,7},{6,4},{7,5},{8,10},{9,11},{10,... | collective-permute-start | bytes 1572872 | tf_op jit(solution)/shard_map/ppermute | solution.py:214
  20.3 1.3 collective-permute-start.10
  21.7 11.4 %collective-permute-done.8 = bf16[256,1024]{1,0:T(8,128)(2,1)S(1)} collective-permute-done((bf16[256,1024]{1,0:T(8,128)(2,1)}, bf16[256,1024]{1,0:T(8,128)(2,1)S(1)}, u32[]{:S(2)}, u32[]{:S(2)}) %collective-permute-start.8) | collective-permute-done | bytes 524320 | tf_op jit(solution)/shard_map/ppermute | solution.py:214
  33.1 22.0 %collective-permute-done.9 = bf16[256,1024]{1,0:T(8,128)(2,1)S(1)} collective-permute-done((bf16[256,1024]{1,0:T(8,128)(2,1)}, bf16[256,1024]{1,0:T(8,128)(2,1)S(1)}, u32[]{:S(2)}, u32[]{:S(2)}) %collective-permute-start.9) | collective-permute-done | bytes 524320 | tf_op jit(solution)/shard_map/ppermute | solution.py:214
  55.0 0.0 collective-permute-done.10
  55.0 0.0 all-to-all-done
  55.1 2.3 pad_maximum_fusion
  57.3 0.0 all-gather.5.cloned.1.call-update
  57.4 0.2 fusion
  57.6 1.3 collective-permute-start.4
  58.9 14.4 %collective-permute-start.2 = (bf16[512,512]{1,0:T(8,128)(2,1)S(1)}, bf16[512,512]{1,0:T(8,128)(2,1)S(1)}, u32[]{:S(2)}, u32[]{:S(2)}) collective-permute-start(bf16[512,512]{1,0:T(8,128)(2,1)S(1)} %bitcast.18), channel_id=1, source_target_pairs={{0,1},{1,2},{2,3},{4,5},{5,6},{6,7},{8,9},{9,10},{10,11},{12,13},{... | collective-permute-start | bytes 1572872 | tf_op jit(solution)/shard_map/ppermute | solution.py:239
  73.3 1.3 collective-permute-start.14
  74.6 4.6 %collective-permute-start = (bf16[512,512]{1,0:T(8,128)(2,1)S(1)}, bf16[512,512]{1,0:T(8,128)(2,1)S(1)}, u32[]{:S(2)}, u32[]{:S(2)}) collective-permute-start(bf16[512,512]{1,0:T(8,128)(2,1)S(1)} %bitcast.14), channel_id=1, source_target_pairs={{0,1},{1,2},{2,3},{4,5},{5,6},{6,7},{8,9},{9,10},{10,11},{12,13},{... | collective-permute-start | bytes 1572872 | tf_op jit(solution)/shard_map/ppermute | solution.py:239
  79.2 4.9 %collective-permute-done.4.refs_4_ = bf16[512,512]{1,0:T(8,128)(2,1)S(1)} collective-permute-done((bf16[512,512]{1,0:T(8,128)(2,1)S(1)}, bf16[512,512]{1,0:T(8,128)(2,1)S(1)}, u32[]{:S(2)}, u32[]{:S(2)}) %collective-permute-start.4) | collective-permute-done | bytes 524320 | tf_op jit(solution)/shard_map/ppermute | solution.py:240
  84.1 1.3 collective-permute-start.5
  85.4 0.2 collective-permute-done.2.refs_1_
  85.6 0.7 collective-permute-start.3
  86.3 9.0 %collective-permute-done.14.refs_4_ = bf16[512,512]{1,0:T(8,128)(2,1)S(1)} collective-permute-done((bf16[512,512]{1,0:T(8,128)(2,1)S(1)}, bf16[512,512]{1,0:T(8,128)(2,1)S(1)}, u32[]{:S(2)}, u32[]{:S(2)}) %collective-permute-start.14) | collective-permute-done | bytes 524320 | tf_op jit(solution)/shard_map/ppermute | solution.py:240
  95.3 1.3 collective-permute-start.15
  96.6 0.0 collective-permute-done.refs_1_
  96.6 1.5 collective-permute-start.1
  98.1 8.5 %collective-permute-done.5.refs_5_ = bf16[512,512]{1,0:T(8,128)(2,1)S(1)} collective-permute-done((bf16[512,512]{1,0:T(8,128)(2,1)S(1)}, bf16[512,512]{1,0:T(8,128)(2,1)S(1)}, u32[]{:S(2)}, u32[]{:S(2)}) %collective-permute-start.5) | collective-permute-done | bytes 524320 | tf_op jit(solution)/shard_map/ppermute | solution.py:240
  106.5 0.0 collective-permute-done.3.refs_2_
  106.6 1.3 collective-permute-start.7
  107.9 5.5 %collective-permute-start.11 = (bf16[512,512]{1,0:T(8,128)(2,1)S(1)}, bf16[512,512]{1,0:T(8,128)(2,1)S(1)}, u32[]{:S(2)}, u32[]{:S(2)}) collective-permute-start(bf16[512,512]{1,0:T(8,128)(2,1)S(1)} %bitcast.10), channel_id=1, source_target_pairs={{0,1},{1,2},{2,3},{4,5},{5,6},{6,7},{8,9},{9,10},{10,11},{12,13},{... | collective-permute-start | bytes 1572872 | tf_op jit(solution)/shard_map/ppermute | solution.py:239
  113.4 1.3 collective-permute-start.12
  114.7 3.2 %collective-permute-done.15.refs_5_ = bf16[512,512]{1,0:T(8,128)(2,1)} collective-permute-done((bf16[512,512]{1,0:T(8,128)(2,1)S(1)}, bf16[512,512]{1,0:T(8,128)(2,1)}, u32[]{:S(2)}, u32[]{:S(2)}) %collective-permute-start.15) | collective-permute-done | bytes 524320 | tf_op jit(solution)/shard_map/ppermute | solution.py:240
  117.9 1.5 collective-permute-start.6
  119.4 1.3 collective-permute-start.16
  120.7 8.3 %collective-permute-done.7.refs_6_ = bf16[512,512]{1,0:T(8,128)(2,1)S(1)} collective-permute-done((bf16[512,512]{1,0:T(8,128)(2,1)S(1)}, bf16[512,512]{1,0:T(8,128)(2,1)S(1)}, u32[]{:S(2)}, u32[]{:S(2)}) %collective-permute-start.7) | collective-permute-done | bytes 524320 | tf_op jit(solution)/shard_map/ppermute | solution.py:240
  129.0 1.5 collective-permute-start.13
  130.5 0.0 collective-permute-done.11.refs_10_.refs_1_
  130.5 1.5 collective-permute-start.17
  132.0 8.3 %collective-permute-done.12.refs_11_.refs_4_ = bf16[512,512]{1,0:T(8,128)(2,1)S(1)} collective-permute-done((bf16[512,512]{1,0:T(8,128)(2,1)S(1)}, bf16[512,512]{1,0:T(8,128)(2,1)S(1)}, u32[]{:S(2)}, u32[]{:S(2)}) %collective-permute-start.12) | collective-permute-done | bytes 524320 | tf_op jit(solution)/shard_map/ppermute | solution.py:240
  140.3 1.3 collective-permute-start.18
  141.6 0.0 all-gather.3.cloned.1.call-done.refs_7_
  141.6 0.0 all-gather.5.cloned.1.call-done.refs_8_
  141.7 18.8 %shard_map.38.refs_10_ = bf16[64,128,1024]{2,1,0:T(8,128)(2,1)} custom-call(s32[1]{0:T(128)} %bitcast.own, bf16[512,512]{1,0:T(8,128)(2,1)} %bitcast.19, bf16[512,512]{1,0:T(8,128)(2,1)} %copy-done.15, bf16[512,512]{1,0:T(8,128)(2,1)} %copy-done.17, bf16[512,512]{1,0:T(8,128)(2,1)} %collective-permute-done.6.refs_3_, bf16[512,512]{1,0:T(8,128)(2,1)} %copy-done.14, ...), custom_call_target="tpu_custom_call" | custom-call | flops 12884901888 | bytes 25165824 | tf_op jit(solution)/shard_map/pallas_call | solution.py:163
  160.5 0.0 collective-permute-done.16.refs_6_
  160.5 0.0 collective-permute-done.17.refs_2_
  160.5 1.7 collective-permute-done.18.refs_5_
  162.2 2.9 %collective-permute-start.19 = (bf16[512,512]{1,0:T(8,128)(2,1)S(1)}, bf16[512,512]{1,0:T(8,128)(2,1)S(1)}, u32[]{:S(2)}, u32[]{:S(2)}) collective-permute-start(bf16[512,512]{1,0:T(8,128)(2,1)S(1)} %bitcast.6), channel_id=1, source_target_pairs={{0,1},{1,2},{2,3},{4,5},{5,6},{6,7},{8,9},{9,10},{10,11},{12,13},{... | collective-permute-start | bytes 1572872 | tf_op jit(solution)/shard_map/ppermute | solution.py:239
  165.1 1.3 collective-permute-start.20
  166.4 0.7 collective-permute-start.24
  167.1 1.3 collective-permute-start.25
  168.4 18.8 %shard_map.39.refs_10_ = bf16[64,128,1024]{2,1,0:T(8,128)(2,1)} custom-call(s32[1]{0:T(128)} %bitcast.own, bf16[512,512]{1,0:T(8,128)(2,1)} %bitcast.15, bf16[512,512]{1,0:T(8,128)(2,1)} %copy-done.5, bf16[512,512]{1,0:T(8,128)(2,1)} %collective-permute-done.1.refs_2_, ...), custom_call_target="tpu_custom_call", output_to_operand_aliasing={{}: (11, {})} | custom-call | flops 12884901888 | bytes 25165824 | tf_op jit(solution)/shard_map/pallas_call | solution.py:163
  187.2 0.0 collective-permute-done.19.refs_1_
  187.2 8.2 %collective-permute-start.22 = (bf16[512,512]{1,0:T(8,128)(2,1)S(1)}, bf16[512,512]{1,0:T(8,128)(2,1)S(1)}, u32[]{:S(2)}, u32[]{:S(2)}) collective-permute-start(bf16[512,512]{1,0:T(8,128)(2,1)S(1)} %bitcast.8), channel_id=1, source_target_pairs={{0,3},{3,0},{4,7},{7,4},{8,11},{11,8},{12,15},{15,12},{16,19},{19,... | collective-permute-start | bytes 1572872 | tf_op jit(solution)/shard_map/ppermute | solution.py:284
  195.4 0.7 collective-permute-start.21
  196.1 1.5 collective-permute-start.23
  197.6 0.0 collective-permute-done.24.refs_3_
  197.6 0.8 copy-done.10
  198.4 0.8 copy-done.11
  199.2 18.7 %shard_map.40.refs_10_ = bf16[64,128,1024]{2,1,0:T(8,128)(2,1)} custom-call(s32[1]{0:T(128)} %bitcast.own, bf16[512,512]{1,0:T(8,128)(2,1)} %bitcast.12, bf16[512,512]{1,0:T(8,128)(2,1)} %copy-done.6, bf16[512,512]{1,0:T(8,128)(2,1)} %collective-permute-done.17.refs_2_, bf16[512,512]{1,0:T(8,128)(2,1)} %copy-done.10, ...), custom_call_target="tpu_custom_call", output_to_operand_aliasing={{}: (11, {})} | custom-call | flops 12884901888 | bytes 25165824 | tf_op jit(solution)/shard_map/pallas_call | solution.py:163
  218.0 0.0 collective-permute-done.22.refs_3_.refs_6_
  218.0 0.0 collective-permute-done.23.refs_5_
  218.0 0.8 copy-done
  218.8 0.2 copy-done.12
  219.0 18.7 %shard_map.41 = bf16[64,128,1024]{2,1,0:T(8,128)(2,1)} custom-call(s32[1]{0:T(128)} %bitcast.own, bf16[512,512]{1,0:T(8,128)(2,1)} %bitcast.9, bf16[512,512]{1,0:T(8,128)(2,1)} %copy-done.8, bf16[512,512]{1,0:T(8,128)(2,1)} %copy-done.12, bf16[512,512]{1,0:T(8,128)(2,1)} %copy-done, bf16[512,512]{1,0:T(8,128)(2,1)} %copy-done.9, ...), custom_call_target="tpu_custom_call", output_to_operand_aliasing={{}: (11, {})} | custom-call | flops 12884901888 | bytes 25165824 | tf_op jit(solution)/shard_map/pallas_call | solution.py:163
  (41 shorter events, 0.1 us)
Async XLA Ops:
  6.5 135.1 %all-gather.3.cloned.1.call-start = ((), (), s32[]{:S(2)}) async-start(), calls=%async_computation.1 | async-start | bytes 4718592 | tf_op jit(solution)/shard_map/all_gather | solution.py:219
  10.9 44.2 %all-to-all-start = ((bf16[8,4,4,16,512]{4,3,2,1,0:T(8,128)(2,1)}), bf16[8,4,4,16,512]{4,3,2,1,0:T(8,128)(2,1)S(1)}, u32[]{:S(2)}, u32[]{:S(2)}) async-start(bf16[8,4,4,16,512]{4,3,2,1,0:T(8,128)(2,1)} %get-tuple-element.30), calls=%async_computation | async-start | bytes 4194304 | tf_op jit(solution)/shard_map/all_to_all | solution.py:215
  16.1 125.6 %all-gather.5.cloned.1.call-start = ((), (), s32[]{:S(2)}) async-start(), calls=%async_computation.2 | async-start | bytes 14155776 | tf_op jit(solution)/shard_map/all_gather | solution.py:219
  16.1 16.9 %collective-permute-start.8 = (bf16[256,1024]{1,0:T(8,128)(2,1)}, bf16[256,1024]{1,0:T(8,128)(2,1)S(1)}, u32[]{:S(2)}, u32[]{:S(2)}) collective-permute-start(bf16[256,1024]{1,0:T(8,128)(2,1)} %get-tuple-element.34), channel_id=1, source_target_pairs={{0,1},{1,2},{2,3},{3,0},{4,5},{5,6},{6,7},{7,4},{8,9},{9,10},{10,1... | collective-permute-start | bytes 1572872 | tf_op jit(solution)/shard_map/ppermute | solution.py:214
  17.7 37.3 %collective-permute-start.9 = (bf16[256,1024]{1,0:T(8,128)(2,1)}, bf16[256,1024]{1,0:T(8,128)(2,1)S(1)}, u32[]{:S(2)}, u32[]{:S(2)}) collective-permute-start(bf16[256,1024]{1,0:T(8,128)(2,1)} %get-tuple-element.35), channel_id=1, source_target_pairs={{0,2},{1,3},{2,0},{3,1},{4,6},{5,7},{6,4},{7,5},{8,10},{9,11},{10,... | collective-permute-start | bytes 1572872 | tf_op jit(solution)/shard_map/ppermute | solution.py:214
  20.3 34.7 %collective-permute-start.10 = (bf16[256,1024]{1,0:T(8,128)(2,1)}, bf16[256,1024]{1,0:T(8,128)(2,1)}, u32[]{:S(2)}, u32[]{:S(2)}) collective-permute-start(bf16[256,1024]{1,0:T(8,128)(2,1)} %get-tuple-element.36), channel_id=1, source_target_pairs={{0,3},{1,0},{2,1},{3,2},{4,7},{5,4},{6,5},{7,6},{8,11},{9,8},{10,9... | collective-permute-start | bytes 1572872 | tf_op jit(solution)/shard_map/ppermute | solution.py:214
  57.6 82.7 %copy-start.3 = (bf16[8,1,4,16,512]{4,3,2,1,0:T(8,128)(2,1)}, bf16[8,1,4,16,512]{4,3,2,1,0:T(8,128)(2,1)S(1)}, u32[]{:S(2)}) copy-start(bf16[8,1,4,16,512]{4,3,2,1,0:T(8,128)(2,1)S(1)} %get-tuple-element.58) | copy-start | bytes 1572868
  57.6 84.0 %copy-start.13 = (bf16[8,1,4,16,512]{4,3,2,1,0:T(8,128)(2,1)}, bf16[8,1,4,16,512]{4,3,2,1,0:T(8,128)(2,1)S(1)}, u32[]{:S(2)}) copy-start(bf16[8,1,4,16,512]{4,3,2,1,0:T(8,128)(2,1)S(1)} %get-tuple-element.57) | copy-start | bytes 1572868
  57.6 102.8 %copy-start.2 = (bf16[8,1,4,16,512]{4,3,2,1,0:T(8,128)(2,1)}, bf16[8,1,4,16,512]{4,3,2,1,0:T(8,128)(2,1)S(1)}, u32[]{:S(2)}) copy-start(bf16[8,1,4,16,512]{4,3,2,1,0:T(8,128)(2,1)S(1)} %get-tuple-element.56) | copy-start | bytes 1572868
  57.6 129.6 %copy-start.1 = (bf16[8,1,4,16,512]{4,3,2,1,0:T(8,128)(2,1)}, bf16[8,1,4,16,512]{4,3,2,1,0:T(8,128)(2,1)S(1)}, u32[]{:S(2)}) copy-start(bf16[8,1,4,16,512]{4,3,2,1,0:T(8,128)(2,1)S(1)} %get-tuple-element.55) | copy-start | bytes 1572868
  57.6 26.5 %collective-permute-start.4 = (bf16[512,512]{1,0:T(8,128)(2,1)S(1)}, bf16[512,512]{1,0:T(8,128)(2,1)S(1)}, u32[]{:S(2)}, u32[]{:S(2)}) collective-permute-start(bf16[512,512]{1,0:T(8,128)(2,1)S(1)} %bitcast.17), channel_id=1, source_target_pairs={{1,0},{2,1},{3,2},{5,4},{6,5},{7,6},{9,8},{10,9},{11,10},{13,12},{... | collective-permute-start | bytes 1572872 | tf_op jit(solution)/shard_map/ppermute | solution.py:240
  58.9 26.7 %collective-permute-start.2 = (bf16[512,512]{1,0:T(8,128)(2,1)S(1)}, bf16[512,512]{1,0:T(8,128)(2,1)S(1)}, u32[]{:S(2)}, u32[]{:S(2)}) collective-permute-start(bf16[512,512]{1,0:T(8,128)(2,1)S(1)} %bitcast.18), channel_id=1, source_target_pairs={{0,1},{1,2},{2,3},{4,5},{5,6},{6,7},{8,9},{9,10},{10,11},{12,13},{... | collective-permute-start | bytes 1572872 | tf_op jit(solution)/shard_map/ppermute | solution.py:239
  73.3 22.0 %collective-permute-start.14 = (bf16[512,512]{1,0:T(8,128)(2,1)S(1)}, bf16[512,512]{1,0:T(8,128)(2,1)S(1)}, u32[]{:S(2)}, u32[]{:S(2)}) collective-permute-start(bf16[512,512]{1,0:T(8,128)(2,1)S(1)} %bitcast.13), channel_id=1, source_target_pairs={{1,0},{2,1},{3,2},{5,4},{6,5},{7,6},{9,8},{10,9},{11,10},{13,12},{... | collective-permute-start | bytes 1572872 | tf_op jit(solution)/shard_map/ppermute | solution.py:240
  74.6 22.0 %collective-permute-start = (bf16[512,512]{1,0:T(8,128)(2,1)S(1)}, bf16[512,512]{1,0:T(8,128)(2,1)S(1)}, u32[]{:S(2)}, u32[]{:S(2)}) collective-permute-start(bf16[512,512]{1,0:T(8,128)(2,1)S(1)} %bitcast.14), channel_id=1, source_target_pairs={{0,1},{1,2},{2,3},{4,5},{5,6},{6,7},{8,9},{9,10},{10,11},{12,13},{... | collective-permute-start | bytes 1572872 | tf_op jit(solution)/shard_map/ppermute | solution.py:239
  84.1 57.5 %copy-start.14 = (bf16[512,512]{1,0:T(8,128)(2,1)}, bf16[512,512]{1,0:T(8,128)(2,1)S(1)}, u32[]{:S(2)}) copy-start(bf16[512,512]{1,0:T(8,128)(2,1)S(1)} %collective-permute-done.4.refs_4_) | copy-start | bytes 1572868
  84.1 22.5 %collective-permute-start.5 = (bf16[512,512]{1,0:T(8,128)(2,1)S(1)}, bf16[512,512]{1,0:T(8,128)(2,1)S(1)}, u32[]{:S(2)}, u32[]{:S(2)}) collective-permute-start(bf16[512,512]{1,0:T(8,128)(2,1)S(1)} %collective-permute-done.4.refs_4_), channel_id=1, source_target_pairs={{1,0},{2,1},{5,4},{6,5},{9,8},{10,9},{13,12},{14,13},{17,16},{18,1... | collective-permute-start | bytes 1572872 | tf_op jit(solution)/shard_map/ppermute | solution.py:240
  85.6 56.0 %copy-start.15 = (bf16[512,512]{1,0:T(8,128)(2,1)}, bf16[512,512]{1,0:T(8,128)(2,1)S(1)}, u32[]{:S(2)}) copy-start(bf16[512,512]{1,0:T(8,128)(2,1)S(1)} %collective-permute-done.2.refs_1_) | copy-start | bytes 1572868
  85.6 21.0 %collective-permute-start.3 = (bf16[512,512]{1,0:T(8,128)(2,1)S(1)}, bf16[512,512]{1,0:T(8,128)(2,1)S(1)}, u32[]{:S(2)}, u32[]{:S(2)}) collective-permute-start(bf16[512,512]{1,0:T(8,128)(2,1)S(1)} %collective-permute-done.2.refs_1_), channel_id=1, source_target_pairs={{1,2},{2,3},{5,6},{6,7},{9,10},{10,11},{13,14},{14,15},{17,18},{18... | collective-permute-start | bytes 1572872 | tf_op jit(solution)/shard_map/ppermute | solution.py:239
  95.3 65.2 %copy-start.4 = (bf16[512,512]{1,0:T(8,128)(2,1)}, bf16[512,512]{1,0:T(8,128)(2,1)S(1)}, u32[]{:S(2)}) copy-start(bf16[512,512]{1,0:T(8,128)(2,1)S(1)} %collective-permute-done.14.refs_4_) | copy-start | bytes 1572868
  95.3 22.6 %collective-permute-start.15 = (bf16[512,512]{1,0:T(8,128)(2,1)S(1)}, bf16[512,512]{1,0:T(8,128)(2,1)}, u32[]{:S(2)}, u32[]{:S(2)}) collective-permute-start(bf16[512,512]{1,0:T(8,128)(2,1)S(1)} %collective-permute-done.14.refs_4_), channel_id=1, source_target_pairs={{1,0},{2,1},{5,4},{6,5},{9,8},{10,9},{13,12},{14,13},{17,16},{18,1... | collective-permute-start | bytes 1572872 | tf_op jit(solution)/shard_map/ppermute | solution.py:240
  96.6 63.9 %copy-start.5 = (bf16[512,512]{1,0:T(8,128)(2,1)}, bf16[512,512]{1,0:T(8,128)(2,1)S(1)}, u32[]{:S(2)}) copy-start(bf16[512,512]{1,0:T(8,128)(2,1)S(1)} %collective-permute-done.refs_1_) | copy-start | bytes 1572868
  96.6 22.8 %collective-permute-start.1 = (bf16[512,512]{1,0:T(8,128)(2,1)S(1)}, bf16[512,512]{1,0:T(8,128)(2,1)}, u32[]{:S(2)}, u32[]{:S(2)}) collective-permute-start(bf16[512,512]{1,0:T(8,128)(2,1)S(1)} %collective-permute-done.refs_1_), channel_id=1, source_target_pairs={{1,2},{2,3},{5,6},{6,7},{9,10},{10,11},{13,14},{14,15},{17,18},{18... | collective-permute-start | bytes 1572872 | tf_op jit(solution)/shard_map/ppermute | solution.py:239
  106.5 35.0 %copy-start.16 = (bf16[512,512]{1,0:T(8,128)(2,1)}, bf16[512,512]{1,0:T(8,128)(2,1)S(1)}, u32[]{:S(2)}) copy-start(bf16[512,512]{1,0:T(8,128)(2,1)S(1)} %collective-permute-done.5.refs_5_) | copy-start | bytes 1572868
  106.6 35.0 %copy-start.17 = (bf16[512,512]{1,0:T(8,128)(2,1)}, bf16[512,512]{1,0:T(8,128)(2,1)S(1)}, u32[]{:S(2)}) copy-start(bf16[512,512]{1,0:T(8,128)(2,1)S(1)} %collective-permute-done.3.refs_2_) | copy-start | bytes 1572868
  106.6 22.5 %collective-permute-start.7 = (bf16[512,512]{1,0:T(8,128)(2,1)S(1)}, bf16[512,512]{1,0:T(8,128)(2,1)S(1)}, u32[]{:S(2)}, u32[]{:S(2)}) collective-permute-start(bf16[512,512]{1,0:T(8,128)(2,1)S(1)} %collective-permute-done.5.refs_5_), channel_id=1, source_target_pairs={{1,0},{5,4},{9,8},{13,12},{17,16},{21,20},{25,24},{29,28}} | collective-permute-start | bytes 1572872 | tf_op jit(solution)/shard_map/ppermute | solution.py:240
  107.9 22.7 %collective-permute-start.11 = (bf16[512,512]{1,0:T(8,128)(2,1)S(1)}, bf16[512,512]{1,0:T(8,128)(2,1)S(1)}, u32[]{:S(2)}, u32[]{:S(2)}) collective-permute-start(bf16[512,512]{1,0:T(8,128)(2,1)S(1)} %bitcast.10), channel_id=1, source_target_pairs={{0,1},{1,2},{2,3},{4,5},{5,6},{6,7},{8,9},{9,10},{10,11},{12,13},{... | collective-permute-start | bytes 1572872 | tf_op jit(solution)/shard_map/ppermute | solution.py:239
  113.4 26.9 %collective-permute-start.12 = (bf16[512,512]{1,0:T(8,128)(2,1)S(1)}, bf16[512,512]{1,0:T(8,128)(2,1)S(1)}, u32[]{:S(2)}, u32[]{:S(2)}) collective-permute-start(bf16[512,512]{1,0:T(8,128)(2,1)S(1)} %bitcast.11), channel_id=1, source_target_pairs={{1,0},{2,1},{3,2},{5,4},{6,5},{7,6},{9,8},{10,9},{11,10},{13,12},{... | collective-permute-start | bytes 1572872 | tf_op jit(solution)/shard_map/ppermute | solution.py:240
  117.9 23.7 %collective-permute-start.6 = (bf16[512,512]{1,0:T(8,128)(2,1)S(1)}, bf16[512,512]{1,0:T(8,128)(2,1)}, u32[]{:S(2)}, u32[]{:S(2)}) collective-permute-start(bf16[512,512]{1,0:T(8,128)(2,1)S(1)} %collective-permute-done.3.refs_2_), channel_id=1, source_target_pairs={{2,3},{6,7},{10,11},{14,15},{18,19},{22,23},{26,27},{30,31}} | collective-permute-start | bytes 1572872 | tf_op jit(solution)/shard_map/ppermute | solution.py:239
  119.4 41.1 %collective-permute-start.16 = (bf16[512,512]{1,0:T(8,128)(2,1)}, bf16[512,512]{1,0:T(8,128)(2,1)}, u32[]{:S(2)}, u32[]{:S(2)}) collective-permute-start(bf16[512,512]{1,0:T(8,128)(2,1)} %collective-permute-done.15.refs_5_), channel_id=1, source_target_pairs={{1,0},{5,4},{9,8},{13,12},{17,16},{21,20},{25,24},{29,28}} | collective-permute-start | bytes 1572872 | tf_op jit(solution)/shard_map/ppermute | solution.py:240
  129.0 12.6 %copy-start.18 = (bf16[512,512]{1,0:T(8,128)(2,1)}, bf16[512,512]{1,0:T(8,128)(2,1)S(1)}, u32[]{:S(2)}) copy-start(bf16[512,512]{1,0:T(8,128)(2,1)S(1)} %collective-permute-done.7.refs_6_) | copy-start | bytes 1572868
  129.0 31.5 %collective-permute-start.13 = (bf16[512,512]{1,0:T(8,128)(2,1)}, bf16[512,512]{1,0:T(8,128)(2,1)}, u32[]{:S(2)}, u32[]{:S(2)}) collective-permute-start(bf16[512,512]{1,0:T(8,128)(2,1)} %collective-permute-done.1.refs_2_), channel_id=1, source_target_pairs={{2,3},{6,7},{10,11},{14,15},{18,19},{22,23},{26,27},{30,31}} | collective-permute-start | bytes 1572872 | tf_op jit(solution)/shard_map/ppermute | solution.py:239
  130.5 11.1 %copy-start.6 = (bf16[512,512]{1,0:T(8,128)(2,1)}, bf16[512,512]{1,0:T(8,128)(2,1)S(1)}, u32[]{:S(2)}) copy-start(bf16[512,512]{1,0:T(8,128)(2,1)S(1)} %collective-permute-done.11.refs_10_.refs_1_) | copy-start | bytes 1572868
  130.5 30.0 %collective-permute-start.17 = (bf16[512,512]{1,0:T(8,128)(2,1)S(1)}, bf16[512,512]{1,0:T(8,128)(2,1)}, u32[]{:S(2)}, u32[]{:S(2)}) collective-permute-start(bf16[512,512]{1,0:T(8,128)(2,1)S(1)} %collective-permute-done.11.refs_10_.refs_1_), channel_id=1, source_target_pairs={{1,2},{2,3},{5,6},{6,7},{9,10},{10,11},{13,14},{14,15},{17,18},{18... | collective-permute-start | bytes 1572872 | tf_op jit(solution)/shard_map/ppermute | solution.py:239
  140.3 1.4 copy-start.7
  140.3 22.0 %collective-permute-start.18 = (bf16[512,512]{1,0:T(8,128)(2,1)S(1)}, bf16[512,512]{1,0:T(8,128)(2,1)}, u32[]{:S(2)}, u32[]{:S(2)}) collective-permute-start(bf16[512,512]{1,0:T(8,128)(2,1)S(1)} %collective-permute-done.12.refs_11_.refs_4_), channel_id=1, source_target_pairs={{1,0},{2,1},{5,4},{6,5},{9,8},{10,9},{13,12},{14,13},{17,16},{18,1... | collective-permute-start | bytes 1572872 | tf_op jit(solution)/shard_map/ppermute | solution.py:240
  162.2 24.9 %collective-permute-start.19 = (bf16[512,512]{1,0:T(8,128)(2,1)S(1)}, bf16[512,512]{1,0:T(8,128)(2,1)S(1)}, u32[]{:S(2)}, u32[]{:S(2)}) collective-permute-start(bf16[512,512]{1,0:T(8,128)(2,1)S(1)} %bitcast.6), channel_id=1, source_target_pairs={{0,1},{1,2},{2,3},{4,5},{5,6},{6,7},{8,9},{9,10},{10,11},{12,13},{... | collective-permute-start | bytes 1572872 | tf_op jit(solution)/shard_map/ppermute | solution.py:239
  165.1 22.1 %collective-permute-start.20 = (bf16[512,512]{1,0:T(8,128)(2,1)S(1)}, bf16[512,512]{1,0:T(8,128)(2,1)S(1)}, u32[]{:S(2)}, u32[]{:S(2)}) collective-permute-start(bf16[512,512]{1,0:T(8,128)(2,1)S(1)} %bitcast.7), channel_id=1, source_target_pairs={{1,0},{2,1},{3,2},{5,4},{6,5},{7,6},{9,8},{10,9},{11,10},{13,12},{... | collective-permute-start | bytes 1572872 | tf_op jit(solution)/shard_map/ppermute | solution.py:240
  166.4 31.2 %collective-permute-start.24 = (bf16[512,512]{1,0:T(8,128)(2,1)}, bf16[512,512]{1,0:T(8,128)(2,1)S(1)}, u32[]{:S(2)}, u32[]{:S(2)}) collective-permute-start(bf16[512,512]{1,0:T(8,128)(2,1)} %collective-permute-done.17.refs_2_), channel_id=1, source_target_pairs={{2,3},{6,7},{10,11},{14,15},{18,19},{22,23},{26,27},{30,31}} | collective-permute-start | bytes 1572872 | tf_op jit(solution)/shard_map/ppermute | solution.py:239
  167.1 30.5 %collective-permute-start.25 = (bf16[512,512]{1,0:T(8,128)(2,1)}, bf16[512,512]{1,0:T(8,128)(2,1)S(1)}, u32[]{:S(2)}, u32[]{:S(2)}) collective-permute-start(bf16[512,512]{1,0:T(8,128)(2,1)} %collective-permute-done.18.refs_5_), channel_id=1, source_target_pairs={{1,0},{5,4},{9,8},{13,12},{17,16},{21,20},{25,24},{29,28}} | collective-permute-start | bytes 1572872 | tf_op jit(solution)/shard_map/ppermute | solution.py:240
  187.2 30.8 %copy-start.8 = (bf16[512,512]{1,0:T(8,128)(2,1)}, bf16[512,512]{1,0:T(8,128)(2,1)S(1)}, u32[]{:S(2)}) copy-start(bf16[512,512]{1,0:T(8,128)(2,1)S(1)} %collective-permute-done.19.refs_1_) | copy-start | bytes 1572868
  187.2 30.8 %copy-start.9 = (bf16[512,512]{1,0:T(8,128)(2,1)}, bf16[512,512]{1,0:T(8,128)(2,1)S(1)}, u32[]{:S(2)}) copy-start(bf16[512,512]{1,0:T(8,128)(2,1)S(1)} %collective-permute-done.20.refs_4_) | copy-start | bytes 1572868
  187.2 30.8 %collective-permute-start.22 = (bf16[512,512]{1,0:T(8,128)(2,1)S(1)}, bf16[512,512]{1,0:T(8,128)(2,1)S(1)}, u32[]{:S(2)}, u32[]{:S(2)}) collective-permute-start(bf16[512,512]{1,0:T(8,128)(2,1)S(1)} %bitcast.8), channel_id=1, source_target_pairs={{0,3},{3,0},{4,7},{7,4},{8,11},{11,8},{12,15},{15,12},{16,19},{19,... | collective-permute-start | bytes 1572872 | tf_op jit(solution)/shard_map/ppermute | solution.py:284
  195.4 22.6 %collective-permute-start.21 = (bf16[512,512]{1,0:T(8,128)(2,1)S(1)}, bf16[512,512]{1,0:T(8,128)(2,1)S(1)}, u32[]{:S(2)}, u32[]{:S(2)}) collective-permute-start(bf16[512,512]{1,0:T(8,128)(2,1)S(1)} %collective-permute-done.19.refs_1_), channel_id=1, source_target_pairs={{1,2},{2,3},{5,6},{6,7},{9,10},{10,11},{13,14},{14,15},{17,18},{18... | collective-permute-start | bytes 1572872 | tf_op jit(solution)/shard_map/ppermute | solution.py:239
  196.1 21.9 %collective-permute-start.23 = (bf16[512,512]{1,0:T(8,128)(2,1)S(1)}, bf16[512,512]{1,0:T(8,128)(2,1)}, u32[]{:S(2)}, u32[]{:S(2)}) collective-permute-start(bf16[512,512]{1,0:T(8,128)(2,1)S(1)} %collective-permute-done.20.refs_4_), channel_id=1, source_target_pairs={{1,0},{2,1},{5,4},{6,5},{9,8},{10,9},{13,12},{14,13},{17,16},{18,1... | collective-permute-start | bytes 1572872 | tf_op jit(solution)/shard_map/ppermute | solution.py:240
  197.6 0.8 copy-start.10
  198.4 0.8 copy-start.11
  218.0 0.8 copy-start
  218.0 1.0 copy-start.12
Sparse Core Ops, SparseCore 0:
  11.0 50.2 all-gather.2
  63.2 76.9 all-gather.4

commit v16 on v14

--- a/solution.py
+++ b/solution.py
@@ -71,9 +71,12 @@
         cols = pl.ds(pl.multiple_of(block * depth, depth), depth)
         return pltpu.make_async_copy(src, t_all.at[:, cols], t_sem.at[s])
 
-    def w_copy(s, slot):
-        src = w_rest.at[:, (s - 1) * width:s * width] if s else w_own
-        return pltpu.make_async_copy(src, w_buf.at[slot], w_sem.at[slot])
+    tiles = per_part // wide
+
+    def w_copy(s, slot, tile):
+        cols = pl.ds(tile * WIDE, WIDE)
+        src = w_rest.at[:, pl.ds((s - 1) * width + tile * WIDE, WIDE)] if s else w_own.at[:, cols]
+        return pltpu.make_async_copy(src, w_buf.at[slot, :, cols], w_sem.at[slot, tile])
 
     blocks = [lax.rem(own[0] - s + parts, parts) for s in range(parts)]
     t_copy(t_own, blocks[0], 0).start()
@@ -85,7 +88,8 @@
         @pl.when(own[0] < s)
         def _():
             t_copy(t_left[parts - s - 1], blocks[s], s).start()
-    w_copy(0, 0).start()
+    for tile in range(tiles):
+        w_copy(0, 0, tile).start()
     ladder_copy = pltpu.make_async_copy(ladder_hbm, ladder, l_sem)
     for s in range(parts):
         t_copy(t_own, blocks[s], s).wait()
@@ -93,18 +97,21 @@
     @pl.loop(0, parts)
     def _(step):
         slot = lax.rem(step, 2)
-        w_copy(0, slot).wait()
+        w_copy(0, slot, 0).wait()
         for s in range(1, parts):
             @pl.when(step + 1 == s)
             def _():
-                w_copy(s, s % 2).start()
+                for tile in range(tiles):
+                    w_copy(s, s % 2, tile).start()
 
         @pl.when(step == parts - 1)
         def _():
             ladder_copy.start()
 
         j0 = lax.rem(own[0] - step + parts, parts) * per_part
-        for tile in range(per_part // wide):
+        for tile in range(tiles):
+            if tile:
+                w_copy(0, slot, tile).wait()
             acc = jnp.dot(
                 t_all[...], w_buf[slot, :, tile * WIDE:(tile + 1) * WIDE], preferred_element_type=jnp.float32)
             for i in range(occupied):
@@ -172,7 +179,7 @@
             pltpu.VMEM((GROUP * (count + PAD), b_local), jnp.float32),
             pltpu.VMEM((2, STEP_A, b_local, count), jnp.bfloat16),
             pltpu.SemaphoreType.DMA((parts,)),
-            pltpu.SemaphoreType.DMA((2,)),
+            pltpu.SemaphoreType.DMA((2, width // WIDE)),
             pltpu.SemaphoreType.DMA,
             pltpu.SemaphoreType.DMA((2,)),
         ],
@@ -214,7 +221,8 @@
         arrived[s] = lax.ppermute(arrived[s], "col", [(c, (c + s) % cols) for c in range(cols)])
     blocks = lax.all_to_all(blocks, "row", split_axis=0, concat_axis=0, tiled=True)
 
-    rest, _ = lax.optimization_barrier((arrived[1:], blocks))
+    held = [blocks[:, q].reshape(occupied * GROUP, depth) for q in range(chunks)]
+    rest, _ = lax.optimization_barrier((arrived[1:], held))
     panel_w = [
         lax.all_gather(part, "row", axis=0, tiled=True) for part in (arrived[0], jnp.concatenate(rest, axis=1))
     ]
@@ -239,10 +247,7 @@
         right.append(lax.ppermute(right[source], "col", [(c, c + step) for c in range(first, cols - step)]))
         left.append(lax.ppermute(left[source], "col", [(c + step, c) for c in range(cols - step - first)]))
 
-    pieces = []
-    for q in range(chunks):
-        held = blocks[:, q].reshape(occupied * GROUP, depth)
-        pieces.append(([held], [held]))
+    pieces = [([block], [block]) for block in held]
 
     if plain:
         for sides in pieces:

time: 245 us -> 246 us (level)
    ppermute x3, waiting for transfers between devices: 44.7 us -> 15.9 us  [local(): lax.ppermute(arrived[s], 'col', [(c, (c + s) % cols) for c in range(cols)])]
    all_to_all x1, waiting for transfers between devices: 0.01 us -> 27.6 us  [local(): lax.all_to_all(blocks, 'row', split_axis=0, concat_axis=0, tiled=True)]
  transfers between devices with their start and end apart: 30 -> 30, of which waited for: 13 -> 12; matrix products, arithmetic and copies ran while one was open for 1% -> 2% of each run, Pallas kernels for 23% -> 23%
where the time goes in v16:
time: 246 us; the launch traced here: 245 us
  waiting for transfers between devices  96.1 us (39%)
  Pallas kernels  79.8 us (32%)
  starting transfers between devices  51 us (21%)
  between operations  13.9 us (6%)
  other arithmetic  2.61 us (1%)
    pallas_call x4, Pallas kernels, chunk_update(): pl.pallas_call(functools.partial(chunk_kernel, starts=starts, parts=parts...  75.5 us
    ppermute x12, waiting for transfers between devices, hop(): lax.ppermute(left[source], 'col', [(c + step, c) for c in range(cols - st...  43.5 us
    all_to_all x1, waiting for transfers between devices, local(): lax.all_to_all(blocks, 'row', split_axis=0, concat_axis=0, tiled=True)  27.6 us
    ppermute x12, starting transfers between devices, hop(): lax.ppermute(right[source], 'col', [(c, c + step) for c in range(first, c...  25.5 us
    ppermute x3, waiting for transfers between devices, local(): lax.ppermute(arrived[s], 'col', [(c, (c + s) % cols) for c in range(cols)])  15.9 us
    ppermute x12, starting transfers between devices, hop(): lax.ppermute(left[source], 'col', [(c + step, c) for c in range(cols - st...  15.7 us
    ppermute x12, waiting for transfers between devices, hop(): lax.ppermute(right[source], 'col', [(c, c + step) for c in range(first, c...  9.09 us
    all_to_all x1, starting transfers between devices, local(): lax.all_to_all(blocks, 'row', split_axis=0, concat_axis=0, tiled=True)  5.21 us
  transfers between devices with their start and end apart: 30, of which 12 were waited for; matrix products, arithmetic and copies ran while one was open for 2% of the time, Pallas kernels for 23%

profile of v16, /device:TPU:0, one launch (start us, length us, event | category | flops | bytes accessed | tf_op | source)
XLA Modules:
  0.0 245.5 jit_solution(10663159973632720409)
XLA Ops:
  6.5 4.3 %shard_map.37 = (bf16[8,4,4,16,512]{4,3,2,1,0:T(8,128)(2,1)}, bf16[256,1024]{1,0:T(8,128)(2,1)}, bf16[256,1024]{1,0:T(8,128)(2,1)}, bf16[256,1024]{1,0:T(8,128)(2,1)}, bf16[256,1024]{1,0:T(8,128)(2,1)}) custom-call(s32[1]{0:T(128)} %bitcast.own, bf16[4,8,4,16,512]{4,3,2,1,0:T(8,128)(2,1)} %bitcast.17, bf16[256,4096]{1,0:T(8,128)(2,1)} %w_ref.1), custom_call_target="tpu_custom_call" | custom-call | bytes 8388608 | tf_op jit(solution)/shard_map/pallas_call | solution.py:46
  10.8 0.0 all-gather.3.cloned.1.call-update
  10.9 5.2 %all-to-all-start = ((bf16[8,4,4,16,512]{4,3,2,1,0:T(8,128)(2,1)}), bf16[8,4,4,16,512]{4,3,2,1,0:T(8,128)(2,1)S(1)}, u32[]{:S(2)}, u32[]{:S(2)}) async-start(bf16[8,4,4,16,512]{4,3,2,1,0:T(8,128)(2,1)} %get-tuple-element.31), calls=%async_computation | async-start | bytes 4194304 | tf_op jit(solution)/shard_map/all_to_all | solution.py:222
  16.1 0.0 all-gather.5.cloned.1.call-start
  16.1 3.6 %collective-permute-start.10 = (bf16[256,1024]{1,0:T(8,128)(2,1)}, bf16[256,1024]{1,0:T(8,128)(2,1)}, u32[]{:S(2)}, u32[]{:S(2)}) collective-permute-start(bf16[256,1024]{1,0:T(8,128)(2,1)} %get-tuple-element.37), channel_id=1, source_target_pairs={{0,3},{1,0},{2,1},{3,2},{4,7},{5,4},{6,5},{7,6},{8,11},{9,8},{10,9... | collective-permute-start | bytes 1572872 | tf_op jit(solution)/shard_map/ppermute | solution.py:221
  19.7 0.0 collective-permute-start.8
  19.8 1.0 collective-permute-start.9
  20.8 27.6 %all-to-all-done = bf16[8,4,4,16,512]{4,3,2,1,0:T(8,128)(2,1)S(1)} async-done(((bf16[8,4,4,16,512]{4,3,2,1,0:T(8,128)(2,1)}), bf16[8,4,4,16,512]{4,3,2,1,0:T(8,128)(2,1)S(1)}, u32[]{:S(2)}, u32[]{:S(2)}) %all-to-all-start) | async-done | bytes 2097184 | tf_op jit(solution)/shard_map/all_to_all | solution.py:222
  48.3 1.2 fusion
  49.5 0.0 collective-permute-done.10
  49.6 0.0 collective-permute-done.8
  49.6 15.9 %collective-permute-done.9 = bf16[256,1024]{1,0:T(8,128)(2,1)} collective-permute-done((bf16[256,1024]{1,0:T(8,128)(2,1)}, bf16[256,1024]{1,0:T(8,128)(2,1)}, u32[]{:S(2)}, u32[]{:S(2)}) %collective-permute-start.9) | collective-permute-done | bytes 524320 | tf_op jit(solution)/shard_map/ppermute | solution.py:221
  65.4 2.6 %pad_maximum_fusion = bf16[256,3072]{1,0:T(8,128)(2,1)} fusion(bf16[256,1024]{1,0:T(8,128)(2,1)} %collective-permute-done.10, bf16[256,1024]{1,0:T(8,128)(2,1)} %collective-permute-done.9, bf16[256,1024]{1,0:T(8,128)(2,1)} %collective-permute-done.8), kind=kLoop, calls=%fused_computation | loop fusion | flops 4718592 | bytes 3145728 | tf_op jit(solution)/shard_map/concatenate | solution.py:227
  68.1 0.0 all-gather.5.cloned.1.call-update
  68.1 1.8 collective-permute-start.2
  69.9 1.3 collective-permute-start.4
  71.2 4.6 %collective-permute-start = (bf16[512,512]{1,0:T(8,128)(2,1)S(1)}, bf16[512,512]{1,0:T(8,128)(2,1)S(1)}, u32[]{:S(2)}, u32[]{:S(2)}) collective-permute-start(bf16[512,512]{1,0:T(8,128)(2,1)S(1)} %bitcast.15), channel_id=1, source_target_pairs={{0,1},{1,2},{2,3},{4,5},{5,6},{6,7},{8,9},{9,10},{10,11},{12,13},{... | collective-permute-start | bytes 1572872 | tf_op jit(solution)/shard_map/ppermute | solution.py:247
  75.8 1.3 collective-permute-start.14
  77.1 5.1 %collective-permute-done.2.refs_1_ = bf16[512,512]{1,0:T(8,128)(2,1)S(1)} collective-permute-done((bf16[512,512]{1,0:T(8,128)(2,1)S(1)}, bf16[512,512]{1,0:T(8,128)(2,1)S(1)}, u32[]{:S(2)}, u32[]{:S(2)}) %collective-permute-start.2) | collective-permute-done | bytes 524320 | tf_op jit(solution)/shard_map/ppermute | solution.py:247
  82.2 0.7 collective-permute-start.3
  82.9 3.7 %collective-permute-done.4.refs_4_ = bf16[512,512]{1,0:T(8,128)(2,1)S(1)} collective-permute-done((bf16[512,512]{1,0:T(8,128)(2,1)S(1)}, bf16[512,512]{1,0:T(8,128)(2,1)S(1)}, u32[]{:S(2)}, u32[]{:S(2)}) %collective-permute-start.4) | collective-permute-done | bytes 524320 | tf_op jit(solution)/shard_map/ppermute | solution.py:248
  86.6 1.3 collective-permute-start.5
  87.9 3.9 %collective-permute-done.refs_1_ = bf16[512,512]{1,0:T(8,128)(2,1)S(1)} collective-permute-done((bf16[512,512]{1,0:T(8,128)(2,1)S(1)}, bf16[512,512]{1,0:T(8,128)(2,1)S(1)}, u32[]{:S(2)}, u32[]{:S(2)}) %collective-permute-start) | collective-permute-done | bytes 524320 | tf_op jit(solution)/shard_map/ppermute | solution.py:247
  91.9 1.5 collective-permute-start.1
  93.4 4.5 %collective-permute-done.14.refs_4_ = bf16[512,512]{1,0:T(8,128)(2,1)S(1)} collective-permute-done((bf16[512,512]{1,0:T(8,128)(2,1)S(1)}, bf16[512,512]{1,0:T(8,128)(2,1)S(1)}, u32[]{:S(2)}, u32[]{:S(2)}) %collective-permute-start.14) | collective-permute-done | bytes 524320 | tf_op jit(solution)/shard_map/ppermute | solution.py:248
  97.9 1.3 collective-permute-start.15
  99.2 0.0 collective-permute-done.3.refs_2_
  99.2 9.9 %collective-permute-done.5.refs_5_ = bf16[512,512]{1,0:T(8,128)(2,1)S(1)} collective-permute-done((bf16[512,512]{1,0:T(8,128)(2,1)S(1)}, bf16[512,512]{1,0:T(8,128)(2,1)S(1)}, u32[]{:S(2)}, u32[]{:S(2)}) %collective-permute-start.5) | collective-permute-done | bytes 524320 | tf_op jit(solution)/shard_map/ppermute | solution.py:248
  109.1 3.8 %collective-permute-start.11 = (bf16[512,512]{1,0:T(8,128)(2,1)S(1)}, bf16[512,512]{1,0:T(8,128)(2,1)S(1)}, u32[]{:S(2)}, u32[]{:S(2)}) collective-permute-start(bf16[512,512]{1,0:T(8,128)(2,1)S(1)} %bitcast.11), channel_id=1, source_target_pairs={{0,1},{1,2},{2,3},{4,5},{5,6},{6,7},{8,9},{9,10},{10,11},{12,13},{... | collective-permute-start | bytes 1572872 | tf_op jit(solution)/shard_map/ppermute | solution.py:247
  112.9 1.3 collective-permute-start.12
  114.2 0.7 collective-permute-start.6
  114.9 0.0 collective-permute-done.1.refs_2_
  114.9 1.3 collective-permute-start.7
  116.2 4.2 %collective-permute-done.15.refs_5_ = bf16[512,512]{1,0:T(8,128)(2,1)} collective-permute-done((bf16[512,512]{1,0:T(8,128)(2,1)S(1)}, bf16[512,512]{1,0:T(8,128)(2,1)}, u32[]{:S(2)}, u32[]{:S(2)}) %collective-permute-start.15) | collective-permute-done | bytes 524320 | tf_op jit(solution)/shard_map/ppermute | solution.py:248
  120.5 1.4 collective-permute-start.13
  121.9 0.0 collective-permute-done.11.refs_10_.refs_1_
  121.9 1.3 collective-permute-start.16
  123.2 8.4 %collective-permute-done.12.refs_11_.refs_4_ = bf16[512,512]{1,0:T(8,128)(2,1)S(1)} collective-permute-done((bf16[512,512]{1,0:T(8,128)(2,1)S(1)}, bf16[512,512]{1,0:T(8,128)(2,1)S(1)}, u32[]{:S(2)}, u32[]{:S(2)}) %collective-permute-start.12) | collective-permute-done | bytes 524320 | tf_op jit(solution)/shard_map/ppermute | solution.py:248
  131.6 1.4 collective-permute-start.17
  133.0 0.0 collective-permute-done.6.refs_3_
  133.1 1.3 collective-permute-start.18
  134.4 8.5 %collective-permute-done.7.refs_6_ = bf16[512,512]{1,0:T(8,128)(2,1)} collective-permute-done((bf16[512,512]{1,0:T(8,128)(2,1)S(1)}, bf16[512,512]{1,0:T(8,128)(2,1)}, u32[]{:S(2)}, u32[]{:S(2)}) %collective-permute-start.7) | collective-permute-done | bytes 524320 | tf_op jit(solution)/shard_map/ppermute | solution.py:248
  142.9 18.9 %shard_map.38.refs_10_ = bf16[64,128,1024]{2,1,0:T(8,128)(2,1)} custom-call(s32[1]{0:T(128)} %bitcast.own, bf16[512,512]{1,0:T(8,128)(2,1)} %bitcast.18, bf16[512,512]{1,0:T(8,128)(2,1)} %copy-done.14, bf16[512,512]{1,0:T(8,128)(2,1)} %copy-done.16, bf16[512,512]{1,0:T(8,128)(2,1)} %copy-done.18, bf16[512,512]{1,0:T(8,128)(2,1)} %copy-done.15, ...), custom_call_target="tpu_custom_call" | custom-call | flops 12884901888 | bytes 25165824 | tf_op jit(solution)/shard_map/pallas_call | solution.py:170
  161.9 0.0 collective-permute-done.13.refs_3_
  161.9 0.0 collective-permute-done.16.refs_6_
  161.9 0.0 collective-permute-done.17.refs_2_
  161.9 1.6 collective-permute-done.18.refs_5_
  163.5 1.4 collective-permute-start.19
  164.9 1.3 collective-permute-start.20
  166.2 0.7 collective-permute-start.25
  166.9 1.3 collective-permute-start.26
  168.2 18.9 %shard_map.39.refs_10_ = bf16[64,128,1024]{2,1,0:T(8,128)(2,1)} custom-call(s32[1]{0:T(128)} %bitcast.own, bf16[512,512]{1,0:T(8,128)(2,1)} %bitcast.14, bf16[512,512]{1,0:T(8,128)(2,1)} %copy-done.3, bf16[512,512]{1,0:T(8,128)(2,1)} %collective-permute-done.1.refs_2_, ...), custom_call_target="tpu_custom_call", output_to_operand_aliasing={{}: (11, {})} | custom-call | flops 12884901888 | bytes 25165824 | tf_op jit(solution)/shard_map/pallas_call | solution.py:170
  187.1 0.0 collective-permute-done.19.refs_1_
  187.1 0.7 collective-permute-start.21
  187.8 6.8 %collective-permute-start.22 = (bf16[512,512]{1,0:T(8,128)(2,1)S(1)}, bf16[512,512]{1,0:T(8,128)(2,1)S(1)}, u32[]{:S(2)}, u32[]{:S(2)}) collective-permute-start(bf16[512,512]{1,0:T(8,128)(2,1)S(1)} %bitcast.8), channel_id=1, source_target_pairs={{0,3},{4,7},{8,11},{12,15},{16,19},{20,23},{24,27},{28,31}} | collective-permute-start | bytes 1572872 | tf_op jit(solution)/shard_map/ppermute | solution.py:247
  194.7 1.3 collective-permute-start.23
  196.0 0.0 collective-permute-done.25.refs_3_
  196.0 1.5 collective-permute-start.24
  197.5 0.8 copy-done.11
  198.3 18.9 %shard_map.40.refs_10_ = bf16[64,128,1024]{2,1,0:T(8,128)(2,1)} custom-call(s32[1]{0:T(128)} %bitcast.own, bf16[512,512]{1,0:T(8,128)(2,1)} %bitcast.13, bf16[512,512]{1,0:T(8,128)(2,1)} %copy-done.5, bf16[512,512]{1,0:T(8,128)(2,1)} %collective-permute-done.17.refs_2_, bf16[512,512]{1,0:T(8,128)(2,1)} %copy-done.9, ...), custom_call_target="tpu_custom_call", output_to_operand_aliasing={{}: (11, {})} | custom-call | flops 12884901888 | bytes 25165824 | tf_op jit(solution)/shard_map/pallas_call | solution.py:170
  217.2 0.0 collective-permute-done.21.refs_2_
  217.2 2.5 %collective-permute-done.23.refs_5_ = bf16[512,512]{1,0:T(8,128)(2,1)} collective-permute-done((bf16[512,512]{1,0:T(8,128)(2,1)S(1)}, bf16[512,512]{1,0:T(8,128)(2,1)}, u32[]{:S(2)}, u32[]{:S(2)}) %collective-permute-start.23) | collective-permute-done | bytes 524320 | tf_op jit(solution)/shard_map/ppermute | solution.py:248
  219.8 0.0 collective-permute-done.24.refs_6_
  219.8 18.9 %shard_map.41 = bf16[64,128,1024]{2,1,0:T(8,128)(2,1)} custom-call(s32[1]{0:T(128)} %bitcast.own, bf16[512,512]{1,0:T(8,128)(2,1)} %bitcast.10, bf16[512,512]{1,0:T(8,128)(2,1)} %copy-done.7, bf16[512,512]{1,0:T(8,128)(2,1)} %copy-done.10, bf16[512,512]{1,0:T(8,128)(2,1)} %copy-done.12, bf16[512,512]{1,0:T(8,128)(2,1)} %copy-done.8, ...), custom_call_target="tpu_custom_call", output_to_operand_aliasing={{}: (11, {})} | custom-call | flops 12884901888 | bytes 25165824 | tf_op jit(solution)/shard_map/pallas_call | solution.py:170
  (43 shorter events, 0.1 us)
Async XLA Ops:
  6.5 136.4 %all-gather.3.cloned.1.call-start = ((), (), s32[]{:S(2)}) async-start(), calls=%async_computation.1 | async-start | bytes 4718592 | tf_op jit(solution)/shard_map/all_gather | solution.py:227
  10.9 37.5 %all-to-all-start = ((bf16[8,4,4,16,512]{4,3,2,1,0:T(8,128)(2,1)}), bf16[8,4,4,16,512]{4,3,2,1,0:T(8,128)(2,1)S(1)}, u32[]{:S(2)}, u32[]{:S(2)}) async-start(bf16[8,4,4,16,512]{4,3,2,1,0:T(8,128)(2,1)} %get-tuple-element.31), calls=%async_computation | async-start | bytes 4194304 | tf_op jit(solution)/shard_map/all_to_all | solution.py:222
  16.1 126.9 %all-gather.5.cloned.1.call-start = ((), (), s32[]{:S(2)}) async-start(), calls=%async_computation.2 | async-start | bytes 14155776 | tf_op jit(solution)/shard_map/all_gather | solution.py:227
  16.1 33.4 %collective-permute-start.10 = (bf16[256,1024]{1,0:T(8,128)(2,1)}, bf16[256,1024]{1,0:T(8,128)(2,1)}, u32[]{:S(2)}, u32[]{:S(2)}) collective-permute-start(bf16[256,1024]{1,0:T(8,128)(2,1)} %get-tuple-element.37), channel_id=1, source_target_pairs={{0,3},{1,0},{2,1},{3,2},{4,7},{5,4},{6,5},{7,6},{8,11},{9,8},{10,9... | collective-permute-start | bytes 1572872 | tf_op jit(solution)/shard_map/ppermute | solution.py:221
  19.7 29.8 %collective-permute-start.8 = (bf16[256,1024]{1,0:T(8,128)(2,1)}, bf16[256,1024]{1,0:T(8,128)(2,1)}, u32[]{:S(2)}, u32[]{:S(2)}) collective-permute-start(bf16[256,1024]{1,0:T(8,128)(2,1)} %get-tuple-element.35), channel_id=1, source_target_pairs={{0,1},{1,2},{2,3},{3,0},{4,5},{5,6},{6,7},{7,4},{8,9},{9,10},{10,1... | collective-permute-start | bytes 1572872 | tf_op jit(solution)/shard_map/ppermute | solution.py:221
  19.8 45.7 %collective-permute-start.9 = (bf16[256,1024]{1,0:T(8,128)(2,1)}, bf16[256,1024]{1,0:T(8,128)(2,1)}, u32[]{:S(2)}, u32[]{:S(2)}) collective-permute-start(bf16[256,1024]{1,0:T(8,128)(2,1)} %get-tuple-element.36), channel_id=1, source_target_pairs={{0,2},{1,3},{2,0},{3,1},{4,6},{5,7},{6,4},{7,5},{8,10},{9,11},{10,... | collective-permute-start | bytes 1572872 | tf_op jit(solution)/shard_map/ppermute | solution.py:221
  49.5 112.3 %copy-start.1 = (bf16[8,1,4,16,512]{4,3,2,1,0:T(8,128)(2,1)}, bf16[8,1,4,16,512]{4,3,2,1,0:T(8,128)(2,1)S(1)}, u32[]{:S(2)}) copy-start(bf16[8,1,4,16,512]{4,3,2,1,0:T(8,128)(2,1)S(1)} %get-tuple-element.58) | copy-start | bytes 1572868
  49.5 146.4 %copy-start = (bf16[8,1,4,16,512]{4,3,2,1,0:T(8,128)(2,1)}, bf16[8,1,4,16,512]{4,3,2,1,0:T(8,128)(2,1)S(1)}, u32[]{:S(2)}) copy-start(bf16[8,1,4,16,512]{4,3,2,1,0:T(8,128)(2,1)S(1)} %get-tuple-element.57) | copy-start | bytes 1572868
  49.5 18.5 %copy-start.13 = (bf16[8,1,4,16,512]{4,3,2,1,0:T(8,128)(2,1)S(1)}, bf16[8,1,4,16,512]{4,3,2,1,0:T(8,128)(2,1)}, u32[]{:S(2)}) copy-start(bf16[8,1,4,16,512]{4,3,2,1,0:T(8,128)(2,1)} %get-tuple-element.59) | copy-start | bytes 1572868
  49.5 21.6 %copy-start.2 = (bf16[8,1,4,16,512]{4,3,2,1,0:T(8,128)(2,1)S(1)}, bf16[8,1,4,16,512]{4,3,2,1,0:T(8,128)(2,1)}, u32[]{:S(2)}) copy-start(bf16[8,1,4,16,512]{4,3,2,1,0:T(8,128)(2,1)} %get-tuple-element.60) | copy-start | bytes 1572868
  68.1 14.1 %collective-permute-start.2 = (bf16[512,512]{1,0:T(8,128)(2,1)S(1)}, bf16[512,512]{1,0:T(8,128)(2,1)S(1)}, u32[]{:S(2)}, u32[]{:S(2)}) collective-permute-start(bf16[512,512]{1,0:T(8,128)(2,1)S(1)} %bitcast.19), channel_id=1, source_target_pairs={{0,1},{1,2},{2,3},{4,5},{5,6},{6,7},{8,9},{9,10},{10,11},{12,13},{... | collective-permute-start | bytes 1572872 | tf_op jit(solution)/shard_map/ppermute | solution.py:247
  69.9 16.8 %collective-permute-start.4 = (bf16[512,512]{1,0:T(8,128)(2,1)S(1)}, bf16[512,512]{1,0:T(8,128)(2,1)S(1)}, u32[]{:S(2)}, u32[]{:S(2)}) collective-permute-start(bf16[512,512]{1,0:T(8,128)(2,1)S(1)} %bitcast.20), channel_id=1, source_target_pairs={{1,0},{2,1},{3,2},{5,4},{6,5},{7,6},{9,8},{10,9},{11,10},{13,12},{... | collective-permute-start | bytes 1572872 | tf_op jit(solution)/shard_map/ppermute | solution.py:248
  71.2 20.7 %collective-permute-start = (bf16[512,512]{1,0:T(8,128)(2,1)S(1)}, bf16[512,512]{1,0:T(8,128)(2,1)S(1)}, u32[]{:S(2)}, u32[]{:S(2)}) collective-permute-start(bf16[512,512]{1,0:T(8,128)(2,1)S(1)} %bitcast.15), channel_id=1, source_target_pairs={{0,1},{1,2},{2,3},{4,5},{5,6},{6,7},{8,9},{9,10},{10,11},{12,13},{... | collective-permute-start | bytes 1572872 | tf_op jit(solution)/shard_map/ppermute | solution.py:247
  75.8 22.1 %collective-permute-start.14 = (bf16[512,512]{1,0:T(8,128)(2,1)S(1)}, bf16[512,512]{1,0:T(8,128)(2,1)S(1)}, u32[]{:S(2)}, u32[]{:S(2)}) collective-permute-start(bf16[512,512]{1,0:T(8,128)(2,1)S(1)} %bitcast.16), channel_id=1, source_target_pairs={{1,0},{2,1},{3,2},{5,4},{6,5},{7,6},{9,8},{10,9},{11,10},{13,12},{... | collective-permute-start | bytes 1572872 | tf_op jit(solution)/shard_map/ppermute | solution.py:248
  82.2 50.8 %copy-start.14 = (bf16[512,512]{1,0:T(8,128)(2,1)}, bf16[512,512]{1,0:T(8,128)(2,1)S(1)}, u32[]{:S(2)}) copy-start(bf16[512,512]{1,0:T(8,128)(2,1)S(1)} %collective-permute-done.2.refs_1_) | copy-start | bytes 1572868
  82.2 17.0 %collective-permute-start.3 = (bf16[512,512]{1,0:T(8,128)(2,1)S(1)}, bf16[512,512]{1,0:T(8,128)(2,1)S(1)}, u32[]{:S(2)}, u32[]{:S(2)}) collective-permute-start(bf16[512,512]{1,0:T(8,128)(2,1)S(1)} %collective-permute-done.2.refs_1_), channel_id=1, source_target_pairs={{1,2},{2,3},{5,6},{6,7},{9,10},{10,11},{13,14},{14,15},{17,18},{18... | collective-permute-start | bytes 1572872 | tf_op jit(solution)/shard_map/ppermute | solution.py:247
  86.6 46.4 %copy-start.15 = (bf16[512,512]{1,0:T(8,128)(2,1)}, bf16[512,512]{1,0:T(8,128)(2,1)S(1)}, u32[]{:S(2)}) copy-start(bf16[512,512]{1,0:T(8,128)(2,1)S(1)} %collective-permute-done.4.refs_4_) | copy-start | bytes 1572868
  86.6 22.5 %collective-permute-start.5 = (bf16[512,512]{1,0:T(8,128)(2,1)S(1)}, bf16[512,512]{1,0:T(8,128)(2,1)S(1)}, u32[]{:S(2)}, u32[]{:S(2)}) collective-permute-start(bf16[512,512]{1,0:T(8,128)(2,1)S(1)} %collective-permute-done.4.refs_4_), channel_id=1, source_target_pairs={{1,0},{2,1},{5,4},{6,5},{9,8},{10,9},{13,12},{14,13},{17,16},{18,1... | collective-permute-start | bytes 1572872 | tf_op jit(solution)/shard_map/ppermute | solution.py:248
  91.9 70.0 %copy-start.3 = (bf16[512,512]{1,0:T(8,128)(2,1)}, bf16[512,512]{1,0:T(8,128)(2,1)S(1)}, u32[]{:S(2)}) copy-start(bf16[512,512]{1,0:T(8,128)(2,1)S(1)} %collective-permute-done.refs_1_) | copy-start | bytes 1572868
  91.9 23.1 %collective-permute-start.1 = (bf16[512,512]{1,0:T(8,128)(2,1)S(1)}, bf16[512,512]{1,0:T(8,128)(2,1)}, u32[]{:S(2)}, u32[]{:S(2)}) collective-permute-start(bf16[512,512]{1,0:T(8,128)(2,1)S(1)} %collective-permute-done.refs_1_), channel_id=1, source_target_pairs={{1,2},{2,3},{5,6},{6,7},{9,10},{10,11},{13,14},{14,15},{17,18},{18... | collective-permute-start | bytes 1572872 | tf_op jit(solution)/shard_map/ppermute | solution.py:247
  97.9 64.0 %copy-start.4 = (bf16[512,512]{1,0:T(8,128)(2,1)}, bf16[512,512]{1,0:T(8,128)(2,1)S(1)}, u32[]{:S(2)}) copy-start(bf16[512,512]{1,0:T(8,128)(2,1)S(1)} %collective-permute-done.14.refs_4_) | copy-start | bytes 1572868
  97.9 22.6 %collective-permute-start.15 = (bf16[512,512]{1,0:T(8,128)(2,1)S(1)}, bf16[512,512]{1,0:T(8,128)(2,1)}, u32[]{:S(2)}, u32[]{:S(2)}) collective-permute-start(bf16[512,512]{1,0:T(8,128)(2,1)S(1)} %collective-permute-done.14.refs_4_), channel_id=1, source_target_pairs={{1,0},{2,1},{5,4},{6,5},{9,8},{10,9},{13,12},{14,13},{17,16},{18,1... | collective-permute-start | bytes 1572872 | tf_op jit(solution)/shard_map/ppermute | solution.py:248
  99.2 35.2 %copy-start.16 = (bf16[512,512]{1,0:T(8,128)(2,1)}, bf16[512,512]{1,0:T(8,128)(2,1)S(1)}, u32[]{:S(2)}) copy-start(bf16[512,512]{1,0:T(8,128)(2,1)S(1)} %collective-permute-done.3.refs_2_) | copy-start | bytes 1572868
  109.1 25.2 %copy-start.17 = (bf16[512,512]{1,0:T(8,128)(2,1)}, bf16[512,512]{1,0:T(8,128)(2,1)S(1)}, u32[]{:S(2)}) copy-start(bf16[512,512]{1,0:T(8,128)(2,1)S(1)} %collective-permute-done.5.refs_5_) | copy-start | bytes 1572868
  109.1 12.8 %collective-permute-start.11 = (bf16[512,512]{1,0:T(8,128)(2,1)S(1)}, bf16[512,512]{1,0:T(8,128)(2,1)S(1)}, u32[]{:S(2)}, u32[]{:S(2)}) collective-permute-start(bf16[512,512]{1,0:T(8,128)(2,1)S(1)} %bitcast.11), channel_id=1, source_target_pairs={{0,1},{1,2},{2,3},{4,5},{5,6},{6,7},{8,9},{9,10},{10,11},{12,13},{... | collective-permute-start | bytes 1572872 | tf_op jit(solution)/shard_map/ppermute | solution.py:247
  112.9 18.7 %collective-permute-start.12 = (bf16[512,512]{1,0:T(8,128)(2,1)S(1)}, bf16[512,512]{1,0:T(8,128)(2,1)S(1)}, u32[]{:S(2)}, u32[]{:S(2)}) collective-permute-start(bf16[512,512]{1,0:T(8,128)(2,1)S(1)} %bitcast.12), channel_id=1, source_target_pairs={{1,0},{2,1},{3,2},{5,4},{6,5},{7,6},{9,8},{10,9},{11,10},{13,12},{... | collective-permute-start | bytes 1572872 | tf_op jit(solution)/shard_map/ppermute | solution.py:248
  114.2 18.8 %collective-permute-start.6 = (bf16[512,512]{1,0:T(8,128)(2,1)S(1)}, bf16[512,512]{1,0:T(8,128)(2,1)S(1)}, u32[]{:S(2)}, u32[]{:S(2)}) collective-permute-start(bf16[512,512]{1,0:T(8,128)(2,1)S(1)} %collective-permute-done.3.refs_2_), channel_id=1, source_target_pairs={{2,3},{6,7},{10,11},{14,15},{18,19},{22,23},{26,27},{30,31}} | collective-permute-start | bytes 1572872 | tf_op jit(solution)/shard_map/ppermute | solution.py:247
  114.9 28.0 %collective-permute-start.7 = (bf16[512,512]{1,0:T(8,128)(2,1)S(1)}, bf16[512,512]{1,0:T(8,128)(2,1)}, u32[]{:S(2)}, u32[]{:S(2)}) collective-permute-start(bf16[512,512]{1,0:T(8,128)(2,1)S(1)} %collective-permute-done.5.refs_5_), channel_id=1, source_target_pairs={{1,0},{5,4},{9,8},{13,12},{17,16},{21,20},{25,24},{29,28}} | collective-permute-start | bytes 1572872 | tf_op jit(solution)/shard_map/ppermute | solution.py:248
  120.5 41.4 %collective-permute-start.13 = (bf16[512,512]{1,0:T(8,128)(2,1)}, bf16[512,512]{1,0:T(8,128)(2,1)}, u32[]{:S(2)}, u32[]{:S(2)}) collective-permute-start(bf16[512,512]{1,0:T(8,128)(2,1)} %collective-permute-done.1.refs_2_), channel_id=1, source_target_pairs={{2,3},{6,7},{10,11},{14,15},{18,19},{22,23},{26,27},{30,31}} | collective-permute-start | bytes 1572872 | tf_op jit(solution)/shard_map/ppermute | solution.py:247
  121.9 21.0 %copy-start.5 = (bf16[512,512]{1,0:T(8,128)(2,1)}, bf16[512,512]{1,0:T(8,128)(2,1)S(1)}, u32[]{:S(2)}) copy-start(bf16[512,512]{1,0:T(8,128)(2,1)S(1)} %collective-permute-done.11.refs_10_.refs_1_) | copy-start | bytes 1572868
  121.9 40.0 %collective-permute-start.16 = (bf16[512,512]{1,0:T(8,128)(2,1)}, bf16[512,512]{1,0:T(8,128)(2,1)}, u32[]{:S(2)}, u32[]{:S(2)}) collective-permute-start(bf16[512,512]{1,0:T(8,128)(2,1)} %collective-permute-done.15.refs_5_), channel_id=1, source_target_pairs={{1,0},{5,4},{9,8},{13,12},{17,16},{21,20},{25,24},{29,28}} | collective-permute-start | bytes 1572872 | tf_op jit(solution)/shard_map/ppermute | solution.py:248
  131.6 11.3 %copy-start.6 = (bf16[512,512]{1,0:T(8,128)(2,1)}, bf16[512,512]{1,0:T(8,128)(2,1)S(1)}, u32[]{:S(2)}) copy-start(bf16[512,512]{1,0:T(8,128)(2,1)S(1)} %collective-permute-done.12.refs_11_.refs_4_) | copy-start | bytes 1572868
  131.6 30.3 %collective-permute-start.17 = (bf16[512,512]{1,0:T(8,128)(2,1)S(1)}, bf16[512,512]{1,0:T(8,128)(2,1)}, u32[]{:S(2)}, u32[]{:S(2)}) collective-permute-start(bf16[512,512]{1,0:T(8,128)(2,1)S(1)} %collective-permute-done.11.refs_10_.refs_1_), channel_id=1, source_target_pairs={{1,2},{2,3},{5,6},{6,7},{9,10},{10,11},{13,14},{14,15},{17,18},{18... | collective-permute-start | bytes 1572872 | tf_op jit(solution)/shard_map/ppermute | solution.py:247
  133.0 1.3 copy-start.18
  133.1 30.5 %collective-permute-start.18 = (bf16[512,512]{1,0:T(8,128)(2,1)S(1)}, bf16[512,512]{1,0:T(8,128)(2,1)}, u32[]{:S(2)}, u32[]{:S(2)}) collective-permute-start(bf16[512,512]{1,0:T(8,128)(2,1)S(1)} %collective-permute-done.12.refs_11_.refs_4_), channel_id=1, source_target_pairs={{1,0},{2,1},{5,4},{6,5},{9,8},{10,9},{13,12},{14,13},{17,16},{18,1... | collective-permute-start | bytes 1572872 | tf_op jit(solution)/shard_map/ppermute | solution.py:248
  163.5 23.6 %collective-permute-start.19 = (bf16[512,512]{1,0:T(8,128)(2,1)S(1)}, bf16[512,512]{1,0:T(8,128)(2,1)S(1)}, u32[]{:S(2)}, u32[]{:S(2)}) collective-permute-start(bf16[512,512]{1,0:T(8,128)(2,1)S(1)} %bitcast.6), channel_id=1, source_target_pairs={{0,1},{1,2},{2,3},{4,5},{5,6},{6,7},{8,9},{9,10},{10,11},{12,13},{... | collective-permute-start | bytes 1572872 | tf_op jit(solution)/shard_map/ppermute | solution.py:247
  164.9 22.2 %collective-permute-start.20 = (bf16[512,512]{1,0:T(8,128)(2,1)S(1)}, bf16[512,512]{1,0:T(8,128)(2,1)S(1)}, u32[]{:S(2)}, u32[]{:S(2)}) collective-permute-start(bf16[512,512]{1,0:T(8,128)(2,1)S(1)} %bitcast.7), channel_id=1, source_target_pairs={{1,0},{2,1},{3,2},{5,4},{6,5},{7,6},{9,8},{10,9},{11,10},{13,12},{... | collective-permute-start | bytes 1572872 | tf_op jit(solution)/shard_map/ppermute | solution.py:248
  166.2 29.8 %collective-permute-start.25 = (bf16[512,512]{1,0:T(8,128)(2,1)}, bf16[512,512]{1,0:T(8,128)(2,1)S(1)}, u32[]{:S(2)}, u32[]{:S(2)}) collective-permute-start(bf16[512,512]{1,0:T(8,128)(2,1)} %collective-permute-done.17.refs_2_), channel_id=1, source_target_pairs={{2,3},{6,7},{10,11},{14,15},{18,19},{22,23},{26,27},{30,31}} | collective-permute-start | bytes 1572872 | tf_op jit(solution)/shard_map/ppermute | solution.py:247
  166.9 30.6 %collective-permute-start.26 = (bf16[512,512]{1,0:T(8,128)(2,1)}, bf16[512,512]{1,0:T(8,128)(2,1)S(1)}, u32[]{:S(2)}, u32[]{:S(2)}) collective-permute-start(bf16[512,512]{1,0:T(8,128)(2,1)} %collective-permute-done.18.refs_5_), channel_id=1, source_target_pairs={{1,0},{5,4},{9,8},{13,12},{17,16},{21,20},{25,24},{29,28}} | collective-permute-start | bytes 1572872 | tf_op jit(solution)/shard_map/ppermute | solution.py:248
  187.1 30.1 %copy-start.7 = (bf16[512,512]{1,0:T(8,128)(2,1)}, bf16[512,512]{1,0:T(8,128)(2,1)S(1)}, u32[]{:S(2)}) copy-start(bf16[512,512]{1,0:T(8,128)(2,1)S(1)} %collective-permute-done.19.refs_1_) | copy-start | bytes 1572868
  187.1 30.1 %copy-start.8 = (bf16[512,512]{1,0:T(8,128)(2,1)}, bf16[512,512]{1,0:T(8,128)(2,1)S(1)}, u32[]{:S(2)}) copy-start(bf16[512,512]{1,0:T(8,128)(2,1)S(1)} %collective-permute-done.20.refs_4_) | copy-start | bytes 1572868
  187.1 30.1 %collective-permute-start.21 = (bf16[512,512]{1,0:T(8,128)(2,1)S(1)}, bf16[512,512]{1,0:T(8,128)(2,1)S(1)}, u32[]{:S(2)}, u32[]{:S(2)}) collective-permute-start(bf16[512,512]{1,0:T(8,128)(2,1)S(1)} %collective-permute-done.19.refs_1_), channel_id=1, source_target_pairs={{1,2},{2,3},{5,6},{6,7},{9,10},{10,11},{13,14},{14,15},{17,18},{18... | collective-permute-start | bytes 1572872 | tf_op jit(solution)/shard_map/ppermute | solution.py:247
  187.8 29.4 %collective-permute-start.22 = (bf16[512,512]{1,0:T(8,128)(2,1)S(1)}, bf16[512,512]{1,0:T(8,128)(2,1)S(1)}, u32[]{:S(2)}, u32[]{:S(2)}) collective-permute-start(bf16[512,512]{1,0:T(8,128)(2,1)S(1)} %bitcast.8), channel_id=1, source_target_pairs={{0,3},{4,7},{8,11},{12,15},{16,19},{20,23},{24,27},{28,31}} | collective-permute-start | bytes 1572872 | tf_op jit(solution)/shard_map/ppermute | solution.py:247
  194.7 25.1 %collective-permute-start.23 = (bf16[512,512]{1,0:T(8,128)(2,1)S(1)}, bf16[512,512]{1,0:T(8,128)(2,1)}, u32[]{:S(2)}, u32[]{:S(2)}) collective-permute-start(bf16[512,512]{1,0:T(8,128)(2,1)S(1)} %collective-permute-done.20.refs_4_), channel_id=1, source_target_pairs={{1,0},{2,1},{5,4},{6,5},{9,8},{10,9},{13,12},{14,13},{17,16},{18,1... | collective-permute-start | bytes 1572872 | tf_op jit(solution)/shard_map/ppermute | solution.py:248
  196.0 1.5 copy-start.9
  196.0 23.8 %collective-permute-start.24 = (bf16[512,512]{1,0:T(8,128)(2,1)S(1)}, bf16[512,512]{1,0:T(8,128)(2,1)}, u32[]{:S(2)}, u32[]{:S(2)}) collective-permute-start(bf16[512,512]{1,0:T(8,128)(2,1)S(1)} %bitcast.9), channel_id=1, source_target_pairs={{3,0},{7,4},{11,8},{15,12},{19,16},{23,20},{27,24},{31,28}} | collective-permute-start | bytes 1572872 | tf_op jit(solution)/shard_map/ppermute | solution.py:248
  197.5 0.8 copy-start.11
  217.2 2.6 %copy-start.10 = (bf16[512,512]{1,0:T(8,128)(2,1)}, bf16[512,512]{1,0:T(8,128)(2,1)S(1)}, u32[]{:S(2)}) copy-start(bf16[512,512]{1,0:T(8,128)(2,1)S(1)} %collective-permute-done.21.refs_2_) | copy-start | bytes 1572868
  217.2 2.5 %copy-start.12 = (bf16[512,512]{1,0:T(8,128)(2,1)}, bf16[512,512]{1,0:T(8,128)(2,1)S(1)}, u32[]{:S(2)}) copy-start(bf16[512,512]{1,0:T(8,128)(2,1)S(1)} %collective-permute-done.22.refs_3_) | copy-start | bytes 1572868
Sparse Core Ops, SparseCore 0:
  11.0 50.2 all-gather.2
  68.2 72.5 all-gather.4

commit v17 on v14

--- a/solution.py
+++ b/solution.py
@@ -11,7 +11,8 @@
 GROUP = 16
 STEP_A = 4
 PAD = 8
-WIDE = 512
+WIDE = 1024
+TALL = 512
 ANY = pl.BlockSpec(memory_space=pl.ANY)
 
 
@@ -130,17 +131,16 @@
         def _():
             out_copy(step - 2, slot).wait()
 
-        for g in range(STEP_A // wide):
-            blocks = []
-            for k in range(wide):
-                row = pl.multiple_of((step * STEP_A + g * wide + k) * pitch, 8)
-                blocks.append(pairs[pl.ds(row, count), :].astype(jnp.bfloat16))
-            both = jnp.concatenate(blocks, axis=1)
-            for m in range(count // 256):
-                rows = slice(m * 256, (m + 1) * 256)
-                mixed = jnp.dot(ladder[rows, :], both, preferred_element_type=jnp.float32)
-                total = (mixed + both[rows, :].astype(jnp.float32)).astype(jnp.bfloat16)
-                out_buf[slot, g * wide:(g + 1) * wide, :, rows] = total.T.reshape(wide, b_local, 256)
+        blocks = []
+        for k in range(STEP_A):
+            row = pl.multiple_of((step * STEP_A + k) * pitch, 8)
+            blocks.append(pairs[pl.ds(row, count), :].astype(jnp.bfloat16))
+        both = jnp.concatenate(blocks, axis=1)
+        for m in range(count // TALL):
+            rows = slice(m * TALL, (m + 1) * TALL)
+            mixed = jnp.dot(ladder[rows, :], both, preferred_element_type=jnp.float32)
+            total = (mixed + both[rows, :].astype(jnp.float32)).astype(jnp.bfloat16)
+            out_buf[slot, :, :, rows] = total.T.reshape(STEP_A, b_local, TALL)
         out_copy(step, slot).start()
 
     for step in range(max(steps - 2, 0), steps):
@@ -221,7 +221,7 @@
 
     per_part = occupied // cols
     plain = (b_local % 128 or WIDE % b_local or depth % 128 or cols < 4
-             or per_part * b_local % WIDE or chunks < 4 or chunks % 2)
+             or per_part * b_local % WIDE or occupied * occupied % TALL or chunks < 4 or chunks % 2)
 
     def flat(sides):
         right, left = sides

time: 245 us -> 246 us (level)
  no operation moved by 1% of the time
where the time goes in v17:
time: 246 us; the launch traced here: 245 us
  waiting for transfers between devices  97.1 us (39%)
  Pallas kernels  79.4 us (32%)
  starting transfers between devices  50.9 us (21%)
  between operations  13.9 us (6%)
    pallas_call x4, Pallas kernels, chunk_update(): pl.pallas_call(functools.partial(chunk_kernel, starts=starts, parts=parts...  75.1 us
    ppermute x3, waiting for transfers between devices, local(): lax.ppermute(arrived[s], 'col', [(c, (c + s) % cols) for c in range(cols)])  44.7 us
    ppermute x12, waiting for transfers between devices, hop(): lax.ppermute(left[source], 'col', [(c + step, c) for c in range(cols - st...  43.3 us
    ppermute x12, starting transfers between devices, hop(): lax.ppermute(right[source], 'col', [(c, c + step) for c in range(first, c...  25.4 us
    ppermute x12, starting transfers between devices, hop(): lax.ppermute(left[source], 'col', [(c + step, c) for c in range(cols - st...  15.7 us
    ppermute x12, waiting for transfers between devices, hop(): lax.ppermute(right[source], 'col', [(c, c + step) for c in range(first, c...  9.13 us
    all_to_all x1, starting transfers between devices, local(): lax.all_to_all(blocks, 'row', split_axis=0, concat_axis=0, tiled=True)  5.21 us
  transfers between devices with their start and end apart: 30, of which 13 were waited for; matrix products, arithmetic and copies ran while one was open for 1% of the time, Pallas kernels for 23%

profile of v17, /device:TPU:0, one launch (start us, length us, event | category | flops | bytes accessed | tf_op | source)
XLA Modules:
  0.0 244.7 jit_solution(15659400532002864588)
XLA Ops:
  6.5 4.3 %shard_map.37 = (bf16[8,4,4,16,512]{4,3,2,1,0:T(8,128)(2,1)}, bf16[256,1024]{1,0:T(8,128)(2,1)}, bf16[256,1024]{1,0:T(8,128)(2,1)}, bf16[256,1024]{1,0:T(8,128)(2,1)}, bf16[256,1024]{1,0:T(8,128)(2,1)}) custom-call(s32[1]{0:T(128)} %bitcast.own, bf16[4,8,4,16,512]{4,3,2,1,0:T(8,128)(2,1)} %bitcast.17, bf16[256,4096]{1,0:T(8,128)(2,1)} %w_ref.1), custom_call_target="tpu_custom_call" | custom-call | bytes 8388608 | tf_op jit(solution)/shard_map/pallas_call | solution.py:47
  10.8 0.0 all-gather.3.cloned.1.call-update
  10.9 5.2 %all-to-all-start = ((bf16[8,4,4,16,512]{4,3,2,1,0:T(8,128)(2,1)}), bf16[8,4,4,16,512]{4,3,2,1,0:T(8,128)(2,1)S(1)}, u32[]{:S(2)}, u32[]{:S(2)}) async-start(bf16[8,4,4,16,512]{4,3,2,1,0:T(8,128)(2,1)} %get-tuple-element.31), calls=%async_computation | async-start | bytes 4194304 | tf_op jit(solution)/shard_map/all_to_all | solution.py:215
  16.1 0.0 all-gather.5.cloned.1.call-start
  16.1 3.6 %collective-permute-start.10 = (bf16[256,1024]{1,0:T(8,128)(2,1)}, bf16[256,1024]{1,0:T(8,128)(2,1)S(1)}, u32[]{:S(2)}, u32[]{:S(2)}) collective-permute-start(bf16[256,1024]{1,0:T(8,128)(2,1)} %get-tuple-element.37), channel_id=1, source_target_pairs={{0,3},{1,0},{2,1},{3,2},{4,7},{5,4},{6,5},{7,6},{8,11},{9,8},{10,9... | collective-permute-start | bytes 1572872 | tf_op jit(solution)/shard_map/ppermute | solution.py:214
  19.7 0.0 collective-permute-start.8
  19.8 1.0 collective-permute-start.9
  20.8 11.6 %collective-permute-done.10 = bf16[256,1024]{1,0:T(8,128)(2,1)S(1)} collective-permute-done((bf16[256,1024]{1,0:T(8,128)(2,1)}, bf16[256,1024]{1,0:T(8,128)(2,1)S(1)}, u32[]{:S(2)}, u32[]{:S(2)}) %collective-permute-start.10) | collective-permute-done | bytes 524320 | tf_op jit(solution)/shard_map/ppermute | solution.py:214
  32.4 12.1 %collective-permute-done.8 = bf16[256,1024]{1,0:T(8,128)(2,1)S(1)} collective-permute-done((bf16[256,1024]{1,0:T(8,128)(2,1)}, bf16[256,1024]{1,0:T(8,128)(2,1)S(1)}, u32[]{:S(2)}, u32[]{:S(2)}) %collective-permute-start.8) | collective-permute-done | bytes 524320 | tf_op jit(solution)/shard_map/ppermute | solution.py:214
  44.4 21.0 %collective-permute-done.9 = bf16[256,1024]{1,0:T(8,128)(2,1)} collective-permute-done((bf16[256,1024]{1,0:T(8,128)(2,1)}, bf16[256,1024]{1,0:T(8,128)(2,1)}, u32[]{:S(2)}, u32[]{:S(2)}) %collective-permute-start.9) | collective-permute-done | bytes 524320 | tf_op jit(solution)/shard_map/ppermute | solution.py:214
  65.4 0.0 all-to-all-done
  65.4 2.3 pad_maximum_fusion
  67.7 0.0 all-gather.5.cloned.1.call-update
  67.8 0.2 fusion
  68.0 1.8 collective-permute-start.2
  69.8 1.3 collective-permute-start.4
  71.1 4.6 %collective-permute-start = (bf16[512,512]{1,0:T(8,128)(2,1)S(1)}, bf16[512,512]{1,0:T(8,128)(2,1)S(1)}, u32[]{:S(2)}, u32[]{:S(2)}) collective-permute-start(bf16[512,512]{1,0:T(8,128)(2,1)S(1)} %bitcast.14), channel_id=1, source_target_pairs={{0,1},{1,2},{2,3},{4,5},{5,6},{6,7},{8,9},{9,10},{10,11},{12,13},{... | collective-permute-start | bytes 1572872 | tf_op jit(solution)/shard_map/ppermute | solution.py:239
  75.7 1.3 collective-permute-start.14
  77.0 5.1 %collective-permute-done.2.refs_1_ = bf16[512,512]{1,0:T(8,128)(2,1)S(1)} collective-permute-done((bf16[512,512]{1,0:T(8,128)(2,1)S(1)}, bf16[512,512]{1,0:T(8,128)(2,1)S(1)}, u32[]{:S(2)}, u32[]{:S(2)}) %collective-permute-start.2) | collective-permute-done | bytes 524320 | tf_op jit(solution)/shard_map/ppermute | solution.py:239
  82.1 0.7 collective-permute-start.3
  82.8 3.7 %collective-permute-done.4.refs_4_ = bf16[512,512]{1,0:T(8,128)(2,1)S(1)} collective-permute-done((bf16[512,512]{1,0:T(8,128)(2,1)S(1)}, bf16[512,512]{1,0:T(8,128)(2,1)S(1)}, u32[]{:S(2)}, u32[]{:S(2)}) %collective-permute-start.4) | collective-permute-done | bytes 524320 | tf_op jit(solution)/shard_map/ppermute | solution.py:240
  86.6 1.3 collective-permute-start.5
  87.8 4.0 %collective-permute-done.refs_1_ = bf16[512,512]{1,0:T(8,128)(2,1)S(1)} collective-permute-done((bf16[512,512]{1,0:T(8,128)(2,1)S(1)}, bf16[512,512]{1,0:T(8,128)(2,1)S(1)}, u32[]{:S(2)}, u32[]{:S(2)}) %collective-permute-start) | collective-permute-done | bytes 524320 | tf_op jit(solution)/shard_map/ppermute | solution.py:239
  91.8 1.4 collective-permute-start.1
  93.3 4.5 %collective-permute-done.14.refs_4_ = bf16[512,512]{1,0:T(8,128)(2,1)S(1)} collective-permute-done((bf16[512,512]{1,0:T(8,128)(2,1)S(1)}, bf16[512,512]{1,0:T(8,128)(2,1)S(1)}, u32[]{:S(2)}, u32[]{:S(2)}) %collective-permute-start.14) | collective-permute-done | bytes 524320 | tf_op jit(solution)/shard_map/ppermute | solution.py:240
  97.8 1.3 collective-permute-start.15
  99.1 0.0 collective-permute-done.3.refs_2_
  99.1 9.9 %collective-permute-done.5.refs_5_ = bf16[512,512]{1,0:T(8,128)(2,1)S(1)} collective-permute-done((bf16[512,512]{1,0:T(8,128)(2,1)S(1)}, bf16[512,512]{1,0:T(8,128)(2,1)S(1)}, u32[]{:S(2)}, u32[]{:S(2)}) %collective-permute-start.5) | collective-permute-done | bytes 524320 | tf_op jit(solution)/shard_map/ppermute | solution.py:240
  109.0 3.8 %collective-permute-start.11 = (bf16[512,512]{1,0:T(8,128)(2,1)S(1)}, bf16[512,512]{1,0:T(8,128)(2,1)S(1)}, u32[]{:S(2)}, u32[]{:S(2)}) collective-permute-start(bf16[512,512]{1,0:T(8,128)(2,1)S(1)} %bitcast.11), channel_id=1, source_target_pairs={{0,1},{1,2},{2,3},{4,5},{5,6},{6,7},{8,9},{9,10},{10,11},{12,13},{... | collective-permute-start | bytes 1572872 | tf_op jit(solution)/shard_map/ppermute | solution.py:239
  112.9 1.3 collective-permute-start.12
  114.2 0.7 collective-permute-start.6
  114.9 0.0 collective-permute-done.1.refs_2_
  114.9 1.3 collective-permute-start.7
  116.2 4.2 %collective-permute-done.15.refs_5_ = bf16[512,512]{1,0:T(8,128)(2,1)} collective-permute-done((bf16[512,512]{1,0:T(8,128)(2,1)S(1)}, bf16[512,512]{1,0:T(8,128)(2,1)}, u32[]{:S(2)}, u32[]{:S(2)}) %collective-permute-start.15) | collective-permute-done | bytes 524320 | tf_op jit(solution)/shard_map/ppermute | solution.py:240
  120.4 1.5 collective-permute-start.13
  121.8 0.0 collective-permute-done.11.refs_10_.refs_1_
  121.8 1.3 collective-permute-start.16
  123.1 8.4 %collective-permute-done.12.refs_11_.refs_4_ = bf16[512,512]{1,0:T(8,128)(2,1)S(1)} collective-permute-done((bf16[512,512]{1,0:T(8,128)(2,1)S(1)}, bf16[512,512]{1,0:T(8,128)(2,1)S(1)}, u32[]{:S(2)}, u32[]{:S(2)}) %collective-permute-start.12) | collective-permute-done | bytes 524320 | tf_op jit(solution)/shard_map/ppermute | solution.py:240
  131.5 1.4 collective-permute-start.17
  132.9 0.0 collective-permute-done.6.refs_3_
  133.0 1.3 collective-permute-start.18
  134.3 8.5 %collective-permute-done.7.refs_6_ = bf16[512,512]{1,0:T(8,128)(2,1)} collective-permute-done((bf16[512,512]{1,0:T(8,128)(2,1)S(1)}, bf16[512,512]{1,0:T(8,128)(2,1)}, u32[]{:S(2)}, u32[]{:S(2)}) %collective-permute-start.7) | collective-permute-done | bytes 524320 | tf_op jit(solution)/shard_map/ppermute | solution.py:240
  142.8 18.8 %shard_map.38.refs_10_ = bf16[64,128,1024]{2,1,0:T(8,128)(2,1)} custom-call(s32[1]{0:T(128)} %bitcast.own, bf16[512,512]{1,0:T(8,128)(2,1)} %bitcast.20, bf16[512,512]{1,0:T(8,128)(2,1)} %copy-done.14, bf16[512,512]{1,0:T(8,128)(2,1)} %copy-done.16, bf16[512,512]{1,0:T(8,128)(2,1)} %copy-done.18, bf16[512,512]{1,0:T(8,128)(2,1)} %copy-done.15, ...), custom_call_target="tpu_custom_call" | custom-call | flops 12884901888 | bytes 25165824 | tf_op jit(solution)/shard_map/pallas_call | solution.py:163
  161.7 0.0 collective-permute-done.13.refs_3_
  161.7 0.0 collective-permute-done.16.refs_6_
  161.7 0.0 collective-permute-done.17.refs_2_
  161.7 1.8 collective-permute-done.18.refs_5_
  163.5 1.4 collective-permute-start.19
  164.8 1.3 collective-permute-start.20
  166.1 0.7 collective-permute-start.25
  166.8 1.3 collective-permute-start.26
  168.1 18.8 %shard_map.39.refs_10_ = bf16[64,128,1024]{2,1,0:T(8,128)(2,1)} custom-call(s32[1]{0:T(128)} %bitcast.own, bf16[512,512]{1,0:T(8,128)(2,1)} %bitcast.16, bf16[512,512]{1,0:T(8,128)(2,1)} %copy-done.3, bf16[512,512]{1,0:T(8,128)(2,1)} %collective-permute-done.1.refs_2_, ...), custom_call_target="tpu_custom_call", output_to_operand_aliasing={{}: (11, {})} | custom-call | flops 12884901888 | bytes 25165824 | tf_op jit(solution)/shard_map/pallas_call | solution.py:163
  186.9 0.0 collective-permute-done.19.refs_1_
  187.0 0.7 collective-permute-start.21
  187.7 6.7 %collective-permute-start.22 = (bf16[512,512]{1,0:T(8,128)(2,1)S(1)}, bf16[512,512]{1,0:T(8,128)(2,1)S(1)}, u32[]{:S(2)}, u32[]{:S(2)}) collective-permute-start(bf16[512,512]{1,0:T(8,128)(2,1)S(1)} %bitcast.8), channel_id=1, source_target_pairs={{0,3},{4,7},{8,11},{12,15},{16,19},{20,23},{24,27},{28,31}} | collective-permute-start | bytes 1572872 | tf_op jit(solution)/shard_map/ppermute | solution.py:239
  194.4 1.3 collective-permute-start.23
  195.7 0.0 collective-permute-done.25.refs_3_
  195.8 1.5 collective-permute-start.24
  197.2 0.0 collective-permute-done.26.refs_6_
  197.3 0.8 copy-done.11
  198.1 18.8 %shard_map.40.refs_10_ = bf16[64,128,1024]{2,1,0:T(8,128)(2,1)} custom-call(s32[1]{0:T(128)} %bitcast.own, bf16[512,512]{1,0:T(8,128)(2,1)} %bitcast.13, bf16[512,512]{1,0:T(8,128)(2,1)} %copy-done.5, bf16[512,512]{1,0:T(8,128)(2,1)} %collective-permute-done.17.refs_2_, bf16[512,512]{1,0:T(8,128)(2,1)} %copy-done.9, ...), custom_call_target="tpu_custom_call", output_to_operand_aliasing={{}: (11, {})} | custom-call | flops 12884901888 | bytes 25165824 | tf_op jit(solution)/shard_map/pallas_call | solution.py:163
  216.9 0.0 collective-permute-done.21.refs_2_
  216.9 2.2 collective-permute-done.23.refs_5_
  219.1 18.8 %shard_map.41 = bf16[64,128,1024]{2,1,0:T(8,128)(2,1)} custom-call(s32[1]{0:T(128)} %bitcast.own, bf16[512,512]{1,0:T(8,128)(2,1)} %bitcast.10, bf16[512,512]{1,0:T(8,128)(2,1)} %copy-done.7, bf16[512,512]{1,0:T(8,128)(2,1)} %copy-done.10, bf16[512,512]{1,0:T(8,128)(2,1)} %copy-done.12, bf16[512,512]{1,0:T(8,128)(2,1)} %copy-done.8, ...), custom_call_target="tpu_custom_call", output_to_operand_aliasing={{}: (11, {})} | custom-call | flops 12884901888 | bytes 25165824 | tf_op jit(solution)/shard_map/pallas_call | solution.py:163
  (43 shorter events, 0.1 us)
Async XLA Ops:
  6.5 136.3 %all-gather.3.cloned.1.call-start = ((), (), s32[]{:S(2)}) async-start(), calls=%async_computation.1 | async-start | bytes 4718592 | tf_op jit(solution)/shard_map/all_gather | solution.py:219
  10.9 54.6 %all-to-all-start = ((bf16[8,4,4,16,512]{4,3,2,1,0:T(8,128)(2,1)}), bf16[8,4,4,16,512]{4,3,2,1,0:T(8,128)(2,1)S(1)}, u32[]{:S(2)}, u32[]{:S(2)}) async-start(bf16[8,4,4,16,512]{4,3,2,1,0:T(8,128)(2,1)} %get-tuple-element.31), calls=%async_computation | async-start | bytes 4194304 | tf_op jit(solution)/shard_map/all_to_all | solution.py:215
  16.1 126.8 %all-gather.5.cloned.1.call-start = ((), (), s32[]{:S(2)}) async-start(), calls=%async_computation.2 | async-start | bytes 14155776 | tf_op jit(solution)/shard_map/all_gather | solution.py:219
  16.1 16.2 %collective-permute-start.10 = (bf16[256,1024]{1,0:T(8,128)(2,1)}, bf16[256,1024]{1,0:T(8,128)(2,1)S(1)}, u32[]{:S(2)}, u32[]{:S(2)}) collective-permute-start(bf16[256,1024]{1,0:T(8,128)(2,1)} %get-tuple-element.37), channel_id=1, source_target_pairs={{0,3},{1,0},{2,1},{3,2},{4,7},{5,4},{6,5},{7,6},{8,11},{9,8},{10,9... | collective-permute-start | bytes 1572872 | tf_op jit(solution)/shard_map/ppermute | solution.py:214
  19.7 24.7 %collective-permute-start.8 = (bf16[256,1024]{1,0:T(8,128)(2,1)}, bf16[256,1024]{1,0:T(8,128)(2,1)S(1)}, u32[]{:S(2)}, u32[]{:S(2)}) collective-permute-start(bf16[256,1024]{1,0:T(8,128)(2,1)} %get-tuple-element.35), channel_id=1, source_target_pairs={{0,1},{1,2},{2,3},{3,0},{4,5},{5,6},{6,7},{7,4},{8,9},{9,10},{10,1... | collective-permute-start | bytes 1572872 | tf_op jit(solution)/shard_map/ppermute | solution.py:214
  19.8 45.7 %collective-permute-start.9 = (bf16[256,1024]{1,0:T(8,128)(2,1)}, bf16[256,1024]{1,0:T(8,128)(2,1)}, u32[]{:S(2)}, u32[]{:S(2)}) collective-permute-start(bf16[256,1024]{1,0:T(8,128)(2,1)} %get-tuple-element.36), channel_id=1, source_target_pairs={{0,2},{1,3},{2,0},{3,1},{4,6},{5,7},{6,4},{7,5},{8,10},{9,11},{10,... | collective-permute-start | bytes 1572872 | tf_op jit(solution)/shard_map/ppermute | solution.py:214
  68.0 63.5 %copy-start.2 = (bf16[8,1,4,16,512]{4,3,2,1,0:T(8,128)(2,1)}, bf16[8,1,4,16,512]{4,3,2,1,0:T(8,128)(2,1)S(1)}, u32[]{:S(2)}) copy-start(bf16[8,1,4,16,512]{4,3,2,1,0:T(8,128)(2,1)S(1)} %get-tuple-element.60) | copy-start | bytes 1572868
  68.0 65.0 %copy-start.13 = (bf16[8,1,4,16,512]{4,3,2,1,0:T(8,128)(2,1)}, bf16[8,1,4,16,512]{4,3,2,1,0:T(8,128)(2,1)S(1)}, u32[]{:S(2)}) copy-start(bf16[8,1,4,16,512]{4,3,2,1,0:T(8,128)(2,1)S(1)} %get-tuple-element.59) | copy-start | bytes 1572868
  68.0 93.6 %copy-start.1 = (bf16[8,1,4,16,512]{4,3,2,1,0:T(8,128)(2,1)}, bf16[8,1,4,16,512]{4,3,2,1,0:T(8,128)(2,1)S(1)}, u32[]{:S(2)}) copy-start(bf16[8,1,4,16,512]{4,3,2,1,0:T(8,128)(2,1)S(1)} %get-tuple-element.58) | copy-start | bytes 1572868
  68.0 127.7 %copy-start = (bf16[8,1,4,16,512]{4,3,2,1,0:T(8,128)(2,1)}, bf16[8,1,4,16,512]{4,3,2,1,0:T(8,128)(2,1)S(1)}, u32[]{:S(2)}) copy-start(bf16[8,1,4,16,512]{4,3,2,1,0:T(8,128)(2,1)S(1)} %get-tuple-element.57) | copy-start | bytes 1572868
  68.0 14.1 %collective-permute-start.2 = (bf16[512,512]{1,0:T(8,128)(2,1)S(1)}, bf16[512,512]{1,0:T(8,128)(2,1)S(1)}, u32[]{:S(2)}, u32[]{:S(2)}) collective-permute-start(bf16[512,512]{1,0:T(8,128)(2,1)S(1)} %bitcast.18), channel_id=1, source_target_pairs={{0,1},{1,2},{2,3},{4,5},{5,6},{6,7},{8,9},{9,10},{10,11},{12,13},{... | collective-permute-start | bytes 1572872 | tf_op jit(solution)/shard_map/ppermute | solution.py:239
  69.8 16.8 %collective-permute-start.4 = (bf16[512,512]{1,0:T(8,128)(2,1)S(1)}, bf16[512,512]{1,0:T(8,128)(2,1)S(1)}, u32[]{:S(2)}, u32[]{:S(2)}) collective-permute-start(bf16[512,512]{1,0:T(8,128)(2,1)S(1)} %bitcast.19), channel_id=1, source_target_pairs={{1,0},{2,1},{3,2},{5,4},{6,5},{7,6},{9,8},{10,9},{11,10},{13,12},{... | collective-permute-start | bytes 1572872 | tf_op jit(solution)/shard_map/ppermute | solution.py:240
  71.1 20.7 %collective-permute-start = (bf16[512,512]{1,0:T(8,128)(2,1)S(1)}, bf16[512,512]{1,0:T(8,128)(2,1)S(1)}, u32[]{:S(2)}, u32[]{:S(2)}) collective-permute-start(bf16[512,512]{1,0:T(8,128)(2,1)S(1)} %bitcast.14), channel_id=1, source_target_pairs={{0,1},{1,2},{2,3},{4,5},{5,6},{6,7},{8,9},{9,10},{10,11},{12,13},{... | collective-permute-start | bytes 1572872 | tf_op jit(solution)/shard_map/ppermute | solution.py:239
  75.7 22.1 %collective-permute-start.14 = (bf16[512,512]{1,0:T(8,128)(2,1)S(1)}, bf16[512,512]{1,0:T(8,128)(2,1)S(1)}, u32[]{:S(2)}, u32[]{:S(2)}) collective-permute-start(bf16[512,512]{1,0:T(8,128)(2,1)S(1)} %bitcast.15), channel_id=1, source_target_pairs={{1,0},{2,1},{3,2},{5,4},{6,5},{7,6},{9,8},{10,9},{11,10},{13,12},{... | collective-permute-start | bytes 1572872 | tf_op jit(solution)/shard_map/ppermute | solution.py:240
  82.1 50.8 %copy-start.14 = (bf16[512,512]{1,0:T(8,128)(2,1)}, bf16[512,512]{1,0:T(8,128)(2,1)S(1)}, u32[]{:S(2)}) copy-start(bf16[512,512]{1,0:T(8,128)(2,1)S(1)} %collective-permute-done.2.refs_1_) | copy-start | bytes 1572868
  82.1 17.0 %collective-permute-start.3 = (bf16[512,512]{1,0:T(8,128)(2,1)S(1)}, bf16[512,512]{1,0:T(8,128)(2,1)S(1)}, u32[]{:S(2)}, u32[]{:S(2)}) collective-permute-start(bf16[512,512]{1,0:T(8,128)(2,1)S(1)} %collective-permute-done.2.refs_1_), channel_id=1, source_target_pairs={{1,2},{2,3},{5,6},{6,7},{9,10},{10,11},{13,14},{14,15},{17,18},{18... | collective-permute-start | bytes 1572872 | tf_op jit(solution)/shard_map/ppermute | solution.py:239
  86.6 47.7 %copy-start.15 = (bf16[512,512]{1,0:T(8,128)(2,1)}, bf16[512,512]{1,0:T(8,128)(2,1)S(1)}, u32[]{:S(2)}) copy-start(bf16[512,512]{1,0:T(8,128)(2,1)S(1)} %collective-permute-done.4.refs_4_) | copy-start | bytes 1572868
  86.6 22.5 %collective-permute-start.5 = (bf16[512,512]{1,0:T(8,128)(2,1)S(1)}, bf16[512,512]{1,0:T(8,128)(2,1)S(1)}, u32[]{:S(2)}, u32[]{:S(2)}) collective-permute-start(bf16[512,512]{1,0:T(8,128)(2,1)S(1)} %collective-permute-done.4.refs_4_), channel_id=1, source_target_pairs={{1,0},{2,1},{5,4},{6,5},{9,8},{10,9},{13,12},{14,13},{17,16},{18,1... | collective-permute-start | bytes 1572872 | tf_op jit(solution)/shard_map/ppermute | solution.py:240
  91.8 69.9 %copy-start.3 = (bf16[512,512]{1,0:T(8,128)(2,1)}, bf16[512,512]{1,0:T(8,128)(2,1)S(1)}, u32[]{:S(2)}) copy-start(bf16[512,512]{1,0:T(8,128)(2,1)S(1)} %collective-permute-done.refs_1_) | copy-start | bytes 1572868
  91.8 23.1 %collective-permute-start.1 = (bf16[512,512]{1,0:T(8,128)(2,1)S(1)}, bf16[512,512]{1,0:T(8,128)(2,1)}, u32[]{:S(2)}, u32[]{:S(2)}) collective-permute-start(bf16[512,512]{1,0:T(8,128)(2,1)S(1)} %collective-permute-done.refs_1_), channel_id=1, source_target_pairs={{1,2},{2,3},{5,6},{6,7},{9,10},{10,11},{13,14},{14,15},{17,18},{18... | collective-permute-start | bytes 1572872 | tf_op jit(solution)/shard_map/ppermute | solution.py:239
  97.8 63.9 %copy-start.4 = (bf16[512,512]{1,0:T(8,128)(2,1)}, bf16[512,512]{1,0:T(8,128)(2,1)S(1)}, u32[]{:S(2)}) copy-start(bf16[512,512]{1,0:T(8,128)(2,1)S(1)} %collective-permute-done.14.refs_4_) | copy-start | bytes 1572868
  97.8 22.6 %collective-permute-start.15 = (bf16[512,512]{1,0:T(8,128)(2,1)S(1)}, bf16[512,512]{1,0:T(8,128)(2,1)}, u32[]{:S(2)}, u32[]{:S(2)}) collective-permute-start(bf16[512,512]{1,0:T(8,128)(2,1)S(1)} %collective-permute-done.14.refs_4_), channel_id=1, source_target_pairs={{1,0},{2,1},{5,4},{6,5},{9,8},{10,9},{13,12},{14,13},{17,16},{18,1... | collective-permute-start | bytes 1572872 | tf_op jit(solution)/shard_map/ppermute | solution.py:240
  99.1 35.2 %copy-start.16 = (bf16[512,512]{1,0:T(8,128)(2,1)}, bf16[512,512]{1,0:T(8,128)(2,1)S(1)}, u32[]{:S(2)}) copy-start(bf16[512,512]{1,0:T(8,128)(2,1)S(1)} %collective-permute-done.3.refs_2_) | copy-start | bytes 1572868
  109.0 25.3 %copy-start.17 = (bf16[512,512]{1,0:T(8,128)(2,1)}, bf16[512,512]{1,0:T(8,128)(2,1)S(1)}, u32[]{:S(2)}) copy-start(bf16[512,512]{1,0:T(8,128)(2,1)S(1)} %collective-permute-done.5.refs_5_) | copy-start | bytes 1572868
  109.0 12.8 %collective-permute-start.11 = (bf16[512,512]{1,0:T(8,128)(2,1)S(1)}, bf16[512,512]{1,0:T(8,128)(2,1)S(1)}, u32[]{:S(2)}, u32[]{:S(2)}) collective-permute-start(bf16[512,512]{1,0:T(8,128)(2,1)S(1)} %bitcast.11), channel_id=1, source_target_pairs={{0,1},{1,2},{2,3},{4,5},{5,6},{6,7},{8,9},{9,10},{10,11},{12,13},{... | collective-permute-start | bytes 1572872 | tf_op jit(solution)/shard_map/ppermute | solution.py:239
  112.9 18.6 %collective-permute-start.12 = (bf16[512,512]{1,0:T(8,128)(2,1)S(1)}, bf16[512,512]{1,0:T(8,128)(2,1)S(1)}, u32[]{:S(2)}, u32[]{:S(2)}) collective-permute-start(bf16[512,512]{1,0:T(8,128)(2,1)S(1)} %bitcast.12), channel_id=1, source_target_pairs={{1,0},{2,1},{3,2},{5,4},{6,5},{7,6},{9,8},{10,9},{11,10},{13,12},{... | collective-permute-start | bytes 1572872 | tf_op jit(solution)/shard_map/ppermute | solution.py:240
  114.2 18.8 %collective-permute-start.6 = (bf16[512,512]{1,0:T(8,128)(2,1)S(1)}, bf16[512,512]{1,0:T(8,128)(2,1)S(1)}, u32[]{:S(2)}, u32[]{:S(2)}) collective-permute-start(bf16[512,512]{1,0:T(8,128)(2,1)S(1)} %collective-permute-done.3.refs_2_), channel_id=1, source_target_pairs={{2,3},{6,7},{10,11},{14,15},{18,19},{22,23},{26,27},{30,31}} | collective-permute-start | bytes 1572872 | tf_op jit(solution)/shard_map/ppermute | solution.py:239
  114.9 28.0 %collective-permute-start.7 = (bf16[512,512]{1,0:T(8,128)(2,1)S(1)}, bf16[512,512]{1,0:T(8,128)(2,1)}, u32[]{:S(2)}, u32[]{:S(2)}) collective-permute-start(bf16[512,512]{1,0:T(8,128)(2,1)S(1)} %collective-permute-done.5.refs_5_), channel_id=1, source_target_pairs={{1,0},{5,4},{9,8},{13,12},{17,16},{21,20},{25,24},{29,28}} | collective-permute-start | bytes 1572872 | tf_op jit(solution)/shard_map/ppermute | solution.py:240
  120.4 41.3 %collective-permute-start.13 = (bf16[512,512]{1,0:T(8,128)(2,1)}, bf16[512,512]{1,0:T(8,128)(2,1)}, u32[]{:S(2)}, u32[]{:S(2)}) collective-permute-start(bf16[512,512]{1,0:T(8,128)(2,1)} %collective-permute-done.1.refs_2_), channel_id=1, source_target_pairs={{2,3},{6,7},{10,11},{14,15},{18,19},{22,23},{26,27},{30,31}} | collective-permute-start | bytes 1572872 | tf_op jit(solution)/shard_map/ppermute | solution.py:239
  121.8 21.0 %copy-start.5 = (bf16[512,512]{1,0:T(8,128)(2,1)}, bf16[512,512]{1,0:T(8,128)(2,1)S(1)}, u32[]{:S(2)}) copy-start(bf16[512,512]{1,0:T(8,128)(2,1)S(1)} %collective-permute-done.11.refs_10_.refs_1_) | copy-start | bytes 1572868
  121.8 39.9 %collective-permute-start.16 = (bf16[512,512]{1,0:T(8,128)(2,1)}, bf16[512,512]{1,0:T(8,128)(2,1)}, u32[]{:S(2)}, u32[]{:S(2)}) collective-permute-start(bf16[512,512]{1,0:T(8,128)(2,1)} %collective-permute-done.15.refs_5_), channel_id=1, source_target_pairs={{1,0},{5,4},{9,8},{13,12},{17,16},{21,20},{25,24},{29,28}} | collective-permute-start | bytes 1572872 | tf_op jit(solution)/shard_map/ppermute | solution.py:240
  131.5 11.3 %copy-start.6 = (bf16[512,512]{1,0:T(8,128)(2,1)}, bf16[512,512]{1,0:T(8,128)(2,1)S(1)}, u32[]{:S(2)}) copy-start(bf16[512,512]{1,0:T(8,128)(2,1)S(1)} %collective-permute-done.12.refs_11_.refs_4_) | copy-start | bytes 1572868
  131.5 30.2 %collective-permute-start.17 = (bf16[512,512]{1,0:T(8,128)(2,1)S(1)}, bf16[512,512]{1,0:T(8,128)(2,1)}, u32[]{:S(2)}, u32[]{:S(2)}) collective-permute-start(bf16[512,512]{1,0:T(8,128)(2,1)S(1)} %collective-permute-done.11.refs_10_.refs_1_), channel_id=1, source_target_pairs={{1,2},{2,3},{5,6},{6,7},{9,10},{10,11},{13,14},{14,15},{17,18},{18... | collective-permute-start | bytes 1572872 | tf_op jit(solution)/shard_map/ppermute | solution.py:239
  133.0 1.3 copy-start.18
  133.0 30.5 %collective-permute-start.18 = (bf16[512,512]{1,0:T(8,128)(2,1)S(1)}, bf16[512,512]{1,0:T(8,128)(2,1)}, u32[]{:S(2)}, u32[]{:S(2)}) collective-permute-start(bf16[512,512]{1,0:T(8,128)(2,1)S(1)} %collective-permute-done.12.refs_11_.refs_4_), channel_id=1, source_target_pairs={{1,0},{2,1},{5,4},{6,5},{9,8},{10,9},{13,12},{14,13},{17,16},{18,1... | collective-permute-start | bytes 1572872 | tf_op jit(solution)/shard_map/ppermute | solution.py:240
  163.5 23.5 %collective-permute-start.19 = (bf16[512,512]{1,0:T(8,128)(2,1)S(1)}, bf16[512,512]{1,0:T(8,128)(2,1)S(1)}, u32[]{:S(2)}, u32[]{:S(2)}) collective-permute-start(bf16[512,512]{1,0:T(8,128)(2,1)S(1)} %bitcast.6), channel_id=1, source_target_pairs={{0,1},{1,2},{2,3},{4,5},{5,6},{6,7},{8,9},{9,10},{10,11},{12,13},{... | collective-permute-start | bytes 1572872 | tf_op jit(solution)/shard_map/ppermute | solution.py:239
  164.8 22.1 %collective-permute-start.20 = (bf16[512,512]{1,0:T(8,128)(2,1)S(1)}, bf16[512,512]{1,0:T(8,128)(2,1)S(1)}, u32[]{:S(2)}, u32[]{:S(2)}) collective-permute-start(bf16[512,512]{1,0:T(8,128)(2,1)S(1)} %bitcast.7), channel_id=1, source_target_pairs={{1,0},{2,1},{3,2},{5,4},{6,5},{7,6},{9,8},{10,9},{11,10},{13,12},{... | collective-permute-start | bytes 1572872 | tf_op jit(solution)/shard_map/ppermute | solution.py:240
  166.1 29.6 %collective-permute-start.25 = (bf16[512,512]{1,0:T(8,128)(2,1)}, bf16[512,512]{1,0:T(8,128)(2,1)S(1)}, u32[]{:S(2)}, u32[]{:S(2)}) collective-permute-start(bf16[512,512]{1,0:T(8,128)(2,1)} %collective-permute-done.17.refs_2_), channel_id=1, source_target_pairs={{2,3},{6,7},{10,11},{14,15},{18,19},{22,23},{26,27},{30,31}} | collective-permute-start | bytes 1572872 | tf_op jit(solution)/shard_map/ppermute | solution.py:239
  166.8 30.4 %collective-permute-start.26 = (bf16[512,512]{1,0:T(8,128)(2,1)}, bf16[512,512]{1,0:T(8,128)(2,1)S(1)}, u32[]{:S(2)}, u32[]{:S(2)}) collective-permute-start(bf16[512,512]{1,0:T(8,128)(2,1)} %collective-permute-done.18.refs_5_), channel_id=1, source_target_pairs={{1,0},{5,4},{9,8},{13,12},{17,16},{21,20},{25,24},{29,28}} | collective-permute-start | bytes 1572872 | tf_op jit(solution)/shard_map/ppermute | solution.py:240
  186.9 29.9 %copy-start.7 = (bf16[512,512]{1,0:T(8,128)(2,1)}, bf16[512,512]{1,0:T(8,128)(2,1)S(1)}, u32[]{:S(2)}) copy-start(bf16[512,512]{1,0:T(8,128)(2,1)S(1)} %collective-permute-done.19.refs_1_) | copy-start | bytes 1572868
  187.0 29.9 %copy-start.8 = (bf16[512,512]{1,0:T(8,128)(2,1)}, bf16[512,512]{1,0:T(8,128)(2,1)S(1)}, u32[]{:S(2)}) copy-start(bf16[512,512]{1,0:T(8,128)(2,1)S(1)} %collective-permute-done.20.refs_4_) | copy-start | bytes 1572868
  187.0 29.9 %collective-permute-start.21 = (bf16[512,512]{1,0:T(8,128)(2,1)S(1)}, bf16[512,512]{1,0:T(8,128)(2,1)S(1)}, u32[]{:S(2)}, u32[]{:S(2)}) collective-permute-start(bf16[512,512]{1,0:T(8,128)(2,1)S(1)} %collective-permute-done.19.refs_1_), channel_id=1, source_target_pairs={{1,2},{2,3},{5,6},{6,7},{9,10},{10,11},{13,14},{14,15},{17,18},{18... | collective-permute-start | bytes 1572872 | tf_op jit(solution)/shard_map/ppermute | solution.py:239
  187.7 29.2 %collective-permute-start.22 = (bf16[512,512]{1,0:T(8,128)(2,1)S(1)}, bf16[512,512]{1,0:T(8,128)(2,1)S(1)}, u32[]{:S(2)}, u32[]{:S(2)}) collective-permute-start(bf16[512,512]{1,0:T(8,128)(2,1)S(1)} %bitcast.8), channel_id=1, source_target_pairs={{0,3},{4,7},{8,11},{12,15},{16,19},{20,23},{24,27},{28,31}} | collective-permute-start | bytes 1572872 | tf_op jit(solution)/shard_map/ppermute | solution.py:239
  194.4 24.7 %collective-permute-start.23 = (bf16[512,512]{1,0:T(8,128)(2,1)S(1)}, bf16[512,512]{1,0:T(8,128)(2,1)}, u32[]{:S(2)}, u32[]{:S(2)}) collective-permute-start(bf16[512,512]{1,0:T(8,128)(2,1)S(1)} %collective-permute-done.20.refs_4_), channel_id=1, source_target_pairs={{1,0},{2,1},{5,4},{6,5},{9,8},{10,9},{13,12},{14,13},{17,16},{18,1... | collective-permute-start | bytes 1572872 | tf_op jit(solution)/shard_map/ppermute | solution.py:240
  195.7 1.5 copy-start.9
  195.8 23.3 %collective-permute-start.24 = (bf16[512,512]{1,0:T(8,128)(2,1)S(1)}, bf16[512,512]{1,0:T(8,128)(2,1)}, u32[]{:S(2)}, u32[]{:S(2)}) collective-permute-start(bf16[512,512]{1,0:T(8,128)(2,1)S(1)} %bitcast.9), channel_id=1, source_target_pairs={{3,0},{7,4},{11,8},{15,12},{19,16},{23,20},{27,24},{31,28}} | collective-permute-start | bytes 1572872 | tf_op jit(solution)/shard_map/ppermute | solution.py:240
  197.3 0.8 copy-start.11
  216.9 2.2 copy-start.10
  216.9 2.2 copy-start.12
Sparse Core Ops, SparseCore 0:
  11.0 50.2 all-gather.2
  67.9 72.5 all-gather.4

commit v18 on v17

--- a/solution.py
+++ b/solution.py
@@ -73,7 +73,7 @@
         return pltpu.make_async_copy(src, t_all.at[:, cols], t_sem.at[s])
 
     def w_copy(s, slot):
-        src = w_rest.at[:, (s - 1) * width:s * width] if s else w_own
+        src = w_rest.at[s - 1] if s else w_own
         return pltpu.make_async_copy(src, w_buf.at[slot], w_sem.at[slot])
 
     blocks = [lax.rem(own[0] - s + parts, parts) for s in range(parts)]
@@ -152,7 +152,7 @@
     rows = GROUP * occupied
     count = occupied * occupied
     k_all, width = panel_w[0].shape
-    parts = 1 + panel_w[1].shape[1] // width
+    parts = 1 + panel_w[1].shape[0]
     args = [*arrays, *panel_w, ladder, *after]
     aliases = {}
     if out is not None:
@@ -189,7 +189,7 @@
     right, left = pieces[1:parts], pieces[parts:]
     by_shift = [pieces[0]] + [jnp.where(own >= s, right[s - 1], left[parts - s - 1]) for s in range(1, parts)]
     panel_t = jnp.transpose(jnp.stack(by_shift, 0)[back], (1, 0, 2)).reshape(rows, -1)
-    cycle = jnp.dot(panel_t, jnp.concatenate(panel_w, axis=1), preferred_element_type=jnp.float32)
+    cycle = jnp.dot(panel_t, jnp.concatenate([panel_w[0], *panel_w[1]], axis=1), preferred_element_type=jnp.float32)
     cycle = cycle.astype(jnp.bfloat16).reshape(occupied, -1, parts, occupied // parts, b_local)[:, :, back]
     cycle = cycle.reshape(occupied, -1, occupied, b_local)
     a_count = cycle.shape[1]
@@ -216,7 +216,8 @@
 
     rest, _ = lax.optimization_barrier((arrived[1:], blocks))
     panel_w = [
-        lax.all_gather(part, "row", axis=0, tiled=True) for part in (arrived[0], jnp.concatenate(rest, axis=1))
+        lax.all_gather(arrived[0], "row", axis=0, tiled=True),
+        lax.all_gather(jnp.stack(rest), "row", axis=1, tiled=True),
     ]
 
     per_part = occupied // cols

time: 246 us -> 246 us (level)
  no operation moved by 1% of the time
where the time goes in v18:
time: 246 us; the launch traced here: 245 us
  waiting for transfers between devices  97.1 us (39%)
  Pallas kernels  79.4 us (32%)
  starting transfers between devices  50.9 us (21%)
  between operations  13.9 us (6%)
    pallas_call x4, Pallas kernels, chunk_update(): pl.pallas_call(functools.partial(chunk_kernel, starts=starts, parts=parts...  75.1 us
    ppermute x3, waiting for transfers between devices, local(): lax.ppermute(arrived[s], 'col', [(c, (c + s) % cols) for c in range(cols)])  44.7 us
    ppermute x12, waiting for transfers between devices, hop(): lax.ppermute(left[source], 'col', [(c + step, c) for c in range(cols - st...  43.3 us
    ppermute x12, starting transfers between devices, hop(): lax.ppermute(right[source], 'col', [(c, c + step) for c in range(first, c...  25.4 us
    ppermute x12, starting transfers between devices, hop(): lax.ppermute(left[source], 'col', [(c + step, c) for c in range(cols - st...  15.7 us
    ppermute x12, waiting for transfers between devices, hop(): lax.ppermute(right[source], 'col', [(c, c + step) for c in range(first, c...  9.13 us
    all_to_all x1, starting transfers between devices, local(): lax.all_to_all(blocks, 'row', split_axis=0, concat_axis=0, tiled=True)  5.21 us
  transfers between devices with their start and end apart: 30, of which 13 were waited for; matrix products, arithmetic and copies ran while one was open for 1% of the time, Pallas kernels for 23%

profile of v18, /device:TPU:0, one launch (start us, length us, event | category | flops | bytes accessed | tf_op | source)
XLA Modules:
  0.0 244.8 jit_solution(10744789814790145289)
XLA Ops:
  6.5 4.3 %shard_map.37 = (bf16[8,4,4,16,512]{4,3,2,1,0:T(8,128)(2,1)}, bf16[256,1024]{1,0:T(8,128)(2,1)}, bf16[256,1024]{1,0:T(8,128)(2,1)}, bf16[256,1024]{1,0:T(8,128)(2,1)}, bf16[256,1024]{1,0:T(8,128)(2,1)}) custom-call(s32[1]{0:T(128)} %bitcast.own, bf16[4,8,4,16,512]{4,3,2,1,0:T(8,128)(2,1)} %bitcast.20, bf16[256,4096]{1,0:T(8,128)(2,1)} %w_ref.1), custom_call_target="tpu_custom_call" | custom-call | bytes 8388608 | tf_op jit(solution)/shard_map/pallas_call | solution.py:47
  10.8 0.0 all-gather.3.cloned.1.call-update
  10.9 5.2 %all-to-all-start = ((bf16[8,4,4,16,512]{4,3,2,1,0:T(8,128)(2,1)}), bf16[8,4,4,16,512]{4,3,2,1,0:T(8,128)(2,1)S(1)}, u32[]{:S(2)}, u32[]{:S(2)}) async-start(bf16[8,4,4,16,512]{4,3,2,1,0:T(8,128)(2,1)} %get-tuple-element.31), calls=%async_computation | async-start | bytes 4194304 | tf_op jit(solution)/shard_map/all_to_all | solution.py:215
  16.1 0.0 all-gather.5.cloned.1.call-start
  16.1 3.6 %collective-permute-start.10 = (bf16[256,1024]{1,0:T(8,128)(2,1)}, bf16[256,1024]{1,0:T(8,128)(2,1)S(1)}, u32[]{:S(2)}, u32[]{:S(2)}) collective-permute-start(bf16[256,1024]{1,0:T(8,128)(2,1)} %get-tuple-element.37), channel_id=1, source_target_pairs={{0,3},{1,0},{2,1},{3,2},{4,7},{5,4},{6,5},{7,6},{8,11},{9,8},{10,9... | collective-permute-start | bytes 1572872 | tf_op jit(solution)/shard_map/ppermute | solution.py:214
  19.7 0.0 collective-permute-start.8
  19.8 1.0 collective-permute-start.9
  20.8 11.6 %collective-permute-done.10 = bf16[256,1024]{1,0:T(8,128)(2,1)S(1)} collective-permute-done((bf16[256,1024]{1,0:T(8,128)(2,1)}, bf16[256,1024]{1,0:T(8,128)(2,1)S(1)}, u32[]{:S(2)}, u32[]{:S(2)}) %collective-permute-start.10) | collective-permute-done | bytes 524320 | tf_op jit(solution)/shard_map/ppermute | solution.py:214
  32.4 12.1 %collective-permute-done.8 = bf16[256,1024]{1,0:T(8,128)(2,1)S(1)} collective-permute-done((bf16[256,1024]{1,0:T(8,128)(2,1)}, bf16[256,1024]{1,0:T(8,128)(2,1)S(1)}, u32[]{:S(2)}, u32[]{:S(2)}) %collective-permute-start.8) | collective-permute-done | bytes 524320 | tf_op jit(solution)/shard_map/ppermute | solution.py:214
  44.4 21.0 %collective-permute-done.9 = bf16[256,1024]{1,0:T(8,128)(2,1)} collective-permute-done((bf16[256,1024]{1,0:T(8,128)(2,1)}, bf16[256,1024]{1,0:T(8,128)(2,1)}, u32[]{:S(2)}, u32[]{:S(2)}) %collective-permute-start.9) | collective-permute-done | bytes 524320 | tf_op jit(solution)/shard_map/ppermute | solution.py:214
  65.4 0.0 all-to-all-done
  65.4 2.4 pad_maximum_fusion
  67.8 0.0 all-gather.5.cloned.1.call-update
  67.8 0.2 fusion
  68.1 1.8 collective-permute-start.2
  69.9 1.3 collective-permute-start.4
  71.2 4.6 %collective-permute-start = (bf16[512,512]{1,0:T(8,128)(2,1)S(1)}, bf16[512,512]{1,0:T(8,128)(2,1)S(1)}, u32[]{:S(2)}, u32[]{:S(2)}) collective-permute-start(bf16[512,512]{1,0:T(8,128)(2,1)S(1)} %bitcast.17), channel_id=1, source_target_pairs={{0,1},{1,2},{2,3},{4,5},{5,6},{6,7},{8,9},{9,10},{10,11},{12,13},{... | collective-permute-start | bytes 1572872 | tf_op jit(solution)/shard_map/ppermute | solution.py:240
  75.7 1.3 collective-permute-start.14
  77.0 5.1 %collective-permute-done.2.refs_1_ = bf16[512,512]{1,0:T(8,128)(2,1)S(1)} collective-permute-done((bf16[512,512]{1,0:T(8,128)(2,1)S(1)}, bf16[512,512]{1,0:T(8,128)(2,1)S(1)}, u32[]{:S(2)}, u32[]{:S(2)}) %collective-permute-start.2) | collective-permute-done | bytes 524320 | tf_op jit(solution)/shard_map/ppermute | solution.py:240
  82.2 0.7 collective-permute-start.3
  82.9 3.7 %collective-permute-done.4.refs_4_ = bf16[512,512]{1,0:T(8,128)(2,1)S(1)} collective-permute-done((bf16[512,512]{1,0:T(8,128)(2,1)S(1)}, bf16[512,512]{1,0:T(8,128)(2,1)S(1)}, u32[]{:S(2)}, u32[]{:S(2)}) %collective-permute-start.4) | collective-permute-done | bytes 524320 | tf_op jit(solution)/shard_map/ppermute | solution.py:241
  86.6 1.3 collective-permute-start.5
  87.9 4.0 %collective-permute-done.refs_1_ = bf16[512,512]{1,0:T(8,128)(2,1)S(1)} collective-permute-done((bf16[512,512]{1,0:T(8,128)(2,1)S(1)}, bf16[512,512]{1,0:T(8,128)(2,1)S(1)}, u32[]{:S(2)}, u32[]{:S(2)}) %collective-permute-start) | collective-permute-done | bytes 524320 | tf_op jit(solution)/shard_map/ppermute | solution.py:240
  91.9 1.4 collective-permute-start.1
  93.3 4.5 %collective-permute-done.14.refs_4_ = bf16[512,512]{1,0:T(8,128)(2,1)S(1)} collective-permute-done((bf16[512,512]{1,0:T(8,128)(2,1)S(1)}, bf16[512,512]{1,0:T(8,128)(2,1)S(1)}, u32[]{:S(2)}, u32[]{:S(2)}) %collective-permute-start.14) | collective-permute-done | bytes 524320 | tf_op jit(solution)/shard_map/ppermute | solution.py:241
  97.8 1.3 collective-permute-start.15
  99.1 0.0 collective-permute-done.3.refs_2_
  99.2 9.9 %collective-permute-done.5.refs_5_ = bf16[512,512]{1,0:T(8,128)(2,1)S(1)} collective-permute-done((bf16[512,512]{1,0:T(8,128)(2,1)S(1)}, bf16[512,512]{1,0:T(8,128)(2,1)S(1)}, u32[]{:S(2)}, u32[]{:S(2)}) %collective-permute-start.5) | collective-permute-done | bytes 524320 | tf_op jit(solution)/shard_map/ppermute | solution.py:241
  109.1 3.8 %collective-permute-start.11 = (bf16[512,512]{1,0:T(8,128)(2,1)S(1)}, bf16[512,512]{1,0:T(8,128)(2,1)S(1)}, u32[]{:S(2)}, u32[]{:S(2)}) collective-permute-start(bf16[512,512]{1,0:T(8,128)(2,1)S(1)} %bitcast.14), channel_id=1, source_target_pairs={{0,1},{1,2},{2,3},{4,5},{5,6},{6,7},{8,9},{9,10},{10,11},{12,13},{... | collective-permute-start | bytes 1572872 | tf_op jit(solution)/shard_map/ppermute | solution.py:240
  112.9 1.3 collective-permute-start.12
  114.2 0.7 collective-permute-start.6
  114.9 0.0 collective-permute-done.1.refs_2_
  114.9 1.3 collective-permute-start.7
  116.2 4.2 %collective-permute-done.15.refs_5_ = bf16[512,512]{1,0:T(8,128)(2,1)} collective-permute-done((bf16[512,512]{1,0:T(8,128)(2,1)S(1)}, bf16[512,512]{1,0:T(8,128)(2,1)}, u32[]{:S(2)}, u32[]{:S(2)}) %collective-permute-start.15) | collective-permute-done | bytes 524320 | tf_op jit(solution)/shard_map/ppermute | solution.py:241
  120.4 1.5 collective-permute-start.13
  121.9 0.0 collective-permute-done.11.refs_10_.refs_1_
  121.9 1.3 collective-permute-start.16
  123.2 8.4 %collective-permute-done.12.refs_11_.refs_4_ = bf16[512,512]{1,0:T(8,128)(2,1)S(1)} collective-permute-done((bf16[512,512]{1,0:T(8,128)(2,1)S(1)}, bf16[512,512]{1,0:T(8,128)(2,1)S(1)}, u32[]{:S(2)}, u32[]{:S(2)}) %collective-permute-start.12) | collective-permute-done | bytes 524320 | tf_op jit(solution)/shard_map/ppermute | solution.py:241
  131.6 1.4 collective-permute-start.17
  133.0 0.0 collective-permute-done.6.refs_3_
  133.0 1.3 collective-permute-start.18
  134.4 8.5 %collective-permute-done.7.refs_6_ = bf16[512,512]{1,0:T(8,128)(2,1)} collective-permute-done((bf16[512,512]{1,0:T(8,128)(2,1)S(1)}, bf16[512,512]{1,0:T(8,128)(2,1)}, u32[]{:S(2)}, u32[]{:S(2)}) %collective-permute-start.7) | collective-permute-done | bytes 524320 | tf_op jit(solution)/shard_map/ppermute | solution.py:241
  142.9 18.8 %shard_map.38.refs_10_ = bf16[64,128,1024]{2,1,0:T(8,128)(2,1)} custom-call(s32[1]{0:T(128)} %bitcast.own, bf16[512,512]{1,0:T(8,128)(2,1)} %bitcast.25, bf16[512,512]{1,0:T(8,128)(2,1)} %copy-done.14, bf16[512,512]{1,0:T(8,128)(2,1)} %copy-done.16, bf16[512,512]{1,0:T(8,128)(2,1)} %copy-done.18, bf16[512,512]{1,0:T(8,128)(2,1)} %copy-done.15, ...), custom_call_target="tpu_custom_call" | custom-call | flops 12884901888 | bytes 25165824 | tf_op jit(solution)/shard_map/pallas_call | solution.py:163
  161.7 0.0 collective-permute-done.13.refs_3_
  161.7 0.0 collective-permute-done.16.refs_6_
  161.8 0.0 collective-permute-done.17.refs_2_
  161.8 1.8 collective-permute-done.18.refs_5_
  163.5 1.4 collective-permute-start.19
  164.9 1.3 collective-permute-start.20
  166.2 0.7 collective-permute-start.25
  166.9 1.3 collective-permute-start.26
  168.2 18.8 %shard_map.39.refs_10_ = bf16[64,128,1024]{2,1,0:T(8,128)(2,1)} custom-call(s32[1]{0:T(128)} %bitcast.own, bf16[512,512]{1,0:T(8,128)(2,1)} %bitcast.19, bf16[512,512]{1,0:T(8,128)(2,1)} %copy-done.3, bf16[512,512]{1,0:T(8,128)(2,1)} %collective-permute-done.1.refs_2_, ...), custom_call_target="tpu_custom_call", output_to_operand_aliasing={{}: (11, {})} | custom-call | flops 12884901888 | bytes 25165824 | tf_op jit(solution)/shard_map/pallas_call | solution.py:163
  187.0 0.0 collective-permute-done.19.refs_1_
  187.0 0.0 collective-permute-done.20.refs_4_
  187.0 0.7 collective-permute-start.21
  187.7 6.7 %collective-permute-start.22 = (bf16[512,512]{1,0:T(8,128)(2,1)S(1)}, bf16[512,512]{1,0:T(8,128)(2,1)S(1)}, u32[]{:S(2)}, u32[]{:S(2)}) collective-permute-start(bf16[512,512]{1,0:T(8,128)(2,1)S(1)} %bitcast.11), channel_id=1, source_target_pairs={{0,3},{4,7},{8,11},{12,15},{16,19},{20,23},{24,27},{28,31}} | collective-permute-start | bytes 1572872 | tf_op jit(solution)/shard_map/ppermute | solution.py:240
  194.5 1.3 collective-permute-start.23
  195.8 1.5 collective-permute-start.24
  197.3 0.8 copy-done.11
  198.1 18.8 %shard_map.40.refs_10_ = bf16[64,128,1024]{2,1,0:T(8,128)(2,1)} custom-call(s32[1]{0:T(128)} %bitcast.own, bf16[512,512]{1,0:T(8,128)(2,1)} %bitcast.16, bf16[512,512]{1,0:T(8,128)(2,1)} %copy-done.5, bf16[512,512]{1,0:T(8,128)(2,1)} %collective-permute-done.17.refs_2_, bf16[512,512]{1,0:T(8,128)(2,1)} %copy-done.9, ...), custom_call_target="tpu_custom_call", output_to_operand_aliasing={{}: (11, {})} | custom-call | flops 12884901888 | bytes 25165824 | tf_op jit(solution)/shard_map/pallas_call | solution.py:163
  216.9 0.0 collective-permute-done.22.refs_3_
  216.9 2.2 collective-permute-done.23.refs_5_
  219.1 0.0 collective-permute-done.24.refs_6_
  219.1 18.8 %shard_map.41 = bf16[64,128,1024]{2,1,0:T(8,128)(2,1)} custom-call(s32[1]{0:T(128)} %bitcast.own, bf16[512,512]{1,0:T(8,128)(2,1)} %bitcast.13, bf16[512,512]{1,0:T(8,128)(2,1)} %copy-done.7, bf16[512,512]{1,0:T(8,128)(2,1)} %copy-done.10, bf16[512,512]{1,0:T(8,128)(2,1)} %copy-done.12, bf16[512,512]{1,0:T(8,128)(2,1)} %copy-done.8, ...), custom_call_target="tpu_custom_call", output_to_operand_aliasing={{}: (11, {})} | custom-call | flops 12884901888 | bytes 25165824 | tf_op jit(solution)/shard_map/pallas_call | solution.py:163
  (43 shorter events, 0.1 us)
Async XLA Ops:
  6.5 136.4 %all-gather.3.cloned.1.call-start = ((), (), s32[]{:S(2)}) async-start(), calls=%async_computation.1 | async-start | bytes 4718592 | tf_op jit(solution)/shard_map/all_gather | solution.py:219
  10.9 54.6 %all-to-all-start = ((bf16[8,4,4,16,512]{4,3,2,1,0:T(8,128)(2,1)}), bf16[8,4,4,16,512]{4,3,2,1,0:T(8,128)(2,1)S(1)}, u32[]{:S(2)}, u32[]{:S(2)}) async-start(bf16[8,4,4,16,512]{4,3,2,1,0:T(8,128)(2,1)} %get-tuple-element.31), calls=%async_computation | async-start | bytes 4194304 | tf_op jit(solution)/shard_map/all_to_all | solution.py:215
  16.1 126.8 %all-gather.5.cloned.1.call-start = ((), (), s32[]{:S(2)}) async-start(), calls=%async_computation.2 | async-start | bytes 14155776 | tf_op jit(solution)/shard_map/all_gather | solution.py:220
  16.1 16.2 %collective-permute-start.10 = (bf16[256,1024]{1,0:T(8,128)(2,1)}, bf16[256,1024]{1,0:T(8,128)(2,1)S(1)}, u32[]{:S(2)}, u32[]{:S(2)}) collective-permute-start(bf16[256,1024]{1,0:T(8,128)(2,1)} %get-tuple-element.37), channel_id=1, source_target_pairs={{0,3},{1,0},{2,1},{3,2},{4,7},{5,4},{6,5},{7,6},{8,11},{9,8},{10,9... | collective-permute-start | bytes 1572872 | tf_op jit(solution)/shard_map/ppermute | solution.py:214
  19.7 24.7 %collective-permute-start.8 = (bf16[256,1024]{1,0:T(8,128)(2,1)}, bf16[256,1024]{1,0:T(8,128)(2,1)S(1)}, u32[]{:S(2)}, u32[]{:S(2)}) collective-permute-start(bf16[256,1024]{1,0:T(8,128)(2,1)} %get-tuple-element.35), channel_id=1, source_target_pairs={{0,1},{1,2},{2,3},{3,0},{4,5},{5,6},{6,7},{7,4},{8,9},{9,10},{10,1... | collective-permute-start | bytes 1572872 | tf_op jit(solution)/shard_map/ppermute | solution.py:214
  19.8 45.7 %collective-permute-start.9 = (bf16[256,1024]{1,0:T(8,128)(2,1)}, bf16[256,1024]{1,0:T(8,128)(2,1)}, u32[]{:S(2)}, u32[]{:S(2)}) collective-permute-start(bf16[256,1024]{1,0:T(8,128)(2,1)} %get-tuple-element.36), channel_id=1, source_target_pairs={{0,2},{1,3},{2,0},{3,1},{4,6},{5,7},{6,4},{7,5},{8,10},{9,11},{10,... | collective-permute-start | bytes 1572872 | tf_op jit(solution)/shard_map/ppermute | solution.py:214
  68.0 63.5 %copy-start.2 = (bf16[8,1,4,16,512]{4,3,2,1,0:T(8,128)(2,1)}, bf16[8,1,4,16,512]{4,3,2,1,0:T(8,128)(2,1)S(1)}, u32[]{:S(2)}) copy-start(bf16[8,1,4,16,512]{4,3,2,1,0:T(8,128)(2,1)S(1)} %get-tuple-element.60) | copy-start | bytes 1572868
  68.1 65.0 %copy-start.13 = (bf16[8,1,4,16,512]{4,3,2,1,0:T(8,128)(2,1)}, bf16[8,1,4,16,512]{4,3,2,1,0:T(8,128)(2,1)S(1)}, u32[]{:S(2)}) copy-start(bf16[8,1,4,16,512]{4,3,2,1,0:T(8,128)(2,1)S(1)} %get-tuple-element.59) | copy-start | bytes 1572868
  68.1 93.6 %copy-start.1 = (bf16[8,1,4,16,512]{4,3,2,1,0:T(8,128)(2,1)}, bf16[8,1,4,16,512]{4,3,2,1,0:T(8,128)(2,1)S(1)}, u32[]{:S(2)}) copy-start(bf16[8,1,4,16,512]{4,3,2,1,0:T(8,128)(2,1)S(1)} %get-tuple-element.58) | copy-start | bytes 1572868
  68.1 127.7 %copy-start = (bf16[8,1,4,16,512]{4,3,2,1,0:T(8,128)(2,1)}, bf16[8,1,4,16,512]{4,3,2,1,0:T(8,128)(2,1)S(1)}, u32[]{:S(2)}) copy-start(bf16[8,1,4,16,512]{4,3,2,1,0:T(8,128)(2,1)S(1)} %get-tuple-element.57) | copy-start | bytes 1572868
  68.1 14.1 %collective-permute-start.2 = (bf16[512,512]{1,0:T(8,128)(2,1)S(1)}, bf16[512,512]{1,0:T(8,128)(2,1)S(1)}, u32[]{:S(2)}, u32[]{:S(2)}) collective-permute-start(bf16[512,512]{1,0:T(8,128)(2,1)S(1)} %bitcast.23), channel_id=1, source_target_pairs={{0,1},{1,2},{2,3},{4,5},{5,6},{6,7},{8,9},{9,10},{10,11},{12,13},{... | collective-permute-start | bytes 1572872 | tf_op jit(solution)/shard_map/ppermute | solution.py:240
  69.9 16.8 %collective-permute-start.4 = (bf16[512,512]{1,0:T(8,128)(2,1)S(1)}, bf16[512,512]{1,0:T(8,128)(2,1)S(1)}, u32[]{:S(2)}, u32[]{:S(2)}) collective-permute-start(bf16[512,512]{1,0:T(8,128)(2,1)S(1)} %bitcast.24), channel_id=1, source_target_pairs={{1,0},{2,1},{3,2},{5,4},{6,5},{7,6},{9,8},{10,9},{11,10},{13,12},{... | collective-permute-start | bytes 1572872 | tf_op jit(solution)/shard_map/ppermute | solution.py:241
  71.2 20.7 %collective-permute-start = (bf16[512,512]{1,0:T(8,128)(2,1)S(1)}, bf16[512,512]{1,0:T(8,128)(2,1)S(1)}, u32[]{:S(2)}, u32[]{:S(2)}) collective-permute-start(bf16[512,512]{1,0:T(8,128)(2,1)S(1)} %bitcast.17), channel_id=1, source_target_pairs={{0,1},{1,2},{2,3},{4,5},{5,6},{6,7},{8,9},{9,10},{10,11},{12,13},{... | collective-permute-start | bytes 1572872 | tf_op jit(solution)/shard_map/ppermute | solution.py:240
  75.7 22.1 %collective-permute-start.14 = (bf16[512,512]{1,0:T(8,128)(2,1)S(1)}, bf16[512,512]{1,0:T(8,128)(2,1)S(1)}, u32[]{:S(2)}, u32[]{:S(2)}) collective-permute-start(bf16[512,512]{1,0:T(8,128)(2,1)S(1)} %bitcast.18), channel_id=1, source_target_pairs={{1,0},{2,1},{3,2},{5,4},{6,5},{7,6},{9,8},{10,9},{11,10},{13,12},{... | collective-permute-start | bytes 1572872 | tf_op jit(solution)/shard_map/ppermute | solution.py:241
  82.2 50.8 %copy-start.14 = (bf16[512,512]{1,0:T(8,128)(2,1)}, bf16[512,512]{1,0:T(8,128)(2,1)S(1)}, u32[]{:S(2)}) copy-start(bf16[512,512]{1,0:T(8,128)(2,1)S(1)} %collective-permute-done.2.refs_1_) | copy-start | bytes 1572868
  82.2 17.0 %collective-permute-start.3 = (bf16[512,512]{1,0:T(8,128)(2,1)S(1)}, bf16[512,512]{1,0:T(8,128)(2,1)S(1)}, u32[]{:S(2)}, u32[]{:S(2)}) collective-permute-start(bf16[512,512]{1,0:T(8,128)(2,1)S(1)} %collective-permute-done.2.refs_1_), channel_id=1, source_target_pairs={{1,2},{2,3},{5,6},{6,7},{9,10},{10,11},{13,14},{14,15},{17,18},{18... | collective-permute-start | bytes 1572872 | tf_op jit(solution)/shard_map/ppermute | solution.py:240
  86.6 47.7 %copy-start.15 = (bf16[512,512]{1,0:T(8,128)(2,1)}, bf16[512,512]{1,0:T(8,128)(2,1)S(1)}, u32[]{:S(2)}) copy-start(bf16[512,512]{1,0:T(8,128)(2,1)S(1)} %collective-permute-done.4.refs_4_) | copy-start | bytes 1572868
  86.6 22.5 %collective-permute-start.5 = (bf16[512,512]{1,0:T(8,128)(2,1)S(1)}, bf16[512,512]{1,0:T(8,128)(2,1)S(1)}, u32[]{:S(2)}, u32[]{:S(2)}) collective-permute-start(bf16[512,512]{1,0:T(8,128)(2,1)S(1)} %collective-permute-done.4.refs_4_), channel_id=1, source_target_pairs={{1,0},{2,1},{5,4},{6,5},{9,8},{10,9},{13,12},{14,13},{17,16},{18,1... | collective-permute-start | bytes 1572872 | tf_op jit(solution)/shard_map/ppermute | solution.py:241
  91.9 69.8 %copy-start.3 = (bf16[512,512]{1,0:T(8,128)(2,1)}, bf16[512,512]{1,0:T(8,128)(2,1)S(1)}, u32[]{:S(2)}) copy-start(bf16[512,512]{1,0:T(8,128)(2,1)S(1)} %collective-permute-done.refs_1_) | copy-start | bytes 1572868
  91.9 23.1 %collective-permute-start.1 = (bf16[512,512]{1,0:T(8,128)(2,1)S(1)}, bf16[512,512]{1,0:T(8,128)(2,1)}, u32[]{:S(2)}, u32[]{:S(2)}) collective-permute-start(bf16[512,512]{1,0:T(8,128)(2,1)S(1)} %collective-permute-done.refs_1_), channel_id=1, source_target_pairs={{1,2},{2,3},{5,6},{6,7},{9,10},{10,11},{13,14},{14,15},{17,18},{18... | collective-permute-start | bytes 1572872 | tf_op jit(solution)/shard_map/ppermute | solution.py:240
  97.8 63.9 %copy-start.4 = (bf16[512,512]{1,0:T(8,128)(2,1)}, bf16[512,512]{1,0:T(8,128)(2,1)S(1)}, u32[]{:S(2)}) copy-start(bf16[512,512]{1,0:T(8,128)(2,1)S(1)} %collective-permute-done.14.refs_4_) | copy-start | bytes 1572868
  97.8 22.6 %collective-permute-start.15 = (bf16[512,512]{1,0:T(8,128)(2,1)S(1)}, bf16[512,512]{1,0:T(8,128)(2,1)}, u32[]{:S(2)}, u32[]{:S(2)}) collective-permute-start(bf16[512,512]{1,0:T(8,128)(2,1)S(1)} %collective-permute-done.14.refs_4_), channel_id=1, source_target_pairs={{1,0},{2,1},{5,4},{6,5},{9,8},{10,9},{13,12},{14,13},{17,16},{18,1... | collective-permute-start | bytes 1572872 | tf_op jit(solution)/shard_map/ppermute | solution.py:241
  99.1 35.2 %copy-start.16 = (bf16[512,512]{1,0:T(8,128)(2,1)}, bf16[512,512]{1,0:T(8,128)(2,1)S(1)}, u32[]{:S(2)}) copy-start(bf16[512,512]{1,0:T(8,128)(2,1)S(1)} %collective-permute-done.3.refs_2_) | copy-start | bytes 1572868
  109.1 25.3 %copy-start.17 = (bf16[512,512]{1,0:T(8,128)(2,1)}, bf16[512,512]{1,0:T(8,128)(2,1)S(1)}, u32[]{:S(2)}) copy-start(bf16[512,512]{1,0:T(8,128)(2,1)S(1)} %collective-permute-done.5.refs_5_) | copy-start | bytes 1572868
  109.1 12.8 %collective-permute-start.11 = (bf16[512,512]{1,0:T(8,128)(2,1)S(1)}, bf16[512,512]{1,0:T(8,128)(2,1)S(1)}, u32[]{:S(2)}, u32[]{:S(2)}) collective-permute-start(bf16[512,512]{1,0:T(8,128)(2,1)S(1)} %bitcast.14), channel_id=1, source_target_pairs={{0,1},{1,2},{2,3},{4,5},{5,6},{6,7},{8,9},{9,10},{10,11},{12,13},{... | collective-permute-start | bytes 1572872 | tf_op jit(solution)/shard_map/ppermute | solution.py:240
  112.9 18.6 %collective-permute-start.12 = (bf16[512,512]{1,0:T(8,128)(2,1)S(1)}, bf16[512,512]{1,0:T(8,128)(2,1)S(1)}, u32[]{:S(2)}, u32[]{:S(2)}) collective-permute-start(bf16[512,512]{1,0:T(8,128)(2,1)S(1)} %bitcast.15), channel_id=1, source_target_pairs={{1,0},{2,1},{3,2},{5,4},{6,5},{7,6},{9,8},{10,9},{11,10},{13,12},{... | collective-permute-start | bytes 1572872 | tf_op jit(solution)/shard_map/ppermute | solution.py:241
  114.2 18.8 %collective-permute-start.6 = (bf16[512,512]{1,0:T(8,128)(2,1)S(1)}, bf16[512,512]{1,0:T(8,128)(2,1)S(1)}, u32[]{:S(2)}, u32[]{:S(2)}) collective-permute-start(bf16[512,512]{1,0:T(8,128)(2,1)S(1)} %collective-permute-done.3.refs_2_), channel_id=1, source_target_pairs={{2,3},{6,7},{10,11},{14,15},{18,19},{22,23},{26,27},{30,31}} | collective-permute-start | bytes 1572872 | tf_op jit(solution)/shard_map/ppermute | solution.py:240
  114.9 28.0 %collective-permute-start.7 = (bf16[512,512]{1,0:T(8,128)(2,1)S(1)}, bf16[512,512]{1,0:T(8,128)(2,1)}, u32[]{:S(2)}, u32[]{:S(2)}) collective-permute-start(bf16[512,512]{1,0:T(8,128)(2,1)S(1)} %collective-permute-done.5.refs_5_), channel_id=1, source_target_pairs={{1,0},{5,4},{9,8},{13,12},{17,16},{21,20},{25,24},{29,28}} | collective-permute-start | bytes 1572872 | tf_op jit(solution)/shard_map/ppermute | solution.py:241
  120.4 41.3 %collective-permute-start.13 = (bf16[512,512]{1,0:T(8,128)(2,1)}, bf16[512,512]{1,0:T(8,128)(2,1)}, u32[]{:S(2)}, u32[]{:S(2)}) collective-permute-start(bf16[512,512]{1,0:T(8,128)(2,1)} %collective-permute-done.1.refs_2_), channel_id=1, source_target_pairs={{2,3},{6,7},{10,11},{14,15},{18,19},{22,23},{26,27},{30,31}} | collective-permute-start | bytes 1572872 | tf_op jit(solution)/shard_map/ppermute | solution.py:240
  121.9 21.0 %copy-start.5 = (bf16[512,512]{1,0:T(8,128)(2,1)}, bf16[512,512]{1,0:T(8,128)(2,1)S(1)}, u32[]{:S(2)}) copy-start(bf16[512,512]{1,0:T(8,128)(2,1)S(1)} %collective-permute-done.11.refs_10_.refs_1_) | copy-start | bytes 1572868
  121.9 39.9 %collective-permute-start.16 = (bf16[512,512]{1,0:T(8,128)(2,1)}, bf16[512,512]{1,0:T(8,128)(2,1)}, u32[]{:S(2)}, u32[]{:S(2)}) collective-permute-start(bf16[512,512]{1,0:T(8,128)(2,1)} %collective-permute-done.15.refs_5_), channel_id=1, source_target_pairs={{1,0},{5,4},{9,8},{13,12},{17,16},{21,20},{25,24},{29,28}} | collective-permute-start | bytes 1572872 | tf_op jit(solution)/shard_map/ppermute | solution.py:241
  131.6 11.3 %copy-start.6 = (bf16[512,512]{1,0:T(8,128)(2,1)}, bf16[512,512]{1,0:T(8,128)(2,1)S(1)}, u32[]{:S(2)}) copy-start(bf16[512,512]{1,0:T(8,128)(2,1)S(1)} %collective-permute-done.12.refs_11_.refs_4_) | copy-start | bytes 1572868
  131.6 30.2 %collective-permute-start.17 = (bf16[512,512]{1,0:T(8,128)(2,1)S(1)}, bf16[512,512]{1,0:T(8,128)(2,1)}, u32[]{:S(2)}, u32[]{:S(2)}) collective-permute-start(bf16[512,512]{1,0:T(8,128)(2,1)S(1)} %collective-permute-done.11.refs_10_.refs_1_), channel_id=1, source_target_pairs={{1,2},{2,3},{5,6},{6,7},{9,10},{10,11},{13,14},{14,15},{17,18},{18... | collective-permute-start | bytes 1572872 | tf_op jit(solution)/shard_map/ppermute | solution.py:240
  133.0 1.3 copy-start.18
  133.0 30.5 %collective-permute-start.18 = (bf16[512,512]{1,0:T(8,128)(2,1)S(1)}, bf16[512,512]{1,0:T(8,128)(2,1)}, u32[]{:S(2)}, u32[]{:S(2)}) collective-permute-start(bf16[512,512]{1,0:T(8,128)(2,1)S(1)} %collective-permute-done.12.refs_11_.refs_4_), channel_id=1, source_target_pairs={{1,0},{2,1},{5,4},{6,5},{9,8},{10,9},{13,12},{14,13},{17,16},{18,1... | collective-permute-start | bytes 1572872 | tf_op jit(solution)/shard_map/ppermute | solution.py:241
  163.5 23.5 %collective-permute-start.19 = (bf16[512,512]{1,0:T(8,128)(2,1)S(1)}, bf16[512,512]{1,0:T(8,128)(2,1)S(1)}, u32[]{:S(2)}, u32[]{:S(2)}) collective-permute-start(bf16[512,512]{1,0:T(8,128)(2,1)S(1)} %bitcast.9), channel_id=1, source_target_pairs={{0,1},{1,2},{2,3},{4,5},{5,6},{6,7},{8,9},{9,10},{10,11},{12,13},{... | collective-permute-start | bytes 1572872 | tf_op jit(solution)/shard_map/ppermute | solution.py:240
  164.9 22.1 %collective-permute-start.20 = (bf16[512,512]{1,0:T(8,128)(2,1)S(1)}, bf16[512,512]{1,0:T(8,128)(2,1)S(1)}, u32[]{:S(2)}, u32[]{:S(2)}) collective-permute-start(bf16[512,512]{1,0:T(8,128)(2,1)S(1)} %bitcast.10), channel_id=1, source_target_pairs={{1,0},{2,1},{3,2},{5,4},{6,5},{7,6},{9,8},{10,9},{11,10},{13,12},{... | collective-permute-start | bytes 1572872 | tf_op jit(solution)/shard_map/ppermute | solution.py:241
  166.2 29.6 %collective-permute-start.25 = (bf16[512,512]{1,0:T(8,128)(2,1)}, bf16[512,512]{1,0:T(8,128)(2,1)S(1)}, u32[]{:S(2)}, u32[]{:S(2)}) collective-permute-start(bf16[512,512]{1,0:T(8,128)(2,1)} %collective-permute-done.17.refs_2_), channel_id=1, source_target_pairs={{2,3},{6,7},{10,11},{14,15},{18,19},{22,23},{26,27},{30,31}} | collective-permute-start | bytes 1572872 | tf_op jit(solution)/shard_map/ppermute | solution.py:240
  166.9 30.4 %collective-permute-start.26 = (bf16[512,512]{1,0:T(8,128)(2,1)}, bf16[512,512]{1,0:T(8,128)(2,1)S(1)}, u32[]{:S(2)}, u32[]{:S(2)}) collective-permute-start(bf16[512,512]{1,0:T(8,128)(2,1)} %collective-permute-done.18.refs_5_), channel_id=1, source_target_pairs={{1,0},{5,4},{9,8},{13,12},{17,16},{21,20},{25,24},{29,28}} | collective-permute-start | bytes 1572872 | tf_op jit(solution)/shard_map/ppermute | solution.py:241
  187.0 29.9 %copy-start.7 = (bf16[512,512]{1,0:T(8,128)(2,1)}, bf16[512,512]{1,0:T(8,128)(2,1)S(1)}, u32[]{:S(2)}) copy-start(bf16[512,512]{1,0:T(8,128)(2,1)S(1)} %collective-permute-done.19.refs_1_) | copy-start | bytes 1572868
  187.0 29.9 %copy-start.8 = (bf16[512,512]{1,0:T(8,128)(2,1)}, bf16[512,512]{1,0:T(8,128)(2,1)S(1)}, u32[]{:S(2)}) copy-start(bf16[512,512]{1,0:T(8,128)(2,1)S(1)} %collective-permute-done.20.refs_4_) | copy-start | bytes 1572868
  187.0 29.9 %collective-permute-start.21 = (bf16[512,512]{1,0:T(8,128)(2,1)S(1)}, bf16[512,512]{1,0:T(8,128)(2,1)S(1)}, u32[]{:S(2)}, u32[]{:S(2)}) collective-permute-start(bf16[512,512]{1,0:T(8,128)(2,1)S(1)} %collective-permute-done.19.refs_1_), channel_id=1, source_target_pairs={{1,2},{2,3},{5,6},{6,7},{9,10},{10,11},{13,14},{14,15},{17,18},{18... | collective-permute-start | bytes 1572872 | tf_op jit(solution)/shard_map/ppermute | solution.py:240
  187.7 29.2 %collective-permute-start.22 = (bf16[512,512]{1,0:T(8,128)(2,1)S(1)}, bf16[512,512]{1,0:T(8,128)(2,1)S(1)}, u32[]{:S(2)}, u32[]{:S(2)}) collective-permute-start(bf16[512,512]{1,0:T(8,128)(2,1)S(1)} %bitcast.11), channel_id=1, source_target_pairs={{0,3},{4,7},{8,11},{12,15},{16,19},{20,23},{24,27},{28,31}} | collective-permute-start | bytes 1572872 | tf_op jit(solution)/shard_map/ppermute | solution.py:240
  194.5 24.7 %collective-permute-start.23 = (bf16[512,512]{1,0:T(8,128)(2,1)S(1)}, bf16[512,512]{1,0:T(8,128)(2,1)}, u32[]{:S(2)}, u32[]{:S(2)}) collective-permute-start(bf16[512,512]{1,0:T(8,128)(2,1)S(1)} %collective-permute-done.20.refs_4_), channel_id=1, source_target_pairs={{1,0},{2,1},{5,4},{6,5},{9,8},{10,9},{13,12},{14,13},{17,16},{18,1... | collective-permute-start | bytes 1572872 | tf_op jit(solution)/shard_map/ppermute | solution.py:241
  195.8 1.5 copy-start.9
  195.8 23.3 %collective-permute-start.24 = (bf16[512,512]{1,0:T(8,128)(2,1)S(1)}, bf16[512,512]{1,0:T(8,128)(2,1)}, u32[]{:S(2)}, u32[]{:S(2)}) collective-permute-start(bf16[512,512]{1,0:T(8,128)(2,1)S(1)} %bitcast.12), channel_id=1, source_target_pairs={{3,0},{7,4},{11,8},{15,12},{19,16},{23,20},{27,24},{31,28}} | collective-permute-start | bytes 1572872 | tf_op jit(solution)/shard_map/ppermute | solution.py:241
  197.3 0.8 copy-start.11
  216.9 2.2 copy-start.10
  216.9 2.2 copy-start.12
Sparse Core Ops, SparseCore 0:
  11.0 50.2 all-gather.2
  67.9 72.5 all-gather.4
